TPU v7x, 256 devices: a whole 4x4x8 slice. The times are simulated.
256 devices in a mesh: gz: 128 (over y, x, z), xy: 2 (over core).
Axes of the slice: x: 4, y: 4, z: 8, core: 2. Of those that a mesh axis runs over, the one named last changes fastest.
Arguments:
- right_side: float32 [256, 512, 640], P('gz', 'xy'), may hold values from -6 to 6
- labels: int32 [256, 512, 640], P('gz', 'xy'), may hold values from 0 to 2
- fraction: float32 [256, 512, 640], P('gz', 'xy'), may hold values from 0.5 to 2
Outputs:
- fine_iterate: float32 [256, 512, 640], P('gz', 'xy')
- plane_iterate: float32 [128, 512, 640], P('gz', 'xy')
- coarse_return: float32 [128, 512, 640], P('gz', 'xy')
Inputs may be any that keep to these rules, and one draw needn't show every extreme that they name: `labels`: 0 marks pore, 1 grain, 2 clay.
All inputs are finite; a program needn't handle non-finite values.
Results may differ from a plain program's by a relative error of at most 0.00002.
Values sent between devices are 32-bit elements; how exact they have to be, the bound alone decides.
No kernel may reach another device: no remote copies, remote signals or barrier semaphores. Data moves between devices by JAX's collectives and lax.ppermute only.
A program may use at most 64 MiB of HBM per device.

v0:
```python
from functools import partial

import jax
import jax.numpy as jnp
from jax import lax
from jax.sharding import PartitionSpec as P

LEVELS = 5


damping = 0.8
pore_value = 1.0
grain_value = 0.1
clay_value = 0.3


def with_halo(block, sides, width):
    for axis, dim in sides:
        count = lax.axis_size(axis)
        forward = [(i, i + 1) for i in range(count - 1)]
        backward = [(target, source) for source, target in forward]
        low = lax.ppermute(
            lax.slice_in_dim(block, block.shape[dim] - width, None, axis=dim), axis, forward
        )
        high = lax.ppermute(lax.slice_in_dim(block, 0, width, axis=dim), axis, backward)
        block = jnp.concatenate([low, block, high], axis=dim)
    return block


def shifted(value, axis, by):
    size = lax.axis_size(axis)
    pairs = [(i, i + by) for i in range(size) if 0 <= i + by < size]
    return lax.ppermute(value, axis, pairs)


def harmonic(one_side, other_side):
    return 2.0 * one_side * other_side / (one_side + other_side)


def later_along(values, along):
    extent = values.shape[along]
    trimmed = lax.slice_in_dim(values, 1, extent, axis=along)
    filler = jnp.zeros_like(lax.slice_in_dim(values, 0, 1, axis=along))
    return jnp.concatenate([trimmed, filler], axis=along)


def earlier_along(values, along):
    extent = values.shape[along]
    trimmed = lax.slice_in_dim(values, 0, extent - 1, axis=along)
    filler = jnp.zeros_like(lax.slice_in_dim(values, 0, 1, axis=along))
    return jnp.concatenate([filler, trimmed], axis=along)


def conductivity(labels, fraction):
    base_value = jnp.where(labels == 0, pore_value, jnp.where(labels == 1, grain_value, clay_value))
    return base_value.astype(fraction.dtype) * fraction


def diagonal_of(face_set):
    face_north = face_set[2]
    face_south = earlier_along(face_north, face_north.ndim - 1)
    return face_set[0] + face_set[1] + face_north + face_south + face_set[3] + face_set[4]


def combine_terms(values, face_set, diagonal, east_rows, west_rows, down_plane, up_plane):
    last_axis = values.ndim - 1
    face_north = face_set[2]
    face_south = earlier_along(face_north, last_axis)
    north_cells = later_along(values, last_axis)
    south_cells = earlier_along(values, last_axis)
    return (
        diagonal * values
        - face_set[0] * east_rows
        - face_set[1] * west_rows
        - face_north * north_cells
        - face_south * south_cells
        - face_set[3] * down_plane
        - face_set[4] * up_plane
    )


def fine_apply(values, face_set, diagonal):
    padded = with_halo(values, (("gz", 0), ("xy", 1)), 1)
    return combine_terms(
        values,
        face_set,
        diagonal,
        padded[1:-1, 2:],
        padded[1:-1, :-2],
        padded[:-2, 1:-1],
        padded[2:, 1:-1],
    )


def plane_apply(values, face_set, diagonal, distance):
    widened = with_halo(values, (("xy", 0),), 1)
    down_plane = shifted(values, "gz", distance)
    up_plane = shifted(values, "gz", -distance)
    return combine_terms(
        values, face_set, diagonal, widened[2:], widened[:-2], down_plane, up_plane
    )


def smooth(source, face_set, diagonal, apply_rule):
    iterate = damping * source / diagonal
    iterate = iterate + damping * (source - apply_rule(iterate, face_set, diagonal)) / diagonal
    return iterate


def on_device(right_side, labels, fraction):
    conduct = conductivity(labels, fraction)
    position = lax.axis_index("gz")
    at_bottom = position == 0
    at_top = position == lax.axis_size("gz") - 1
    padded = with_halo(conduct, (("gz", 0), ("xy", 1)), 1)
    planes = lax.broadcasted_iota(jnp.int32, conduct.shape, 0)
    face_set = (
        harmonic(conduct, padded[1:-1, 2:]),
        harmonic(conduct, padded[1:-1, :-2]),
        harmonic(conduct, later_along(conduct, 2)),
        jnp.where((planes == 0) & at_bottom, 2.0 * conduct, harmonic(conduct, padded[:-2, 1:-1])),
        jnp.where(
            (planes == conduct.shape[0] - 1) & at_top,
            2.0 * conduct,
            harmonic(conduct, padded[2:, 1:-1]),
        ),
    )
    diagonal = diagonal_of(face_set)
    fine_iterate = smooth(right_side, face_set, diagonal, fine_apply)
    residual = right_side - fine_apply(fine_iterate, face_set, diagonal)
    source = residual[0] + residual[1]
    face_set = jnp.stack(
        [
            face_set[0][0] + face_set[0][1],
            face_set[1][0] + face_set[1][1],
            face_set[2][0] + face_set[2][1],
            face_set[3][0],
            face_set[4][1],
        ]
    )
    iterates = []
    distance = 1
    for level_no in range(1, LEVELS + 1):
        diagonal = diagonal_of(face_set)
        apply_rule = partial(plane_apply, distance=distance)
        iterate = smooth(source, face_set, diagonal, apply_rule)
        iterates.append(iterate)
        if level_no < LEVELS:
            residual = source - apply_rule(iterate, face_set, diagonal)
            bundle = jnp.concatenate([residual[None], face_set], axis=0)
            high_part = shifted(bundle, "gz", -distance)
            source = bundle[0] + high_part[0]
            face_set = jnp.stack(
                [
                    bundle[1] + high_part[1],
                    bundle[2] + high_part[2],
                    bundle[3] + high_part[3],
                    bundle[4],
                    high_part[5],
                ]
            )
            distance = distance * 2
    running = jnp.zeros_like(iterates[0])
    for level_no in range(LEVELS, 1, -1):
        running = running + iterates[level_no - 1]
        half_span = 2 ** (level_no - 2)
        incoming = shifted(running, "gz", half_span)
        running = jnp.where(position % (2 * half_span) == half_span, incoming, running)
    return (fine_iterate, iterates[0][None], running[None])


def solution(mesh):
    return jax.shard_map(
        on_device,
        mesh=mesh,
        in_specs=(P("gz", "xy", None), P("gz", "xy", None), P("gz", "xy", None)),
        out_specs=(P("gz", "xy", None), P("gz", "xy", None), P("gz", "xy", None)),
        check_vma=False,
    )
```

profile of v0, /device:TPU:8, one launch (start us, length us, event | category | flops | bytes accessed | tf_op | source)
XLA Modules:
  0.0 1053.2 jit_solution(12687613814268923369)
XLA Ops:
  7.5 7.9 collective-permute-start.1
  16.1 12.3 %collective-permute-done = f32[1,256,640]{2,1,0:T(8,128)S(1)} collective-permute-done((f32[1,256,640]{2,1,0:T(8,128)}, f32[1,256,640]{2,1,0:T(8,128)S(1)}, u32[]{:S(2)}, u32[]{:S(2)}) %collective-permute-start) | collective-permute-done | bytes 655392 | tf_op jit(solution)/shard_map/ppermute | solution.py:22
  41.0 8.6 collective-permute-start.5
  49.6 13.3 %collective-permute-done.4 = f32[1,256,640]{2,1,0:T(8,128)S(1)} collective-permute-done((f32[1,256,640]{2,1,0:T(8,128)S(1)}, f32[1,256,640]{2,1,0:T(8,128)S(1)}, u32[]{:S(2)}, u32[]{:S(2)}) %collective-permute-start.4) | collective-permute-done | bytes 655392 | tf_op jit(solution)/shard_map/ppermute | solution.py:22
  73.6 8.6 collective-permute-start.9
  82.3 13.2 %collective-permute-done.8 = f32[1,256,640]{2,1,0:T(8,128)S(1)} collective-permute-done((f32[1,256,640]{2,1,0:T(8,128)S(1)}, f32[1,256,640]{2,1,0:T(8,128)S(1)}, u32[]{:S(2)}, u32[]{:S(2)}) %collective-permute-start.8) | collective-permute-done | bytes 655392 | tf_op jit(solution)/shard_map/ppermute | solution.py:22
  106.3 8.6 collective-permute-start.15
  120.1 8.1 collective-permute-done.14
  132.2 8.6 collective-permute-start.19
  155.6 8.6 collective-permute-start.20
  164.2 83.0 %collective-permute-done.20 = f32[6,256,640]{2,1,0:T(8,128)S(1)} collective-permute-done((f32[6,256,640]{2,1,0:T(8,128)S(1)}, f32[6,256,640]{2,1,0:T(8,128)S(1)}, u32[]{:S(2)}, u32[]{:S(2)}) %collective-permute-start.20) | collective-permute-done | bytes 3932192 | tf_op jit(solution)/shard_map/ppermute | solution.py:33
  249.6 9.0 collective-permute-start.24
  263.8 19.3 %collective-permute-done.23 = f32[256,640]{1,0:T(8,128)S(1)} collective-permute-done((f32[256,640]{1,0:T(8,128)S(1)}, f32[256,640]{1,0:T(8,128)S(1)}, u32[]{:S(2)}, u32[]{:S(2)}) %collective-permute-start.23) | collective-permute-done | bytes 655392 | tf_op jit(solution)/shard_map/ppermute | solution.py:33
  286.0 9.0 collective-permute-start.28
  300.2 18.5 %collective-permute-done.27 = f32[256,640]{1,0:T(8,128)S(1)} collective-permute-done((f32[256,640]{1,0:T(8,128)S(1)}, f32[256,640]{1,0:T(8,128)S(1)}, u32[]{:S(2)}, u32[]{:S(2)}) %collective-permute-start.27) | collective-permute-done | bytes 655392 | tf_op jit(solution)/shard_map/ppermute | solution.py:33
  324.9 77.5 %collective-permute-done.29 = f32[6,256,640]{2,1,0:T(8,128)S(1)} collective-permute-done((f32[6,256,640]{2,1,0:T(8,128)S(1)}, f32[6,256,640]{2,1,0:T(8,128)S(1)}, u32[]{:S(2)}, u32[]{:S(2)}) %collective-permute-start.29) | collective-permute-done | bytes 3932192 | tf_op jit(solution)/shard_map/ppermute | solution.py:33
  420.8 23.9 %collective-permute-done.32 = f32[256,640]{1,0:T(8,128)S(1)} collective-permute-done((f32[256,640]{1,0:T(8,128)S(1)}, f32[256,640]{1,0:T(8,128)S(1)}, u32[]{:S(2)}, u32[]{:S(2)}) %collective-permute-start.32) | collective-permute-done | bytes 655392 | tf_op jit(solution)/shard_map/ppermute | solution.py:33
  444.7 26.9 %collective-permute-done.33 = f32[256,640]{1,0:T(8,128)S(1)} collective-permute-done((f32[256,640]{1,0:T(8,128)S(1)}, f32[256,640]{1,0:T(8,128)S(1)}, u32[]{:S(2)}, u32[]{:S(2)}) %collective-permute-start.33) | collective-permute-done | bytes 655392 | tf_op jit(solution)/shard_map/ppermute | solution.py:33
  474.3 10.8 %collective-permute-start.37 = (f32[256,640]{1,0:T(8,128)S(1)}, f32[256,640]{1,0:T(8,128)S(1)}, u32[]{:S(2)}, u32[]{:S(2)}) collective-permute-start(f32[256,640]{1,0:T(8,128)S(1)} %fusion.93), channel_id=1, source_target_pairs={{8,0},{10,2},{12,4},{14,6},{16,8},{18,10},{20,12},{22,14},{24,16},... | collective-permute-start | bytes 1966088 | tf_op jit(solution)/shard_map/ppermute | solution.py:33
  490.3 17.8 %collective-permute-done.36 = f32[256,640]{1,0:T(8,128)S(1)} collective-permute-done((f32[256,640]{1,0:T(8,128)S(1)}, f32[256,640]{1,0:T(8,128)S(1)}, u32[]{:S(2)}, u32[]{:S(2)}) %collective-permute-start.36) | collective-permute-done | bytes 655392 | tf_op jit(solution)/shard_map/ppermute | solution.py:33
  508.1 17.1 %collective-permute-done.37 = f32[256,640]{1,0:T(8,128)S(1)} collective-permute-done((f32[256,640]{1,0:T(8,128)S(1)}, f32[256,640]{1,0:T(8,128)S(1)}, u32[]{:S(2)}, u32[]{:S(2)}) %collective-permute-start.37) | collective-permute-done | bytes 655392 | tf_op jit(solution)/shard_map/ppermute | solution.py:33
  533.5 165.0 %collective-permute-done.38 = f32[6,256,640]{2,1,0:T(8,128)S(1)} collective-permute-done((f32[6,256,640]{2,1,0:T(8,128)S(1)}, f32[6,256,640]{2,1,0:T(8,128)S(1)}, u32[]{:S(2)}, u32[]{:S(2)}) %collective-permute-start.38) | collective-permute-done | bytes 3932192 | tf_op jit(solution)/shard_map/ppermute | solution.py:33
  712.1 7.5 collective-permute-done.41
  751.1 82.1 %collective-permute-done.47 = f32[6,256,640]{2,1,0:T(8,128)S(1)} collective-permute-done((f32[6,256,640]{2,1,0:T(8,128)S(1)}, f32[6,256,640]{2,1,0:T(8,128)S(1)}, u32[]{:S(2)}, u32[]{:S(2)}) %collective-permute-start.47) | collective-permute-done | bytes 3932192 | tf_op jit(solution)/shard_map/ppermute | solution.py:33
  847.0 8.6 collective-permute-done.50
  855.6 10.1 collective-permute-done.51
  869.8 14.3 %collective-permute-done.52 = f32[256,640]{1,0:T(8,128)} collective-permute-done((f32[256,640]{1,0:T(8,128)S(1)}, f32[256,640]{1,0:T(8,128)}, u32[]{:S(2)}, u32[]{:S(2)}) %collective-permute-start.52) | collective-permute-done | bytes 655392 | tf_op jit(solution)/shard_map/ppermute | solution.py:33
  887.0 18.2 %collective-permute-done.53 = f32[256,640]{1,0:T(8,128)S(1)} collective-permute-done((f32[256,640]{1,0:T(8,128)S(1)}, f32[256,640]{1,0:T(8,128)S(1)}, u32[]{:S(2)}, u32[]{:S(2)}) %collective-permute-start.53) | collective-permute-done | bytes 655392 | tf_op jit(solution)/shard_map/ppermute | solution.py:33
  905.2 24.5 %collective-permute-start.54 = (f32[256,640]{1,0:T(8,128)S(1)}, f32[256,640]{1,0:T(8,128)S(1)}, u32[]{:S(2)}, u32[]{:S(2)}) collective-permute-start(f32[256,640]{1,0:T(8,128)S(1)} %select_add_fusion.1), channel_id=1, source_target_pairs={{0,4},{2,6},{4,8},{6,10},{8,12},{10,14},{12,16},{14,18},{16,20},{1... | collective-permute-start | bytes 1966088 | tf_op jit(solution)/shard_map/ppermute | solution.py:33
  929.8 9.1 collective-permute-done.54
  939.0 100.6 %collective-permute-start.55 = (f32[256,640]{1,0:T(8,128)S(1)}, f32[256,640]{1,0:T(8,128)S(1)}, u32[]{:S(2)}, u32[]{:S(2)}) collective-permute-start(f32[256,640]{1,0:T(8,128)S(1)} %select_add_fusion), channel_id=1, source_target_pairs={{0,2},{2,4},{4,6},{6,8},{8,10},{10,12},{12,14},{14,16},{16,18},{18... | collective-permute-start | bytes 1966088 | tf_op jit(solution)/shard_map/ppermute | solution.py:33
  1039.6 12.7 %collective-permute-done.55 = f32[256,640]{1,0:T(8,128)S(1)} collective-permute-done((f32[256,640]{1,0:T(8,128)S(1)}, f32[256,640]{1,0:T(8,128)S(1)}, u32[]{:S(2)}, u32[]{:S(2)}) %collective-permute-start.55) | collective-permute-done | bytes 655392 | tf_op jit(solution)/shard_map/ppermute | solution.py:33
  (162 shorter events, 187.9 us)
Async XLA Ops:
  3.7 24.8 %collective-permute-start = (f32[1,256,640]{2,1,0:T(8,128)}, f32[1,256,640]{2,1,0:T(8,128)S(1)}, u32[]{:S(2)}, u32[]{:S(2)}) collective-permute-start(f32[1,256,640]{2,1,0:T(8,128)} %get-tuple-element.42), channel_id=1, source_target_pairs={{0,2},{2,4},{4,6},{6,8},{8,10},{10,12},{12,14},{14,16},{16,18},{18... | collective-permute-start | bytes 1966088 | tf_op jit(solution)/shard_map/ppermute | solution.py:22
  7.5 22.2 %collective-permute-start.1 = (f32[1,256,640]{2,1,0:T(8,128)}, f32[1,256,640]{2,1,0:T(8,128)}, u32[]{:S(2)}, u32[]{:S(2)}) collective-permute-start(f32[1,256,640]{2,1,0:T(8,128)} %get-tuple-element.43), channel_id=1, source_target_pairs={{2,0},{4,2},{6,4},{8,6},{10,8},{12,10},{14,12},{16,14},{18,16},{20... | collective-permute-start | bytes 1966088 | tf_op jit(solution)/shard_map/ppermute | solution.py:25
  39.1 23.8 %collective-permute-start.4 = (f32[1,256,640]{2,1,0:T(8,128)S(1)}, f32[1,256,640]{2,1,0:T(8,128)S(1)}, u32[]{:S(2)}, u32[]{:S(2)}) collective-permute-start(f32[1,256,640]{2,1,0:T(8,128)S(1)} %get-tuple-element.40), channel_id=1, source_target_pairs={{0,2},{2,4},{4,6},{6,8},{8,10},{10,12},{12,14},{14,16},{16,18},{18... | collective-permute-start | bytes 1966088 | tf_op jit(solution)/shard_map/ppermute | solution.py:22
  41.0 23.1 %collective-permute-start.5 = (f32[1,256,640]{2,1,0:T(8,128)S(1)}, f32[1,256,640]{2,1,0:T(8,128)S(1)}, u32[]{:S(2)}, u32[]{:S(2)}) collective-permute-start(f32[1,256,640]{2,1,0:T(8,128)S(1)} %get-tuple-element.41), channel_id=1, source_target_pairs={{2,0},{4,2},{6,4},{8,6},{10,8},{12,10},{14,12},{16,14},{18,16},{20... | collective-permute-start | bytes 1966088 | tf_op jit(solution)/shard_map/ppermute | solution.py:25
  71.6 23.8 %collective-permute-start.8 = (f32[1,256,640]{2,1,0:T(8,128)S(1)}, f32[1,256,640]{2,1,0:T(8,128)S(1)}, u32[]{:S(2)}, u32[]{:S(2)}) collective-permute-start(f32[1,256,640]{2,1,0:T(8,128)S(1)} %get-tuple-element.36), channel_id=1, source_target_pairs={{0,2},{2,4},{4,6},{6,8},{8,10},{10,12},{12,14},{14,16},{16,18},{18... | collective-permute-start | bytes 1966088 | tf_op jit(solution)/shard_map/ppermute | solution.py:22
  73.6 23.1 %collective-permute-start.9 = (f32[1,256,640]{2,1,0:T(8,128)S(1)}, f32[1,256,640]{2,1,0:T(8,128)S(1)}, u32[]{:S(2)}, u32[]{:S(2)}) collective-permute-start(f32[1,256,640]{2,1,0:T(8,128)S(1)} %get-tuple-element.37), channel_id=1, source_target_pairs={{2,0},{4,2},{6,4},{8,6},{10,8},{12,10},{14,12},{16,14},{18,16},{20... | collective-permute-start | bytes 1966088 | tf_op jit(solution)/shard_map/ppermute | solution.py:25
  104.4 23.8 %collective-permute-start.14 = (f32[256,640]{1,0:T(8,128)S(1)}, f32[256,640]{1,0:T(8,128)S(1)}, u32[]{:S(2)}, u32[]{:S(2)}) collective-permute-start(f32[256,640]{1,0:T(8,128)S(1)} %get-tuple-element.20), channel_id=1, source_target_pairs={{0,2},{2,4},{4,6},{6,8},{8,10},{10,12},{12,14},{14,16},{16,18},{18... | collective-permute-start | bytes 1966088 | tf_op jit(solution)/shard_map/ppermute | solution.py:33
  106.3 23.1 %collective-permute-start.15 = (f32[256,640]{1,0:T(8,128)S(1)}, f32[256,640]{1,0:T(8,128)S(1)}, u32[]{:S(2)}, u32[]{:S(2)}) collective-permute-start(f32[256,640]{1,0:T(8,128)S(1)} %get-tuple-element.20), channel_id=1, source_target_pairs={{2,0},{4,2},{6,4},{8,6},{10,8},{12,10},{14,12},{16,14},{18,16},{20... | collective-permute-start | bytes 1966088 | tf_op jit(solution)/shard_map/ppermute | solution.py:33
  130.3 23.0 %collective-permute-start.18 = (f32[256,640]{1,0:T(8,128)S(1)}, f32[256,640]{1,0:T(8,128)S(1)}, u32[]{:S(2)}, u32[]{:S(2)}) collective-permute-start(f32[256,640]{1,0:T(8,128)S(1)} %fusion.137), channel_id=1, source_target_pairs={{0,2},{2,4},{4,6},{6,8},{8,10},{10,12},{12,14},{14,16},{16,18},{18... | collective-permute-start | bytes 1966088 | tf_op jit(solution)/shard_map/ppermute | solution.py:33
  132.2 22.3 %collective-permute-start.19 = (f32[256,640]{1,0:T(8,128)S(1)}, f32[256,640]{1,0:T(8,128)S(1)}, u32[]{:S(2)}, u32[]{:S(2)}) collective-permute-start(f32[256,640]{1,0:T(8,128)S(1)} %fusion.137), channel_id=1, source_target_pairs={{2,0},{4,2},{6,4},{8,6},{10,8},{12,10},{14,12},{16,14},{18,16},{20... | collective-permute-start | bytes 1966088 | tf_op jit(solution)/shard_map/ppermute | solution.py:33
  155.6 91.6 %collective-permute-start.20 = (f32[6,256,640]{2,1,0:T(8,128)S(1)}, f32[6,256,640]{2,1,0:T(8,128)S(1)}, u32[]{:S(2)}, u32[]{:S(2)}) collective-permute-start(f32[6,256,640]{2,1,0:T(8,128)S(1)} %slice_dynamic-update-slice_fusion.3), channel_id=1, source_target_pairs={{2,0},{4,2},{6,4},{8,6},{10,8},{12,10},{14,12},{16,14},{18,16},{20... | collective-permute-start | bytes 11796488 | tf_op jit(solution)/shard_map/ppermute | solution.py:33
  247.7 35.4 %collective-permute-start.23 = (f32[256,640]{1,0:T(8,128)S(1)}, f32[256,640]{1,0:T(8,128)S(1)}, u32[]{:S(2)}, u32[]{:S(2)}) collective-permute-start(f32[256,640]{1,0:T(8,128)S(1)} %get-tuple-element.15), channel_id=1, source_target_pairs={{0,4},{2,6},{4,8},{6,10},{8,12},{10,14},{12,16},{14,18},{16,20},{1... | collective-permute-start | bytes 1966088 | tf_op jit(solution)/shard_map/ppermute | solution.py:33
  249.6 33.5 %collective-permute-start.24 = (f32[256,640]{1,0:T(8,128)S(1)}, f32[256,640]{1,0:T(8,128)S(1)}, u32[]{:S(2)}, u32[]{:S(2)}) collective-permute-start(f32[256,640]{1,0:T(8,128)S(1)} %get-tuple-element.15), channel_id=1, source_target_pairs={{4,0},{6,2},{8,4},{10,6},{12,8},{14,10},{16,12},{18,14},{20,16},{2... | collective-permute-start | bytes 1966088 | tf_op jit(solution)/shard_map/ppermute | solution.py:33
  284.0 34.6 %collective-permute-start.27 = (f32[256,640]{1,0:T(8,128)S(1)}, f32[256,640]{1,0:T(8,128)S(1)}, u32[]{:S(2)}, u32[]{:S(2)}) collective-permute-start(f32[256,640]{1,0:T(8,128)S(1)} %fusion.115), channel_id=1, source_target_pairs={{0,4},{2,6},{4,8},{6,10},{8,12},{10,14},{12,16},{14,18},{16,20},{1... | collective-permute-start | bytes 1966088 | tf_op jit(solution)/shard_map/ppermute | solution.py:33
  286.0 32.7 %collective-permute-start.28 = (f32[256,640]{1,0:T(8,128)S(1)}, f32[256,640]{1,0:T(8,128)S(1)}, u32[]{:S(2)}, u32[]{:S(2)}) collective-permute-start(f32[256,640]{1,0:T(8,128)S(1)} %fusion.115), channel_id=1, source_target_pairs={{4,0},{6,2},{8,4},{10,6},{12,8},{14,10},{16,12},{18,14},{20,16},{2... | collective-permute-start | bytes 1966088 | tf_op jit(solution)/shard_map/ppermute | solution.py:33
  319.8 82.6 %collective-permute-start.29 = (f32[6,256,640]{2,1,0:T(8,128)S(1)}, f32[6,256,640]{2,1,0:T(8,128)S(1)}, u32[]{:S(2)}, u32[]{:S(2)}) collective-permute-start(f32[6,256,640]{2,1,0:T(8,128)S(1)} %slice_dynamic-update-slice_fusion.2), channel_id=1, source_target_pairs={{4,0},{6,2},{8,4},{10,6},{12,8},{14,10},{16,12},{18,14},{20,16},{2... | collective-permute-start | bytes 11796488 | tf_op jit(solution)/shard_map/ppermute | solution.py:33
  402.9 41.8 %collective-permute-start.32 = (f32[256,640]{1,0:T(8,128)S(1)}, f32[256,640]{1,0:T(8,128)S(1)}, u32[]{:S(2)}, u32[]{:S(2)}) collective-permute-start(f32[256,640]{1,0:T(8,128)S(1)} %get-tuple-element.10), channel_id=1, source_target_pairs={{0,8},{2,10},{4,12},{6,14},{8,16},{10,18},{12,20},{14,22},{16,24},... | collective-permute-start | bytes 1966088 | tf_op jit(solution)/shard_map/ppermute | solution.py:33
  410.2 61.3 %collective-permute-start.33 = (f32[256,640]{1,0:T(8,128)S(1)}, f32[256,640]{1,0:T(8,128)S(1)}, u32[]{:S(2)}, u32[]{:S(2)}) collective-permute-start(f32[256,640]{1,0:T(8,128)S(1)} %get-tuple-element.10), channel_id=1, source_target_pairs={{8,0},{10,2},{12,4},{14,6},{16,8},{18,10},{20,12},{22,14},{24,16},... | collective-permute-start | bytes 1966088 | tf_op jit(solution)/shard_map/ppermute | solution.py:33
  472.4 35.7 %collective-permute-start.36 = (f32[256,640]{1,0:T(8,128)S(1)}, f32[256,640]{1,0:T(8,128)S(1)}, u32[]{:S(2)}, u32[]{:S(2)}) collective-permute-start(f32[256,640]{1,0:T(8,128)S(1)} %fusion.93), channel_id=1, source_target_pairs={{0,8},{2,10},{4,12},{6,14},{8,16},{10,18},{12,20},{14,22},{16,24},... | collective-permute-start | bytes 1966088 | tf_op jit(solution)/shard_map/ppermute | solution.py:33
  474.3 50.9 %collective-permute-start.37 = (f32[256,640]{1,0:T(8,128)S(1)}, f32[256,640]{1,0:T(8,128)S(1)}, u32[]{:S(2)}, u32[]{:S(2)}) collective-permute-start(f32[256,640]{1,0:T(8,128)S(1)} %fusion.93), channel_id=1, source_target_pairs={{8,0},{10,2},{12,4},{14,6},{16,8},{18,10},{20,12},{22,14},{24,16},... | collective-permute-start | bytes 1966088 | tf_op jit(solution)/shard_map/ppermute | solution.py:33
  526.5 172.0 %collective-permute-start.38 = (f32[6,256,640]{2,1,0:T(8,128)S(1)}, f32[6,256,640]{2,1,0:T(8,128)S(1)}, u32[]{:S(2)}, u32[]{:S(2)}) collective-permute-start(f32[6,256,640]{2,1,0:T(8,128)S(1)} %slice_dynamic-update-slice_fusion.1), channel_id=1, source_target_pairs={{8,0},{10,2},{12,4},{14,6},{16,8},{18,10},{20,12},{22,14},{24,16},... | collective-permute-start | bytes 11796488 | tf_op jit(solution)/shard_map/ppermute | solution.py:33
  699.0 20.7 %collective-permute-start.41 = (f32[256,640]{1,0:T(8,128)S(1)}, f32[256,640]{1,0:T(8,128)S(1)}, u32[]{:S(2)}, u32[]{:S(2)}) collective-permute-start(f32[256,640]{1,0:T(8,128)S(1)} %get-tuple-element.5), channel_id=1, source_target_pairs={{0,16},{2,18},{4,20},{6,22},{8,24},{10,26},{12,28},{14,30},{16,32}... | collective-permute-start | bytes 1966088 | tf_op jit(solution)/shard_map/ppermute | solution.py:33
  700.9 19.9 %collective-permute-start.42 = (f32[256,640]{1,0:T(8,128)S(1)}, f32[256,640]{1,0:T(8,128)S(1)}, u32[]{:S(2)}, u32[]{:S(2)}) collective-permute-start(f32[256,640]{1,0:T(8,128)S(1)} %get-tuple-element.5), channel_id=1, source_target_pairs={{16,0},{18,2},{20,4},{22,6},{24,8},{26,10},{28,12},{30,14},{32,16}... | collective-permute-start | bytes 1966088 | tf_op jit(solution)/shard_map/ppermute | solution.py:33
  721.7 20.2 %collective-permute-start.45 = (f32[256,640]{1,0:T(8,128)S(1)}, f32[256,640]{1,0:T(8,128)S(1)}, u32[]{:S(2)}, u32[]{:S(2)}) collective-permute-start(f32[256,640]{1,0:T(8,128)S(1)} %fusion.71), channel_id=1, source_target_pairs={{0,16},{2,18},{4,20},{6,22},{8,24},{10,26},{12,28},{14,30},{16,32}... | collective-permute-start | bytes 1966088 | tf_op jit(solution)/shard_map/ppermute | solution.py:33
  723.6 19.5 %collective-permute-start.46 = (f32[256,640]{1,0:T(8,128)S(1)}, f32[256,640]{1,0:T(8,128)S(1)}, u32[]{:S(2)}, u32[]{:S(2)}) collective-permute-start(f32[256,640]{1,0:T(8,128)S(1)} %fusion.71), channel_id=1, source_target_pairs={{16,0},{18,2},{20,4},{22,6},{24,8},{26,10},{28,12},{30,14},{32,16}... | collective-permute-start | bytes 1966088 | tf_op jit(solution)/shard_map/ppermute | solution.py:33
  744.4 88.8 %collective-permute-start.47 = (f32[6,256,640]{2,1,0:T(8,128)S(1)}, f32[6,256,640]{2,1,0:T(8,128)S(1)}, u32[]{:S(2)}, u32[]{:S(2)}) collective-permute-start(f32[6,256,640]{2,1,0:T(8,128)S(1)} %slice_dynamic-update-slice_fusion), channel_id=1, source_target_pairs={{16,0},{18,2},{20,4},{22,6},{24,8},{26,10},{28,12},{30,14},{32,16}... | collective-permute-start | bytes 11796488 | tf_op jit(solution)/shard_map/ppermute | solution.py:33
  833.6 22.0 %collective-permute-start.50 = (f32[256,640]{1,0:T(8,128)S(1)}, f32[256,640]{1,0:T(8,128)S(1)}, u32[]{:S(2)}, u32[]{:S(2)}) collective-permute-start(f32[256,640]{1,0:T(8,128)S(1)} %fusion.144), channel_id=1, source_target_pairs={{0,32},{2,34},{4,36},{6,38},{8,40},{10,42},{12,44},{14,46},{16,48}... | collective-permute-start | bytes 1966088 | tf_op jit(solution)/shard_map/ppermute | solution.py:33
  837.9 27.9 %collective-permute-start.51 = (f32[256,640]{1,0:T(8,128)S(1)}, f32[256,640]{1,0:T(8,128)S(1)}, u32[]{:S(2)}, u32[]{:S(2)}) collective-permute-start(f32[256,640]{1,0:T(8,128)S(1)} %fusion.144), channel_id=1, source_target_pairs={{32,0},{34,2},{36,4},{38,6},{40,8},{42,10},{44,12},{46,14},{48,16}... | collective-permute-start | bytes 1966088 | tf_op jit(solution)/shard_map/ppermute | solution.py:33
  866.6 17.6 %collective-permute-start.52 = (f32[256,640]{1,0:T(8,128)S(1)}, f32[256,640]{1,0:T(8,128)}, u32[]{:S(2)}, u32[]{:S(2)}) collective-permute-start(f32[256,640]{1,0:T(8,128)S(1)} %fusion.46), channel_id=1, source_target_pairs={{0,16},{2,18},{4,20},{6,22},{8,24},{10,26},{12,28},{14,30},{16,32}... | collective-permute-start | bytes 1966088 | tf_op jit(solution)/shard_map/ppermute | solution.py:33
  884.3 20.9 %collective-permute-start.53 = (f32[256,640]{1,0:T(8,128)S(1)}, f32[256,640]{1,0:T(8,128)S(1)}, u32[]{:S(2)}, u32[]{:S(2)}) collective-permute-start(f32[256,640]{1,0:T(8,128)S(1)} %select_add_fusion.2), channel_id=1, source_target_pairs={{0,8},{2,10},{4,12},{6,14},{8,16},{10,18},{12,20},{14,22},{16,24},... | collective-permute-start | bytes 1966088 | tf_op jit(solution)/shard_map/ppermute | solution.py:33
  905.2 33.7 %collective-permute-start.54 = (f32[256,640]{1,0:T(8,128)S(1)}, f32[256,640]{1,0:T(8,128)S(1)}, u32[]{:S(2)}, u32[]{:S(2)}) collective-permute-start(f32[256,640]{1,0:T(8,128)S(1)} %select_add_fusion.1), channel_id=1, source_target_pairs={{0,4},{2,6},{4,8},{6,10},{8,12},{10,14},{12,16},{14,18},{16,20},{1... | collective-permute-start | bytes 1966088 | tf_op jit(solution)/shard_map/ppermute | solution.py:33
  939.0 113.3 %collective-permute-start.55 = (f32[256,640]{1,0:T(8,128)S(1)}, f32[256,640]{1,0:T(8,128)S(1)}, u32[]{:S(2)}, u32[]{:S(2)}) collective-permute-start(f32[256,640]{1,0:T(8,128)S(1)} %select_add_fusion), channel_id=1, source_target_pairs={{0,2},{2,4},{4,6},{6,8},{8,10},{10,12},{12,14},{14,16},{16,18},{18... | collective-permute-start | bytes 1966088 | tf_op jit(solution)/shard_map/ppermute | solution.py:33
  (27 other events, 175.4 us)
where the time goes:
time: 1060 us; the launch traced here: 1050 us
  waiting for transfers between devices  687 us (65%)
  starting transfers between devices  336 us (32%)
  other arithmetic  22.6 us (2%)
    ppermute x26, waiting for transfers between devices, shifted(): return lax.ppermute(value, axis, pairs)  638 us
    ppermute x26, starting transfers between devices, shifted(): return lax.ppermute(value, axis, pairs)  252 us
    ppermute x15, waiting for transfers between devices, with_halo(): lax.ppermute(lax.slice_in_dim(block, block.shape[dim] - width, None, axis...  45.2 us
    ppermute x15, starting transfers between devices, with_halo(): lax.ppermute(lax.slice_in_dim(block, block.shape[dim] - width, None, axis...  44.2 us
    ppermute x15, starting transfers between devices, with_halo(): lax.ppermute(lax.slice_in_dim(block, 0, width, axis=dim), axis, backward)  40.7 us
  transfers between devices with their start and end apart: 56, of which 42 were waited for; matrix products, arithmetic and copies ran while one was open for 0% of the time, Pallas kernels for 0%

commit v1 on v0

v1 whole, which is shorter than its diff:
```python
from functools import partial

import jax
import jax.numpy as jnp
from jax import lax
from jax.experimental import pallas as pl
from jax.experimental.pallas import tpu as pltpu
from jax.sharding import PartitionSpec as P

RING = 8
HALO = 8
THIN = 4
damping = 0.8
pore_value = 1.0
grain_value = 0.1
clay_value = 0.3
TINY = 1e-30


def ring_groups(count):
    return [[r * RING + k for k in range(RING)] for r in range(count // RING)]


def shifted(value, by):
    size = lax.axis_size("gz")
    pairs = [(i, i + by) for i in range(size) if 0 <= i + by < size]
    return lax.ppermute(value, "gz", pairs)


def row_shifted(value, by):
    pairs = []
    for ring in range(lax.axis_size("gz") // RING):
        for t in range(2 * RING):
            u = t + by
            if 0 <= u < 2 * RING:
                pairs.append(((ring * RING + t % RING) * 2 + t // RING, (ring * RING + u % RING) * 2 + u // RING))
    return lax.ppermute(value, ("gz", "xy"), pairs)


def partner(value):
    size = lax.axis_size("gz")
    return lax.ppermute(value, "gz", [(i, i + RING if (i // RING) % 2 == 0 else i - RING) for i in range(size)])


def transposed(value):
    return lax.all_to_all(value, "gz", 0, 0, axis_index_groups=ring_groups(lax.axis_size("gz")), tiled=True)


def conductivity(labels, fraction):
    return jnp.where(labels == 0, pore_value, jnp.where(labels == 1, grain_value, clay_value)) * fraction


def harmonic(one_side, other_side):
    return (2.0 * one_side * other_side) / jnp.maximum(one_side + other_side, TINY)


def next_row(v):
    return pltpu.roll(v, v.shape[0] - 1, 0)


def previous_row(v):
    return pltpu.roll(v, 1, 0)


def next_column(v):
    return pltpu.roll(v, v.shape[1] - 1, 1)


def previous_column(v):
    return pltpu.roll(v, 1, 1)


def neighbours(v, below, above, east, north, down, up):
    return (
        east * next_row(v)
        + previous_row(east * v)
        + north * next_column(v)
        + previous_column(north * v)
        + down * below
        + up * above
    )


def weight(c, east, north, down, up):
    diagonal = east + previous_row(east) + north + previous_column(north) + down + up
    return jnp.where(c > 0, damping / jnp.where(c > 0, diagonal, 1.0), 0.0)


def loop(count, body):
    def step(k, carry):
        body(k)
        return carry

    lax.fori_loop(0, count, step, 0)


def call(kernel, outs, scratch, *args):
    shapes = [jax.ShapeDtypeStruct(s, jnp.float32) for s in outs]
    vmem = pl.BlockSpec(memory_space=pltpu.VMEM)
    return pl.pallas_call(
        kernel,
        out_shape=shapes,
        in_specs=[vmem] * len(args),
        out_specs=[vmem] * len(shapes),
        scratch_shapes=[pltpu.VMEM(s, jnp.float32) for s in scratch],
        compiler_params=pltpu.CompilerParams(vmem_limit_bytes=48 * 1024 * 1024),
    )(*args)


def cut_conduct(labels, fraction, top, bottom, out, full):
    planes, rows, _ = labels.shape
    strip = rows // RING
    for p in range(planes):
        full[p, :HALO] = top[p]
        full[p, HALO + rows:] = bottom[p]

        def fill(k):
            at = pl.multiple_of(k * strip, strip)
            full[p, pl.ds(at + HALO, strip)] = conductivity(labels[p, pl.ds(at, strip)], fraction[p, pl.ds(at, strip)])

        loop(RING, fill)
        for k in range(RING):
            out[k, p] = full[p, k * strip:k * strip + strip + 2 * HALO]


def cut_source(source, top, bottom, out):
    planes, rows, _ = source.shape
    strip = rows // RING
    for p in range(planes):
        for k in range(RING):
            start = k * strip
            if k == 0:
                out[k, p, :THIN] = top[p, HALO - THIN:]
            else:
                out[k, p, :THIN] = source[p, start - THIN:start]
            out[k, p, THIN:THIN + strip] = source[p, start:start + strip]
            if k == RING - 1:
                out[k, p, THIN + strip:] = bottom[p, :THIN]
            else:
                out[k, p, THIN + strip:] = source[p, start + strip:start + strip + THIN]


def make_faces(c_own, c_low, c_high, east0, north0, z0, w0, east1, north1, w1, east2, north2, z2, w2,
               east3, north3, z3, w3, east4, north4, z4, w4, c):
    rows, columns = c_own.shape[1:]
    c[0:3] = c_low[...]
    c[3:19] = c_own[...]
    c[19:22] = c_high[...]
    last = lax.broadcasted_iota(jnp.int32, (rows, columns), 1) == columns - 1

    def z_face(i):
        z0[i] = harmonic(c[i], c[i + 1])

    loop(21, z_face)
    z0[2] = jnp.where(c[2] > 0, z0[2], 2.0 * c[3])
    z0[18] = jnp.where(c[19] > 0, z0[18], 2.0 * c[18])

    def plane(i):
        here = c[i + 1]
        east = harmonic(here, next_row(here))
        north = jnp.where(last, 0.0, harmonic(here, next_column(here)))
        east0[i] = east
        north0[i] = north
        w0[i] = weight(here, east, north, z0[i], z0[i + 1])

    loop(20, plane)

    def plane1(j):
        east = east0[2 * j] + east0[2 * j + 1]
        north = north0[2 * j] + north0[2 * j + 1]
        east1[j] = east
        north1[j] = north
        w1[j] = weight(c[2 * j + 1], east, north, z0[2 * j], z0[2 * j + 2])

    loop(10, plane1)
    for q in range(4):
        east2[q] = east1[2 * q + 1] + east1[2 * q + 2]
        north2[q] = north1[2 * q + 1] + north1[2 * q + 2]
        z2[q] = z0[4 * q + 2]
    z2[4] = z0[18]
    for q in range(4):
        w2[q] = weight(c[3], east2[q], north2[q], z2[q], z2[q + 1])
    for q in range(2):
        east3[q] = east2[2 * q] + east2[2 * q + 1]
        north3[q] = north2[2 * q] + north2[2 * q + 1]
        z3[q] = z2[2 * q]
    z3[2] = z2[4]
    for q in range(2):
        w3[q] = weight(c[3], east3[q], north3[q], z3[q], z3[q + 1])
    east4[0] = east3[0] + east3[1]
    north4[0] = north3[0] + north3[1]
    z4[0] = z3[0]
    z4[1] = z3[2]
    w4[0] = weight(c[3], east4[0], north4[0], z4[0], z4[1])


def make_last_faces(east4, north4, w4, other, down, up, east5, north5, w5):
    east5[0] = east4[0] + other[0]
    north5[0] = north4[0] + other[1]
    w5[0] = weight(w4[0], east5[0], north5[0], down[0], up[0])


def fine_level(s_own, s_low, s_high, east0, north0, z0, w0, w1, fine, source1, edge_down, edge_up, s, first, total, second):
    rows = east0.shape[1]
    strip = fine.shape[2]
    inner = slice(HALO - THIN, HALO + strip + THIN)
    blank = jnp.zeros((HALO - THIN, s.shape[2]), jnp.float32)

    def place(k, value):
        s[k, :HALO - THIN] = blank
        s[k, inner] = value
        s[k, HALO + strip + THIN:] = blank

    for k in range(2):
        place(k, s_low[k])
        place(18 + k, s_high[k])
    loop(16, lambda k: place(k + 2, s_own[k]))

    def start(i):
        first[i] = w0[i] * s[i]

    loop(20, start)

    def sweep(k):
        i = k + 1
        t = 1.2 * s[i] + neighbours(first[i], first[i - 1], first[i + 1], east0[i], north0[i], z0[i], z0[i + 1])
        total[i] = t
        second[i] = w0[i] * t

    loop(18, sweep)

    def rest(i):
        return s[i] - damping * total[i] + neighbours(
            second[i], second[i - 1], second[i + 1], east0[i], north0[i], z0[i], z0[i + 1])

    def pair(q):
        source1[q] = rest(2 * q + 2) + rest(2 * q + 3)
        fine[q, 0] = second[2 * q + 2, HALO:HALO + strip]
        fine[q, 1] = second[2 * q + 3, HALO:HALO + strip]

    loop(8, pair)
    edge_down[0] = source1[0, inner]
    edge_down[1] = w1[2, inner] * source1[1, inner]
    edge_up[0] = w1[7, inner] * source1[6, inner]
    edge_up[1] = source1[7, inner]


def first_coarse_level(source1, low, high, east1, north1, z0, w1, plane_out, source2, top, bottom, s, first, total, second):
    strip = plane_out.shape[1]
    inner = slice(HALO - THIN, HALO + strip + THIN)
    blank = jnp.zeros((HALO - THIN, s.shape[2]), jnp.float32)
    for ref, k, value in ((s, 0, low[1]), (s, 9, high[0]), (first, 0, low[0]), (first, 11, high[1])):
        ref[k, :HALO - THIN] = blank
        ref[k, inner] = value
        ref[k, HALO + strip + THIN:] = blank
    s[1:9] = source1[...]

    def start(j):
        first[j + 1] = w1[j] * s[j]

    loop(10, start)

    def sweep(j):
        t = 1.2 * s[j] + neighbours(first[j + 1], first[j], first[j + 2], east1[j], north1[j], z0[2 * j], z0[2 * j + 2])
        total[j] = t
        second[j] = w1[j] * t

    loop(10, sweep)

    def rest(j):
        return s[j] - damping * total[j] + neighbours(
            second[j], second[j - 1], second[j + 1], east1[j], north1[j], z0[2 * j], z0[2 * j + 2])

    def pair(q):
        value = rest(2 * q + 1) + rest(2 * q + 2)
        source2[q] = value[HALO:HALO + strip]
        top[q] = value[HALO:2 * HALO]
        bottom[q] = value[strip:HALO + strip]
        plane_out[2 * q] = second[2 * q + 1, HALO:HALO + strip]
        plane_out[2 * q + 1] = second[2 * q + 2, HALO:HALO + strip]

    loop(4, pair)


def widen(source2, above, below, w2, s, first, edge_low, edge_high):
    count, strip, _ = source2.shape
    for q in range(count):
        s[q, :HALO] = above[q]
        s[q, HALO:HALO + strip] = source2[q]
        s[q, HALO + strip:] = below[q]
        first[q] = w2[q] * s[q]
    edge_low[0] = first[0]
    edge_high[0] = first[count - 1]


def around(ref, low, high, q):
    count = ref.shape[0]
    return (ref[q], low[0] if q == 0 else ref[q - 1], high[0] if q == count - 1 else ref[q + 1])


def sweep_level(s, first, low, high, east, north, z, w, total, second, *edges):
    count = s.shape[0]
    for q in range(count):
        t = 1.2 * s[q] + neighbours(*around(first, low, high, q), east[q], north[q], z[q], z[q + 1])
        total[q] = t
        second[q] = w[q] * t
    if edges:
        edges[0][0] = second[0]
        edges[1][0] = second[count - 1]


def rest_level(s, total, second, low, high, east, north, z, w_next, s_next, first_next, *edges):
    count = s.shape[0]

    def rest(q):
        return s[q] - damping * total[q] + neighbours(*around(second, low, high, q), east[q], north[q], z[q], z[q + 1])

    for q in range(count // 2):
        value = rest(2 * q) + rest(2 * q + 1)
        s_next[q] = value
        first_next[q] = w_next[q] * value
    if edges:
        edges[0][0] = first_next[0]
        edges[1][0] = first_next[count // 2 - 1]


def rest_last(s, total, second, low, high, east, north, z, out):
    out[0] = s[0] - damping * total[0] + neighbours(second[0], low[0], high[0], east[0], north[0], z[0], z[1])


def finish(s, first, low, high, east, north, down, up, w, second2, second3, second4, out):
    strip = out.shape[1]
    second5 = w[0] * (1.2 * s[0] + neighbours(first[0], low[0], high[0], east[0], north[0], down[0], up[0]))
    own = slice(HALO, HALO + strip)
    for k in range(RING):
        out[k] = ((second2[k // 2, own] + second3[k // 4, own]) + second4[0, own]) + second5[own]


def exchange(edge_low, edge_high, distance=RING):
    return shifted(edge_high, distance), shifted(edge_low, -distance)


def on_device(right_side, labels, fraction):
    planes, rows, columns = right_side.shape
    strip = rows // RING
    frame = strip + 2 * HALO
    at_core = lax.axis_index("xy")
    even_ring = (lax.axis_index("gz") // RING) % 2 == 0

    def edges_of(first_rows, last_rows):
        got = lax.ppermute(jnp.where(at_core == 0, last_rows, first_rows), "xy", [(0, 1), (1, 0)])
        return jnp.where(at_core == 1, got, 0.0), jnp.where(at_core == 0, got, 0.0)

    c_top, c_bottom = edges_of(conductivity(labels[:, :HALO], fraction[:, :HALO]),
                               conductivity(labels[:, rows - HALO:], fraction[:, rows - HALO:]))
    s_top, s_bottom = edges_of(right_side[:, :HALO], right_side[:, rows - HALO:])
    (c_cut,) = call(cut_conduct, [(RING, planes, frame, columns)], [(planes, rows + 2 * HALO, columns)],
                    labels, fraction, c_top, c_bottom)
    c = transposed(c_cut).reshape(RING * planes, frame, columns)
    (s_cut,) = call(cut_source, [(RING, planes, strip + 2 * THIN, columns)], [], right_side, s_top, s_bottom)
    s = transposed(s_cut).reshape(RING * planes, strip + 2 * THIN, columns)

    c_low, c_high = exchange(c[:3], c[-3:])

    def shape(n):
        return (n, frame, columns)

    (east0, north0, z0, w0, east1, north1, w1, east2, north2, z2, w2, east3, north3, z3, w3,
     east4, north4, z4, w4) = call(
        make_faces,
        [shape(n) for n in (20, 20, 21, 20, 10, 10, 10, 4, 4, 5, 4, 2, 2, 3, 2, 1, 1, 2, 1)],
        [shape(22)], c, c_low, c_high)
    outer = jnp.where(even_ring, z4[:1], z4[1:])
    other = partner(jnp.concatenate([east4, north4, outer], axis=0))
    down5 = jnp.where(even_ring, z4[:1], other[2:])
    up5 = jnp.where(even_ring, other[2:], z4[1:])
    east5, north5, w5 = call(make_last_faces, [shape(1)] * 3, [], east4, north4, w4, other, down5, up5)

    s_low, s_high = exchange(s[:2], s[-2:])
    thin = (2, strip + 2 * THIN, columns)
    fine, source1, edge_down, edge_up = call(
        fine_level, [(RING, planes, strip, columns), shape(8), thin, thin],
        [shape(20)] * 4, s, s_low, s_high, east0, north0, z0, w0, w1)

    low, high = exchange(edge_down, edge_up)
    plane_out, source2, top, bottom = call(
        first_coarse_level,
        [(8, strip, columns), (4, strip, columns), (4, HALO, columns), (4, HALO, columns)],
        [shape(10), shape(12), shape(10), shape(10)], source1, low, high, east1, north1, z0, w1)

    above = row_shifted(bottom, 1)
    below = row_shifted(top, -1)
    s2, first2, a, b = call(widen, [shape(4), shape(4), shape(1), shape(1)], [], source2, above, below, w2)
    low, high = exchange(a, b)
    total2, second2, a, b = call(sweep_level, [shape(4), shape(4), shape(1), shape(1)], [],
                                 s2, first2, low, high, east2, north2, z2, w2)
    low, high = exchange(a, b)
    s3, first3, a, b = call(rest_level, [shape(2), shape(2), shape(1), shape(1)], [],
                            s2, total2, second2, low, high, east2, north2, z2, w3)
    low, high = exchange(a, b)
    total3, second3, a, b = call(sweep_level, [shape(2), shape(2), shape(1), shape(1)], [],
                                 s3, first3, low, high, east3, north3, z3, w3)
    low, high = exchange(a, b)
    s4, first4 = call(rest_level, [shape(1), shape(1)], [], s3, total3, second3, low, high, east3, north3, z3, w4)
    low, high = exchange(first4, first4)
    total4, second4 = call(sweep_level, [shape(1), shape(1)], [], s4, first4, low, high, east4, north4, z4, w4)
    low, high = exchange(second4, second4)
    (rest4,) = call(rest_last, [shape(1)], [], s4, total4, second4, low, high, east4, north4, z4)
    s5 = rest4 + partner(rest4)
    first5 = w5 * s5
    low, high = exchange(first5, first5, 2 * RING)
    (summed,) = call(finish, [(RING, strip, columns)], [],
                     s5, first5, low, high, east5, north5, down5, up5, w5, second2, second3, second4)

    fine_iterate = jnp.transpose(transposed(fine), (1, 0, 2, 3)).reshape(planes, rows, columns)
    plane_iterate = transposed(plane_out).reshape(1, rows, columns)
    coarse_return = transposed(summed).reshape(1, rows, columns)
    return fine_iterate, plane_iterate, coarse_return


def solution(mesh):
    spec = P("gz", "xy", None)
    return jax.shard_map(
        on_device,
        mesh=mesh,
        in_specs=(spec, spec, spec),
        out_specs=(spec, spec, spec),
        check_vma=False,
    )
```

time: 1060 us -> 340 us (0.32)
  waiting for transfers between devices: 687 us -> 151 us
  starting transfers between devices: 336 us -> 105 us
  Pallas kernels: 0 us -> 33.3 us
  blocking collectives: 0 us -> 22.4 us
  other arithmetic: 22.6 us -> 0.98 us
  local copies, waits for them, and re-layouts: 5.2 us -> 23.1 us
    ppermute x56 -> x26, waiting for transfers between devices: 687 us -> 61.2 us  [the longest x20 30.1 us: shifted(): return lax.ppermute(value, 'gz', pairs)]
    ppermute x56 -> x26, starting transfers between devices: 336 us -> 81.5 us  [the longest x20 76.1 us: shifted(): return lax.ppermute(value, 'gz', pairs)]
    all_to_all x0 -> x4, waiting for transfers between devices: none -> 90.2 us  [transposed(): lax.all_to_all(value, 'gz', 0, 0, axis_index_groups=ring_groups(lax.axis_...]
    pallas_call x0 -> x14, Pallas kernels: none -> 33.3 us  [call(): pl.pallas_call(kernel, out_shape=shapes, in_specs=[vmem] * len(args), out...]
    all_to_all x0 -> x4, starting transfers between devices: none -> 23.6 us  [transposed(): lax.all_to_all(value, 'gz', 0, 0, axis_index_groups=ring_groups(lax.axis_...]
    all_to_all x0 -> x1, blocking collectives: none -> 22.4 us  [transposed(): lax.all_to_all(value, 'gz', 0, 0, axis_index_groups=ring_groups(lax.axis_...]
    unnamed x12 -> x66, local copies, waits for them, and re-layouts: 0.29 us -> 19.3 us
  transfers between devices with their start and end apart: 56 -> 30, of which waited for: 42 -> 24; matrix products, arithmetic and copies ran while one was open for 0% -> 1% of each run, Pallas kernels for 0% -> 5%
where the time goes in v1:
time: 340 us; the launch traced here: 337 us
  waiting for transfers between devices  151 us (44%)
  starting transfers between devices  105 us (31%)
  Pallas kernels  33.3 us (10%)
  local copies, waits for them, and re-layouts  23.1 us (7%)
  blocking collectives  22.4 us (7%)
    all_to_all x4, waiting for transfers between devices, transposed(): lax.all_to_all(value, 'gz', 0, 0, axis_index_groups=ring_groups(lax.axis_...  90.2 us
    ppermute x20, starting transfers between devices, shifted(): return lax.ppermute(value, 'gz', pairs)  76.1 us
    pallas_call x14, Pallas kernels, call(): pl.pallas_call(kernel, out_shape=shapes, in_specs=[vmem] * len(args), out...  33.3 us
    ppermute x20, waiting for transfers between devices, shifted(): return lax.ppermute(value, 'gz', pairs)  30.1 us
    ppermute x2, waiting for transfers between devices, row_shifted(): return lax.ppermute(value, ('gz', 'xy'), pairs)  24 us
    all_to_all x4, starting transfers between devices, transposed(): lax.all_to_all(value, 'gz', 0, 0, axis_index_groups=ring_groups(lax.axis_...  23.6 us
    all_to_all x1, blocking collectives, transposed(): lax.all_to_all(value, 'gz', 0, 0, axis_index_groups=ring_groups(lax.axis_...  22.4 us
    unnamed x66, local copies, waits for them, and re-layouts  19.3 us
  transfers between devices with their start and end apart: 30, of which 24 were waited for; matrix products, arithmetic and copies ran while one was open for 1% of the time, Pallas kernels for 5%

profile of v1, /device:TPU:8, one launch (start us, length us, event | category | flops | bytes accessed | tf_op | source)
XLA Modules:
  0.0 337.4 jit_solution(9988688283320413036)
XLA Ops:
  7.2 8.6 %all-to-all-start.1 = ((f32[8,2,48,640]{3,2,1,0:T(8,128)}), f32[8,2,48,640]{3,2,1,0:T(8,128)}, u32[]{:S(2)}, u32[]{:S(2)}) async-start(f32[8,2,48,640]{3,2,1,0:T(8,128)} %shard_map.59), calls=%async_computation.1 | async-start | bytes 3932160 | tf_op jit(solution)/shard_map/all_to_all | solution.py:46
  18.5 46.1 %all-to-all-done.1 = f32[8,2,48,640]{3,2,1,0:T(8,128)} async-done(((f32[8,2,48,640]{3,2,1,0:T(8,128)}), f32[8,2,48,640]{3,2,1,0:T(8,128)}, u32[]{:S(2)}, u32[]{:S(2)}) %all-to-all-start.1) | async-done | bytes 1966112 | tf_op jit(solution)/shard_map/all_to_all | solution.py:46
  64.6 3.6 %all-to-all-start = ((f32[8,2,40,640]{3,2,1,0:T(8,128)}), f32[8,2,40,640]{3,2,1,0:T(8,128)S(1)}, u32[]{:S(2)}, u32[]{:S(2)}) async-start(f32[8,2,40,640]{3,2,1,0:T(8,128)} %shard_map.58), calls=%async_computation | async-start | bytes 3276800 | tf_op jit(solution)/shard_map/all_to_all | solution.py:46
  69.3 4.6 %collective-permute-start.5 = (f32[3,48,640]{2,1,0:T(8,128)S(1)}, f32[3,48,640]{2,1,0:T(8,128)S(1)}, u32[]{:S(2)}, u32[]{:S(2)}) collective-permute-start(f32[3,48,640]{2,1,0:T(8,128)S(1)} %get-tuple-element.105), channel_id=1, source_target_pairs={{16,0},{18,2},{20,4},{22,6},{24,8},{26,10},{28,12},{30,14},{32,16}... | collective-permute-start | bytes 1105928 | tf_op jit(solution)/shard_map/ppermute | solution.py:27
  75.8 31.9 %all-to-all-done = f32[8,2,40,640]{3,2,1,0:T(8,128)S(1)} async-done(((f32[8,2,40,640]{3,2,1,0:T(8,128)}), f32[8,2,40,640]{3,2,1,0:T(8,128)S(1)}, u32[]{:S(2)}, u32[]{:S(2)}) %all-to-all-start) | async-done | bytes 1638432 | tf_op jit(solution)/shard_map/all_to_all | solution.py:46
  107.8 4.6 %collective-permute-start.2 = (f32[2,40,640]{2,1,0:T(8,128)S(1)}, f32[2,40,640]{2,1,0:T(8,128)S(1)}, u32[]{:S(2)}, u32[]{:S(2)}) collective-permute-start(f32[2,40,640]{2,1,0:T(8,128)S(1)} %get-tuple-element.107), channel_id=1, source_target_pairs={{16,0},{18,2},{20,4},{22,6},{24,8},{26,10},{28,12},{30,14},{32,16}... | collective-permute-start | bytes 614408 | tf_op jit(solution)/shard_map/ppermute | solution.py:27
  117.7 12.4 %shard_map.60 = (f32[20,48,640]{2,1,0:T(8,128)}, f32[20,48,640]{2,1,0:T(8,128)}, f32[21,48,640]{2,1,0:T(8,128)}, f32[20,48,640]{2,1,0:T(8,128)}, f32[10,48,640]{...) custom-call(f32[16,48,640]{2,1,0:T(8,128)} %bitcast.3.c_own, ...), custom_call_target="tpu_custom_call" | custom-call | tf_op jit(solution)/shard_map/pallas_call | solution.py:100
  136.3 9.6 %shard_map.61 = (f32[8,2,32,640]{3,2,1,0:T(8,128)S(1)}, f32[8,48,640]{2,1,0:T(8,128)S(1)}, f32[2,40,640]{2,1,0:T(8,128)S(1)}, f32[2,40,640]{2,1,0:T(8,128)S(1)}) custom-call(f32[16,40,640]{2,1,0:T(8,128)S(1)} %bitcast.10, f32[2,40,640]{2,1,0:T(8,128)S(1)} %collective-permute-done.1.s_low, f32[2,40,640]{2,1,0:T(8,128)S(1)} %collective-permute-done.2.s_high, ...), custom_call_target="tpu_custom_call" | custom-call | tf_op jit(solution)/shard_map/pallas_call | solution.py:100
  149.8 5.2 %collective-permute-start.7 = (f32[2,40,640]{2,1,0:T(8,128)S(1)}, f32[2,40,640]{2,1,0:T(8,128)S(1)}, u32[]{:S(2)}, u32[]{:S(2)}) collective-permute-start(f32[2,40,640]{2,1,0:T(8,128)S(1)} %get-tuple-element.61), channel_id=1, source_target_pairs={{16,0},{18,2},{20,4},{22,6},{24,8},{26,10},{28,12},{30,14},{32,16}... | collective-permute-start | bytes 614408 | tf_op jit(solution)/shard_map/ppermute | solution.py:27
  158.9 4.3 %shard_map.62 = (f32[8,32,640]{2,1,0:T(8,128)S(1)}, f32[4,32,640]{2,1,0:T(8,128)S(1)}, f32[4,8,640]{2,1,0:T(8,128)S(1)}, f32[4,8,640]{2,1,0:T(8,128)S(1)}) custom-call(f32[8,48,640]{2,1,0:T(8,128)S(1)} %get-tuple-element.59.source1, f32[2,40,640]{2,1,0:T(8,128)S(1)} %collective-permute-done.6.low, f32[2,40,640]{2,1,0:T(8,128)S(1)} %collective-permute-done.7.high, ...), custom_call_target="tpu_custom_call" | custom-call | tf_op jit(solution)/shard_map/pallas_call | solution.py:100
  163.3 22.4 %all_to_all.25 = f32[8,32,640]{2,1,0:T(8,128)} all-to-all(f32[8,32,640]{2,1,0:T(8,128)S(1)} %get-tuple-element.64), channel_id=1, replica_groups={{0,2,4,6,8,10,12,14},{16,18,20,22,24,26,28,30},{32,34,36,38,40,42,44,46..., dimensions={0} | all-to-all | bytes 1310720 | tf_op jit(solution)/shard_map/all_to_all | solution.py:46
  185.6 4.4 %all-to-all-start.2 = ((f32[8,2,32,640]{3,2,1,0:T(8,128)}), f32[8,2,32,640]{3,2,1,0:T(8,128)}, u32[]{:S(2)}, u32[]{:S(2)}) async-start(f32[8,2,32,640]{3,2,1,0:T(8,128)} %copy-done.13), calls=%async_computation.2 | async-start | bytes 2621440 | tf_op jit(solution)/shard_map/all_to_all | solution.py:46
  190.0 3.8 %collective-permute-start.8 = (f32[4,8,640]{2,1,0:T(8,128)S(1)}, f32[4,8,640]{2,1,0:T(8,128)S(1)}, u32[]{:S(2)}, u32[]{:S(2)}) collective-permute-start(f32[4,8,640]{2,1,0:T(8,128)S(1)} %get-tuple-element.66), channel_id=1, source_target_pairs={{0,2},{2,4},{4,6},{6,8},{8,10},{10,12},{12,14},{14,1},{1,3},{3,5},... | collective-permute-start | bytes 245768 | tf_op jit(solution)/shard_map/ppermute | solution.py:37
  195.1 20.3 %collective-permute-done.8.above = f32[4,8,640]{2,1,0:T(8,128)S(1)} collective-permute-done((f32[4,8,640]{2,1,0:T(8,128)S(1)}, f32[4,8,640]{2,1,0:T(8,128)S(1)}, u32[]{:S(2)}, u32[]{:S(2)}) %collective-permute-start.8) | collective-permute-done | bytes 81952 | tf_op jit(solution)/shard_map/ppermute | solution.py:37
  215.4 3.7 %collective-permute-done.9.below = f32[4,8,640]{2,1,0:T(8,128)S(1)} collective-permute-done((f32[4,8,640]{2,1,0:T(8,128)S(1)}, f32[4,8,640]{2,1,0:T(8,128)S(1)}, u32[]{:S(2)}, u32[]{:S(2)}) %collective-permute-start.9) | collective-permute-done | bytes 81952 | tf_op jit(solution)/shard_map/ppermute | solution.py:37
  219.2 3.9 %collective-permute-start.10 = (f32[1,48,640]{2,1,0:T(8,128)S(1)}, f32[1,48,640]{2,1,0:T(8,128)S(1)}, u32[]{:S(2)}, u32[]{:S(2)}) collective-permute-start(f32[1,48,640]{2,1,0:T(8,128)S(1)} %get-tuple-element.71), channel_id=1, source_target_pairs={{0,16},{2,18},{4,20},{6,22},{8,24},{10,26},{12,28},{14,30},{16,32}... | collective-permute-start | bytes 368648 | tf_op jit(solution)/shard_map/ppermute | solution.py:27
  223.2 4.5 %collective-permute-start.11 = (f32[1,48,640]{2,1,0:T(8,128)S(1)}, f32[1,48,640]{2,1,0:T(8,128)S(1)}, u32[]{:S(2)}, u32[]{:S(2)}) collective-permute-start(f32[1,48,640]{2,1,0:T(8,128)S(1)} %get-tuple-element.72), channel_id=1, source_target_pairs={{16,0},{18,2},{20,4},{22,6},{24,8},{26,10},{28,12},{30,14},{32,16}... | collective-permute-start | bytes 368648 | tf_op jit(solution)/shard_map/ppermute | solution.py:27
  232.1 3.8 %collective-permute-start.12 = (f32[1,48,640]{2,1,0:T(8,128)}, f32[1,48,640]{2,1,0:T(8,128)S(1)}, u32[]{:S(2)}, u32[]{:S(2)}) collective-permute-start(f32[1,48,640]{2,1,0:T(8,128)} %get-tuple-element.78), channel_id=1, source_target_pairs={{0,16},{2,18},{4,20},{6,22},{8,24},{10,26},{12,28},{14,30},{16,32}... | collective-permute-start | bytes 368648 | tf_op jit(solution)/shard_map/ppermute | solution.py:27
  236.0 4.5 %collective-permute-start.13 = (f32[1,48,640]{2,1,0:T(8,128)}, f32[1,48,640]{2,1,0:T(8,128)S(1)}, u32[]{:S(2)}, u32[]{:S(2)}) collective-permute-start(f32[1,48,640]{2,1,0:T(8,128)} %get-tuple-element.79), channel_id=1, source_target_pairs={{16,0},{18,2},{20,4},{22,6},{24,8},{26,10},{28,12},{30,14},{32,16}... | collective-permute-start | bytes 368648 | tf_op jit(solution)/shard_map/ppermute | solution.py:27
  247.3 3.9 %collective-permute-start.14 = (f32[1,48,640]{2,1,0:T(8,128)S(1)}, f32[1,48,640]{2,1,0:T(8,128)S(1)}, u32[]{:S(2)}, u32[]{:S(2)}) collective-permute-start(f32[1,48,640]{2,1,0:T(8,128)S(1)} %get-tuple-element.83), channel_id=1, source_target_pairs={{0,16},{2,18},{4,20},{6,22},{8,24},{10,26},{12,28},{14,30},{16,32}... | collective-permute-start | bytes 368648 | tf_op jit(solution)/shard_map/ppermute | solution.py:27
  251.2 4.5 %collective-permute-start.15 = (f32[1,48,640]{2,1,0:T(8,128)S(1)}, f32[1,48,640]{2,1,0:T(8,128)S(1)}, u32[]{:S(2)}, u32[]{:S(2)}) collective-permute-start(f32[1,48,640]{2,1,0:T(8,128)S(1)} %get-tuple-element.84), channel_id=1, source_target_pairs={{16,0},{18,2},{20,4},{22,6},{24,8},{26,10},{28,12},{30,14},{32,16}... | collective-permute-start | bytes 368648 | tf_op jit(solution)/shard_map/ppermute | solution.py:27
  258.5 3.9 %collective-permute-start.16 = (f32[1,48,640]{2,1,0:T(8,128)S(1)}, f32[1,48,640]{2,1,0:T(8,128)S(1)}, u32[]{:S(2)}, u32[]{:S(2)}) collective-permute-start(f32[1,48,640]{2,1,0:T(8,128)S(1)} %get-tuple-element.90), channel_id=1, source_target_pairs={{0,16},{2,18},{4,20},{6,22},{8,24},{10,26},{12,28},{14,30},{16,32}... | collective-permute-start | bytes 368648 | tf_op jit(solution)/shard_map/ppermute | solution.py:27
  262.3 4.5 %collective-permute-start.17 = (f32[1,48,640]{2,1,0:T(8,128)S(1)}, f32[1,48,640]{2,1,0:T(8,128)S(1)}, u32[]{:S(2)}, u32[]{:S(2)}) collective-permute-start(f32[1,48,640]{2,1,0:T(8,128)S(1)} %get-tuple-element.91), channel_id=1, source_target_pairs={{16,0},{18,2},{20,4},{22,6},{24,8},{26,10},{28,12},{30,14},{32,16}... | collective-permute-start | bytes 368648 | tf_op jit(solution)/shard_map/ppermute | solution.py:27
  269.9 6.5 %collective-permute-start.19 = (f32[1,48,640]{2,1,0:T(8,128)S(1)}, f32[1,48,640]{2,1,0:T(8,128)S(1)}, u32[]{:S(2)}, u32[]{:S(2)}) collective-permute-start(f32[1,48,640]{2,1,0:T(8,128)S(1)} %get-tuple-element.94.first), channel_id=1, source_target_pairs={{16,0},{18,2},{20,4},{22,6},{24,8},{26,10},{28,12},{30,14},{32,16}... | collective-permute-start | bytes 368648 | tf_op jit(solution)/shard_map/ppermute | solution.py:27
  279.5 6.2 %collective-permute-done.18.low = f32[1,48,640]{2,1,0:T(8,128)S(1)} collective-permute-done((f32[1,48,640]{2,1,0:T(8,128)S(1)}, f32[1,48,640]{2,1,0:T(8,128)S(1)}, u32[]{:S(2)}, u32[]{:S(2)}) %collective-permute-start.18) | collective-permute-done | bytes 122912 | tf_op jit(solution)/shard_map/ppermute | solution.py:27
  287.8 3.9 %collective-permute-start.20 = (f32[1,48,640]{2,1,0:T(8,128)S(1)}, f32[1,48,640]{2,1,0:T(8,128)S(1)}, u32[]{:S(2)}, u32[]{:S(2)}) collective-permute-start(f32[1,48,640]{2,1,0:T(8,128)S(1)} %get-tuple-element.99.second.second4), channel_id=1, source_target_pairs={{0,16},{2,18},{4,20},{6,22},{8,24},{10,26},{12,28},{14,30},{16,32}... | collective-permute-start | bytes 368648 | tf_op jit(solution)/shard_map/ppermute | solution.py:27
  293.4 3.3 collective-permute-done.20.low
  297.1 4.7 %collective-permute-done.22 = f32[1,48,640]{2,1,0:T(8,128)S(1)} collective-permute-done((f32[1,48,640]{2,1,0:T(8,128)S(1)}, f32[1,48,640]{2,1,0:T(8,128)S(1)}, u32[]{:S(2)}, u32[]{:S(2)}) %collective-permute-start.22) | collective-permute-done | bytes 122912 | tf_op jit(solution)/shard_map/ppermute | solution.py:42
  303.8 5.4 %collective-permute-start.24 = (f32[1,48,640]{2,1,0:T(8,128)S(1)}, f32[1,48,640]{2,1,0:T(8,128)S(1)}, u32[]{:S(2)}, u32[]{:S(2)}) collective-permute-start(f32[1,48,640]{2,1,0:T(8,128)S(1)} %get-tuple-element.103.first), channel_id=1, source_target_pairs={{0,32},{2,34},{4,36},{6,38},{8,40},{10,42},{12,44},{14,46},{16,48}... | collective-permute-start | bytes 368648 | tf_op jit(solution)/shard_map/ppermute | solution.py:27
  310.1 2.8 collective-permute-done.24.low
  314.0 7.0 %all-to-all-start.4 = ((f32[8,32,640]{2,1,0:T(8,128)}), f32[8,32,640]{2,1,0:T(8,128)S(1)}, u32[]{:S(2)}, u32[]{:S(2)}) async-start(f32[8,32,640]{2,1,0:T(8,128)} %shard_map.71), calls=%async_computation.4 | async-start | bytes 1310720 | tf_op jit(solution)/shard_map/all_to_all | solution.py:46
  323.5 12.2 %all-to-all-done.4 = f32[8,32,640]{2,1,0:T(8,128)S(1)} async-done(((f32[8,32,640]{2,1,0:T(8,128)}), f32[8,32,640]{2,1,0:T(8,128)S(1)}, u32[]{:S(2)}, u32[]{:S(2)}) %all-to-all-start.4) | async-done | bytes 655392 | tf_op jit(solution)/shard_map/all_to_all | solution.py:46
  (120 shorter events, 65.2 us)
Async XLA Ops:
  1.5 1.3 collective-permute-start.3
  7.2 57.4 %all-to-all-start.1 = ((f32[8,2,48,640]{3,2,1,0:T(8,128)}), f32[8,2,48,640]{3,2,1,0:T(8,128)}, u32[]{:S(2)}, u32[]{:S(2)}) async-start(f32[8,2,48,640]{3,2,1,0:T(8,128)} %shard_map.59), calls=%async_computation.1 | async-start | bytes 3932160 | tf_op jit(solution)/shard_map/all_to_all | solution.py:46
  15.8 1.3 collective-permute-start
  64.6 43.2 %all-to-all-start = ((f32[8,2,40,640]{3,2,1,0:T(8,128)}), f32[8,2,40,640]{3,2,1,0:T(8,128)S(1)}, u32[]{:S(2)}, u32[]{:S(2)}) async-start(f32[8,2,40,640]{3,2,1,0:T(8,128)} %shard_map.58), calls=%async_computation | async-start | bytes 3276800 | tf_op jit(solution)/shard_map/all_to_all | solution.py:46
  69.3 44.9 %collective-permute-start.5 = (f32[3,48,640]{2,1,0:T(8,128)S(1)}, f32[3,48,640]{2,1,0:T(8,128)S(1)}, u32[]{:S(2)}, u32[]{:S(2)}) collective-permute-start(f32[3,48,640]{2,1,0:T(8,128)S(1)} %get-tuple-element.105), channel_id=1, source_target_pairs={{16,0},{18,2},{20,4},{22,6},{24,8},{26,10},{28,12},{30,14},{32,16}... | collective-permute-start | bytes 1105928 | tf_op jit(solution)/shard_map/ppermute | solution.py:27
  73.9 41.1 %collective-permute-start.4 = (f32[3,48,640]{2,1,0:T(8,128)S(1)}, f32[3,48,640]{2,1,0:T(8,128)S(1)}, u32[]{:S(2)}, u32[]{:S(2)}) collective-permute-start(f32[3,48,640]{2,1,0:T(8,128)S(1)} %get-tuple-element.106), channel_id=1, source_target_pairs={{0,16},{2,18},{4,20},{6,22},{8,24},{10,26},{12,28},{14,30},{16,32}... | collective-permute-start | bytes 1105928 | tf_op jit(solution)/shard_map/ppermute | solution.py:27
  107.8 27.1 %collective-permute-start.2 = (f32[2,40,640]{2,1,0:T(8,128)S(1)}, f32[2,40,640]{2,1,0:T(8,128)S(1)}, u32[]{:S(2)}, u32[]{:S(2)}) collective-permute-start(f32[2,40,640]{2,1,0:T(8,128)S(1)} %get-tuple-element.107), channel_id=1, source_target_pairs={{16,0},{18,2},{20,4},{22,6},{24,8},{26,10},{28,12},{30,14},{32,16}... | collective-permute-start | bytes 614408 | tf_op jit(solution)/shard_map/ppermute | solution.py:27
  112.3 22.5 %collective-permute-start.1 = (f32[2,40,640]{2,1,0:T(8,128)S(1)}, f32[2,40,640]{2,1,0:T(8,128)S(1)}, u32[]{:S(2)}, u32[]{:S(2)}) collective-permute-start(f32[2,40,640]{2,1,0:T(8,128)S(1)} %get-tuple-element.108), channel_id=1, source_target_pairs={{0,16},{2,18},{4,20},{6,22},{8,24},{10,26},{12,28},{14,30},{16,32}... | collective-permute-start | bytes 614408 | tf_op jit(solution)/shard_map/ppermute | solution.py:27
  136.3 22.6 %copy-start.14 = (f32[10,48,640]{2,1,0:T(8,128)S(1)}, f32[10,48,640]{2,1,0:T(8,128)}, u32[]{:S(2)}) copy-start(f32[10,48,640]{2,1,0:T(8,128)} %get-tuple-element.63.north1) | copy-start | bytes 3686404
  147.0 10.7 %collective-permute-start.6 = (f32[2,40,640]{2,1,0:T(8,128)S(1)}, f32[2,40,640]{2,1,0:T(8,128)S(1)}, u32[]{:S(2)}, u32[]{:S(2)}) collective-permute-start(f32[2,40,640]{2,1,0:T(8,128)S(1)} %get-tuple-element.60), channel_id=1, source_target_pairs={{0,16},{2,18},{4,20},{6,22},{8,24},{10,26},{12,28},{14,30},{16,32}... | collective-permute-start | bytes 614408 | tf_op jit(solution)/shard_map/ppermute | solution.py:27
  149.8 9.1 %collective-permute-start.7 = (f32[2,40,640]{2,1,0:T(8,128)S(1)}, f32[2,40,640]{2,1,0:T(8,128)S(1)}, u32[]{:S(2)}, u32[]{:S(2)}) collective-permute-start(f32[2,40,640]{2,1,0:T(8,128)S(1)} %get-tuple-element.61), channel_id=1, source_target_pairs={{16,0},{18,2},{20,4},{22,6},{24,8},{26,10},{28,12},{30,14},{32,16}... | collective-permute-start | bytes 614408 | tf_op jit(solution)/shard_map/ppermute | solution.py:27
  185.6 33.5 %copy-start.3 = (f32[4,48,640]{2,1,0:T(8,128)S(1)}, f32[4,48,640]{2,1,0:T(8,128)}, u32[]{:S(2)}) copy-start(f32[4,48,640]{2,1,0:T(8,128)} %copy-done.2) | copy-start | bytes 1474564
  185.6 128.3 %all-to-all-start.2 = ((f32[8,2,32,640]{3,2,1,0:T(8,128)}), f32[8,2,32,640]{3,2,1,0:T(8,128)}, u32[]{:S(2)}, u32[]{:S(2)}) async-start(f32[8,2,32,640]{3,2,1,0:T(8,128)} %copy-done.13), calls=%async_computation.2 | async-start | bytes 2621440 | tf_op jit(solution)/shard_map/all_to_all | solution.py:46
  190.0 25.4 %collective-permute-start.8 = (f32[4,8,640]{2,1,0:T(8,128)S(1)}, f32[4,8,640]{2,1,0:T(8,128)S(1)}, u32[]{:S(2)}, u32[]{:S(2)}) collective-permute-start(f32[4,8,640]{2,1,0:T(8,128)S(1)} %get-tuple-element.66), channel_id=1, source_target_pairs={{0,2},{2,4},{4,6},{6,8},{8,10},{10,12},{12,14},{14,1},{1,3},{3,5},... | collective-permute-start | bytes 245768 | tf_op jit(solution)/shard_map/ppermute | solution.py:37
  193.8 25.3 %collective-permute-start.9 = (f32[4,8,640]{2,1,0:T(8,128)S(1)}, f32[4,8,640]{2,1,0:T(8,128)S(1)}, u32[]{:S(2)}, u32[]{:S(2)}) collective-permute-start(f32[4,8,640]{2,1,0:T(8,128)S(1)} %get-tuple-element.67), channel_id=1, source_target_pairs={{2,0},{4,2},{6,4},{8,6},{10,8},{12,10},{14,12},{1,14},{3,1},{5,3},... | collective-permute-start | bytes 245768 | tf_op jit(solution)/shard_map/ppermute | solution.py:37
  219.2 9.3 %collective-permute-start.10 = (f32[1,48,640]{2,1,0:T(8,128)S(1)}, f32[1,48,640]{2,1,0:T(8,128)S(1)}, u32[]{:S(2)}, u32[]{:S(2)}) collective-permute-start(f32[1,48,640]{2,1,0:T(8,128)S(1)} %get-tuple-element.71), channel_id=1, source_target_pairs={{0,16},{2,18},{4,20},{6,22},{8,24},{10,26},{12,28},{14,30},{16,32}... | collective-permute-start | bytes 368648 | tf_op jit(solution)/shard_map/ppermute | solution.py:27
  223.2 7.0 %collective-permute-start.11 = (f32[1,48,640]{2,1,0:T(8,128)S(1)}, f32[1,48,640]{2,1,0:T(8,128)S(1)}, u32[]{:S(2)}, u32[]{:S(2)}) collective-permute-start(f32[1,48,640]{2,1,0:T(8,128)S(1)} %get-tuple-element.72), channel_id=1, source_target_pairs={{16,0},{18,2},{20,4},{22,6},{24,8},{26,10},{28,12},{30,14},{32,16}... | collective-permute-start | bytes 368648 | tf_op jit(solution)/shard_map/ppermute | solution.py:27
  232.1 9.5 %collective-permute-start.12 = (f32[1,48,640]{2,1,0:T(8,128)}, f32[1,48,640]{2,1,0:T(8,128)S(1)}, u32[]{:S(2)}, u32[]{:S(2)}) collective-permute-start(f32[1,48,640]{2,1,0:T(8,128)} %get-tuple-element.78), channel_id=1, source_target_pairs={{0,16},{2,18},{4,20},{6,22},{8,24},{10,26},{12,28},{14,30},{16,32}... | collective-permute-start | bytes 368648 | tf_op jit(solution)/shard_map/ppermute | solution.py:27
  236.0 7.3 %collective-permute-start.13 = (f32[1,48,640]{2,1,0:T(8,128)}, f32[1,48,640]{2,1,0:T(8,128)S(1)}, u32[]{:S(2)}, u32[]{:S(2)}) collective-permute-start(f32[1,48,640]{2,1,0:T(8,128)} %get-tuple-element.79), channel_id=1, source_target_pairs={{16,0},{18,2},{20,4},{22,6},{24,8},{26,10},{28,12},{30,14},{32,16}... | collective-permute-start | bytes 368648 | tf_op jit(solution)/shard_map/ppermute | solution.py:27
  247.3 9.3 %collective-permute-start.14 = (f32[1,48,640]{2,1,0:T(8,128)S(1)}, f32[1,48,640]{2,1,0:T(8,128)S(1)}, u32[]{:S(2)}, u32[]{:S(2)}) collective-permute-start(f32[1,48,640]{2,1,0:T(8,128)S(1)} %get-tuple-element.83), channel_id=1, source_target_pairs={{0,16},{2,18},{4,20},{6,22},{8,24},{10,26},{12,28},{14,30},{16,32}... | collective-permute-start | bytes 368648 | tf_op jit(solution)/shard_map/ppermute | solution.py:27
  251.2 7.0 %collective-permute-start.15 = (f32[1,48,640]{2,1,0:T(8,128)S(1)}, f32[1,48,640]{2,1,0:T(8,128)S(1)}, u32[]{:S(2)}, u32[]{:S(2)}) collective-permute-start(f32[1,48,640]{2,1,0:T(8,128)S(1)} %get-tuple-element.84), channel_id=1, source_target_pairs={{16,0},{18,2},{20,4},{22,6},{24,8},{26,10},{28,12},{30,14},{32,16}... | collective-permute-start | bytes 368648 | tf_op jit(solution)/shard_map/ppermute | solution.py:27
  258.5 9.3 %collective-permute-start.16 = (f32[1,48,640]{2,1,0:T(8,128)S(1)}, f32[1,48,640]{2,1,0:T(8,128)S(1)}, u32[]{:S(2)}, u32[]{:S(2)}) collective-permute-start(f32[1,48,640]{2,1,0:T(8,128)S(1)} %get-tuple-element.90), channel_id=1, source_target_pairs={{0,16},{2,18},{4,20},{6,22},{8,24},{10,26},{12,28},{14,30},{16,32}... | collective-permute-start | bytes 368648 | tf_op jit(solution)/shard_map/ppermute | solution.py:27
  262.3 7.3 %collective-permute-start.17 = (f32[1,48,640]{2,1,0:T(8,128)S(1)}, f32[1,48,640]{2,1,0:T(8,128)S(1)}, u32[]{:S(2)}, u32[]{:S(2)}) collective-permute-start(f32[1,48,640]{2,1,0:T(8,128)S(1)} %get-tuple-element.91), channel_id=1, source_target_pairs={{16,0},{18,2},{20,4},{22,6},{24,8},{26,10},{28,12},{30,14},{32,16}... | collective-permute-start | bytes 368648 | tf_op jit(solution)/shard_map/ppermute | solution.py:27
  266.9 30.0 %collective-permute-start.23 = (f32[3,48,640]{2,1,0:T(8,128)S(1)}, f32[3,48,640]{2,1,0:T(8,128)S(1)}, u32[]{:S(2)}, u32[]{:S(2)}) collective-permute-start(f32[3,48,640]{2,1,0:T(8,128)S(1)} %pad_maximum_fusion), channel_id=1, source_target_pairs={{0,16},{2,18},{4,20},{6,22},{8,24},{10,26},{12,28},{14,30},{16,0},... | collective-permute-start | bytes 1105928 | tf_op jit(solution)/shard_map/ppermute | solution.py:42
  269.9 9.5 %collective-permute-start.19 = (f32[1,48,640]{2,1,0:T(8,128)S(1)}, f32[1,48,640]{2,1,0:T(8,128)S(1)}, u32[]{:S(2)}, u32[]{:S(2)}) collective-permute-start(f32[1,48,640]{2,1,0:T(8,128)S(1)} %get-tuple-element.94.first), channel_id=1, source_target_pairs={{16,0},{18,2},{20,4},{22,6},{24,8},{26,10},{28,12},{30,14},{32,16}... | collective-permute-start | bytes 368648 | tf_op jit(solution)/shard_map/ppermute | solution.py:27
  276.4 9.3 %collective-permute-start.18 = (f32[1,48,640]{2,1,0:T(8,128)S(1)}, f32[1,48,640]{2,1,0:T(8,128)S(1)}, u32[]{:S(2)}, u32[]{:S(2)}) collective-permute-start(f32[1,48,640]{2,1,0:T(8,128)S(1)} %get-tuple-element.94.first), channel_id=1, source_target_pairs={{0,16},{2,18},{4,20},{6,22},{8,24},{10,26},{12,28},{14,30},{16,32}... | collective-permute-start | bytes 368648 | tf_op jit(solution)/shard_map/ppermute | solution.py:27
  285.9 7.6 %collective-permute-start.21 = (f32[1,48,640]{2,1,0:T(8,128)S(1)}, f32[1,48,640]{2,1,0:T(8,128)S(1)}, u32[]{:S(2)}, u32[]{:S(2)}) collective-permute-start(f32[1,48,640]{2,1,0:T(8,128)S(1)} %get-tuple-element.99.second.second4), channel_id=1, source_target_pairs={{16,0},{18,2},{20,4},{22,6},{24,8},{26,10},{28,12},{30,14},{32,16}... | collective-permute-start | bytes 368648 | tf_op jit(solution)/shard_map/ppermute | solution.py:27
  287.8 8.9 %collective-permute-start.20 = (f32[1,48,640]{2,1,0:T(8,128)S(1)}, f32[1,48,640]{2,1,0:T(8,128)S(1)}, u32[]{:S(2)}, u32[]{:S(2)}) collective-permute-start(f32[1,48,640]{2,1,0:T(8,128)S(1)} %get-tuple-element.99.second.second4), channel_id=1, source_target_pairs={{0,16},{2,18},{4,20},{6,22},{8,24},{10,26},{12,28},{14,30},{16,32}... | collective-permute-start | bytes 368648 | tf_op jit(solution)/shard_map/ppermute | solution.py:27
  296.9 5.0 %collective-permute-start.22 = (f32[1,48,640]{2,1,0:T(8,128)S(1)}, f32[1,48,640]{2,1,0:T(8,128)S(1)}, u32[]{:S(2)}, u32[]{:S(2)}) collective-permute-start(f32[1,48,640]{2,1,0:T(8,128)S(1)} %shard_map.69), channel_id=1, source_target_pairs={{0,16},{2,18},{4,20},{6,22},{8,24},{10,26},{12,28},{14,30},{16,0},... | collective-permute-start | bytes 368648 | tf_op jit(solution)/shard_map/ppermute | solution.py:42
  301.8 8.3 %collective-permute-start.25 = (f32[1,48,640]{2,1,0:T(8,128)S(1)}, f32[1,48,640]{2,1,0:T(8,128)S(1)}, u32[]{:S(2)}, u32[]{:S(2)}) collective-permute-start(f32[1,48,640]{2,1,0:T(8,128)S(1)} %get-tuple-element.103.first), channel_id=1, source_target_pairs={{32,0},{34,2},{36,4},{38,6},{40,8},{42,10},{44,12},{46,14},{48,16}... | collective-permute-start | bytes 368648 | tf_op jit(solution)/shard_map/ppermute | solution.py:27
  303.8 9.2 %collective-permute-start.24 = (f32[1,48,640]{2,1,0:T(8,128)S(1)}, f32[1,48,640]{2,1,0:T(8,128)S(1)}, u32[]{:S(2)}, u32[]{:S(2)}) collective-permute-start(f32[1,48,640]{2,1,0:T(8,128)S(1)} %get-tuple-element.103.first), channel_id=1, source_target_pairs={{0,32},{2,34},{4,36},{6,38},{8,40},{10,42},{12,44},{14,46},{16,48}... | collective-permute-start | bytes 368648 | tf_op jit(solution)/shard_map/ppermute | solution.py:27
  314.0 21.7 %all-to-all-start.4 = ((f32[8,32,640]{2,1,0:T(8,128)}), f32[8,32,640]{2,1,0:T(8,128)S(1)}, u32[]{:S(2)}, u32[]{:S(2)}) async-start(f32[8,32,640]{2,1,0:T(8,128)} %shard_map.71), calls=%async_computation.4 | async-start | bytes 1310720 | tf_op jit(solution)/shard_map/all_to_all | solution.py:46
  (30 other events, 161.9 us)

commit v2 on v1

v2 whole, which is shorter than its diff:
```python
from functools import partial

import jax
import jax.numpy as jnp
from jax import lax
from jax.experimental import pallas as pl
from jax.experimental.pallas import tpu as pltpu
from jax.sharding import PartitionSpec as P

RING = 8
HALO = 8
THIN = 4
damping = 0.8
pore_value = 1.0
grain_value = 0.1
clay_value = 0.3
TINY = 1e-30


def ring_groups(count):
    return [[r * RING + k for k in range(RING)] for r in range(count // RING)]


def shifted(value, by):
    size = lax.axis_size("gz")
    pairs = [(i, i + by) for i in range(size) if 0 <= i + by < size]
    return lax.ppermute(value, "gz", pairs)


def row_shifted(value, by):
    pairs = []
    for ring in range(lax.axis_size("gz") // RING):
        for t in range(2 * RING):
            u = t + by
            if 0 <= u < 2 * RING:
                pairs.append(((ring * RING + t % RING) * 2 + t // RING, (ring * RING + u % RING) * 2 + u // RING))
    return lax.ppermute(value, ("gz", "xy"), pairs)


def partner(value):
    size = lax.axis_size("gz")
    return lax.ppermute(value, "gz", [(i, i + RING if (i // RING) % 2 == 0 else i - RING) for i in range(size)])


def transposed(value):
    return lax.all_to_all(value, "gz", 0, 0, axis_index_groups=ring_groups(lax.axis_size("gz")), tiled=True)


def conductivity(labels, fraction):
    return jnp.where(labels == 0, pore_value, jnp.where(labels == 1, grain_value, clay_value)) * fraction


def harmonic(one_side, other_side):
    return (2.0 * one_side * other_side) / jnp.maximum(one_side + other_side, TINY)


def next_row(v):
    return pltpu.roll(v, v.shape[0] - 1, 0)


def previous_row(v):
    return pltpu.roll(v, 1, 0)


def next_column(v):
    return pltpu.roll(v, v.shape[1] - 1, 1)


def previous_column(v):
    return pltpu.roll(v, 1, 1)


def neighbours(v, below, above, east, north, down, up):
    return (
        east * next_row(v)
        + previous_row(east * v)
        + north * next_column(v)
        + previous_column(north * v)
        + down * below
        + up * above
    )


def weight(c, east, north, down, up):
    diagonal = east + previous_row(east) + north + previous_column(north) + down + up
    return jnp.where(c > 0, damping / jnp.where(c > 0, diagonal, 1.0), 0.0)


def loop(count, body):
    def step(k, carry):
        body(k)
        return carry

    lax.fori_loop(0, count, step, 0)


def call(kernel, outs, scratch, *args, limit=8, work=0.0):
    shapes = [jax.ShapeDtypeStruct(s, jnp.float32) for s in outs]
    vmem = pl.BlockSpec(memory_space=pltpu.VMEM)
    cost = pl.CostEstimate(flops=int(work * 1.0e9), bytes_accessed=int(work * 3.0e6), transcendentals=0) if work else None
    return pl.pallas_call(
        kernel,
        out_shape=shapes,
        in_specs=[vmem] * len(args),
        out_specs=[vmem] * len(shapes),
        scratch_shapes=[pltpu.VMEM(s, jnp.float32) for s in scratch],
        compiler_params=pltpu.CompilerParams(vmem_limit_bytes=limit * 1024 * 1024),
        cost_estimate=cost,
    )(*args)


def cut_conduct(labels, fraction, out):
    planes, rows, _ = labels.shape
    strip = rows // RING
    for p in range(planes):
        for k in range(RING):
            at = slice(k * strip, (k + 1) * strip)
            out[k, p] = conductivity(labels[p, at], fraction[p, at])


def cut_source(source, top, bottom, out):
    planes, rows, _ = source.shape
    strip = rows // RING
    for p in range(planes):
        for k in range(RING):
            start = k * strip
            if k == 0:
                out[k, p, :THIN] = top[p, HALO - THIN:]
            else:
                out[k, p, :THIN] = source[p, start - THIN:start]
            out[k, p, THIN:THIN + strip] = source[p, start:start + strip]
            if k == RING - 1:
                out[k, p, THIN + strip:] = bottom[p, :THIN]
            else:
                out[k, p, THIN + strip:] = source[p, start + strip:start + strip + THIN]


def plane_faces(c):
    last = lax.broadcasted_iota(jnp.int32, c.shape, 1) == c.shape[1] - 1
    return harmonic(c, next_row(c)), jnp.where(last, 0.0, harmonic(c, next_column(c)))


def make_faces(c_own, above, below, c, east0, north0, east1, north1, east2, north2, east3, north3, east4, north4,
               bundle_down, bundle_up):
    strip = c_own.shape[1]

    def plane(p):
        c[p, :HALO] = above[p]
        c[p, HALO:HALO + strip] = c_own[p]
        c[p, HALO + strip:] = below[p]
        east0[p], north0[p] = plane_faces(c[p])

    loop(16, plane)

    def plane1(q):
        east1[q] = east0[2 * q] + east0[2 * q + 1]
        north1[q] = north0[2 * q] + north0[2 * q + 1]

    loop(8, plane1)
    for finer, coarser in ((east1, east2), (north1, north2), (east2, east3), (north2, north3), (east3, east4), (north3, north4)):
        for q in range(coarser.shape[0]):
            coarser[q] = finer[2 * q] + finer[2 * q + 1]
    middle = harmonic(c[7], c[8])
    for bundle, first, edge2, face2, edge3 in ((bundle_down, 0, 0, 4, 0), (bundle_up, 13, 3, 12, 1)):
        for k in range(3):
            bundle[k] = c[first + k]
        bundle[3] = east2[edge2]
        bundle[4] = north2[edge2]
        bundle[5] = harmonic(c[face2 - 1], c[face2])
        bundle[6] = east3[edge3]
        bundle[7] = north3[edge3]
        bundle[8] = middle


def make_weights(c, low, high, east0, north0, east1, north1, east2, north2, east3, north3, east4, north4,
                 z0, z1, z2, z3, z4, w0, w1, w2, w3, w4, halo0, halo1, halo2, halo3):
    def z_face(p):
        z0[p] = harmonic(c[p - 1], c[p])

    loop(15, lambda k: z_face(k + 1))
    z0[0] = jnp.where(low[2] > 0, harmonic(low[2], c[0]), 2.0 * c[0])
    z0[16] = jnp.where(high[0] > 0, harmonic(c[15], high[0]), 2.0 * c[15])

    def weigh(p):
        w0[p] = weight(c[p], east0[p], north0[p], z0[p], z0[p + 1])

    loop(16, weigh)
    loop(9, lambda q: z1.__setitem__(q, z0[2 * q]))

    def weigh1(q):
        w1[q] = weight(c[0], east1[q], north1[q], z1[q], z1[q + 1])

    loop(8, weigh1)
    for z_fine, z, east, north, w in ((z1, z2, east2, north2, w2), (z2, z3, east3, north3, w3), (z3, z4, east4, north4, w4)):
        for q in range(z.shape[0]):
            z[q] = z_fine[2 * q]
        for q in range(w.shape[0]):
            w[q] = weight(c[0], east[q], north[q], z[q], z[q + 1])

    for side, bundle, near, far, last, face in ((0, low, 2, 1, 0, 0), (1, high, 0, 1, 2, 16)):
        shared = z0[face]
        middle = harmonic(bundle[near], bundle[far])
        outer = harmonic(bundle[far], bundle[last])
        east_near, north_near = plane_faces(bundle[near])
        east_far, north_far = plane_faces(bundle[far])
        halo0[side] = east_near
        halo0[2 + side] = north_near
        halo0[4 + side] = middle
        halo0[6 + side] = weight(bundle[near], east_near, north_near, shared, middle)
        halo0[8 + side] = weight(bundle[far], east_far, north_far, middle, outer)
        halo1[side] = east_near + east_far
        halo1[2 + side] = north_near + north_far
        halo1[4 + side] = outer
        halo1[6 + side] = weight(bundle[near], east_near + east_far, north_near + north_far, shared, outer)
        for halo, at in ((halo2, 3), (halo3, 6)):
            halo[side] = bundle[at]
            halo[2 + side] = bundle[at + 1]
            halo[4 + side] = bundle[at + 2]
            halo[6 + side] = weight(bundle[near], bundle[at], bundle[at + 1], shared, bundle[at + 2])


def make_last_faces(east4, north4, w4, other, down, up, east5, north5, w5):
    east5[0] = east4[0] + other[0]
    north5[0] = north4[0] + other[1]
    w5[0] = weight(w4[0], east5[0], north5[0], down[0], up[0])


def sweep_and_rest(s, first, total, second, east, north, z, w, halo):
    count = w.shape[0]

    def sweep(q):
        t = 1.2 * s[q + 1] + neighbours(first[q + 2], first[q + 1], first[q + 3], east[q], north[q], z[q], z[q + 1])
        total[q] = t
        second[q + 1] = w[q] * t

    loop(count, sweep)
    for side, q, down, up in ((0, -1, halo[4], z[0]), (1, count, z[count], halo[5])):
        second[q + 1] = halo[6 + side] * (1.2 * s[q + 1] + neighbours(
            first[q + 2], first[q + 1], first[q + 3], halo[side], halo[2 + side], down, up))

    def rest(q):
        return s[q + 1] - damping * total[q] + neighbours(
            second[q + 1], second[q], second[q + 2], east[q], north[q], z[q], z[q + 1])

    return rest


def fine_level(s_own, s_low, s_high, east, north, z, w, halo, w_next, fine, s_next, edge_down, edge_up, s, first, total, second):
    strip = fine.shape[2]
    columns = s.shape[2]
    blank = jnp.zeros((HALO - THIN, columns), jnp.float32)

    def place(k, value):
        s[k, :HALO - THIN] = blank
        s[k, HALO - THIN:HALO + strip + THIN] = value
        s[k, HALO + strip + THIN:] = blank

    place(0, s_low[0])
    first[0] = halo[8] * s[0]
    place(0, s_high[1])
    first[19] = halo[9] * s[0]
    place(0, s_low[1])
    first[1] = halo[6] * s[0]
    place(17, s_high[0])
    first[18] = halo[7] * s[17]

    def start(q):
        place(q + 1, s_own[q])
        first[q + 2] = w[q] * s[q + 1]

    loop(16, start)
    rest = sweep_and_rest(s, first, total, second, east, north, z, w, halo)

    def pair(q):
        s_next[q] = rest(2 * q) + rest(2 * q + 1)
        fine[q, 0] = second[2 * q + 1, HALO:HALO + strip]
        fine[q, 1] = second[2 * q + 2, HALO:HALO + strip]

    loop(8, pair)
    edge_down[0] = s_next[0]
    edge_down[1] = w_next[1] * s_next[1]
    edge_up[0] = w_next[6] * s_next[6]
    edge_up[1] = s_next[7]


def open_level(s_own, w, low, high, halo, s, first):
    count = w.shape[0]
    s[0] = low[1]
    s[count + 1] = high[0]
    first[0] = low[0]
    first[1] = halo[6] * low[1]
    first[count + 2] = halo[7] * high[0]
    first[count + 3] = high[1]

    def start(q):
        s[q + 1] = s_own[q]
        first[q + 2] = w[q] * s_own[q]

    loop(count, start)


def first_coarse_level(s_own, low, high, east, north, z, w, halo, out, s_next, top, bottom, s, first, total, second):
    strip = out.shape[1]
    open_level(s_own, w, low, high, halo, s, first)
    rest = sweep_and_rest(s, first, total, second, east, north, z, w, halo)

    def pair(q):
        value = rest(2 * q) + rest(2 * q + 1)
        s_next[q] = value[HALO:HALO + strip]
        top[q] = value[HALO:2 * HALO]
        bottom[q] = value[strip:HALO + strip]
        out[2 * q] = second[2 * q + 1, HALO:HALO + strip]
        out[2 * q + 1] = second[2 * q + 2, HALO:HALO + strip]

    loop(4, pair)


def middle_level(s_own, low, high, east, north, z, w, halo, w_next, out, s_next, *rest_refs):
    edges, (s, first, total, second) = rest_refs[:-4], rest_refs[-4:]
    count = w.shape[0]
    strip = out.shape[1]
    open_level(s_own, w, low, high, halo, s, first)
    rest = sweep_and_rest(s, first, total, second, east, north, z, w, halo)
    for q in range(count // 2):
        s_next[q] = rest(2 * q) + rest(2 * q + 1)
    for q in range(count):
        out[q] = second[q + 1, HALO:HALO + strip]
    if len(edges) == 2:
        edge_down, edge_up = edges
        edge_down[0] = s_next[0]
        edge_down[1] = w_next[1] * s_next[1]
        edge_up[0] = w_next[count // 2 - 2] * s_next[count // 2 - 2]
        edge_up[1] = s_next[count // 2 - 1]
    else:
        edges[0][0] = w_next[0] * s_next[0]


def widen(source2, above, below, w2, fine, plane_out, s, edge_down, edge_up, back):
    count, strip, _ = source2.shape
    for q in range(count):
        s[q, :HALO] = above[q]
        s[q, HALO:HALO + strip] = source2[q]
        s[q, HALO + strip:] = below[q]
    edge_down[0] = s[0]
    edge_down[1] = w2[1] * s[1]
    edge_up[0] = w2[count - 2] * s[count - 2]
    edge_up[1] = s[count - 1]

    def gather(k):
        back[k, 0] = fine[k, 0]
        back[k, 1] = fine[k, 1]
        back[k, 2] = plane_out[k]

    loop(RING, gather)


def sweep_last(s, first, low, high, east, north, z, w, total, second):
    t = 1.2 * s[0] + neighbours(first[0], low[0], high[0], east[0], north[0], z[0], z[1])
    total[0] = t
    second[0] = w[0] * t


def rest_last(s, total, second, low, high, east, north, z, out):
    out[0] = s[0] - damping * total[0] + neighbours(second[0], low[0], high[0], east[0], north[0], z[0], z[1])


def finish(s, first, low, high, east, north, down, up, w, second2, second3, second4, settled, out):
    strip = out.shape[1]
    second5 = w[0] * (1.2 * s[0] + neighbours(first[0], low[0], high[0], east[0], north[0], down[0], up[0]))
    own = slice(HALO, HALO + strip)
    for k in range(RING):
        out[k] = ((second2[k // 2] + second3[k // 4]) + second4[0, own]) + second5[own]


def exchange(edge_low, edge_high, distance=RING):
    return shifted(edge_high, distance), shifted(edge_low, -distance)


def on_device(right_side, labels, fraction):
    planes, rows, columns = right_side.shape
    strip = rows // RING
    frame = strip + 2 * HALO
    at_core = lax.axis_index("xy")
    even_ring = (lax.axis_index("gz") // RING) % 2 == 0

    def edges_of(first_rows, last_rows):
        got = lax.ppermute(jnp.where(at_core == 0, last_rows, first_rows), "xy", [(0, 1), (1, 0)])
        return jnp.where(at_core == 1, got, 0.0), jnp.where(at_core == 0, got, 0.0)

    def shape(n):
        return (n, frame, columns)

    (c_cut,) = call(cut_conduct, [(RING, planes, strip, columns)], [], labels, fraction, limit=10)
    c_own = transposed(c_cut).reshape(RING * planes, strip, columns)
    s_top, s_bottom = edges_of(right_side[:, :HALO], right_side[:, rows - HALO:])
    (s_cut,) = call(cut_source, [(RING, planes, strip + 2 * THIN, columns)], [], right_side, s_top, s_bottom, limit=10)
    s_own = transposed(s_cut).reshape(RING * planes, strip + 2 * THIN, columns)

    above = row_shifted(c_own[:, strip - HALO:], 1)
    below = row_shifted(c_own[:, :HALO], -1)
    c, *plane_set, bundle_down, bundle_up = call(
        make_faces, [shape(n) for n in (16, 16, 16, 8, 8, 4, 4, 2, 2, 1, 1, 9, 9)], [], c_own, above, below, limit=18, work=8.0)
    c_low, c_high = exchange(bundle_down, bundle_up)
    z0, z1, z2, z3, z4, w0, w1, w2, w3, w4, halo0, halo1, halo2, halo3 = call(
        make_weights, [shape(n) for n in (17, 9, 5, 3, 2, 16, 8, 4, 2, 1, 10, 8, 8, 8)], [],
        c, c_low, c_high, *plane_set, limit=26, work=8.0)
    east0, north0, east1, north1, east2, north2, east3, north3, east4, north4 = plane_set
    outer = jnp.where(even_ring, z4[:1], z4[1:])
    other = partner(jnp.concatenate([east4, north4, outer], axis=0))
    down5 = jnp.where(even_ring, z4[:1], other[2:])
    up5 = jnp.where(even_ring, other[2:], z4[1:])
    east5, north5, w5 = call(make_last_faces, [shape(1)] * 3, [], east4, north4, w4, other, down5, up5)

    s_low, s_high = exchange(s_own[:2], s_own[-2:])
    fine, s1, edge_down, edge_up = call(
        fine_level, [(RING, planes, strip, columns), shape(8), shape(2), shape(2)],
        [shape(18), shape(20), shape(16), shape(18)],
        s_own, s_low, s_high, east0, north0, z0, w0, halo0, w1, limit=26, work=8.0)

    low, high = exchange(edge_down, edge_up)
    plane_out, s2, top, bottom = call(
        first_coarse_level,
        [(8, strip, columns), (4, strip, columns), (4, HALO, columns), (4, HALO, columns)],
        [shape(10), shape(12), shape(8), shape(10)], s1, low, high, east1, north1, z1, w1, halo1, limit=15, work=4.0)

    above = row_shifted(bottom, 1)
    below = row_shifted(top, -1)
    s2, edge_down, edge_up, back = call(
        widen, [shape(4), shape(2), shape(2), (RING, planes + 1, strip, columns)], [], s2, above, below, w2, fine, plane_out, limit=10)
    low, high = exchange(edge_down, edge_up)
    second2, s3, edge_down, edge_up = call(
        middle_level, [(4, strip, columns), shape(2), shape(2), shape(2)], [shape(6), shape(8), shape(4), shape(6)],
        s2, low, high, east2, north2, z2, w2, halo2, w3, limit=10)
    low, high = exchange(edge_down, edge_up)
    second3, s4, first4 = call(
        middle_level, [(2, strip, columns), shape(1), shape(1)], [shape(4), shape(6), shape(2), shape(4)],
        s3, low, high, east3, north3, z3, w3, halo3, w4)
    low, high = exchange(first4, first4)
    total4, second4 = call(sweep_last, [shape(1), shape(1)], [], s4, first4, low, high, east4, north4, z4, w4)
    low, high = exchange(second4, second4)
    (rest4,) = call(rest_last, [shape(1)], [], s4, total4, second4, low, high, east4, north4, z4)
    s5 = rest4 + partner(rest4)
    first5 = w5 * s5
    low, high = exchange(first5, first5, 2 * RING)
    back = transposed(back)
    (summed,) = call(finish, [(RING, strip, columns)], [],
                     s5, first5, low, high, east5, north5, down5, up5, w5, second2, second3, second4, back[0, 0, :HALO])

    fine_iterate = jnp.transpose(back[:, :planes], (1, 0, 2, 3)).reshape(planes, rows, columns)
    plane_iterate = back[:, planes].reshape(1, rows, columns)
    coarse_return = transposed(summed).reshape(1, rows, columns)
    return fine_iterate, plane_iterate, coarse_return


def solution(mesh):
    spec = P("gz", "xy", None)
    return jax.shard_map(
        on_device,
        mesh=mesh,
        in_specs=(spec, spec, spec),
        out_specs=(spec, spec, spec),
        check_vma=False,
    )
```

time: 340 us -> 303 us (0.89)
  blocking collectives: 22.4 us -> 0 us
  waiting for transfers between devices: 151 us -> 130 us
  local copies, waits for them, and re-layouts: 23.1 us -> 36 us
  Pallas kernels: 33.3 us -> 27.7 us
    all_to_all x4, waiting for transfers between devices: 90.2 us -> 41.8 us  [transposed(): lax.all_to_all(value, 'gz', 0, 0, axis_index_groups=ring_groups(lax.axis_...]
    all_to_all x1 -> x0, blocking collectives: 22.4 us -> none  [transposed(): lax.all_to_all(value, 'gz', 0, 0, axis_index_groups=ring_groups(lax.axis_...]
    ppermute x2 -> x4, waiting for transfers between devices: 24 us -> 42.2 us  [row_shifted(): return lax.ppermute(value, ('gz', 'xy'), pairs)]
    unnamed x66 -> x89, local copies, waits for them, and re-layouts: 19.3 us -> 30.6 us
    ppermute x20 -> x16, starting transfers between devices: 76.1 us -> 65.4 us  [shifted(): return lax.ppermute(value, 'gz', pairs)]
    ppermute x20 -> x16, waiting for transfers between devices: 30.1 us -> 40.3 us  [shifted(): return lax.ppermute(value, 'gz', pairs)]
    ppermute x2 -> x4, starting transfers between devices: 5.08 us -> 11 us  [row_shifted(): return lax.ppermute(value, ('gz', 'xy'), pairs)]
    pallas_call x14 -> x13, Pallas kernels: 33.3 us -> 27.7 us  [call(): pl.pallas_call(kernel, out_shape=shapes, in_specs=[vmem] * len(args), out...]
  transfers between devices with their start and end apart: 30 -> 27, of which waited for: 24 -> 22; matrix products, arithmetic and copies ran while one was open for 1% -> 2% of each run, Pallas kernels for 5% -> 5%
where the time goes in v2:
time: 303 us; the launch traced here: 301 us
  waiting for transfers between devices  130 us (43%)
  starting transfers between devices  107 us (35%)
  local copies, waits for them, and re-layouts  36 us (12%)
  Pallas kernels  27.7 us (9%)
    ppermute x16, starting transfers between devices, shifted(): return lax.ppermute(value, 'gz', pairs)  65.4 us
    ppermute x4, waiting for transfers between devices, row_shifted(): return lax.ppermute(value, ('gz', 'xy'), pairs)  42.2 us
    all_to_all x4, waiting for transfers between devices, transposed(): lax.all_to_all(value, 'gz', 0, 0, axis_index_groups=ring_groups(lax.axis_...  41.8 us
    ppermute x16, waiting for transfers between devices, shifted(): return lax.ppermute(value, 'gz', pairs)  40.3 us
    unnamed x89, local copies, waits for them, and re-layouts  30.6 us
    all_to_all x4, starting transfers between devices, transposed(): lax.all_to_all(value, 'gz', 0, 0, axis_index_groups=ring_groups(lax.axis_...  28.7 us
    pallas_call x13, Pallas kernels, call(): pl.pallas_call(kernel, out_shape=shapes, in_specs=[vmem] * len(args), out...  27.7 us
    ppermute x4, starting transfers between devices, row_shifted(): return lax.ppermute(value, ('gz', 'xy'), pairs)  11 us
  transfers between devices with their start and end apart: 27, of which 22 were waited for; matrix products, arithmetic and copies ran while one was open for 2% of the time, Pallas kernels for 5%

profile of v2, /device:TPU:8, one launch (start us, length us, event | category | flops | bytes accessed | tf_op | source)
XLA Modules:
  0.0 301.2 jit_solution(14323265495105272979)
XLA Ops:
  4.6 8.6 %all-to-all-start.1 = ((f32[8,2,32,640]{3,2,1,0:T(8,128)}), f32[8,2,32,640]{3,2,1,0:T(8,128)S(1)}, u32[]{:S(2)}, u32[]{:S(2)}) async-start(f32[8,2,32,640]{3,2,1,0:T(8,128)} %shard_map.59), calls=%async_computation.1 | async-start | bytes 2621440 | tf_op jit(solution)/shard_map/all_to_all | solution.py:46
  15.9 31.6 %all-to-all-done.1 = f32[8,2,32,640]{3,2,1,0:T(8,128)S(1)} async-done(((f32[8,2,32,640]{3,2,1,0:T(8,128)}), f32[8,2,32,640]{3,2,1,0:T(8,128)S(1)}, u32[]{:S(2)}, u32[]{:S(2)}) %all-to-all-start.1) | async-done | bytes 1310752 | tf_op jit(solution)/shard_map/all_to_all | solution.py:46
  47.6 3.6 %all-to-all-start = ((f32[8,2,40,640]{3,2,1,0:T(8,128)}), f32[8,2,40,640]{3,2,1,0:T(8,128)S(1)}, u32[]{:S(2)}, u32[]{:S(2)}) async-start(f32[8,2,40,640]{3,2,1,0:T(8,128)} %shard_map.58), calls=%async_computation | async-start | bytes 3276800 | tf_op jit(solution)/shard_map/all_to_all | solution.py:46
  51.2 3.8 %collective-permute-start.3 = (f32[16,8,640]{2,1,0:T(8,128)S(1)}, f32[16,8,640]{2,1,0:T(8,128)S(1)}, u32[]{:S(2)}, u32[]{:S(2)}) collective-permute-start(f32[16,8,640]{2,1,0:T(8,128)S(1)} %get-tuple-element.110), channel_id=1, source_target_pairs={{0,2},{2,4},{4,6},{6,8},{8,10},{10,12},{12,14},{14,1},{1,3},{3,5},... | collective-permute-start | bytes 983048 | tf_op jit(solution)/shard_map/ppermute | solution.py:37
  56.4 37.7 %collective-permute-done.3.above = f32[16,8,640]{2,1,0:T(8,128)S(1)} collective-permute-done((f32[16,8,640]{2,1,0:T(8,128)S(1)}, f32[16,8,640]{2,1,0:T(8,128)S(1)}, u32[]{:S(2)}, u32[]{:S(2)}) %collective-permute-start.3) | collective-permute-done | bytes 327712 | tf_op jit(solution)/shard_map/ppermute | solution.py:37
  96.0 3.8 %shard_map.60 = (f32[16,48,640]{2,1,0:T(8,128)S(1)}, f32[16,48,640]{2,1,0:T(8,128)S(1)}, f32[16,48,640]{2,1,0:T(8,128)S(1)}, f32[8,48,640]{2,1,0:T(8,128)S(1)}, ...) custom-call(f32[16,32,640]{2,1,0:T(8,128)S(1)} %bitcast.14, ...), custom_call_target="tpu_custom_call" | custom-call | flops 8000000000 | bytes 24000000 | tf_op jit(solution)/shard_map/pallas_call | solution.py:101
  108.6 3.4 %collective-permute-start.5 = (f32[9,48,640]{2,1,0:T(8,128)}, f32[9,48,640]{2,1,0:T(8,128)S(1)}, u32[]{:S(2)}, u32[]{:S(2)}) collective-permute-start(f32[9,48,640]{2,1,0:T(8,128)} %get-tuple-element.57), channel_id=1, source_target_pairs={{0,16},{2,18},{4,20},{6,22},{8,24},{10,26},{12,28},{14,30},{16,32}... | collective-permute-start | bytes 3317768 | tf_op jit(solution)/shard_map/ppermute | solution.py:27
  112.0 4.6 %collective-permute-start.6 = (f32[9,48,640]{2,1,0:T(8,128)}, f32[9,48,640]{2,1,0:T(8,128)}, u32[]{:S(2)}, u32[]{:S(2)}) collective-permute-start(f32[9,48,640]{2,1,0:T(8,128)} %get-tuple-element.58), channel_id=1, source_target_pairs={{16,0},{18,2},{20,4},{22,6},{24,8},{26,10},{28,12},{30,14},{32,16}... | collective-permute-start | bytes 3317768 | tf_op jit(solution)/shard_map/ppermute | solution.py:27
  118.5 6.0 %collective-permute-start.2 = (f32[2,40,640]{2,1,0:T(8,128)S(1)}, f32[2,40,640]{2,1,0:T(8,128)S(1)}, u32[]{:S(2)}, u32[]{:S(2)}) collective-permute-start(f32[2,40,640]{2,1,0:T(8,128)S(1)} %get-tuple-element.107), channel_id=1, source_target_pairs={{16,0},{18,2},{20,4},{22,6},{24,8},{26,10},{28,12},{30,14},{32,16}... | collective-permute-start | bytes 614408 | tf_op jit(solution)/shard_map/ppermute | solution.py:27
  124.5 15.6 %collective-permute-done.5.low = f32[9,48,640]{2,1,0:T(8,128)S(1)} collective-permute-done((f32[9,48,640]{2,1,0:T(8,128)}, f32[9,48,640]{2,1,0:T(8,128)S(1)}, u32[]{:S(2)}, u32[]{:S(2)}) %collective-permute-start.5) | collective-permute-done | bytes 1105952 | tf_op jit(solution)/shard_map/ppermute | solution.py:27
  153.9 6.3 %shard_map.61 = (f32[17,48,640]{2,1,0:T(8,128)S(1)}, f32[9,48,640]{2,1,0:T(8,128)S(1)}, f32[5,48,640]{2,1,0:T(8,128)S(1)}, f32[3,48,640]{2,1,0:T(8,128)S(1)}, f3...) custom-call(f32[16,48,640]{2,1,0:T(8,128)S(1)} %copy-done.43, ...), custom_call_target="tpu_custom_call" | custom-call | flops 8000000000 | bytes 24000000 | tf_op jit(solution)/shard_map/pallas_call | solution.py:101
  161.1 5.5 %shard_map.62 = (f32[8,2,32,640]{3,2,1,0:T(8,128)S(1)}, f32[8,48,640]{2,1,0:T(8,128)S(1)}, f32[2,48,640]{2,1,0:T(8,128)S(1)}, f32[2,48,640]{2,1,0:T(8,128)S(1)}) custom-call(f32[16,40,640]{2,1,0:T(8,128)S(1)} %bitcast.15, f32[2,40,640]{2,1,0:T(8,128)S(1)} %collective-permute-done.1.s_low, f32[2,40,640]{2,1,0:T(8,128)S(1)} %collective-permute-done.2.s_high, ...), custom_call_target="tpu_custom_call" | custom-call | flops 8000000000 | bytes 24000000 | tf_op jit(solution)/shard_map/pallas_call | solution.py:101
  166.7 3.2 %collective-permute-start.7 = (f32[2,48,640]{2,1,0:T(8,128)S(1)}, f32[2,48,640]{2,1,0:T(8,128)S(1)}, u32[]{:S(2)}, u32[]{:S(2)}) collective-permute-start(f32[2,48,640]{2,1,0:T(8,128)S(1)} %get-tuple-element.72), channel_id=1, source_target_pairs={{0,16},{2,18},{4,20},{6,22},{8,24},{10,26},{12,28},{14,30},{16,32}... | collective-permute-start | bytes 737288 | tf_op jit(solution)/shard_map/ppermute | solution.py:27
  169.9 5.2 %collective-permute-start.8 = (f32[2,48,640]{2,1,0:T(8,128)S(1)}, f32[2,48,640]{2,1,0:T(8,128)S(1)}, u32[]{:S(2)}, u32[]{:S(2)}) collective-permute-start(f32[2,48,640]{2,1,0:T(8,128)S(1)} %get-tuple-element.73), channel_id=1, source_target_pairs={{16,0},{18,2},{20,4},{22,6},{24,8},{26,10},{28,12},{30,14},{32,16}... | collective-permute-start | bytes 737288 | tf_op jit(solution)/shard_map/ppermute | solution.py:27
  182.8 4.6 %collective-permute-start.9 = (f32[4,8,640]{2,1,0:T(8,128)S(1)}, f32[4,8,640]{2,1,0:T(8,128)S(1)}, u32[]{:S(2)}, u32[]{:S(2)}) collective-permute-start(f32[4,8,640]{2,1,0:T(8,128)S(1)} %get-tuple-element.77), channel_id=1, source_target_pairs={{0,2},{2,4},{4,6},{6,8},{8,10},{10,12},{12,14},{14,1},{1,3},{3,5},... | collective-permute-start | bytes 245768 | tf_op jit(solution)/shard_map/ppermute | solution.py:37
  193.6 9.6 %all-to-all-start.2 = ((f32[8,3,32,640]{3,2,1,0:T(8,128)}), f32[8,3,32,640]{3,2,1,0:T(8,128)}, u32[]{:S(2)}, u32[]{:S(2)}) async-start(f32[8,3,32,640]{3,2,1,0:T(8,128)} %get-tuple-element.82), calls=%async_computation.2 | async-start | bytes 3932160 | tf_op jit(solution)/shard_map/all_to_all | solution.py:46
  203.2 3.9 %collective-permute-start.11 = (f32[2,48,640]{2,1,0:T(8,128)}, f32[2,48,640]{2,1,0:T(8,128)}, u32[]{:S(2)}, u32[]{:S(2)}) collective-permute-start(f32[2,48,640]{2,1,0:T(8,128)} %copy-done.30), channel_id=1, source_target_pairs={{0,16},{2,18},{4,20},{6,22},{8,24},{10,26},{12,28},{14,30},{16,32}... | collective-permute-start | bytes 737288 | tf_op jit(solution)/shard_map/ppermute | solution.py:27
  207.1 4.5 %collective-permute-start.12 = (f32[2,48,640]{2,1,0:T(8,128)}, f32[2,48,640]{2,1,0:T(8,128)}, u32[]{:S(2)}, u32[]{:S(2)}) collective-permute-start(f32[2,48,640]{2,1,0:T(8,128)} %copy-done.29), channel_id=1, source_target_pairs={{16,0},{18,2},{20,4},{22,6},{24,8},{26,10},{28,12},{30,14},{32,16}... | collective-permute-start | bytes 737288 | tf_op jit(solution)/shard_map/ppermute | solution.py:27
  211.7 2.8 collective-permute-done.11.low
  217.7 2.8 shard_map.65
  220.5 4.0 %collective-permute-start.13 = (f32[2,48,640]{2,1,0:T(8,128)S(1)}, f32[2,48,640]{2,1,0:T(8,128)S(1)}, u32[]{:S(2)}, u32[]{:S(2)}) collective-permute-start(f32[2,48,640]{2,1,0:T(8,128)S(1)} %get-tuple-element.90), channel_id=1, source_target_pairs={{0,16},{2,18},{4,20},{6,22},{8,24},{10,26},{12,28},{14,30},{16,32}... | collective-permute-start | bytes 737288 | tf_op jit(solution)/shard_map/ppermute | solution.py:27
  224.6 4.5 %collective-permute-start.14 = (f32[2,48,640]{2,1,0:T(8,128)S(1)}, f32[2,48,640]{2,1,0:T(8,128)S(1)}, u32[]{:S(2)}, u32[]{:S(2)}) collective-permute-start(f32[2,48,640]{2,1,0:T(8,128)S(1)} %get-tuple-element.91), channel_id=1, source_target_pairs={{16,0},{18,2},{20,4},{22,6},{24,8},{26,10},{28,12},{30,14},{32,16}... | collective-permute-start | bytes 737288 | tf_op jit(solution)/shard_map/ppermute | solution.py:27
  231.3 4.0 %collective-permute-done.14.high = f32[2,48,640]{2,1,0:T(8,128)S(1)} collective-permute-done((f32[2,48,640]{2,1,0:T(8,128)S(1)}, f32[2,48,640]{2,1,0:T(8,128)S(1)}, u32[]{:S(2)}, u32[]{:S(2)}) %collective-permute-start.14) | collective-permute-done | bytes 245792 | tf_op jit(solution)/shard_map/ppermute | solution.py:27
  238.2 6.0 %collective-permute-start.16 = (f32[1,48,640]{2,1,0:T(8,128)S(1)}, f32[1,48,640]{2,1,0:T(8,128)S(1)}, u32[]{:S(2)}, u32[]{:S(2)}) collective-permute-start(f32[1,48,640]{2,1,0:T(8,128)S(1)} %get-tuple-element.96.first), channel_id=1, source_target_pairs={{16,0},{18,2},{20,4},{22,6},{24,8},{26,10},{28,12},{30,14},{32,16}... | collective-permute-start | bytes 368648 | tf_op jit(solution)/shard_map/ppermute | solution.py:27
  247.4 3.9 %collective-permute-start.17 = (f32[1,48,640]{2,1,0:T(8,128)S(1)}, f32[1,48,640]{2,1,0:T(8,128)S(1)}, u32[]{:S(2)}, u32[]{:S(2)}) collective-permute-start(f32[1,48,640]{2,1,0:T(8,128)S(1)} %get-tuple-element.99.second.second4), channel_id=1, source_target_pairs={{0,16},{2,18},{4,20},{6,22},{8,24},{10,26},{12,28},{14,30},{16,32}... | collective-permute-start | bytes 368648 | tf_op jit(solution)/shard_map/ppermute | solution.py:27
  251.3 4.0 %collective-permute-start.18 = (f32[1,48,640]{2,1,0:T(8,128)S(1)}, f32[1,48,640]{2,1,0:T(8,128)S(1)}, u32[]{:S(2)}, u32[]{:S(2)}) collective-permute-start(f32[1,48,640]{2,1,0:T(8,128)S(1)} %get-tuple-element.99.second.second4), channel_id=1, source_target_pairs={{16,0},{18,2},{20,4},{22,6},{24,8},{26,10},{28,12},{30,14},{32,16}... | collective-permute-start | bytes 368648 | tf_op jit(solution)/shard_map/ppermute | solution.py:27
  259.7 4.2 %collective-permute-done.19 = f32[1,48,640]{2,1,0:T(8,128)S(1)} collective-permute-done((f32[1,48,640]{2,1,0:T(8,128)S(1)}, f32[1,48,640]{2,1,0:T(8,128)S(1)}, u32[]{:S(2)}, u32[]{:S(2)}) %collective-permute-start.19) | collective-permute-done | bytes 122912 | tf_op jit(solution)/shard_map/ppermute | solution.py:42
  264.0 5.5 %collective-permute-start.21 = (f32[1,48,640]{2,1,0:T(8,128)S(1)}, f32[1,48,640]{2,1,0:T(8,128)S(1)}, u32[]{:S(2)}, u32[]{:S(2)}) collective-permute-start(f32[1,48,640]{2,1,0:T(8,128)S(1)} %get-tuple-element.105.first), channel_id=1, source_target_pairs={{0,32},{2,34},{4,36},{6,38},{8,40},{10,42},{12,44},{14,46},{16,48}... | collective-permute-start | bytes 368648 | tf_op jit(solution)/shard_map/ppermute | solution.py:27
  269.5 2.7 collective-permute-start.22
  273.1 4.6 %collective-permute-done.22.high = f32[1,48,640]{2,1,0:T(8,128)S(1)} collective-permute-done((f32[1,48,640]{2,1,0:T(8,128)S(1)}, f32[1,48,640]{2,1,0:T(8,128)S(1)}, u32[]{:S(2)}, u32[]{:S(2)}) %collective-permute-start.22) | collective-permute-done | bytes 122912 | tf_op jit(solution)/shard_map/ppermute | solution.py:27
  278.8 6.9 %all-to-all-start.3 = ((f32[8,32,640]{2,1,0:T(8,128)}), f32[8,32,640]{2,1,0:T(8,128)S(1)}, u32[]{:S(2)}, u32[]{:S(2)}) async-start(f32[8,32,640]{2,1,0:T(8,128)} %shard_map.70), calls=%async_computation.3 | async-start | bytes 1310720 | tf_op jit(solution)/shard_map/all_to_all | solution.py:46
  290.3 10.1 %all-to-all-done.3 = f32[8,32,640]{2,1,0:T(8,128)S(1)} async-done(((f32[8,32,640]{2,1,0:T(8,128)}), f32[8,32,640]{2,1,0:T(8,128)S(1)}, u32[]{:S(2)}, u32[]{:S(2)}) %all-to-all-start.3) | async-done | bytes 655392 | tf_op jit(solution)/shard_map/all_to_all | solution.py:46
  (136 shorter events, 72.5 us)
Async XLA Ops:
  4.6 43.0 %all-to-all-start.1 = ((f32[8,2,32,640]{3,2,1,0:T(8,128)}), f32[8,2,32,640]{3,2,1,0:T(8,128)S(1)}, u32[]{:S(2)}, u32[]{:S(2)}) async-start(f32[8,2,32,640]{3,2,1,0:T(8,128)} %shard_map.59), calls=%async_computation.1 | async-start | bytes 2621440 | tf_op jit(solution)/shard_map/all_to_all | solution.py:46
  13.2 1.3 collective-permute-start
  47.6 68.9 %all-to-all-start = ((f32[8,2,40,640]{3,2,1,0:T(8,128)}), f32[8,2,40,640]{3,2,1,0:T(8,128)S(1)}, u32[]{:S(2)}, u32[]{:S(2)}) async-start(f32[8,2,40,640]{3,2,1,0:T(8,128)} %shard_map.58), calls=%async_computation | async-start | bytes 3276800 | tf_op jit(solution)/shard_map/all_to_all | solution.py:46
  51.2 42.8 %collective-permute-start.3 = (f32[16,8,640]{2,1,0:T(8,128)S(1)}, f32[16,8,640]{2,1,0:T(8,128)S(1)}, u32[]{:S(2)}, u32[]{:S(2)}) collective-permute-start(f32[16,8,640]{2,1,0:T(8,128)S(1)} %get-tuple-element.110), channel_id=1, source_target_pairs={{0,2},{2,4},{4,6},{6,8},{8,10},{10,12},{12,14},{14,1},{1,3},{3,5},... | collective-permute-start | bytes 983048 | tf_op jit(solution)/shard_map/ppermute | solution.py:37
  55.1 40.9 %collective-permute-start.4 = (f32[16,8,640]{2,1,0:T(8,128)S(1)}, f32[16,8,640]{2,1,0:T(8,128)S(1)}, u32[]{:S(2)}, u32[]{:S(2)}) collective-permute-start(f32[16,8,640]{2,1,0:T(8,128)S(1)} %get-tuple-element.109), channel_id=1, source_target_pairs={{2,0},{4,2},{6,4},{8,6},{10,8},{12,10},{14,12},{1,14},{3,1},{5,3},... | collective-permute-start | bytes 983048 | tf_op jit(solution)/shard_map/ppermute | solution.py:37
  108.6 31.5 %collective-permute-start.5 = (f32[9,48,640]{2,1,0:T(8,128)}, f32[9,48,640]{2,1,0:T(8,128)S(1)}, u32[]{:S(2)}, u32[]{:S(2)}) collective-permute-start(f32[9,48,640]{2,1,0:T(8,128)} %get-tuple-element.57), channel_id=1, source_target_pairs={{0,16},{2,18},{4,20},{6,22},{8,24},{10,26},{12,28},{14,30},{16,32}... | collective-permute-start | bytes 3317768 | tf_op jit(solution)/shard_map/ppermute | solution.py:27
  112.0 29.7 %collective-permute-start.6 = (f32[9,48,640]{2,1,0:T(8,128)}, f32[9,48,640]{2,1,0:T(8,128)}, u32[]{:S(2)}, u32[]{:S(2)}) collective-permute-start(f32[9,48,640]{2,1,0:T(8,128)} %get-tuple-element.58), channel_id=1, source_target_pairs={{16,0},{18,2},{20,4},{22,6},{24,8},{26,10},{28,12},{30,14},{32,16}... | collective-permute-start | bytes 3317768 | tf_op jit(solution)/shard_map/ppermute | solution.py:27
  116.6 44.5 %collective-permute-start.1 = (f32[2,40,640]{2,1,0:T(8,128)S(1)}, f32[2,40,640]{2,1,0:T(8,128)S(1)}, u32[]{:S(2)}, u32[]{:S(2)}) collective-permute-start(f32[2,40,640]{2,1,0:T(8,128)S(1)} %get-tuple-element.108), channel_id=1, source_target_pairs={{0,16},{2,18},{4,20},{6,22},{8,24},{10,26},{12,28},{14,30},{16,32}... | collective-permute-start | bytes 614408 | tf_op jit(solution)/shard_map/ppermute | solution.py:27
  118.5 42.6 %collective-permute-start.2 = (f32[2,40,640]{2,1,0:T(8,128)S(1)}, f32[2,40,640]{2,1,0:T(8,128)S(1)}, u32[]{:S(2)}, u32[]{:S(2)}) collective-permute-start(f32[2,40,640]{2,1,0:T(8,128)S(1)} %get-tuple-element.107), channel_id=1, source_target_pairs={{16,0},{18,2},{20,4},{22,6},{24,8},{26,10},{28,12},{30,14},{32,16}... | collective-permute-start | bytes 614408 | tf_op jit(solution)/shard_map/ppermute | solution.py:27
  161.1 17.7 %copy-start.33 = (f32[8,48,640]{2,1,0:T(8,128)S(1)}, f32[8,48,640]{2,1,0:T(8,128)}, u32[]{:S(2)}) copy-start(f32[8,48,640]{2,1,0:T(8,128)} %copy-done.31) | copy-start | bytes 2949124
  166.7 10.7 %collective-permute-start.7 = (f32[2,48,640]{2,1,0:T(8,128)S(1)}, f32[2,48,640]{2,1,0:T(8,128)S(1)}, u32[]{:S(2)}, u32[]{:S(2)}) collective-permute-start(f32[2,48,640]{2,1,0:T(8,128)S(1)} %get-tuple-element.72), channel_id=1, source_target_pairs={{0,16},{2,18},{4,20},{6,22},{8,24},{10,26},{12,28},{14,30},{16,32}... | collective-permute-start | bytes 737288 | tf_op jit(solution)/shard_map/ppermute | solution.py:27
  169.9 8.9 %collective-permute-start.8 = (f32[2,48,640]{2,1,0:T(8,128)S(1)}, f32[2,48,640]{2,1,0:T(8,128)S(1)}, u32[]{:S(2)}, u32[]{:S(2)}) collective-permute-start(f32[2,48,640]{2,1,0:T(8,128)S(1)} %get-tuple-element.73), channel_id=1, source_target_pairs={{16,0},{18,2},{20,4},{22,6},{24,8},{26,10},{28,12},{30,14},{32,16}... | collective-permute-start | bytes 737288 | tf_op jit(solution)/shard_map/ppermute | solution.py:27
  181.5 6.3 %collective-permute-start.10 = (f32[4,8,640]{2,1,0:T(8,128)S(1)}, f32[4,8,640]{2,1,0:T(8,128)S(1)}, u32[]{:S(2)}, u32[]{:S(2)}) collective-permute-start(f32[4,8,640]{2,1,0:T(8,128)S(1)} %get-tuple-element.78), channel_id=1, source_target_pairs={{2,0},{4,2},{6,4},{8,6},{10,8},{12,10},{14,12},{1,14},{3,1},{5,3},... | collective-permute-start | bytes 245768 | tf_op jit(solution)/shard_map/ppermute | solution.py:37
  182.8 7.1 %collective-permute-start.9 = (f32[4,8,640]{2,1,0:T(8,128)S(1)}, f32[4,8,640]{2,1,0:T(8,128)S(1)}, u32[]{:S(2)}, u32[]{:S(2)}) collective-permute-start(f32[4,8,640]{2,1,0:T(8,128)S(1)} %get-tuple-element.77), channel_id=1, source_target_pairs={{0,2},{2,4},{4,6},{6,8},{8,10},{10,12},{12,14},{14,1},{1,3},{3,5},... | collective-permute-start | bytes 245768 | tf_op jit(solution)/shard_map/ppermute | solution.py:37
  193.6 22.1 %copy-start.6 = (f32[8,48,640]{2,1,0:T(8,128)S(1)}, f32[8,48,640]{2,1,0:T(8,128)}, u32[]{:S(2)}) copy-start(f32[8,48,640]{2,1,0:T(8,128)} %copy-done.5) | copy-start | bytes 2949124
  193.6 22.1 %copy-start.8 = (f32[5,48,640]{2,1,0:T(8,128)S(1)}, f32[5,48,640]{2,1,0:T(8,128)}, u32[]{:S(2)}) copy-start(f32[5,48,640]{2,1,0:T(8,128)} %copy-done.7) | copy-start | bytes 1843204
  193.6 22.1 %copy-start.11 = (f32[4,48,640]{2,1,0:T(8,128)S(1)}, f32[4,48,640]{2,1,0:T(8,128)}, u32[]{:S(2)}) copy-start(f32[4,48,640]{2,1,0:T(8,128)} %copy-done.9) | copy-start | bytes 1474564
  193.6 78.6 %all-to-all-start.2 = ((f32[8,3,32,640]{3,2,1,0:T(8,128)}), f32[8,3,32,640]{3,2,1,0:T(8,128)}, u32[]{:S(2)}, u32[]{:S(2)}) async-start(f32[8,3,32,640]{3,2,1,0:T(8,128)} %get-tuple-element.82), calls=%async_computation.2 | async-start | bytes 3932160 | tf_op jit(solution)/shard_map/all_to_all | solution.py:46
  203.2 11.2 %collective-permute-start.11 = (f32[2,48,640]{2,1,0:T(8,128)}, f32[2,48,640]{2,1,0:T(8,128)}, u32[]{:S(2)}, u32[]{:S(2)}) collective-permute-start(f32[2,48,640]{2,1,0:T(8,128)} %copy-done.30), channel_id=1, source_target_pairs={{0,16},{2,18},{4,20},{6,22},{8,24},{10,26},{12,28},{14,30},{16,32}... | collective-permute-start | bytes 737288 | tf_op jit(solution)/shard_map/ppermute | solution.py:27
  207.1 8.5 %collective-permute-start.12 = (f32[2,48,640]{2,1,0:T(8,128)}, f32[2,48,640]{2,1,0:T(8,128)}, u32[]{:S(2)}, u32[]{:S(2)}) collective-permute-start(f32[2,48,640]{2,1,0:T(8,128)} %copy-done.29), channel_id=1, source_target_pairs={{16,0},{18,2},{20,4},{22,6},{24,8},{26,10},{28,12},{30,14},{32,16}... | collective-permute-start | bytes 737288 | tf_op jit(solution)/shard_map/ppermute | solution.py:27
  220.5 10.8 %collective-permute-start.13 = (f32[2,48,640]{2,1,0:T(8,128)S(1)}, f32[2,48,640]{2,1,0:T(8,128)S(1)}, u32[]{:S(2)}, u32[]{:S(2)}) collective-permute-start(f32[2,48,640]{2,1,0:T(8,128)S(1)} %get-tuple-element.90), channel_id=1, source_target_pairs={{0,16},{2,18},{4,20},{6,22},{8,24},{10,26},{12,28},{14,30},{16,32}... | collective-permute-start | bytes 737288 | tf_op jit(solution)/shard_map/ppermute | solution.py:27
  224.6 10.7 %collective-permute-start.14 = (f32[2,48,640]{2,1,0:T(8,128)S(1)}, f32[2,48,640]{2,1,0:T(8,128)S(1)}, u32[]{:S(2)}, u32[]{:S(2)}) collective-permute-start(f32[2,48,640]{2,1,0:T(8,128)S(1)} %get-tuple-element.91), channel_id=1, source_target_pairs={{16,0},{18,2},{20,4},{22,6},{24,8},{26,10},{28,12},{30,14},{32,16}... | collective-permute-start | bytes 737288 | tf_op jit(solution)/shard_map/ppermute | solution.py:27
  229.2 30.4 %collective-permute-start.20 = (f32[3,48,640]{2,1,0:T(8,128)S(1)}, f32[3,48,640]{2,1,0:T(8,128)S(1)}, u32[]{:S(2)}, u32[]{:S(2)}) collective-permute-start(f32[3,48,640]{2,1,0:T(8,128)S(1)} %pad_maximum_fusion), channel_id=1, source_target_pairs={{0,16},{2,18},{4,20},{6,22},{8,24},{10,26},{12,28},{14,30},{16,0},... | collective-permute-start | bytes 1105928 | tf_op jit(solution)/shard_map/ppermute | solution.py:42
  236.3 8.9 %collective-permute-start.15 = (f32[1,48,640]{2,1,0:T(8,128)S(1)}, f32[1,48,640]{2,1,0:T(8,128)S(1)}, u32[]{:S(2)}, u32[]{:S(2)}) collective-permute-start(f32[1,48,640]{2,1,0:T(8,128)S(1)} %get-tuple-element.96.first), channel_id=1, source_target_pairs={{0,16},{2,18},{4,20},{6,22},{8,24},{10,26},{12,28},{14,30},{16,32}... | collective-permute-start | bytes 368648 | tf_op jit(solution)/shard_map/ppermute | solution.py:27
  238.2 9.0 %collective-permute-start.16 = (f32[1,48,640]{2,1,0:T(8,128)S(1)}, f32[1,48,640]{2,1,0:T(8,128)S(1)}, u32[]{:S(2)}, u32[]{:S(2)}) collective-permute-start(f32[1,48,640]{2,1,0:T(8,128)S(1)} %get-tuple-element.96.first), channel_id=1, source_target_pairs={{16,0},{18,2},{20,4},{22,6},{24,8},{26,10},{28,12},{30,14},{32,16}... | collective-permute-start | bytes 368648 | tf_op jit(solution)/shard_map/ppermute | solution.py:27
  247.4 8.9 %collective-permute-start.17 = (f32[1,48,640]{2,1,0:T(8,128)S(1)}, f32[1,48,640]{2,1,0:T(8,128)S(1)}, u32[]{:S(2)}, u32[]{:S(2)}) collective-permute-start(f32[1,48,640]{2,1,0:T(8,128)S(1)} %get-tuple-element.99.second.second4), channel_id=1, source_target_pairs={{0,16},{2,18},{4,20},{6,22},{8,24},{10,26},{12,28},{14,30},{16,32}... | collective-permute-start | bytes 368648 | tf_op jit(solution)/shard_map/ppermute | solution.py:27
  251.3 6.8 %collective-permute-start.18 = (f32[1,48,640]{2,1,0:T(8,128)S(1)}, f32[1,48,640]{2,1,0:T(8,128)S(1)}, u32[]{:S(2)}, u32[]{:S(2)}) collective-permute-start(f32[1,48,640]{2,1,0:T(8,128)S(1)} %get-tuple-element.99.second.second4), channel_id=1, source_target_pairs={{16,0},{18,2},{20,4},{22,6},{24,8},{26,10},{28,12},{30,14},{32,16}... | collective-permute-start | bytes 368648 | tf_op jit(solution)/shard_map/ppermute | solution.py:27
  258.2 19.6 %copy-start.20 = (f32[4,32,640]{2,1,0:T(8,128)S(1)}, f32[4,32,640]{2,1,0:T(8,128)}, u32[]{:S(2)}) copy-start(f32[4,32,640]{2,1,0:T(8,128)} %copy-done.19) | copy-start | bytes 983044
  258.2 5.7 %collective-permute-start.19 = (f32[1,48,640]{2,1,0:T(8,128)S(1)}, f32[1,48,640]{2,1,0:T(8,128)S(1)}, u32[]{:S(2)}, u32[]{:S(2)}) collective-permute-start(f32[1,48,640]{2,1,0:T(8,128)S(1)} %shard_map.68), channel_id=1, source_target_pairs={{0,16},{2,18},{4,20},{6,22},{8,24},{10,26},{12,28},{14,30},{16,0},... | collective-permute-start | bytes 368648 | tf_op jit(solution)/shard_map/ppermute | solution.py:42
  264.0 9.2 %collective-permute-start.21 = (f32[1,48,640]{2,1,0:T(8,128)S(1)}, f32[1,48,640]{2,1,0:T(8,128)S(1)}, u32[]{:S(2)}, u32[]{:S(2)}) collective-permute-start(f32[1,48,640]{2,1,0:T(8,128)S(1)} %get-tuple-element.105.first), channel_id=1, source_target_pairs={{0,32},{2,34},{4,36},{6,38},{8,40},{10,42},{12,44},{14,46},{16,48}... | collective-permute-start | bytes 368648 | tf_op jit(solution)/shard_map/ppermute | solution.py:27
  269.5 8.3 %collective-permute-start.22 = (f32[1,48,640]{2,1,0:T(8,128)S(1)}, f32[1,48,640]{2,1,0:T(8,128)S(1)}, u32[]{:S(2)}, u32[]{:S(2)}) collective-permute-start(f32[1,48,640]{2,1,0:T(8,128)S(1)} %get-tuple-element.105.first), channel_id=1, source_target_pairs={{32,0},{34,2},{36,4},{38,6},{40,8},{42,10},{44,12},{46,14},{48,16}... | collective-permute-start | bytes 368648 | tf_op jit(solution)/shard_map/ppermute | solution.py:27
  278.8 21.6 %all-to-all-start.3 = ((f32[8,32,640]{2,1,0:T(8,128)}), f32[8,32,640]{2,1,0:T(8,128)S(1)}, u32[]{:S(2)}, u32[]{:S(2)}) async-start(f32[8,32,640]{2,1,0:T(8,128)} %shard_map.70), calls=%async_computation.3 | async-start | bytes 1310720 | tf_op jit(solution)/shard_map/all_to_all | solution.py:46
  (39 other events, 163.2 us)

commit v3 on v2

--- a/solution.py
+++ b/solution.py
@@ -9,6 +9,7 @@
 
 RING = 8
 HALO = 8
+REACH = 9
 THIN = 4
 damping = 0.8
 pore_value = 1.0
@@ -107,6 +108,20 @@
         compiler_params=pltpu.CompilerParams(vmem_limit_bytes=limit * 1024 * 1024),
         cost_estimate=cost,
     )(*args)
+
+
+def after(value, *settled):
+    def nothing(*refs):
+        pass
+
+    there = pl.BlockSpec(memory_space=pl.ANY)
+    return pl.pallas_call(
+        nothing,
+        out_shape=jax.ShapeDtypeStruct(value.shape, value.dtype),
+        in_specs=[there] * (1 + len(settled)),
+        out_specs=there,
+        input_output_aliases={0: 0},
+    )(value, *settled)
 
 
 def cut_conduct(labels, fraction, out):
@@ -140,93 +155,99 @@
     return harmonic(c, next_row(c)), jnp.where(last, 0.0, harmonic(c, next_column(c)))
 
 
-def make_faces(c_own, above, below, c, east0, north0, east1, north1, east2, north2, east3, north3, east4, north4,
-               bundle_down, bundle_up):
+def parts(faces, count):
+    east, north = faces.at[0:count], faces.at[count:2 * count]
+    z, w = faces.at[2 * count:3 * count + 1], faces.at[3 * count + 1:4 * count + 1]
+    return east, north, z, w, faces.at[4 * count + 1:] if count > 1 else None
+
+
+def planes_of(count):
+    return 4 * count + 1 + (0 if count == 1 else 10 if count == 16 else 8)
+
+
+def frames(c_own, above, below, c, low, high):
     strip = c_own.shape[1]
 
-    def plane(p):
-        c[p, :HALO] = above[p]
-        c[p, HALO:HALO + strip] = c_own[p]
-        c[p, HALO + strip:] = below[p]
-        east0[p], north0[p] = plane_faces(c[p])
-
-    loop(16, plane)
-
-    def plane1(q):
-        east1[q] = east0[2 * q] + east0[2 * q + 1]
-        north1[q] = north0[2 * q] + north0[2 * q + 1]
-
-    loop(8, plane1)
-    for finer, coarser in ((east1, east2), (north1, north2), (east2, east3), (north2, north3), (east3, east4), (north3, north4)):
-        for q in range(coarser.shape[0]):
-            coarser[q] = finer[2 * q] + finer[2 * q + 1]
-    middle = harmonic(c[7], c[8])
-    for bundle, first, edge2, face2, edge3 in ((bundle_down, 0, 0, 4, 0), (bundle_up, 13, 3, 12, 1)):
-        for k in range(3):
-            bundle[k] = c[first + k]
-        bundle[3] = east2[edge2]
-        bundle[4] = north2[edge2]
-        bundle[5] = harmonic(c[face2 - 1], c[face2])
-        bundle[6] = east3[edge3]
-        bundle[7] = north3[edge3]
-        bundle[8] = middle
-
-
-def make_weights(c, low, high, east0, north0, east1, north1, east2, north2, east3, north3, east4, north4,
-                 z0, z1, z2, z3, z4, w0, w1, w2, w3, w4, halo0, halo1, halo2, halo3):
+    def place(ref, k, p):
+        ref[k, :HALO] = above[p]
+        ref[k, HALO:HALO + strip] = c_own[p]
+        ref[k, HALO + strip:] = below[p]
+
+    loop(16, lambda p: place(c, p, p))
+    loop(REACH, lambda p: place(low, p, p))
+    loop(REACH, lambda p: place(high, p, p + 16 - REACH))
+
+
+def make_faces(c, low, high, faces0, faces1, faces2, faces3, faces4):
+    east0, north0, z0, w0, halo0 = parts(faces0, 16)
+
     def z_face(p):
         z0[p] = harmonic(c[p - 1], c[p])
 
     loop(15, lambda k: z_face(k + 1))
-    z0[0] = jnp.where(low[2] > 0, harmonic(low[2], c[0]), 2.0 * c[0])
+    z0[0] = jnp.where(low[REACH - 1] > 0, harmonic(low[REACH - 1], c[0]), 2.0 * c[0])
     z0[16] = jnp.where(high[0] > 0, harmonic(c[15], high[0]), 2.0 * c[15])
 
     def weigh(p):
-        w0[p] = weight(c[p], east0[p], north0[p], z0[p], z0[p + 1])
+        east, north = plane_faces(c[p])
+        east0[p] = east
+        north0[p] = north
+        w0[p] = weight(c[p], east, north, z0[p], z0[p + 1])
 
     loop(16, weigh)
-    loop(9, lambda q: z1.__setitem__(q, z0[2 * q]))
-
-    def weigh1(q):
-        w1[q] = weight(c[0], east1[q], north1[q], z1[q], z1[q + 1])
-
-    loop(8, weigh1)
-    for z_fine, z, east, north, w in ((z1, z2, east2, north2, w2), (z2, z3, east3, north3, w3), (z3, z4, east4, north4, w4)):
-        for q in range(z.shape[0]):
-            z[q] = z_fine[2 * q]
-        for q in range(w.shape[0]):
-            w[q] = weight(c[0], east[q], north[q], z[q], z[q + 1])
-
-    for side, bundle, near, far, last, face in ((0, low, 2, 1, 0, 0), (1, high, 0, 1, 2, 16)):
+    finer, count = faces0, 16
+    for coarser in (faces1, faces2, faces3, faces4):
+        east_f, north_f, z_f, _, _ = parts(finer, count)
+        count //= 2
+        east, north, z, w, _ = parts(coarser, count)
+
+        def faces_and_weight(q):
+            east_q = east_f[2 * q] + east_f[2 * q + 1]
+            north_q = north_f[2 * q] + north_f[2 * q + 1]
+            east[q] = east_q
+            north[q] = north_q
+            z[q] = z_f[2 * q]
+            w[q] = weight(c[0], east_q, north_q, z_f[2 * q], z_f[2 * q + 2])
+
+        loop(count, faces_and_weight)
+        z[count] = z_f[2 * count]
+        finer = coarser
+
+    for side, ref, at, face in ((0, low, [REACH - 1 - k for k in range(REACH)], 0), (1, high, list(range(REACH)), 16)):
         shared = z0[face]
-        middle = harmonic(bundle[near], bundle[far])
-        outer = harmonic(bundle[far], bundle[last])
-        east_near, north_near = plane_faces(bundle[near])
-        east_far, north_far = plane_faces(bundle[far])
-        halo0[side] = east_near
-        halo0[2 + side] = north_near
+        near = ref[at[0]]
+        middle = harmonic(near, ref[at[1]])
+        east_sum, north_sum = plane_faces(near)
+        halo0[side] = east_sum
+        halo0[2 + side] = north_sum
         halo0[4 + side] = middle
-        halo0[6 + side] = weight(bundle[near], east_near, north_near, shared, middle)
-        halo0[8 + side] = weight(bundle[far], east_far, north_far, middle, outer)
-        halo1[side] = east_near + east_far
-        halo1[2 + side] = north_near + north_far
-        halo1[4 + side] = outer
-        halo1[6 + side] = weight(bundle[near], east_near + east_far, north_near + north_far, shared, outer)
-        for halo, at in ((halo2, 3), (halo3, 6)):
-            halo[side] = bundle[at]
-            halo[2 + side] = bundle[at + 1]
-            halo[4 + side] = bundle[at + 2]
-            halo[6 + side] = weight(bundle[near], bundle[at], bundle[at + 1], shared, bundle[at + 2])
-
-
-def make_last_faces(east4, north4, w4, other, down, up, east5, north5, w5):
+        halo0[6 + side] = weight(near, east_sum, north_sum, shared, middle)
+        thick = 1
+        for faces, count in ((faces1, 8), (faces2, 4), (faces3, 2)):
+            for k in range(thick, 2 * thick):
+                east_k, north_k = plane_faces(ref[at[k]])
+                if k == 1:
+                    halo0[8 + side] = weight(ref[at[1]], east_k, north_k, middle, harmonic(ref[at[1]], ref[at[2]]))
+                east_sum = east_sum + east_k
+                north_sum = north_sum + north_k
+            thick *= 2
+            halo = parts(faces, count)[4]
+            outer = harmonic(ref[at[thick - 1]], ref[at[thick]])
+            halo[side] = east_sum
+            halo[2 + side] = north_sum
+            halo[4 + side] = outer
+            halo[6 + side] = weight(near, east_sum, north_sum, shared, outer)
+
+
+def make_last_faces(faces4, other, down, up, east5, north5, w5):
+    east4, north4, _, w4, _ = parts(faces4, 1)
     east5[0] = east4[0] + other[0]
     north5[0] = north4[0] + other[1]
     w5[0] = weight(w4[0], east5[0], north5[0], down[0], up[0])
 
 
-def sweep_and_rest(s, first, total, second, east, north, z, w, halo):
-    count = w.shape[0]
+def sweep_and_rest(s, first, total, second, faces, count):
+    east, north, z, w, halo = parts(faces, count)
 
     def sweep(q):
         t = 1.2 * s[q + 1] + neighbours(first[q + 2], first[q + 1], first[q + 3], east[q], north[q], z[q], z[q + 1])
@@ -245,9 +266,11 @@
     return rest
 
 
-def fine_level(s_own, s_low, s_high, east, north, z, w, halo, w_next, fine, s_next, edge_down, edge_up, s, first, total, second):
+def fine_level(s_own, s_low, s_high, faces, faces_next, fine, s_next, edge_down, edge_up, s, first, total, second):
     strip = fine.shape[2]
     columns = s.shape[2]
+    _, _, _, w, halo = parts(faces, 16)
+    w_next = parts(faces_next, 8)[3]
     blank = jnp.zeros((HALO - THIN, columns), jnp.float32)
 
     def place(k, value):
@@ -269,7 +292,7 @@
         first[q + 2] = w[q] * s[q + 1]
 
     loop(16, start)
-    rest = sweep_and_rest(s, first, total, second, east, north, z, w, halo)
+    rest = sweep_and_rest(s, first, total, second, faces, 16)
 
     def pair(q):
         s_next[q] = rest(2 * q) + rest(2 * q + 1)
@@ -283,8 +306,9 @@
     edge_up[1] = s_next[7]
 
 
-def open_level(s_own, w, low, high, halo, s, first):
-    count = w.shape[0]
+def open_level(s_own, faces, low, high, s, first):
+    count = s_own.shape[0]
+    _, _, _, w, halo = parts(faces, count)
     s[0] = low[1]
     s[count + 1] = high[0]
     first[0] = low[0]
@@ -299,10 +323,10 @@
     loop(count, start)
 
 
-def first_coarse_level(s_own, low, high, east, north, z, w, halo, out, s_next, top, bottom, s, first, total, second):
+def first_coarse_level(s_own, low, high, faces, out, s_next, top, bottom, s, first, total, second):
     strip = out.shape[1]
-    open_level(s_own, w, low, high, halo, s, first)
-    rest = sweep_and_rest(s, first, total, second, east, north, z, w, halo)
+    open_level(s_own, faces, low, high, s, first)
+    rest = sweep_and_rest(s, first, total, second, faces, s_own.shape[0])
 
     def pair(q):
         value = rest(2 * q) + rest(2 * q + 1)
@@ -315,12 +339,13 @@
     loop(4, pair)
 
 
-def middle_level(s_own, low, high, east, north, z, w, halo, w_next, out, s_next, *rest_refs):
+def middle_level(s_own, low, high, faces, faces_next, out, s_next, *rest_refs):
     edges, (s, first, total, second) = rest_refs[:-4], rest_refs[-4:]
-    count = w.shape[0]
+    count = s_own.shape[0]
+    w_next = parts(faces_next, count // 2)[3]
     strip = out.shape[1]
-    open_level(s_own, w, low, high, halo, s, first)
-    rest = sweep_and_rest(s, first, total, second, east, north, z, w, halo)
+    open_level(s_own, faces, low, high, s, first)
+    rest = sweep_and_rest(s, first, total, second, faces, s_own.shape[0])
     for q in range(count // 2):
         s_next[q] = rest(2 * q) + rest(2 * q + 1)
     for q in range(count):
@@ -335,8 +360,9 @@
         edges[0][0] = w_next[0] * s_next[0]
 
 
-def widen(source2, above, below, w2, fine, plane_out, s, edge_down, edge_up, back):
+def widen(source2, above, below, faces2, fine, plane_out, s, edge_down, edge_up, back):
     count, strip, _ = source2.shape
+    w2 = parts(faces2, count)[3]
     for q in range(count):
         s[q, :HALO] = above[q]
         s[q, HALO:HALO + strip] = source2[q]
@@ -354,13 +380,15 @@
     loop(RING, gather)
 
 
-def sweep_last(s, first, low, high, east, north, z, w, total, second):
+def sweep_last(s, first, low, high, faces, total, second):
+    east, north, z, w, _ = parts(faces, 1)
     t = 1.2 * s[0] + neighbours(first[0], low[0], high[0], east[0], north[0], z[0], z[1])
     total[0] = t
     second[0] = w[0] * t
 
 
-def rest_last(s, total, second, low, high, east, north, z, out):
+def rest_last(s, total, second, low, high, faces, out):
+    east, north, z, _, _ = parts(faces, 1)
     out[0] = s[0] - damping * total[0] + neighbours(second[0], low[0], high[0], east[0], north[0], z[0], z[1])
 
 
@@ -392,53 +420,51 @@
 
     (c_cut,) = call(cut_conduct, [(RING, planes, strip, columns)], [], labels, fraction, limit=10)
     c_own = transposed(c_cut).reshape(RING * planes, strip, columns)
-    s_top, s_bottom = edges_of(right_side[:, :HALO], right_side[:, rows - HALO:])
-    (s_cut,) = call(cut_source, [(RING, planes, strip + 2 * THIN, columns)], [], right_side, s_top, s_bottom, limit=10)
-    s_own = transposed(s_cut).reshape(RING * planes, strip + 2 * THIN, columns)
-
     above = row_shifted(c_own[:, strip - HALO:], 1)
     below = row_shifted(c_own[:, :HALO], -1)
-    c, *plane_set, bundle_down, bundle_up = call(
-        make_faces, [shape(n) for n in (16, 16, 16, 8, 8, 4, 4, 2, 2, 1, 1, 9, 9)], [], c_own, above, below, limit=18, work=8.0)
+    s_top, s_bottom = edges_of(right_side[:, :HALO], right_side[:, rows - HALO:])
+    (s_cut,) = call(cut_source, [(RING, planes, strip + 2 * THIN, columns)], [],
+                    right_side, s_top, s_bottom, limit=10, work=4.0)
+    s_own = transposed(after(s_cut, above[0], below[0])).reshape(RING * planes, strip + 2 * THIN, columns)
+
+    c, bundle_down, bundle_up = call(frames, [shape(16), shape(REACH), shape(REACH)], [], c_own, above, below, limit=10, work=2.0)
     c_low, c_high = exchange(bundle_down, bundle_up)
-    z0, z1, z2, z3, z4, w0, w1, w2, w3, w4, halo0, halo1, halo2, halo3 = call(
-        make_weights, [shape(n) for n in (17, 9, 5, 3, 2, 16, 8, 4, 2, 1, 10, 8, 8, 8)], [],
-        c, c_low, c_high, *plane_set, limit=26, work=8.0)
-    east0, north0, east1, north1, east2, north2, east3, north3, east4, north4 = plane_set
-    outer = jnp.where(even_ring, z4[:1], z4[1:])
-    other = partner(jnp.concatenate([east4, north4, outer], axis=0))
-    down5 = jnp.where(even_ring, z4[:1], other[2:])
-    up5 = jnp.where(even_ring, other[2:], z4[1:])
-    east5, north5, w5 = call(make_last_faces, [shape(1)] * 3, [], east4, north4, w4, other, down5, up5)
+    faces0, faces1, faces2, faces3, faces4 = call(
+        make_faces, [shape(planes_of(n)) for n in (16, 8, 4, 2, 1)], [], c, c_low, c_high, limit=28, work=12.0)
+    east4, north4, z_low, z_high = faces4[0:1], faces4[1:2], faces4[2:3], faces4[3:4]
+    other = partner(jnp.concatenate([east4, north4, jnp.where(even_ring, z_low, z_high)], axis=0))
+    down5 = jnp.where(even_ring, z_low, other[2:])
+    up5 = jnp.where(even_ring, other[2:], z_high)
+    east5, north5, w5 = call(make_last_faces, [shape(1)] * 3, [], faces4, other, down5, up5)
 
     s_low, s_high = exchange(s_own[:2], s_own[-2:])
     fine, s1, edge_down, edge_up = call(
         fine_level, [(RING, planes, strip, columns), shape(8), shape(2), shape(2)],
         [shape(18), shape(20), shape(16), shape(18)],
-        s_own, s_low, s_high, east0, north0, z0, w0, halo0, w1, limit=26, work=8.0)
+        s_own, s_low, s_high, faces0, faces1, limit=30, work=8.0)
 
     low, high = exchange(edge_down, edge_up)
     plane_out, s2, top, bottom = call(
         first_coarse_level,
         [(8, strip, columns), (4, strip, columns), (4, HALO, columns), (4, HALO, columns)],
-        [shape(10), shape(12), shape(8), shape(10)], s1, low, high, east1, north1, z1, w1, halo1, limit=15, work=4.0)
+        [shape(10), shape(12), shape(8), shape(10)], s1, low, high, faces1, limit=15, work=4.0)
 
     above = row_shifted(bottom, 1)
     below = row_shifted(top, -1)
     s2, edge_down, edge_up, back = call(
-        widen, [shape(4), shape(2), shape(2), (RING, planes + 1, strip, columns)], [], s2, above, below, w2, fine, plane_out, limit=10)
+        widen, [shape(4), shape(2), shape(2), (RING, planes + 1, strip, columns)], [], s2, above, below, faces2, fine, plane_out, limit=10)
     low, high = exchange(edge_down, edge_up)
     second2, s3, edge_down, edge_up = call(
         middle_level, [(4, strip, columns), shape(2), shape(2), shape(2)], [shape(6), shape(8), shape(4), shape(6)],
-        s2, low, high, east2, north2, z2, w2, halo2, w3, limit=10)
+        s2, low, high, faces2, faces3, limit=10)
     low, high = exchange(edge_down, edge_up)
     second3, s4, first4 = call(
         middle_level, [(2, strip, columns), shape(1), shape(1)], [shape(4), shape(6), shape(2), shape(4)],
-        s3, low, high, east3, north3, z3, w3, halo3, w4)
+        s3, low, high, faces3, faces4)
     low, high = exchange(first4, first4)
-    total4, second4 = call(sweep_last, [shape(1), shape(1)], [], s4, first4, low, high, east4, north4, z4, w4)
+    total4, second4 = call(sweep_last, [shape(1), shape(1)], [], s4, first4, low, high, faces4)
     low, high = exchange(second4, second4)
-    (rest4,) = call(rest_last, [shape(1)], [], s4, total4, second4, low, high, east4, north4, z4)
+    (rest4,) = call(rest_last, [shape(1)], [], s4, total4, second4, low, high, faces4)
     s5 = rest4 + partner(rest4)
     first5 = w5 * s5
     low, high = exchange(first5, first5, 2 * RING)

time: 303 us -> 270 us (0.89)
  waiting for transfers between devices: 130 us -> 113 us
  local copies, waits for them, and re-layouts: 36 us -> 24.9 us
  starting transfers between devices: 107 us -> 101 us
    ppermute x4, waiting for transfers between devices: 42.2 us -> 10.4 us  [row_shifted(): return lax.ppermute(value, ('gz', 'xy'), pairs)]
    all_to_all x4, waiting for transfers between devices: 41.8 us -> 73.1 us  [transposed(): lax.all_to_all(value, 'gz', 0, 0, axis_index_groups=ring_groups(lax.axis_...]
    ppermute x16, waiting for transfers between devices: 40.3 us -> 25 us  [shifted(): return lax.ppermute(value, 'gz', pairs)]
    unnamed x89 -> x39, local copies, waits for them, and re-layouts: 30.6 us -> 17.3 us
    all_to_all x4, starting transfers between devices: 28.7 us -> 24.9 us  [transposed(): lax.all_to_all(value, 'gz', 0, 0, axis_index_groups=ring_groups(lax.axis_...]
  transfers between devices with their start and end apart: 27 -> 27, of which waited for: 22 -> 20; matrix products, arithmetic and copies ran while one was open for 2% -> 3% of each run, Pallas kernels for 5% -> 5%
where the time goes in v3:
time: 270 us; the launch traced here: 268 us
  waiting for transfers between devices  113 us (42%)
  starting transfers between devices  101 us (37%)
  Pallas kernels  28.2 us (10%)
  local copies, waits for them, and re-layouts  24.9 us (9%)
    all_to_all x4, waiting for transfers between devices, transposed(): lax.all_to_all(value, 'gz', 0, 0, axis_index_groups=ring_groups(lax.axis_...  73.1 us
    ppermute x16, starting transfers between devices, shifted(): return lax.ppermute(value, 'gz', pairs)  64.8 us
    pallas_call x13, Pallas kernels, call(): pl.pallas_call(kernel, out_shape=shapes, in_specs=[vmem] * len(args), out...  28.2 us
    ppermute x16, waiting for transfers between devices, shifted(): return lax.ppermute(value, 'gz', pairs)  25 us
    all_to_all x4, starting transfers between devices, transposed(): lax.all_to_all(value, 'gz', 0, 0, axis_index_groups=ring_groups(lax.axis_...  24.9 us
    unnamed x39, local copies, waits for them, and re-layouts  17.3 us
    ppermute x4, waiting for transfers between devices, row_shifted(): return lax.ppermute(value, ('gz', 'xy'), pairs)  10.4 us
    ppermute x4, starting transfers between devices, row_shifted(): return lax.ppermute(value, ('gz', 'xy'), pairs)  9.53 us
  transfers between devices with their start and end apart: 27, of which 20 were waited for; matrix products, arithmetic and copies ran while one was open for 3% of the time, Pallas kernels for 5%

profile of v3, /device:TPU:8, one launch (start us, length us, event | category | flops | bytes accessed | tf_op | source)
XLA Modules:
  0.0 268.3 jit_solution(1239015265058508729)
XLA Ops:
  4.6 8.6 %all-to-all-start = ((f32[8,2,32,640]{3,2,1,0:T(8,128)}), f32[8,2,32,640]{3,2,1,0:T(8,128)S(1)}, u32[]{:S(2)}, u32[]{:S(2)}) async-start(f32[8,2,32,640]{3,2,1,0:T(8,128)} %shard_map.59), calls=%async_computation | async-start | bytes 2621440 | tf_op jit(solution)/shard_map/all_to_all | solution.py:47
  14.5 33.1 %all-to-all-done = f32[8,2,32,640]{3,2,1,0:T(8,128)S(1)} async-done(((f32[8,2,32,640]{3,2,1,0:T(8,128)}), f32[8,2,32,640]{3,2,1,0:T(8,128)S(1)}, u32[]{:S(2)}, u32[]{:S(2)}) %all-to-all-start) | async-done | bytes 1310752 | tf_op jit(solution)/shard_map/all_to_all | solution.py:47
  47.6 2.4 collective-permute-start.1
  52.7 8.4 %collective-permute-done.2.below = f32[16,8,640]{2,1,0:T(8,128)S(1)} collective-permute-done((f32[16,8,640]{2,1,0:T(8,128)S(1)}, f32[16,8,640]{2,1,0:T(8,128)S(1)}, u32[]{:S(2)}, u32[]{:S(2)}) %collective-permute-start.2) | collective-permute-done | bytes 327712 | tf_op jit(solution)/shard_map/ppermute | solution.py:38
  63.0 4.4 %all-to-all-start.1 = ((f32[8,2,40,640]{3,2,1,0:T(8,128)}), f32[8,2,40,640]{3,2,1,0:T(8,128)}, u32[]{:S(2)}, u32[]{:S(2)}) async-start(f32[8,2,40,640]{3,2,1,0:T(8,128)} %shard_map.60), calls=%async_computation.1 | async-start | bytes 3276800 | tf_op jit(solution)/shard_map/all_to_all | solution.py:47
  70.1 3.4 %collective-permute-start.5 = (f32[9,48,640]{2,1,0:T(8,128)}, f32[9,48,640]{2,1,0:T(8,128)S(1)}, u32[]{:S(2)}, u32[]{:S(2)}) collective-permute-start(f32[9,48,640]{2,1,0:T(8,128)} %get-tuple-element.36), channel_id=1, source_target_pairs={{0,16},{2,18},{4,20},{6,22},{8,24},{10,26},{12,28},{14,30},{16,32}... | collective-permute-start | bytes 3317768 | tf_op jit(solution)/shard_map/ppermute | solution.py:28
  73.5 4.6 %collective-permute-start.6 = (f32[9,48,640]{2,1,0:T(8,128)S(1)}, f32[9,48,640]{2,1,0:T(8,128)}, u32[]{:S(2)}, u32[]{:S(2)}) collective-permute-start(f32[9,48,640]{2,1,0:T(8,128)S(1)} %get-tuple-element.37), channel_id=1, source_target_pairs={{16,0},{18,2},{20,4},{22,6},{24,8},{26,10},{28,12},{30,14},{32,16}... | collective-permute-start | bytes 3317768 | tf_op jit(solution)/shard_map/ppermute | solution.py:28
  78.1 29.9 %all-to-all-done.1 = f32[8,2,40,640]{3,2,1,0:T(8,128)} async-done(((f32[8,2,40,640]{3,2,1,0:T(8,128)}), f32[8,2,40,640]{3,2,1,0:T(8,128)}, u32[]{:S(2)}, u32[]{:S(2)}) %all-to-all-start.1) | async-done | bytes 1638432 | tf_op jit(solution)/shard_map/all_to_all | solution.py:47
  109.0 3.4 %collective-permute-start.3 = (f32[2,40,640]{2,1,0:T(8,128)S(1)}, f32[2,40,640]{2,1,0:T(8,128)S(1)}, u32[]{:S(2)}, u32[]{:S(2)}) collective-permute-start(f32[2,40,640]{2,1,0:T(8,128)S(1)} %get-tuple-element.70), channel_id=1, source_target_pairs={{0,16},{2,18},{4,20},{6,22},{8,24},{10,26},{12,28},{14,30},{16,32}... | collective-permute-start | bytes 614408 | tf_op jit(solution)/shard_map/ppermute | solution.py:28
  112.4 4.6 %collective-permute-start.4 = (f32[2,40,640]{2,1,0:T(8,128)S(1)}, f32[2,40,640]{2,1,0:T(8,128)S(1)}, u32[]{:S(2)}, u32[]{:S(2)}) collective-permute-start(f32[2,40,640]{2,1,0:T(8,128)S(1)} %get-tuple-element.69), channel_id=1, source_target_pairs={{16,0},{18,2},{20,4},{22,6},{24,8},{26,10},{28,12},{30,14},{32,16}... | collective-permute-start | bytes 614408 | tf_op jit(solution)/shard_map/ppermute | solution.py:28
  120.8 9.2 %shard_map.62 = (f32[75,48,640]{2,1,0:T(8,128)S(1)}, f32[41,48,640]{2,1,0:T(8,128)S(1)}, f32[25,48,640]{2,1,0:T(8,128)S(1)}, f32[17,48,640]{2,1,0:T(8,128)S(1)}, f32[5,48,640]{2,1,0:T(8,128)S(1)}) custom-call(f32[16,48,640]{2,1,0:T(8,128)S(1)} %copy-done.18, f32[9,48,640]{2,1,0:T(8,128)S(1)} %copy-done.14, f32[9,48,640]{2,1,0:T(8,128)} %collective-permute-done.6.high), custom_call_target="tpu_custom_call" | custom-call | flops 12000000000 | bytes 36000000 | tf_op jit(solution)/shard_map/pallas_call | solution.py:102
  130.0 8.4 %shard_map.63 = (f32[8,2,32,640]{3,2,1,0:T(8,128)S(1)}, f32[8,48,640]{2,1,0:T(8,128)S(1)}, f32[2,48,640]{2,1,0:T(8,128)S(1)}, f32[2,48,640]{2,1,0:T(8,128)S(1)}) custom-call(f32[16,40,640]{2,1,0:T(8,128)} %bitcast.3.s_own, f32[2,40,640]{2,1,0:T(8,128)S(1)} %collective-permute-done.3.s_low, f32[2,40,640]{2,1,0:T(8,128)S(1)} %collective-permute-done.4.s_high, ...), custom_call_target="tpu_custom_call" | custom-call | flops 8000000000 | bytes 24000000 | tf_op jit(solution)/shard_map/pallas_call | solution.py:102
  140.3 6.0 %collective-permute-start.8 = (f32[2,48,640]{2,1,0:T(8,128)S(1)}, f32[2,48,640]{2,1,0:T(8,128)S(1)}, u32[]{:S(2)}, u32[]{:S(2)}) collective-permute-start(f32[2,48,640]{2,1,0:T(8,128)S(1)} %get-tuple-element.42), channel_id=1, source_target_pairs={{16,0},{18,2},{20,4},{22,6},{24,8},{26,10},{28,12},{30,14},{32,16}... | collective-permute-start | bytes 737288 | tf_op jit(solution)/shard_map/ppermute | solution.py:28
  146.4 2.2 collective-permute-done.7.low
  150.1 2.6 shard_map.64
  154.0 4.6 %collective-permute-start.9 = (f32[4,8,640]{2,1,0:T(8,128)S(1)}, f32[4,8,640]{2,1,0:T(8,128)S(1)}, u32[]{:S(2)}, u32[]{:S(2)}) collective-permute-start(f32[4,8,640]{2,1,0:T(8,128)S(1)} %get-tuple-element.44), channel_id=1, source_target_pairs={{0,2},{2,4},{4,6},{6,8},{8,10},{10,12},{12,14},{14,1},{1,3},{3,5},... | collective-permute-start | bytes 245768 | tf_op jit(solution)/shard_map/ppermute | solution.py:38
  163.4 5.0 %all-to-all-start.2 = ((f32[8,3,32,640]{3,2,1,0:T(8,128)}), f32[8,3,32,640]{3,2,1,0:T(8,128)}, u32[]{:S(2)}, u32[]{:S(2)}) async-start(f32[8,3,32,640]{3,2,1,0:T(8,128)} %copy-done.3), calls=%async_computation.2 | async-start | bytes 3932160 | tf_op jit(solution)/shard_map/all_to_all | solution.py:47
  170.4 6.5 %collective-permute-start.12 = (f32[2,48,640]{2,1,0:T(8,128)}, f32[2,48,640]{2,1,0:T(8,128)}, u32[]{:S(2)}, u32[]{:S(2)}) collective-permute-start(f32[2,48,640]{2,1,0:T(8,128)} %copy-done.15), channel_id=1, source_target_pairs={{16,0},{18,2},{20,4},{22,6},{24,8},{26,10},{28,12},{30,14},{32,16}... | collective-permute-start | bytes 737288 | tf_op jit(solution)/shard_map/ppermute | solution.py:28
  176.9 3.5 %collective-permute-done.11.low = f32[2,48,640]{2,1,0:T(8,128)S(1)} collective-permute-done((f32[2,48,640]{2,1,0:T(8,128)}, f32[2,48,640]{2,1,0:T(8,128)S(1)}, u32[]{:S(2)}, u32[]{:S(2)}) %collective-permute-start.11) | collective-permute-done | bytes 245792 | tf_op jit(solution)/shard_map/ppermute | solution.py:28
  184.5 2.6 shard_map.66
  187.1 3.9 %collective-permute-start.13 = (f32[2,48,640]{2,1,0:T(8,128)S(1)}, f32[2,48,640]{2,1,0:T(8,128)S(1)}, u32[]{:S(2)}, u32[]{:S(2)}) collective-permute-start(f32[2,48,640]{2,1,0:T(8,128)S(1)} %get-tuple-element.55), channel_id=1, source_target_pairs={{0,16},{2,18},{4,20},{6,22},{8,24},{10,26},{12,28},{14,30},{16,32}... | collective-permute-start | bytes 737288 | tf_op jit(solution)/shard_map/ppermute | solution.py:28
  191.1 4.5 %collective-permute-start.14 = (f32[2,48,640]{2,1,0:T(8,128)S(1)}, f32[2,48,640]{2,1,0:T(8,128)S(1)}, u32[]{:S(2)}, u32[]{:S(2)}) collective-permute-start(f32[2,48,640]{2,1,0:T(8,128)S(1)} %get-tuple-element.56), channel_id=1, source_target_pairs={{16,0},{18,2},{20,4},{22,6},{24,8},{26,10},{28,12},{30,14},{32,16}... | collective-permute-start | bytes 737288 | tf_op jit(solution)/shard_map/ppermute | solution.py:28
  195.8 2.2 collective-permute-done.13.low
  198.0 3.8 %collective-permute-done.14.high = f32[2,48,640]{2,1,0:T(8,128)S(1)} collective-permute-done((f32[2,48,640]{2,1,0:T(8,128)S(1)}, f32[2,48,640]{2,1,0:T(8,128)S(1)}, u32[]{:S(2)}, u32[]{:S(2)}) %collective-permute-start.14) | collective-permute-done | bytes 245792 | tf_op jit(solution)/shard_map/ppermute | solution.py:28
  205.4 6.0 %collective-permute-start.16 = (f32[1,48,640]{2,1,0:T(8,128)S(1)}, f32[1,48,640]{2,1,0:T(8,128)S(1)}, u32[]{:S(2)}, u32[]{:S(2)}) collective-permute-start(f32[1,48,640]{2,1,0:T(8,128)S(1)} %get-tuple-element.59.first), channel_id=1, source_target_pairs={{16,0},{18,2},{20,4},{22,6},{24,8},{26,10},{28,12},{30,14},{32,16}... | collective-permute-start | bytes 368648 | tf_op jit(solution)/shard_map/ppermute | solution.py:28
  214.5 3.9 %collective-permute-start.17 = (f32[1,48,640]{2,1,0:T(8,128)S(1)}, f32[1,48,640]{2,1,0:T(8,128)S(1)}, u32[]{:S(2)}, u32[]{:S(2)}) collective-permute-start(f32[1,48,640]{2,1,0:T(8,128)S(1)} %get-tuple-element.61.second.second4), channel_id=1, source_target_pairs={{0,16},{2,18},{4,20},{6,22},{8,24},{10,26},{12,28},{14,30},{16,32}... | collective-permute-start | bytes 368648 | tf_op jit(solution)/shard_map/ppermute | solution.py:28
  218.4 4.0 %collective-permute-start.18 = (f32[1,48,640]{2,1,0:T(8,128)S(1)}, f32[1,48,640]{2,1,0:T(8,128)S(1)}, u32[]{:S(2)}, u32[]{:S(2)}) collective-permute-start(f32[1,48,640]{2,1,0:T(8,128)S(1)} %get-tuple-element.61.second.second4), channel_id=1, source_target_pairs={{16,0},{18,2},{20,4},{22,6},{24,8},{26,10},{28,12},{30,14},{32,16}... | collective-permute-start | bytes 368648 | tf_op jit(solution)/shard_map/ppermute | solution.py:28
  226.8 3.5 %collective-permute-done.19 = f32[1,48,640]{2,1,0:T(8,128)S(1)} collective-permute-done((f32[1,48,640]{2,1,0:T(8,128)S(1)}, f32[1,48,640]{2,1,0:T(8,128)S(1)}, u32[]{:S(2)}, u32[]{:S(2)}) %collective-permute-start.19) | collective-permute-done | bytes 122912 | tf_op jit(solution)/shard_map/ppermute | solution.py:43
  230.4 6.3 %collective-permute-start.21 = (f32[1,48,640]{2,1,0:T(8,128)S(1)}, f32[1,48,640]{2,1,0:T(8,128)S(1)}, u32[]{:S(2)}, u32[]{:S(2)}) collective-permute-start(f32[1,48,640]{2,1,0:T(8,128)S(1)} %get-tuple-element.67.first), channel_id=1, source_target_pairs={{0,32},{2,34},{4,36},{6,38},{8,40},{10,42},{12,44},{14,46},{16,48}... | collective-permute-start | bytes 368648 | tf_op jit(solution)/shard_map/ppermute | solution.py:28
  239.5 5.4 %collective-permute-done.22.high = f32[1,48,640]{2,1,0:T(8,128)S(1)} collective-permute-done((f32[1,48,640]{2,1,0:T(8,128)S(1)}, f32[1,48,640]{2,1,0:T(8,128)S(1)}, u32[]{:S(2)}, u32[]{:S(2)}) %collective-permute-start.22) | collective-permute-done | bytes 122912 | tf_op jit(solution)/shard_map/ppermute | solution.py:28
  245.9 6.8 %all-to-all-start.3 = ((f32[8,32,640]{2,1,0:T(8,128)}), f32[8,32,640]{2,1,0:T(8,128)S(1)}, u32[]{:S(2)}, u32[]{:S(2)}) async-start(f32[8,32,640]{2,1,0:T(8,128)} %shard_map.71), calls=%async_computation.3 | async-start | bytes 1310720 | tf_op jit(solution)/shard_map/all_to_all | solution.py:47
  257.3 10.1 %all-to-all-done.3 = f32[8,32,640]{2,1,0:T(8,128)S(1)} async-done(((f32[8,32,640]{2,1,0:T(8,128)}), f32[8,32,640]{2,1,0:T(8,128)S(1)}, u32[]{:S(2)}, u32[]{:S(2)}) %all-to-all-start.3) | async-done | bytes 655392 | tf_op jit(solution)/shard_map/all_to_all | solution.py:47
  (90 shorter events, 53.4 us)
Async XLA Ops:
  4.5 8.6 %copy-start.10 = (f32[2,256,640]{2,1,0:T(8,128)S(1)}, f32[2,256,640]{2,1,0:T(8,128)}, u32[]{:S(2)}) copy-start(f32[2,256,640]{2,1,0:T(8,128)} %source.1) | copy-start | bytes 3932164
  4.6 43.0 %all-to-all-start = ((f32[8,2,32,640]{3,2,1,0:T(8,128)}), f32[8,2,32,640]{3,2,1,0:T(8,128)S(1)}, u32[]{:S(2)}, u32[]{:S(2)}) async-start(f32[8,2,32,640]{3,2,1,0:T(8,128)} %shard_map.59), calls=%async_computation | async-start | bytes 2621440 | tf_op jit(solution)/shard_map/all_to_all | solution.py:47
  13.2 1.3 collective-permute-start
  47.6 14.8 %collective-permute-start.1 = (f32[16,8,640]{2,1,0:T(8,128)S(1)}, f32[16,8,640]{2,1,0:T(8,128)S(1)}, u32[]{:S(2)}, u32[]{:S(2)}) collective-permute-start(f32[16,8,640]{2,1,0:T(8,128)S(1)} %get-tuple-element.72), channel_id=1, source_target_pairs={{0,2},{2,4},{4,6},{6,8},{8,10},{10,12},{12,14},{14,1},{1,3},{3,5},... | collective-permute-start | bytes 983048 | tf_op jit(solution)/shard_map/ppermute | solution.py:38
  50.0 11.0 %collective-permute-start.2 = (f32[16,8,640]{2,1,0:T(8,128)S(1)}, f32[16,8,640]{2,1,0:T(8,128)S(1)}, u32[]{:S(2)}, u32[]{:S(2)}) collective-permute-start(f32[16,8,640]{2,1,0:T(8,128)S(1)} %get-tuple-element.71), channel_id=1, source_target_pairs={{2,0},{4,2},{6,4},{8,6},{10,8},{12,10},{14,12},{1,14},{3,1},{5,3},... | collective-permute-start | bytes 983048 | tf_op jit(solution)/shard_map/ppermute | solution.py:38
  63.0 4.4 %copy-start.12 = (f32[16,8,640]{2,1,0:T(8,128)S(1)}, f32[16,8,640]{2,1,0:T(8,128)}, u32[]{:S(2)}) copy-start(f32[16,8,640]{2,1,0:T(8,128)} %copy-done.11) | copy-start | bytes 983044
  63.0 44.9 %all-to-all-start.1 = ((f32[8,2,40,640]{3,2,1,0:T(8,128)}), f32[8,2,40,640]{3,2,1,0:T(8,128)}, u32[]{:S(2)}, u32[]{:S(2)}) async-start(f32[8,2,40,640]{3,2,1,0:T(8,128)} %shard_map.60), calls=%async_computation.1 | async-start | bytes 3276800 | tf_op jit(solution)/shard_map/all_to_all | solution.py:47
  70.1 46.9 %collective-permute-start.5 = (f32[9,48,640]{2,1,0:T(8,128)}, f32[9,48,640]{2,1,0:T(8,128)S(1)}, u32[]{:S(2)}, u32[]{:S(2)}) collective-permute-start(f32[9,48,640]{2,1,0:T(8,128)} %get-tuple-element.36), channel_id=1, source_target_pairs={{0,16},{2,18},{4,20},{6,22},{8,24},{10,26},{12,28},{14,30},{16,32}... | collective-permute-start | bytes 3317768 | tf_op jit(solution)/shard_map/ppermute | solution.py:28
  73.5 44.5 %collective-permute-start.6 = (f32[9,48,640]{2,1,0:T(8,128)S(1)}, f32[9,48,640]{2,1,0:T(8,128)}, u32[]{:S(2)}, u32[]{:S(2)}) collective-permute-start(f32[9,48,640]{2,1,0:T(8,128)S(1)} %get-tuple-element.37), channel_id=1, source_target_pairs={{16,0},{18,2},{20,4},{22,6},{24,8},{26,10},{28,12},{30,14},{32,16}... | collective-permute-start | bytes 3317768 | tf_op jit(solution)/shard_map/ppermute | solution.py:28
  109.0 20.9 %collective-permute-start.3 = (f32[2,40,640]{2,1,0:T(8,128)S(1)}, f32[2,40,640]{2,1,0:T(8,128)S(1)}, u32[]{:S(2)}, u32[]{:S(2)}) collective-permute-start(f32[2,40,640]{2,1,0:T(8,128)S(1)} %get-tuple-element.70), channel_id=1, source_target_pairs={{0,16},{2,18},{4,20},{6,22},{8,24},{10,26},{12,28},{14,30},{16,32}... | collective-permute-start | bytes 614408 | tf_op jit(solution)/shard_map/ppermute | solution.py:28
  112.4 17.5 %collective-permute-start.4 = (f32[2,40,640]{2,1,0:T(8,128)S(1)}, f32[2,40,640]{2,1,0:T(8,128)S(1)}, u32[]{:S(2)}, u32[]{:S(2)}) collective-permute-start(f32[2,40,640]{2,1,0:T(8,128)S(1)} %get-tuple-element.69), channel_id=1, source_target_pairs={{16,0},{18,2},{20,4},{22,6},{24,8},{26,10},{28,12},{30,14},{32,16}... | collective-permute-start | bytes 614408 | tf_op jit(solution)/shard_map/ppermute | solution.py:28
  130.0 30.6 %copy-start = (f32[25,48,640]{2,1,0:T(8,128)}, f32[25,48,640]{2,1,0:T(8,128)S(1)}, u32[]{:S(2)}) copy-start(f32[25,48,640]{2,1,0:T(8,128)S(1)} %get-tuple-element.46.faces2.faces) | copy-start | bytes 9216004
  138.4 10.2 %collective-permute-start.7 = (f32[2,48,640]{2,1,0:T(8,128)S(1)}, f32[2,48,640]{2,1,0:T(8,128)S(1)}, u32[]{:S(2)}, u32[]{:S(2)}) collective-permute-start(f32[2,48,640]{2,1,0:T(8,128)S(1)} %get-tuple-element.41), channel_id=1, source_target_pairs={{0,16},{2,18},{4,20},{6,22},{8,24},{10,26},{12,28},{14,30},{16,32}... | collective-permute-start | bytes 737288 | tf_op jit(solution)/shard_map/ppermute | solution.py:28
  140.3 9.7 %collective-permute-start.8 = (f32[2,48,640]{2,1,0:T(8,128)S(1)}, f32[2,48,640]{2,1,0:T(8,128)S(1)}, u32[]{:S(2)}, u32[]{:S(2)}) collective-permute-start(f32[2,48,640]{2,1,0:T(8,128)S(1)} %get-tuple-element.42), channel_id=1, source_target_pairs={{16,0},{18,2},{20,4},{22,6},{24,8},{26,10},{28,12},{30,14},{32,16}... | collective-permute-start | bytes 737288 | tf_op jit(solution)/shard_map/ppermute | solution.py:28
  152.7 6.3 %collective-permute-start.10 = (f32[4,8,640]{2,1,0:T(8,128)S(1)}, f32[4,8,640]{2,1,0:T(8,128)S(1)}, u32[]{:S(2)}, u32[]{:S(2)}) collective-permute-start(f32[4,8,640]{2,1,0:T(8,128)S(1)} %get-tuple-element.45), channel_id=1, source_target_pairs={{2,0},{4,2},{6,4},{8,6},{10,8},{12,10},{14,12},{1,14},{3,1},{5,3},... | collective-permute-start | bytes 245768 | tf_op jit(solution)/shard_map/ppermute | solution.py:38
  154.0 6.6 %collective-permute-start.9 = (f32[4,8,640]{2,1,0:T(8,128)S(1)}, f32[4,8,640]{2,1,0:T(8,128)S(1)}, u32[]{:S(2)}, u32[]{:S(2)}) collective-permute-start(f32[4,8,640]{2,1,0:T(8,128)S(1)} %get-tuple-element.44), channel_id=1, source_target_pairs={{0,2},{2,4},{4,6},{6,8},{8,10},{10,12},{12,14},{14,1},{1,3},{3,5},... | collective-permute-start | bytes 245768 | tf_op jit(solution)/shard_map/ppermute | solution.py:38
  163.4 75.2 %all-to-all-start.2 = ((f32[8,3,32,640]{3,2,1,0:T(8,128)}), f32[8,3,32,640]{3,2,1,0:T(8,128)}, u32[]{:S(2)}, u32[]{:S(2)}) async-start(f32[8,3,32,640]{3,2,1,0:T(8,128)} %copy-done.3), calls=%async_computation.2 | async-start | bytes 3932160 | tf_op jit(solution)/shard_map/all_to_all | solution.py:47
  168.5 11.9 %collective-permute-start.11 = (f32[2,48,640]{2,1,0:T(8,128)}, f32[2,48,640]{2,1,0:T(8,128)S(1)}, u32[]{:S(2)}, u32[]{:S(2)}) collective-permute-start(f32[2,48,640]{2,1,0:T(8,128)} %copy-done.16), channel_id=1, source_target_pairs={{0,16},{2,18},{4,20},{6,22},{8,24},{10,26},{12,28},{14,30},{16,32}... | collective-permute-start | bytes 737288 | tf_op jit(solution)/shard_map/ppermute | solution.py:28
  170.4 11.3 %collective-permute-start.12 = (f32[2,48,640]{2,1,0:T(8,128)}, f32[2,48,640]{2,1,0:T(8,128)}, u32[]{:S(2)}, u32[]{:S(2)}) collective-permute-start(f32[2,48,640]{2,1,0:T(8,128)} %copy-done.15), channel_id=1, source_target_pairs={{16,0},{18,2},{20,4},{22,6},{24,8},{26,10},{28,12},{30,14},{32,16}... | collective-permute-start | bytes 737288 | tf_op jit(solution)/shard_map/ppermute | solution.py:28
  181.7 1.9 copy-start.1
  187.1 10.8 %collective-permute-start.13 = (f32[2,48,640]{2,1,0:T(8,128)S(1)}, f32[2,48,640]{2,1,0:T(8,128)S(1)}, u32[]{:S(2)}, u32[]{:S(2)}) collective-permute-start(f32[2,48,640]{2,1,0:T(8,128)S(1)} %get-tuple-element.55), channel_id=1, source_target_pairs={{0,16},{2,18},{4,20},{6,22},{8,24},{10,26},{12,28},{14,30},{16,32}... | collective-permute-start | bytes 737288 | tf_op jit(solution)/shard_map/ppermute | solution.py:28
  191.1 10.7 %collective-permute-start.14 = (f32[2,48,640]{2,1,0:T(8,128)S(1)}, f32[2,48,640]{2,1,0:T(8,128)S(1)}, u32[]{:S(2)}, u32[]{:S(2)}) collective-permute-start(f32[2,48,640]{2,1,0:T(8,128)S(1)} %get-tuple-element.56), channel_id=1, source_target_pairs={{16,0},{18,2},{20,4},{22,6},{24,8},{26,10},{28,12},{30,14},{32,16}... | collective-permute-start | bytes 737288 | tf_op jit(solution)/shard_map/ppermute | solution.py:28
  195.7 31.0 %collective-permute-start.20 = (f32[3,48,640]{2,1,0:T(8,128)S(1)}, f32[3,48,640]{2,1,0:T(8,128)S(1)}, u32[]{:S(2)}, u32[]{:S(2)}) collective-permute-start(f32[3,48,640]{2,1,0:T(8,128)S(1)} %pad_maximum_fusion), channel_id=1, source_target_pairs={{0,16},{2,18},{4,20},{6,22},{8,24},{10,26},{12,28},{14,30},{16,0},... | collective-permute-start | bytes 1105928 | tf_op jit(solution)/shard_map/ppermute | solution.py:43
  203.5 8.9 %collective-permute-start.15 = (f32[1,48,640]{2,1,0:T(8,128)S(1)}, f32[1,48,640]{2,1,0:T(8,128)S(1)}, u32[]{:S(2)}, u32[]{:S(2)}) collective-permute-start(f32[1,48,640]{2,1,0:T(8,128)S(1)} %get-tuple-element.59.first), channel_id=1, source_target_pairs={{0,16},{2,18},{4,20},{6,22},{8,24},{10,26},{12,28},{14,30},{16,32}... | collective-permute-start | bytes 368648 | tf_op jit(solution)/shard_map/ppermute | solution.py:28
  205.4 8.9 %collective-permute-start.16 = (f32[1,48,640]{2,1,0:T(8,128)S(1)}, f32[1,48,640]{2,1,0:T(8,128)S(1)}, u32[]{:S(2)}, u32[]{:S(2)}) collective-permute-start(f32[1,48,640]{2,1,0:T(8,128)S(1)} %get-tuple-element.59.first), channel_id=1, source_target_pairs={{16,0},{18,2},{20,4},{22,6},{24,8},{26,10},{28,12},{30,14},{32,16}... | collective-permute-start | bytes 368648 | tf_op jit(solution)/shard_map/ppermute | solution.py:28
  214.5 8.9 %collective-permute-start.17 = (f32[1,48,640]{2,1,0:T(8,128)S(1)}, f32[1,48,640]{2,1,0:T(8,128)S(1)}, u32[]{:S(2)}, u32[]{:S(2)}) collective-permute-start(f32[1,48,640]{2,1,0:T(8,128)S(1)} %get-tuple-element.61.second.second4), channel_id=1, source_target_pairs={{0,16},{2,18},{4,20},{6,22},{8,24},{10,26},{12,28},{14,30},{16,32}... | collective-permute-start | bytes 368648 | tf_op jit(solution)/shard_map/ppermute | solution.py:28
  218.4 6.8 %collective-permute-start.18 = (f32[1,48,640]{2,1,0:T(8,128)S(1)}, f32[1,48,640]{2,1,0:T(8,128)S(1)}, u32[]{:S(2)}, u32[]{:S(2)}) collective-permute-start(f32[1,48,640]{2,1,0:T(8,128)S(1)} %get-tuple-element.61.second.second4), channel_id=1, source_target_pairs={{16,0},{18,2},{20,4},{22,6},{24,8},{26,10},{28,12},{30,14},{32,16}... | collective-permute-start | bytes 368648 | tf_op jit(solution)/shard_map/ppermute | solution.py:28
  225.4 19.6 %copy-start.9 = (f32[2,32,640]{2,1,0:T(8,128)S(1)}, f32[2,32,640]{2,1,0:T(8,128)}, u32[]{:S(2)}) copy-start(f32[2,32,640]{2,1,0:T(8,128)} %copy-done.8) | copy-start | bytes 491524
  225.4 5.0 %collective-permute-start.19 = (f32[1,48,640]{2,1,0:T(8,128)S(1)}, f32[1,48,640]{2,1,0:T(8,128)S(1)}, u32[]{:S(2)}, u32[]{:S(2)}) collective-permute-start(f32[1,48,640]{2,1,0:T(8,128)S(1)} %shard_map.69), channel_id=1, source_target_pairs={{0,16},{2,18},{4,20},{6,22},{8,24},{10,26},{12,28},{14,30},{16,0},... | collective-permute-start | bytes 368648 | tf_op jit(solution)/shard_map/ppermute | solution.py:43
  230.4 9.2 %collective-permute-start.21 = (f32[1,48,640]{2,1,0:T(8,128)S(1)}, f32[1,48,640]{2,1,0:T(8,128)S(1)}, u32[]{:S(2)}, u32[]{:S(2)}) collective-permute-start(f32[1,48,640]{2,1,0:T(8,128)S(1)} %get-tuple-element.67.first), channel_id=1, source_target_pairs={{0,32},{2,34},{4,36},{6,38},{8,40},{10,42},{12,44},{14,46},{16,48}... | collective-permute-start | bytes 368648 | tf_op jit(solution)/shard_map/ppermute | solution.py:28
  236.6 8.3 %collective-permute-start.22 = (f32[1,48,640]{2,1,0:T(8,128)S(1)}, f32[1,48,640]{2,1,0:T(8,128)S(1)}, u32[]{:S(2)}, u32[]{:S(2)}) collective-permute-start(f32[1,48,640]{2,1,0:T(8,128)S(1)} %get-tuple-element.67.first), channel_id=1, source_target_pairs={{32,0},{34,2},{36,4},{38,6},{40,8},{42,10},{44,12},{46,14},{48,16}... | collective-permute-start | bytes 368648 | tf_op jit(solution)/shard_map/ppermute | solution.py:28
  245.9 21.5 %all-to-all-start.3 = ((f32[8,32,640]{2,1,0:T(8,128)}), f32[8,32,640]{2,1,0:T(8,128)S(1)}, u32[]{:S(2)}, u32[]{:S(2)}) async-start(f32[8,32,640]{2,1,0:T(8,128)} %shard_map.71), calls=%async_computation.3 | async-start | bytes 1310720 | tf_op jit(solution)/shard_map/all_to_all | solution.py:47
  (14 other events, 14.6 us)

commit v4 on v3

--- a/solution.py
+++ b/solution.py
@@ -95,19 +95,29 @@
     lax.fori_loop(0, count, step, 0)
 
 
-def call(kernel, outs, scratch, *args, limit=8, work=0.0):
+def call(kernel, outs, scratch, *args, limit=8, work=0.0, settled=()):
     shapes = [jax.ShapeDtypeStruct(s, jnp.float32) for s in outs]
     vmem = pl.BlockSpec(memory_space=pltpu.VMEM)
+    smem = pl.BlockSpec(memory_space=pltpu.SMEM)
     cost = pl.CostEstimate(flops=int(work * 1.0e9), bytes_accessed=int(work * 3.0e6), transcendentals=0) if work else None
+
+    def body(*refs):
+        kernel(*refs[len(settled):])
+
     return pl.pallas_call(
-        kernel,
+        body,
         out_shape=shapes,
-        in_specs=[vmem] * len(args),
+        in_specs=[pl.BlockSpec(memory_space=pl.ANY)] * len(settled) + [smem if a.dtype == jnp.int32 and a.ndim == 1 else vmem for a in args],
         out_specs=[vmem] * len(shapes),
         scratch_shapes=[pltpu.VMEM(s, jnp.float32) for s in scratch],
         compiler_params=pltpu.CompilerParams(vmem_limit_bytes=limit * 1024 * 1024),
         cost_estimate=cost,
-    )(*args)
+    )(*settled, *args)
+
+
+def ring_permuted(value, by):
+    size = lax.axis_size("gz")
+    return lax.ppermute(value, "gz", [(i, i // RING * RING + (i + by) % RING) for i in range(size)])
 
 
 def after(value, *settled):
@@ -124,30 +134,43 @@
     )(value, *settled)
 
 
-def cut_conduct(labels, fraction, out):
+def cut_conduct(place, labels, fraction, top, bottom, *rest):
+    outs, full = rest[:-1], rest[-1]
     planes, rows, _ = labels.shape
     strip = rows // RING
     for p in range(planes):
+        full[p, :HALO] = top[p]
+        full[p, HALO + rows:] = bottom[p]
         for k in range(RING):
-            at = slice(k * strip, (k + 1) * strip)
-            out[k, p] = conductivity(labels[p, at], fraction[p, at])
-
-
-def cut_source(source, top, bottom, out):
+            at = k * strip
+            full[p, HALO + at:HALO + at + strip] = conductivity(labels[p, at:at + strip], fraction[p, at:at + strip])
+        for k in range(RING):
+            start = pl.multiple_of(((place[0] + k) % RING) * strip, strip)
+            outs[k][p] = full[p, pl.ds(start, strip + 2 * HALO)]
+
+
+def cut_source(place, source, top, bottom, *rest):
+    outs, full = rest[:-1], rest[-1]
     planes, rows, _ = source.shape
     strip = rows // RING
     for p in range(planes):
+        full[p, :HALO] = top[p]
+        full[p, HALO + rows:] = bottom[p]
+        full[p, HALO:HALO + rows] = source[p]
         for k in range(RING):
-            start = k * strip
-            if k == 0:
-                out[k, p, :THIN] = top[p, HALO - THIN:]
-            else:
-                out[k, p, :THIN] = source[p, start - THIN:start]
-            out[k, p, THIN:THIN + strip] = source[p, start:start + strip]
-            if k == RING - 1:
-                out[k, p, THIN + strip:] = bottom[p, :THIN]
-            else:
-                out[k, p, THIN + strip:] = source[p, start + strip:start + strip + THIN]
+            start = pl.multiple_of(((place[0] + k) % RING) * strip, strip)
+            outs[k][p] = full[p, pl.ds(start, strip + 2 * HALO)][HALO - THIN:HALO + strip + THIN]
+
+
+def join(place, *refs):
+    out, low, high = refs[RING:]
+    for k in range(RING):
+        start = ((place[0] + RING - k) % RING) * 2
+        out[start] = refs[k][0]
+        out[start + 1] = refs[k][1]
+    reach = low.shape[0]
+    loop(reach, lambda p: low.__setitem__(p, out[p]))
+    loop(reach, lambda p: high.__setitem__(p, out[p + 16 - reach]))
 
 
 def plane_faces(c):
@@ -163,19 +186,6 @@
 
 def planes_of(count):
     return 4 * count + 1 + (0 if count == 1 else 10 if count == 16 else 8)
-
-
-def frames(c_own, above, below, c, low, high):
-    strip = c_own.shape[1]
-
-    def place(ref, k, p):
-        ref[k, :HALO] = above[p]
-        ref[k, HALO:HALO + strip] = c_own[p]
-        ref[k, HALO + strip:] = below[p]
-
-    loop(16, lambda p: place(c, p, p))
-    loop(REACH, lambda p: place(low, p, p))
-    loop(REACH, lambda p: place(high, p, p + 16 - REACH))
 
 
 def make_faces(c, low, high, faces0, faces1, faces2, faces3, faces4):
@@ -418,16 +428,22 @@
     def shape(n):
         return (n, frame, columns)
 
-    (c_cut,) = call(cut_conduct, [(RING, planes, strip, columns)], [], labels, fraction, limit=10)
-    c_own = transposed(c_cut).reshape(RING * planes, strip, columns)
-    above = row_shifted(c_own[:, strip - HALO:], 1)
-    below = row_shifted(c_own[:, :HALO], -1)
+    place = jnp.reshape(lax.axis_index("gz") % RING, (1,)).astype(jnp.int32)
+    c_top, c_bottom = edges_of(conductivity(labels[:, :HALO], fraction[:, :HALO]),
+                               conductivity(labels[:, rows - HALO:], fraction[:, rows - HALO:]))
+    cuts = call(cut_conduct, [(planes, frame, columns)] * RING, [(planes, rows + 2 * HALO, columns)],
+                place, labels, fraction, c_top, c_bottom, limit=10)
     s_top, s_bottom = edges_of(right_side[:, :HALO], right_side[:, rows - HALO:])
-    (s_cut,) = call(cut_source, [(RING, planes, strip + 2 * THIN, columns)], [],
-                    right_side, s_top, s_bottom, limit=10, work=4.0)
-    s_own = transposed(after(s_cut, above[0], below[0])).reshape(RING * planes, strip + 2 * THIN, columns)
-
-    c, bundle_down, bundle_up = call(frames, [shape(16), shape(REACH), shape(REACH)], [], c_own, above, below, limit=10, work=2.0)
+    thin = strip + 2 * THIN
+    s_cuts = call(cut_source, [(planes, thin, columns)] * RING, [(planes, rows + 2 * HALO, columns)],
+                  place, right_side, s_top, s_bottom, limit=10)
+    c_parts = [cuts[0]] + [ring_permuted(cuts[k], k) for k in range(1, RING)]
+    s_cuts = list(s_cuts)
+    for k in (1, RING - 1):
+        s_cuts[k] = after(s_cuts[k], c_parts[1], c_parts[2])
+    s_parts = [s_cuts[0]] + [ring_permuted(s_cuts[k], k) for k in range(1, RING)]
+
+    c, bundle_down, bundle_up = call(join, [shape(16), shape(REACH), shape(REACH)], [], place, *c_parts, limit=10, settled=(s_parts[1], s_parts[7]))
     c_low, c_high = exchange(bundle_down, bundle_up)
     faces0, faces1, faces2, faces3, faces4 = call(
         make_faces, [shape(planes_of(n)) for n in (16, 8, 4, 2, 1)], [], c, c_low, c_high, limit=28, work=12.0)
@@ -437,7 +453,9 @@
     up5 = jnp.where(even_ring, other[2:], z_high)
     east5, north5, w5 = call(make_last_faces, [shape(1)] * 3, [], faces4, other, down5, up5)
 
-    s_low, s_high = exchange(s_own[:2], s_own[-2:])
+    s_own, edge_down, edge_up = call(
+        join, [(16, thin, columns), (2, thin, columns), (2, thin, columns)], [], place, *s_parts, limit=10, settled=(faces4,))
+    s_low, s_high = exchange(edge_down, edge_up)
     fine, s1, edge_down, edge_up = call(
         fine_level, [(RING, planes, strip, columns), shape(8), shape(2), shape(2)],
         [shape(18), shape(20), shape(16), shape(18)],

time: 270 us -> 276 us (1.022)
  starting transfers between devices: 101 us -> 120 us
  local copies, waits for them, and re-layouts: 24.9 us -> 18.9 us
  waiting for transfers between devices: 113 us -> 109 us
  Pallas kernels: 28.2 us -> 24.4 us
    all_to_all x4 -> x2, waiting for transfers between devices: 73.1 us -> 10.1 us  [transposed(): lax.all_to_all(value, 'gz', 0, 0, axis_index_groups=ring_groups(lax.axis_...]
    ppermute x0 -> x14, starting transfers between devices: none -> 42.8 us  [ring_permuted(): lax.ppermute(value, 'gz', [(i, i // RING * RING + (i + by) % RING) for i...]
    ppermute x0 -> x14, waiting for transfers between devices: none -> 41.9 us  [ring_permuted(): lax.ppermute(value, 'gz', [(i, i // RING * RING + (i + by) % RING) for i...]
    ppermute x16, waiting for transfers between devices: 25 us -> 43.7 us  [shifted(): return lax.ppermute(value, 'gz', pairs)]
    all_to_all x4 -> x2, starting transfers between devices: 24.9 us -> 13.3 us  [transposed(): lax.all_to_all(value, 'gz', 0, 0, axis_index_groups=ring_groups(lax.axis_...]
    ppermute x4 -> x2, starting transfers between devices: 9.53 us -> 2.59 us  [row_shifted(): return lax.ppermute(value, ('gz', 'xy'), pairs)]
    pallas_call x13 -> x14, Pallas kernels: 28.2 us -> 24.4 us  [call(): pl.pallas_call(body, out_shape=shapes, in_specs=[pl.BlockSpec(memory_spac...]
    unnamed x39 -> x37, local copies, waits for them, and re-layouts: 17.3 us -> 13.6 us
  transfers between devices with their start and end apart: 27 -> 38, of which waited for: 20 -> 27; matrix products, arithmetic and copies ran while one was open for 3% -> 2% of each run, Pallas kernels for 5% -> 5%
where the time goes in v4:
time: 276 us; the launch traced here: 275 us
  starting transfers between devices  120 us (43%)
  waiting for transfers between devices  109 us (39%)
  Pallas kernels  24.4 us (9%)
  local copies, waits for them, and re-layouts  18.9 us (7%)
    ppermute x16, starting transfers between devices, shifted(): return lax.ppermute(value, 'gz', pairs)  61.5 us
    ppermute x16, waiting for transfers between devices, shifted(): return lax.ppermute(value, 'gz', pairs)  43.7 us
    ppermute x14, starting transfers between devices, ring_permuted(): lax.ppermute(value, 'gz', [(i, i // RING * RING + (i + by) % RING) for i...  42.8 us
    ppermute x14, waiting for transfers between devices, ring_permuted(): lax.ppermute(value, 'gz', [(i, i // RING * RING + (i + by) % RING) for i...  41.9 us
    pallas_call x14, Pallas kernels, call(): pl.pallas_call(body, out_shape=shapes, in_specs=[pl.BlockSpec(memory_spac...  24.4 us
    unnamed x37, local copies, waits for them, and re-layouts  13.6 us
    all_to_all x2, starting transfers between devices, transposed(): lax.all_to_all(value, 'gz', 0, 0, axis_index_groups=ring_groups(lax.axis_...  13.3 us
    all_to_all x2, waiting for transfers between devices, transposed(): lax.all_to_all(value, 'gz', 0, 0, axis_index_groups=ring_groups(lax.axis_...  10.1 us
  transfers between devices with their start and end apart: 38, of which 27 were waited for; matrix products, arithmetic and copies ran while one was open for 2% of the time, Pallas kernels for 5%

profile of v4, /device:TPU:8, one launch (start us, length us, event | category | flops | bytes accessed | tf_op | source)
XLA Modules:
  0.0 275.0 jit_solution(494512001728225303)
XLA Ops:
  11.8 4.1 %collective-permute-start.6 = (f32[2,48,640]{2,1,0:T(8,128)}, f32[2,48,640]{2,1,0:T(8,128)S(1)}, u32[]{:S(2)}, u32[]{:S(2)}) collective-permute-start(f32[2,48,640]{2,1,0:T(8,128)} %get-tuple-element.59), channel_id=1, source_target_pairs={{0,6},{2,8},{4,10},{6,12},{8,14},{10,0},{12,2},{14,4},{16,22},{18,... | collective-permute-start | bytes 737288 | tf_op jit(solution)/shard_map/ppermute | solution.py:120
  16.5 4.9 %collective-permute-start.8 = (f32[2,48,640]{2,1,0:T(8,128)S(1)}, f32[2,48,640]{2,1,0:T(8,128)S(1)}, u32[]{:S(2)}, u32[]{:S(2)}) collective-permute-start(f32[2,48,640]{2,1,0:T(8,128)S(1)} %get-tuple-element.61), channel_id=1, source_target_pairs={{0,10},{2,12},{4,14},{6,0},{8,2},{10,4},{12,6},{14,8},{16,26},{18,... | collective-permute-start | bytes 737288 | tf_op jit(solution)/shard_map/ppermute | solution.py:120
  21.4 5.3 %collective-permute-start.9 = (f32[2,48,640]{2,1,0:T(8,128)S(1)}, f32[2,48,640]{2,1,0:T(8,128)S(1)}, u32[]{:S(2)}, u32[]{:S(2)}) collective-permute-start(f32[2,48,640]{2,1,0:T(8,128)S(1)} %get-tuple-element.62), channel_id=1, source_target_pairs={{0,12},{2,14},{4,0},{6,2},{8,4},{10,6},{12,8},{14,10},{16,28},{18,... | collective-permute-start | bytes 737288 | tf_op jit(solution)/shard_map/ppermute | solution.py:120
  26.8 5.6 %collective-permute-done.3.refs_2_.refs_5_ = f32[2,48,640]{2,1,0:T(8,128)S(1)} collective-permute-done((f32[2,48,640]{2,1,0:T(8,128)S(1)}, f32[2,48,640]{2,1,0:T(8,128)S(1)}, u32[]{:S(2)}, u32[]{:S(2)}) %collective-permute-start.3) | collective-permute-done | bytes 245792 | tf_op jit(solution)/shard_map/ppermute | solution.py:120
  37.7 12.7 %collective-permute-done.6.refs_6_ = f32[2,48,640]{2,1,0:T(8,128)S(1)} collective-permute-done((f32[2,48,640]{2,1,0:T(8,128)}, f32[2,48,640]{2,1,0:T(8,128)S(1)}, u32[]{:S(2)}, u32[]{:S(2)}) %collective-permute-start.6) | collective-permute-done | bytes 245792 | tf_op jit(solution)/shard_map/ppermute | solution.py:120
  53.8 5.1 %collective-permute-done.9.refs_9_ = f32[2,48,640]{2,1,0:T(8,128)S(1)} collective-permute-done((f32[2,48,640]{2,1,0:T(8,128)S(1)}, f32[2,48,640]{2,1,0:T(8,128)S(1)}, u32[]{:S(2)}, u32[]{:S(2)}) %collective-permute-start.9) | collective-permute-done | bytes 245792 | tf_op jit(solution)/shard_map/ppermute | solution.py:120
  62.1 3.6 %collective-permute-done.5.refs_1_.refs_9_ = f32[2,40,640]{2,1,0:T(8,128)S(1)} collective-permute-done((f32[2,40,640]{2,1,0:T(8,128)}, f32[2,40,640]{2,1,0:T(8,128)S(1)}, u32[]{:S(2)}, u32[]{:S(2)}) %collective-permute-start.5) | collective-permute-done | bytes 204832 | tf_op jit(solution)/shard_map/ppermute | solution.py:120
  68.0 3.4 %collective-permute-start.11 = (f32[9,48,640]{2,1,0:T(8,128)S(1)}, f32[9,48,640]{2,1,0:T(8,128)S(1)}, u32[]{:S(2)}, u32[]{:S(2)}) collective-permute-start(f32[9,48,640]{2,1,0:T(8,128)S(1)} %get-tuple-element.65), channel_id=1, source_target_pairs={{0,16},{2,18},{4,20},{6,22},{8,24},{10,26},{12,28},{14,30},{16,32}... | collective-permute-start | bytes 3317768 | tf_op jit(solution)/shard_map/ppermute | solution.py:28
  71.4 4.6 %collective-permute-start.12 = (f32[9,48,640]{2,1,0:T(8,128)S(1)}, f32[9,48,640]{2,1,0:T(8,128)S(1)}, u32[]{:S(2)}, u32[]{:S(2)}) collective-permute-start(f32[9,48,640]{2,1,0:T(8,128)S(1)} %get-tuple-element.66), channel_id=1, source_target_pairs={{16,0},{18,2},{20,4},{22,6},{24,8},{26,10},{28,12},{30,14},{32,16}... | collective-permute-start | bytes 3317768 | tf_op jit(solution)/shard_map/ppermute | solution.py:28
  75.9 3.7 %collective-permute-start.13 = (f32[2,40,640]{2,1,0:T(8,128)}, f32[2,40,640]{2,1,0:T(8,128)S(1)}, u32[]{:S(2)}, u32[]{:S(2)}) collective-permute-start(f32[2,40,640]{2,1,0:T(8,128)} %get-tuple-element.69), channel_id=1, source_target_pairs={{0,4},{2,6},{4,8},{6,10},{8,12},{10,14},{12,0},{14,2},{16,20},{18,... | collective-permute-start | bytes 614408 | tf_op jit(solution)/shard_map/ppermute | solution.py:120
  80.4 4.8 %collective-permute-start.15 = (f32[2,40,640]{2,1,0:T(8,128)}, f32[2,40,640]{2,1,0:T(8,128)S(1)}, u32[]{:S(2)}, u32[]{:S(2)}) collective-permute-start(f32[2,40,640]{2,1,0:T(8,128)} %get-tuple-element.71), channel_id=1, source_target_pairs={{0,8},{2,10},{4,12},{6,14},{8,0},{10,2},{12,4},{14,6},{16,24},{18,... | collective-permute-start | bytes 614408 | tf_op jit(solution)/shard_map/ppermute | solution.py:120
  85.3 12.3 %collective-permute-done.11.refs_1_ = f32[9,48,640]{2,1,0:T(8,128)S(1)} collective-permute-done((f32[9,48,640]{2,1,0:T(8,128)S(1)}, f32[9,48,640]{2,1,0:T(8,128)S(1)}, u32[]{:S(2)}, u32[]{:S(2)}) %collective-permute-start.11) | collective-permute-done | bytes 1105952 | tf_op jit(solution)/shard_map/ppermute | solution.py:28
  100.4 4.4 %collective-permute-start.17 = (f32[2,40,640]{2,1,0:T(8,128)}, f32[2,40,640]{2,1,0:T(8,128)S(1)}, u32[]{:S(2)}, u32[]{:S(2)}) collective-permute-start(f32[2,40,640]{2,1,0:T(8,128)} %get-tuple-element.73), channel_id=1, source_target_pairs={{0,12},{2,14},{4,0},{6,2},{8,4},{10,6},{12,8},{14,10},{16,28},{18,... | collective-permute-start | bytes 614408 | tf_op jit(solution)/shard_map/ppermute | solution.py:120
  104.8 7.9 %shard_map.63 = (f32[75,48,640]{2,1,0:T(8,128)S(1)}, f32[41,48,640]{2,1,0:T(8,128)S(1)}, f32[25,48,640]{2,1,0:T(8,128)S(1)}, f32[17,48,640]{2,1,0:T(8,128)S(1)}, f32[5,48,640]{2,1,0:T(8,128)S(1)}) custom-call(f32[16,48,640]{2,1,0:T(8,128)S(1)} %get-tuple-element.64.refs_0_, f32[9,48,640]{2,1,0:T(8,128)S(1)} %collective-permute-done.11.refs_1_, ...), custom_call_target="tpu_custom_call" | custom-call | flops 12000000000 | bytes 36000000 | tf_op jit(solution)/shard_map/pallas_call | solution.py:107
  115.4 8.9 %collective-permute-done.17.refs_8_ = f32[2,40,640]{2,1,0:T(8,128)S(1)} collective-permute-done((f32[2,40,640]{2,1,0:T(8,128)}, f32[2,40,640]{2,1,0:T(8,128)S(1)}, u32[]{:S(2)}, u32[]{:S(2)}) %collective-permute-start.17) | collective-permute-done | bytes 204832 | tf_op jit(solution)/shard_map/ppermute | solution.py:120
  126.4 6.0 %collective-permute-start.19 = (f32[2,40,640]{2,1,0:T(8,128)S(1)}, f32[2,40,640]{2,1,0:T(8,128)S(1)}, u32[]{:S(2)}, u32[]{:S(2)}) collective-permute-start(f32[2,40,640]{2,1,0:T(8,128)S(1)} %get-tuple-element.76), channel_id=1, source_target_pairs={{16,0},{18,2},{20,4},{22,6},{24,8},{26,10},{28,12},{30,14},{32,16}... | collective-permute-start | bytes 614408 | tf_op jit(solution)/shard_map/ppermute | solution.py:28
  136.7 6.1 %shard_map.65 = (f32[8,2,32,640]{3,2,1,0:T(8,128)S(1)}, f32[8,48,640]{2,1,0:T(8,128)S(1)}, f32[2,48,640]{2,1,0:T(8,128)S(1)}, f32[2,48,640]{2,1,0:T(8,128)S(1)}) custom-call(f32[16,40,640]{2,1,0:T(8,128)S(1)} %get-tuple-element.74.refs_0_, f32[2,40,640]{2,1,0:T(8,128)S(1)} %collective-permute-done.18.refs_1_, ...), custom_call_target="tpu_custom_call" | custom-call | flops 8000000000 | bytes 24000000 | tf_op jit(solution)/shard_map/pallas_call | solution.py:107
  144.6 6.5 %collective-permute-start.21 = (f32[2,48,640]{2,1,0:T(8,128)S(1)}, f32[2,48,640]{2,1,0:T(8,128)S(1)}, u32[]{:S(2)}, u32[]{:S(2)}) collective-permute-start(f32[2,48,640]{2,1,0:T(8,128)S(1)} %get-tuple-element.81), channel_id=1, source_target_pairs={{16,0},{18,2},{20,4},{22,6},{24,8},{26,10},{28,12},{30,14},{32,16}... | collective-permute-start | bytes 737288 | tf_op jit(solution)/shard_map/ppermute | solution.py:28
  161.1 6.5 %collective-permute-done.23.refs_2_ = f32[4,8,640]{2,1,0:T(8,128)S(1)} collective-permute-done((f32[4,8,640]{2,1,0:T(8,128)S(1)}, f32[4,8,640]{2,1,0:T(8,128)S(1)}, u32[]{:S(2)}, u32[]{:S(2)}) %collective-permute-start.23) | collective-permute-done | bytes 81952 | tf_op jit(solution)/shard_map/ppermute | solution.py:38
  170.5 4.3 %all-to-all-start = ((f32[8,3,32,640]{3,2,1,0:T(8,128)}), f32[8,3,32,640]{3,2,1,0:T(8,128)}, u32[]{:S(2)}, u32[]{:S(2)}) async-start(f32[8,3,32,640]{3,2,1,0:T(8,128)} %copy-done.6), calls=%async_computation | async-start | bytes 3932160 | tf_op jit(solution)/shard_map/all_to_all | solution.py:47
  174.9 3.9 %collective-permute-start.24 = (f32[2,48,640]{2,1,0:T(8,128)}, f32[2,48,640]{2,1,0:T(8,128)S(1)}, u32[]{:S(2)}, u32[]{:S(2)}) collective-permute-start(f32[2,48,640]{2,1,0:T(8,128)} %copy-done.17), channel_id=1, source_target_pairs={{0,16},{2,18},{4,20},{6,22},{8,24},{10,26},{12,28},{14,30},{16,32}... | collective-permute-start | bytes 737288 | tf_op jit(solution)/shard_map/ppermute | solution.py:28
  178.8 4.5 %collective-permute-start.25 = (f32[2,48,640]{2,1,0:T(8,128)}, f32[2,48,640]{2,1,0:T(8,128)}, u32[]{:S(2)}, u32[]{:S(2)}) collective-permute-start(f32[2,48,640]{2,1,0:T(8,128)} %copy-done.16), channel_id=1, source_target_pairs={{16,0},{18,2},{20,4},{22,6},{24,8},{26,10},{28,12},{30,14},{32,16}... | collective-permute-start | bytes 737288 | tf_op jit(solution)/shard_map/ppermute | solution.py:28
  192.8 3.9 %collective-permute-start.26 = (f32[2,48,640]{2,1,0:T(8,128)S(1)}, f32[2,48,640]{2,1,0:T(8,128)S(1)}, u32[]{:S(2)}, u32[]{:S(2)}) collective-permute-start(f32[2,48,640]{2,1,0:T(8,128)S(1)} %get-tuple-element.94), channel_id=1, source_target_pairs={{0,16},{2,18},{4,20},{6,22},{8,24},{10,26},{12,28},{14,30},{16,32}... | collective-permute-start | bytes 737288 | tf_op jit(solution)/shard_map/ppermute | solution.py:28
  196.7 4.5 %collective-permute-start.27 = (f32[2,48,640]{2,1,0:T(8,128)S(1)}, f32[2,48,640]{2,1,0:T(8,128)S(1)}, u32[]{:S(2)}, u32[]{:S(2)}) collective-permute-start(f32[2,48,640]{2,1,0:T(8,128)S(1)} %get-tuple-element.95), channel_id=1, source_target_pairs={{16,0},{18,2},{20,4},{22,6},{24,8},{26,10},{28,12},{30,14},{32,16}... | collective-permute-start | bytes 737288 | tf_op jit(solution)/shard_map/ppermute | solution.py:28
  207.9 5.2 %collective-permute-start.29 = (f32[1,48,640]{2,1,0:T(8,128)S(1)}, f32[1,48,640]{2,1,0:T(8,128)S(1)}, u32[]{:S(2)}, u32[]{:S(2)}) collective-permute-start(f32[1,48,640]{2,1,0:T(8,128)S(1)} %get-tuple-element.97.refs_1_), channel_id=1, source_target_pairs={{16,0},{18,2},{20,4},{22,6},{24,8},{26,10},{28,12},{30,14},{32,16}... | collective-permute-start | bytes 368648 | tf_op jit(solution)/shard_map/ppermute | solution.py:28
  215.5 6.5 %collective-permute-done.28.refs_2_ = f32[1,48,640]{2,1,0:T(8,128)S(1)} collective-permute-done((f32[1,48,640]{2,1,0:T(8,128)S(1)}, f32[1,48,640]{2,1,0:T(8,128)S(1)}, u32[]{:S(2)}, u32[]{:S(2)}) %collective-permute-start.28) | collective-permute-done | bytes 122912 | tf_op jit(solution)/shard_map/ppermute | solution.py:28
  224.1 3.9 %collective-permute-start.30 = (f32[1,48,640]{2,1,0:T(8,128)S(1)}, f32[1,48,640]{2,1,0:T(8,128)S(1)}, u32[]{:S(2)}, u32[]{:S(2)}) collective-permute-start(f32[1,48,640]{2,1,0:T(8,128)S(1)} %get-tuple-element.99.refs_2_.refs_11_), channel_id=1, source_target_pairs={{0,16},{2,18},{4,20},{6,22},{8,24},{10,26},{12,28},{14,30},{16,32}... | collective-permute-start | bytes 368648 | tf_op jit(solution)/shard_map/ppermute | solution.py:28
  229.0 4.0 %collective-permute-done.30.refs_3_ = f32[1,48,640]{2,1,0:T(8,128)S(1)} collective-permute-done((f32[1,48,640]{2,1,0:T(8,128)S(1)}, f32[1,48,640]{2,1,0:T(8,128)S(1)}, u32[]{:S(2)}, u32[]{:S(2)}) %collective-permute-start.30) | collective-permute-done | bytes 122912 | tf_op jit(solution)/shard_map/ppermute | solution.py:28
  233.4 4.9 %collective-permute-done.32 = f32[1,48,640]{2,1,0:T(8,128)S(1)} collective-permute-done((f32[1,48,640]{2,1,0:T(8,128)S(1)}, f32[1,48,640]{2,1,0:T(8,128)S(1)}, u32[]{:S(2)}, u32[]{:S(2)}) %collective-permute-start.32) | collective-permute-done | bytes 122912 | tf_op jit(solution)/shard_map/ppermute | solution.py:43
  240.3 5.4 %collective-permute-start.34 = (f32[1,48,640]{2,1,0:T(8,128)S(1)}, f32[1,48,640]{2,1,0:T(8,128)S(1)}, u32[]{:S(2)}, u32[]{:S(2)}) collective-permute-start(f32[1,48,640]{2,1,0:T(8,128)S(1)} %get-tuple-element.105.refs_1_), channel_id=1, source_target_pairs={{0,32},{2,34},{4,36},{6,38},{8,40},{10,42},{12,44},{14,46},{16,48}... | collective-permute-start | bytes 368648 | tf_op jit(solution)/shard_map/ppermute | solution.py:28
  250.5 9.0 %all-to-all-start.1 = ((f32[8,32,640]{2,1,0:T(8,128)}), f32[8,32,640]{2,1,0:T(8,128)S(1)}, u32[]{:S(2)}, u32[]{:S(2)}) async-start(f32[8,32,640]{2,1,0:T(8,128)} %shard_map.73), calls=%async_computation.1 | async-start | bytes 1310720 | tf_op jit(solution)/shard_map/all_to_all | solution.py:47
  264.0 10.1 %all-to-all-done.1 = f32[8,32,640]{2,1,0:T(8,128)S(1)} async-done(((f32[8,32,640]{2,1,0:T(8,128)}), f32[8,32,640]{2,1,0:T(8,128)S(1)}, u32[]{:S(2)}, u32[]{:S(2)}) %all-to-all-start.1) | async-done | bytes 655392 | tf_op jit(solution)/shard_map/all_to_all | solution.py:47
  (110 shorter events, 87.2 us)
Async XLA Ops:
  6.5 14.9 %collective-permute-start.2 = (f32[2,48,640]{2,1,0:T(8,128)S(1)}, f32[2,48,640]{2,1,0:T(8,128)S(1)}, u32[]{:S(2)}, u32[]{:S(2)}) collective-permute-start(f32[2,48,640]{2,1,0:T(8,128)S(1)} %get-tuple-element.55), channel_id=1, source_target_pairs={{0,2},{2,4},{4,6},{6,8},{8,10},{10,12},{12,14},{14,0},{16,18},{18,... | collective-permute-start | bytes 737288 | tf_op jit(solution)/shard_map/ppermute | solution.py:120
  8.4 23.9 %collective-permute-start.3 = (f32[2,48,640]{2,1,0:T(8,128)S(1)}, f32[2,48,640]{2,1,0:T(8,128)S(1)}, u32[]{:S(2)}, u32[]{:S(2)}) collective-permute-start(f32[2,48,640]{2,1,0:T(8,128)S(1)} %get-tuple-element.56), channel_id=1, source_target_pairs={{0,4},{2,6},{4,8},{6,10},{8,12},{10,14},{12,0},{14,2},{16,20},{18,... | collective-permute-start | bytes 737288 | tf_op jit(solution)/shard_map/ppermute | solution.py:120
  11.8 38.6 %collective-permute-start.6 = (f32[2,48,640]{2,1,0:T(8,128)}, f32[2,48,640]{2,1,0:T(8,128)S(1)}, u32[]{:S(2)}, u32[]{:S(2)}) collective-permute-start(f32[2,48,640]{2,1,0:T(8,128)} %get-tuple-element.59), channel_id=1, source_target_pairs={{0,6},{2,8},{4,10},{6,12},{8,14},{10,0},{12,2},{14,4},{16,22},{18,... | collective-permute-start | bytes 737288 | tf_op jit(solution)/shard_map/ppermute | solution.py:120
  15.9 37.8 %collective-permute-start.7 = (f32[2,48,640]{2,1,0:T(8,128)S(1)}, f32[2,48,640]{2,1,0:T(8,128)S(1)}, u32[]{:S(2)}, u32[]{:S(2)}) collective-permute-start(f32[2,48,640]{2,1,0:T(8,128)S(1)} %get-tuple-element.60), channel_id=1, source_target_pairs={{0,8},{2,10},{4,12},{6,14},{8,0},{10,2},{12,4},{14,6},{16,24},{18,... | collective-permute-start | bytes 737288 | tf_op jit(solution)/shard_map/ppermute | solution.py:120
  16.5 37.2 %collective-permute-start.8 = (f32[2,48,640]{2,1,0:T(8,128)S(1)}, f32[2,48,640]{2,1,0:T(8,128)S(1)}, u32[]{:S(2)}, u32[]{:S(2)}) collective-permute-start(f32[2,48,640]{2,1,0:T(8,128)S(1)} %get-tuple-element.61), channel_id=1, source_target_pairs={{0,10},{2,12},{4,14},{6,0},{8,2},{10,4},{12,6},{14,8},{16,26},{18,... | collective-permute-start | bytes 737288 | tf_op jit(solution)/shard_map/ppermute | solution.py:120
  21.4 37.5 %collective-permute-start.9 = (f32[2,48,640]{2,1,0:T(8,128)S(1)}, f32[2,48,640]{2,1,0:T(8,128)S(1)}, u32[]{:S(2)}, u32[]{:S(2)}) collective-permute-start(f32[2,48,640]{2,1,0:T(8,128)S(1)} %get-tuple-element.62), channel_id=1, source_target_pairs={{0,12},{2,14},{4,0},{6,2},{8,4},{10,6},{12,8},{14,10},{16,28},{18,... | collective-permute-start | bytes 737288 | tf_op jit(solution)/shard_map/ppermute | solution.py:120
  32.3 29.8 %collective-permute-start.10 = (f32[2,48,640]{2,1,0:T(8,128)S(1)}, f32[2,48,640]{2,1,0:T(8,128)S(1)}, u32[]{:S(2)}, u32[]{:S(2)}) collective-permute-start(f32[2,48,640]{2,1,0:T(8,128)S(1)} %get-tuple-element.63), channel_id=1, source_target_pairs={{0,14},{2,0},{4,2},{6,4},{8,6},{10,8},{12,10},{14,12},{16,30},{18,... | collective-permute-start | bytes 737288 | tf_op jit(solution)/shard_map/ppermute | solution.py:120
  50.5 11.7 %collective-permute-start.4 = (f32[2,40,640]{2,1,0:T(8,128)}, f32[2,40,640]{2,1,0:T(8,128)S(1)}, u32[]{:S(2)}, u32[]{:S(2)}) collective-permute-start(f32[2,40,640]{2,1,0:T(8,128)} %shard_map.60), channel_id=1, source_target_pairs={{0,2},{2,4},{4,6},{6,8},{8,10},{10,12},{12,14},{14,0},{16,18},{18,... | collective-permute-start | bytes 614408 | tf_op jit(solution)/shard_map/ppermute | solution.py:120
  53.7 12.0 %collective-permute-start.5 = (f32[2,40,640]{2,1,0:T(8,128)}, f32[2,40,640]{2,1,0:T(8,128)S(1)}, u32[]{:S(2)}, u32[]{:S(2)}) collective-permute-start(f32[2,40,640]{2,1,0:T(8,128)} %shard_map.61), channel_id=1, source_target_pairs={{0,14},{2,0},{4,2},{6,4},{8,6},{10,8},{12,10},{14,12},{16,30},{18,... | collective-permute-start | bytes 614408 | tf_op jit(solution)/shard_map/ppermute | solution.py:120
  68.0 29.6 %collective-permute-start.11 = (f32[9,48,640]{2,1,0:T(8,128)S(1)}, f32[9,48,640]{2,1,0:T(8,128)S(1)}, u32[]{:S(2)}, u32[]{:S(2)}) collective-permute-start(f32[9,48,640]{2,1,0:T(8,128)S(1)} %get-tuple-element.65), channel_id=1, source_target_pairs={{0,16},{2,18},{4,20},{6,22},{8,24},{10,26},{12,28},{14,30},{16,32}... | collective-permute-start | bytes 3317768 | tf_op jit(solution)/shard_map/ppermute | solution.py:28
  71.4 29.0 %collective-permute-start.12 = (f32[9,48,640]{2,1,0:T(8,128)S(1)}, f32[9,48,640]{2,1,0:T(8,128)S(1)}, u32[]{:S(2)}, u32[]{:S(2)}) collective-permute-start(f32[9,48,640]{2,1,0:T(8,128)S(1)} %get-tuple-element.66), channel_id=1, source_target_pairs={{16,0},{18,2},{20,4},{22,6},{24,8},{26,10},{28,12},{30,14},{32,16}... | collective-permute-start | bytes 3317768 | tf_op jit(solution)/shard_map/ppermute | solution.py:28
  75.9 36.7 %collective-permute-start.13 = (f32[2,40,640]{2,1,0:T(8,128)}, f32[2,40,640]{2,1,0:T(8,128)S(1)}, u32[]{:S(2)}, u32[]{:S(2)}) collective-permute-start(f32[2,40,640]{2,1,0:T(8,128)} %get-tuple-element.69), channel_id=1, source_target_pairs={{0,4},{2,6},{4,8},{6,10},{8,12},{10,14},{12,0},{14,2},{16,20},{18,... | collective-permute-start | bytes 614408 | tf_op jit(solution)/shard_map/ppermute | solution.py:120
  79.6 33.1 %collective-permute-start.14 = (f32[2,40,640]{2,1,0:T(8,128)}, f32[2,40,640]{2,1,0:T(8,128)S(1)}, u32[]{:S(2)}, u32[]{:S(2)}) collective-permute-start(f32[2,40,640]{2,1,0:T(8,128)} %get-tuple-element.70), channel_id=1, source_target_pairs={{0,6},{2,8},{4,10},{6,12},{8,14},{10,0},{12,2},{14,4},{16,22},{18,... | collective-permute-start | bytes 614408 | tf_op jit(solution)/shard_map/ppermute | solution.py:120
  80.4 32.3 %collective-permute-start.15 = (f32[2,40,640]{2,1,0:T(8,128)}, f32[2,40,640]{2,1,0:T(8,128)S(1)}, u32[]{:S(2)}, u32[]{:S(2)}) collective-permute-start(f32[2,40,640]{2,1,0:T(8,128)} %get-tuple-element.71), channel_id=1, source_target_pairs={{0,8},{2,10},{4,12},{6,14},{8,0},{10,2},{12,4},{14,6},{16,24},{18,... | collective-permute-start | bytes 614408 | tf_op jit(solution)/shard_map/ppermute | solution.py:120
  97.6 17.8 %collective-permute-start.16 = (f32[2,40,640]{2,1,0:T(8,128)}, f32[2,40,640]{2,1,0:T(8,128)S(1)}, u32[]{:S(2)}, u32[]{:S(2)}) collective-permute-start(f32[2,40,640]{2,1,0:T(8,128)} %get-tuple-element.72), channel_id=1, source_target_pairs={{0,10},{2,12},{4,14},{6,0},{8,2},{10,4},{12,6},{14,8},{16,26},{18,... | collective-permute-start | bytes 614408 | tf_op jit(solution)/shard_map/ppermute | solution.py:120
  100.4 24.0 %collective-permute-start.17 = (f32[2,40,640]{2,1,0:T(8,128)}, f32[2,40,640]{2,1,0:T(8,128)S(1)}, u32[]{:S(2)}, u32[]{:S(2)}) collective-permute-start(f32[2,40,640]{2,1,0:T(8,128)} %get-tuple-element.73), channel_id=1, source_target_pairs={{0,12},{2,14},{4,0},{6,2},{8,4},{10,6},{12,8},{14,10},{16,28},{18,... | collective-permute-start | bytes 614408 | tf_op jit(solution)/shard_map/ppermute | solution.py:120
  124.5 11.0 %collective-permute-start.18 = (f32[2,40,640]{2,1,0:T(8,128)S(1)}, f32[2,40,640]{2,1,0:T(8,128)S(1)}, u32[]{:S(2)}, u32[]{:S(2)}) collective-permute-start(f32[2,40,640]{2,1,0:T(8,128)S(1)} %get-tuple-element.75), channel_id=1, source_target_pairs={{0,16},{2,18},{4,20},{6,22},{8,24},{10,26},{12,28},{14,30},{16,32}... | collective-permute-start | bytes 614408 | tf_op jit(solution)/shard_map/ppermute | solution.py:28
  126.4 10.2 %collective-permute-start.19 = (f32[2,40,640]{2,1,0:T(8,128)S(1)}, f32[2,40,640]{2,1,0:T(8,128)S(1)}, u32[]{:S(2)}, u32[]{:S(2)}) collective-permute-start(f32[2,40,640]{2,1,0:T(8,128)S(1)} %get-tuple-element.76), channel_id=1, source_target_pairs={{16,0},{18,2},{20,4},{22,6},{24,8},{26,10},{28,12},{30,14},{32,16}... | collective-permute-start | bytes 614408 | tf_op jit(solution)/shard_map/ppermute | solution.py:28
  142.7 11.4 %collective-permute-start.20 = (f32[2,48,640]{2,1,0:T(8,128)S(1)}, f32[2,48,640]{2,1,0:T(8,128)S(1)}, u32[]{:S(2)}, u32[]{:S(2)}) collective-permute-start(f32[2,48,640]{2,1,0:T(8,128)S(1)} %get-tuple-element.80), channel_id=1, source_target_pairs={{0,16},{2,18},{4,20},{6,22},{8,24},{10,26},{12,28},{14,30},{16,32}... | collective-permute-start | bytes 737288 | tf_op jit(solution)/shard_map/ppermute | solution.py:28
  144.6 10.7 %collective-permute-start.21 = (f32[2,48,640]{2,1,0:T(8,128)S(1)}, f32[2,48,640]{2,1,0:T(8,128)S(1)}, u32[]{:S(2)}, u32[]{:S(2)}) collective-permute-start(f32[2,48,640]{2,1,0:T(8,128)S(1)} %get-tuple-element.81), channel_id=1, source_target_pairs={{16,0},{18,2},{20,4},{22,6},{24,8},{26,10},{28,12},{30,14},{32,16}... | collective-permute-start | bytes 737288 | tf_op jit(solution)/shard_map/ppermute | solution.py:28
  159.1 8.5 %collective-permute-start.23 = (f32[4,8,640]{2,1,0:T(8,128)S(1)}, f32[4,8,640]{2,1,0:T(8,128)S(1)}, u32[]{:S(2)}, u32[]{:S(2)}) collective-permute-start(f32[4,8,640]{2,1,0:T(8,128)S(1)} %get-tuple-element.84), channel_id=1, source_target_pairs={{2,0},{4,2},{6,4},{8,6},{10,8},{12,10},{14,12},{1,14},{3,1},{5,3},... | collective-permute-start | bytes 245768 | tf_op jit(solution)/shard_map/ppermute | solution.py:38
  170.5 75.2 %all-to-all-start = ((f32[8,3,32,640]{3,2,1,0:T(8,128)}), f32[8,3,32,640]{3,2,1,0:T(8,128)}, u32[]{:S(2)}, u32[]{:S(2)}) async-start(f32[8,3,32,640]{3,2,1,0:T(8,128)} %copy-done.6), calls=%async_computation | async-start | bytes 3932160 | tf_op jit(solution)/shard_map/all_to_all | solution.py:47
  174.9 10.9 %collective-permute-start.24 = (f32[2,48,640]{2,1,0:T(8,128)}, f32[2,48,640]{2,1,0:T(8,128)S(1)}, u32[]{:S(2)}, u32[]{:S(2)}) collective-permute-start(f32[2,48,640]{2,1,0:T(8,128)} %copy-done.17), channel_id=1, source_target_pairs={{0,16},{2,18},{4,20},{6,22},{8,24},{10,26},{12,28},{14,30},{16,32}... | collective-permute-start | bytes 737288 | tf_op jit(solution)/shard_map/ppermute | solution.py:28
  178.8 8.5 %collective-permute-start.25 = (f32[2,48,640]{2,1,0:T(8,128)}, f32[2,48,640]{2,1,0:T(8,128)}, u32[]{:S(2)}, u32[]{:S(2)}) collective-permute-start(f32[2,48,640]{2,1,0:T(8,128)} %copy-done.16), channel_id=1, source_target_pairs={{16,0},{18,2},{20,4},{22,6},{24,8},{26,10},{28,12},{30,14},{32,16}... | collective-permute-start | bytes 737288 | tf_op jit(solution)/shard_map/ppermute | solution.py:28
  192.8 10.7 %collective-permute-start.26 = (f32[2,48,640]{2,1,0:T(8,128)S(1)}, f32[2,48,640]{2,1,0:T(8,128)S(1)}, u32[]{:S(2)}, u32[]{:S(2)}) collective-permute-start(f32[2,48,640]{2,1,0:T(8,128)S(1)} %get-tuple-element.94), channel_id=1, source_target_pairs={{0,16},{2,18},{4,20},{6,22},{8,24},{10,26},{12,28},{14,30},{16,32}... | collective-permute-start | bytes 737288 | tf_op jit(solution)/shard_map/ppermute | solution.py:28
  196.7 9.5 %collective-permute-start.27 = (f32[2,48,640]{2,1,0:T(8,128)S(1)}, f32[2,48,640]{2,1,0:T(8,128)S(1)}, u32[]{:S(2)}, u32[]{:S(2)}) collective-permute-start(f32[2,48,640]{2,1,0:T(8,128)S(1)} %get-tuple-element.95), channel_id=1, source_target_pairs={{16,0},{18,2},{20,4},{22,6},{24,8},{26,10},{28,12},{30,14},{32,16}... | collective-permute-start | bytes 737288 | tf_op jit(solution)/shard_map/ppermute | solution.py:28
  201.3 31.9 %collective-permute-start.33 = (f32[3,48,640]{2,1,0:T(8,128)S(1)}, f32[3,48,640]{2,1,0:T(8,128)S(1)}, u32[]{:S(2)}, u32[]{:S(2)}) collective-permute-start(f32[3,48,640]{2,1,0:T(8,128)S(1)} %pad_maximum_fusion), channel_id=1, source_target_pairs={{0,16},{2,18},{4,20},{6,22},{8,24},{10,26},{12,28},{14,30},{16,0},... | collective-permute-start | bytes 1105928 | tf_op jit(solution)/shard_map/ppermute | solution.py:43
  213.1 8.9 %collective-permute-start.28 = (f32[1,48,640]{2,1,0:T(8,128)S(1)}, f32[1,48,640]{2,1,0:T(8,128)S(1)}, u32[]{:S(2)}, u32[]{:S(2)}) collective-permute-start(f32[1,48,640]{2,1,0:T(8,128)S(1)} %get-tuple-element.97.refs_1_), channel_id=1, source_target_pairs={{0,16},{2,18},{4,20},{6,22},{8,24},{10,26},{12,28},{14,30},{16,32}... | collective-permute-start | bytes 368648 | tf_op jit(solution)/shard_map/ppermute | solution.py:28
  224.1 8.9 %collective-permute-start.30 = (f32[1,48,640]{2,1,0:T(8,128)S(1)}, f32[1,48,640]{2,1,0:T(8,128)S(1)}, u32[]{:S(2)}, u32[]{:S(2)}) collective-permute-start(f32[1,48,640]{2,1,0:T(8,128)S(1)} %get-tuple-element.99.refs_2_.refs_11_), channel_id=1, source_target_pairs={{0,16},{2,18},{4,20},{6,22},{8,24},{10,26},{12,28},{14,30},{16,32}... | collective-permute-start | bytes 368648 | tf_op jit(solution)/shard_map/ppermute | solution.py:28
  238.3 8.3 %collective-permute-start.35 = (f32[1,48,640]{2,1,0:T(8,128)S(1)}, f32[1,48,640]{2,1,0:T(8,128)S(1)}, u32[]{:S(2)}, u32[]{:S(2)}) collective-permute-start(f32[1,48,640]{2,1,0:T(8,128)S(1)} %get-tuple-element.105.refs_1_), channel_id=1, source_target_pairs={{32,0},{34,2},{36,4},{38,6},{40,8},{42,10},{44,12},{46,14},{48,16}... | collective-permute-start | bytes 368648 | tf_op jit(solution)/shard_map/ppermute | solution.py:28
  240.3 9.2 %collective-permute-start.34 = (f32[1,48,640]{2,1,0:T(8,128)S(1)}, f32[1,48,640]{2,1,0:T(8,128)S(1)}, u32[]{:S(2)}, u32[]{:S(2)}) collective-permute-start(f32[1,48,640]{2,1,0:T(8,128)S(1)} %get-tuple-element.105.refs_1_), channel_id=1, source_target_pairs={{0,32},{2,34},{4,36},{6,38},{8,40},{10,42},{12,44},{14,46},{16,48}... | collective-permute-start | bytes 368648 | tf_op jit(solution)/shard_map/ppermute | solution.py:28
  250.5 23.7 %all-to-all-start.1 = ((f32[8,32,640]{2,1,0:T(8,128)}), f32[8,32,640]{2,1,0:T(8,128)S(1)}, u32[]{:S(2)}, u32[]{:S(2)}) async-start(f32[8,32,640]{2,1,0:T(8,128)} %shard_map.73), calls=%async_computation.1 | async-start | bytes 1310720 | tf_op jit(solution)/shard_map/all_to_all | solution.py:47
  (24 other events, 139.7 us)

commit v5 on v4

--- a/solution.py
+++ b/solution.py
@@ -130,6 +130,7 @@
         out_shape=jax.ShapeDtypeStruct(value.shape, value.dtype),
         in_specs=[there] * (1 + len(settled)),
         out_specs=there,
+        compiler_params=pltpu.CompilerParams(vmem_limit_bytes=1024 * 1024),
         input_output_aliases={0: 0},
     )(value, *settled)
 
@@ -149,21 +150,20 @@
             outs[k][p] = full[p, pl.ds(start, strip + 2 * HALO)]
 
 
-def cut_source(place, source, top, bottom, *rest):
-    outs, full = rest[:-1], rest[-1]
+def cut_source(source, top, bottom, out):
     planes, rows, _ = source.shape
     strip = rows // RING
     for p in range(planes):
-        full[p, :HALO] = top[p]
-        full[p, HALO + rows:] = bottom[p]
-        full[p, HALO:HALO + rows] = source[p]
         for k in range(RING):
-            start = pl.multiple_of(((place[0] + k) % RING) * strip, strip)
-            outs[k][p] = full[p, pl.ds(start, strip + 2 * HALO)][HALO - THIN:HALO + strip + THIN]
+            start = k * strip
+            out[k, p, :THIN] = top[p, HALO - THIN:] if k == 0 else source[p, start - THIN:start]
+            out[k, p, THIN:THIN + strip] = source[p, start:start + strip]
+            out[k, p, THIN + strip:] = bottom[p, :THIN] if k == RING - 1 else source[p, start + strip:start + strip + THIN]
 
 
 def join(place, *refs):
-    out, low, high = refs[RING:]
+    out, low, high, ready = refs[RING:]
+    ready[...] = refs[0][0, :HALO]
     for k in range(RING):
         start = ((place[0] + RING - k) % RING) * 2
         out[start] = refs[k][0]
@@ -435,15 +435,10 @@
                 place, labels, fraction, c_top, c_bottom, limit=10)
     s_top, s_bottom = edges_of(right_side[:, :HALO], right_side[:, rows - HALO:])
     thin = strip + 2 * THIN
-    s_cuts = call(cut_source, [(planes, thin, columns)] * RING, [(planes, rows + 2 * HALO, columns)],
-                  place, right_side, s_top, s_bottom, limit=10)
+    (s_cut,) = call(cut_source, [(RING, planes, thin, columns)], [], right_side, s_top, s_bottom, limit=10)
     c_parts = [cuts[0]] + [ring_permuted(cuts[k], k) for k in range(1, RING)]
-    s_cuts = list(s_cuts)
-    for k in (1, RING - 1):
-        s_cuts[k] = after(s_cuts[k], c_parts[1], c_parts[2])
-    s_parts = [s_cuts[0]] + [ring_permuted(s_cuts[k], k) for k in range(1, RING)]
-
-    c, bundle_down, bundle_up = call(join, [shape(16), shape(REACH), shape(REACH)], [], place, *c_parts, limit=10, settled=(s_parts[1], s_parts[7]))
+    c, bundle_down, bundle_up, ready = call(join, [shape(16), shape(REACH), shape(REACH), (HALO, columns)], [], place, *c_parts, limit=10, settled=(s_cut,))
+    s_own = transposed(after(s_cut, ready))
     c_low, c_high = exchange(bundle_down, bundle_up)
     faces0, faces1, faces2, faces3, faces4 = call(
         make_faces, [shape(planes_of(n)) for n in (16, 8, 4, 2, 1)], [], c, c_low, c_high, limit=28, work=12.0)
@@ -453,9 +448,8 @@
     up5 = jnp.where(even_ring, other[2:], z_high)
     east5, north5, w5 = call(make_last_faces, [shape(1)] * 3, [], faces4, other, down5, up5)
 
-    s_own, edge_down, edge_up = call(
-        join, [(16, thin, columns), (2, thin, columns), (2, thin, columns)], [], place, *s_parts, limit=10, settled=(faces4,))
-    s_low, s_high = exchange(edge_down, edge_up)
+    s_own = after(s_own, faces4).reshape(RING * planes, thin, columns)
+    s_low, s_high = exchange(s_own[:2], s_own[-2:])
     fine, s1, edge_down, edge_up = call(
         fine_level, [(RING, planes, strip, columns), shape(8), shape(2), shape(2)],
         [shape(18), shape(20), shape(16), shape(18)],

time: 276 us -> 281 us (1.018)
  local copies, waits for them, and re-layouts: 18.9 us -> 32.8 us
  starting transfers between devices: 120 us -> 110 us
    ppermute x14 -> x7, starting transfers between devices: 42.8 us -> 23 us  [ring_permuted(): lax.ppermute(value, 'gz', [(i, i // RING * RING + (i + by) % RING) for i...]
    ppermute x16, waiting for transfers between devices: 43.7 us -> 57.7 us  [shifted(): return lax.ppermute(value, 'gz', pairs)]
    unnamed x37 -> x39, local copies, waits for them, and re-layouts: 13.6 us -> 26.4 us
    ppermute x14 -> x7, waiting for transfers between devices: 41.9 us -> 30.3 us  [ring_permuted(): lax.ppermute(value, 'gz', [(i, i // RING * RING + (i + by) % RING) for i...]
    all_to_all x2 -> x3, starting transfers between devices: 13.3 us -> 18.1 us  [transposed(): lax.all_to_all(value, 'gz', 0, 0, axis_index_groups=ring_groups(lax.axis_...]
    ppermute x2, starting transfers between devices: 2.59 us -> 5.61 us  [row_shifted(): return lax.ppermute(value, ('gz', 'xy'), pairs)]
    pallas_call x14 -> x13, Pallas kernels: 24.4 us -> 24.8 us  [call(): pl.pallas_call(body, out_shape=shapes, in_specs=[pl.BlockSpec(memory_spac...]
    all_to_all x2 -> x3, waiting for transfers between devices: 10.1 us -> 10.1 us  [transposed(): lax.all_to_all(value, 'gz', 0, 0, axis_index_groups=ring_groups(lax.axis_...]
  transfers between devices with their start and end apart: 38 -> 32, of which waited for: 27 -> 25; matrix products, arithmetic and copies ran while one was open for 2% -> 2% of each run, Pallas kernels for 5% -> 5%
where the time goes in v5:
time: 281 us; the launch traced here: 279 us
  starting transfers between devices  110 us (39%)
  waiting for transfers between devices  110 us (39%)
  local copies, waits for them, and re-layouts  32.8 us (12%)
  Pallas kernels  24.8 us (9%)
    ppermute x16, starting transfers between devices, shifted(): return lax.ppermute(value, 'gz', pairs)  62.8 us
    ppermute x16, waiting for transfers between devices, shifted(): return lax.ppermute(value, 'gz', pairs)  57.7 us
    ppermute x7, waiting for transfers between devices, ring_permuted(): lax.ppermute(value, 'gz', [(i, i // RING * RING + (i + by) % RING) for i...  30.3 us
    unnamed x39, local copies, waits for them, and re-layouts  26.4 us
    pallas_call x13, Pallas kernels, call(): pl.pallas_call(body, out_shape=shapes, in_specs=[pl.BlockSpec(memory_spac...  24.8 us
    ppermute x7, starting transfers between devices, ring_permuted(): lax.ppermute(value, 'gz', [(i, i // RING * RING + (i + by) % RING) for i...  23 us
    all_to_all x3, starting transfers between devices, transposed(): lax.all_to_all(value, 'gz', 0, 0, axis_index_groups=ring_groups(lax.axis_...  18.1 us
    all_to_all x3, waiting for transfers between devices, transposed(): lax.all_to_all(value, 'gz', 0, 0, axis_index_groups=ring_groups(lax.axis_...  10.1 us
  transfers between devices with their start and end apart: 32, of which 25 were waited for; matrix products, arithmetic and copies ran while one was open for 2% of the time, Pallas kernels for 5%

profile of v5, /device:TPU:8, one launch (start us, length us, event | category | flops | bytes accessed | tf_op | source)
XLA Modules:
  0.0 279.3 jit_solution(17099382221033115280)
XLA Ops:
  7.9 3.3 %collective-permute-start.3 = (f32[2,48,640]{2,1,0:T(8,128)S(1)}, f32[2,48,640]{2,1,0:T(8,128)S(1)}, u32[]{:S(2)}, u32[]{:S(2)}) collective-permute-start(f32[2,48,640]{2,1,0:T(8,128)S(1)} %get-tuple-element.46), channel_id=1, source_target_pairs={{0,4},{2,6},{4,8},{6,10},{8,12},{10,14},{12,0},{14,2},{16,20},{18,... | collective-permute-start | bytes 737288 | tf_op jit(solution)/shard_map/ppermute | solution.py:120
  11.2 4.1 %collective-permute-start.4 = (f32[2,48,640]{2,1,0:T(8,128)S(1)}, f32[2,48,640]{2,1,0:T(8,128)S(1)}, u32[]{:S(2)}, u32[]{:S(2)}) collective-permute-start(f32[2,48,640]{2,1,0:T(8,128)S(1)} %get-tuple-element.47), channel_id=1, source_target_pairs={{0,6},{2,8},{4,10},{6,12},{8,14},{10,0},{12,2},{14,4},{16,22},{18,... | collective-permute-start | bytes 737288 | tf_op jit(solution)/shard_map/ppermute | solution.py:120
  16.1 4.8 %collective-permute-start.6 = (f32[2,48,640]{2,1,0:T(8,128)S(1)}, f32[2,48,640]{2,1,0:T(8,128)S(1)}, u32[]{:S(2)}, u32[]{:S(2)}) collective-permute-start(f32[2,48,640]{2,1,0:T(8,128)S(1)} %get-tuple-element.49), channel_id=1, source_target_pairs={{0,10},{2,12},{4,14},{6,0},{8,2},{10,4},{12,6},{14,8},{16,26},{18,... | collective-permute-start | bytes 737288 | tf_op jit(solution)/shard_map/ppermute | solution.py:120
  20.9 5.3 %collective-permute-start.7 = (f32[2,48,640]{2,1,0:T(8,128)S(1)}, f32[2,48,640]{2,1,0:T(8,128)S(1)}, u32[]{:S(2)}, u32[]{:S(2)}) collective-permute-start(f32[2,48,640]{2,1,0:T(8,128)S(1)} %get-tuple-element.50), channel_id=1, source_target_pairs={{0,12},{2,14},{4,0},{6,2},{8,4},{10,6},{12,8},{14,10},{16,28},{18,... | collective-permute-start | bytes 737288 | tf_op jit(solution)/shard_map/ppermute | solution.py:120
  26.2 5.5 %collective-permute-done.3.refs_4_ = f32[2,48,640]{2,1,0:T(8,128)S(1)} collective-permute-done((f32[2,48,640]{2,1,0:T(8,128)S(1)}, f32[2,48,640]{2,1,0:T(8,128)S(1)}, u32[]{:S(2)}, u32[]{:S(2)}) %collective-permute-start.3) | collective-permute-done | bytes 245792 | tf_op jit(solution)/shard_map/ppermute | solution.py:120
  36.0 13.9 %collective-permute-done.4.refs_5_ = f32[2,48,640]{2,1,0:T(8,128)S(1)} collective-permute-done((f32[2,48,640]{2,1,0:T(8,128)S(1)}, f32[2,48,640]{2,1,0:T(8,128)S(1)}, u32[]{:S(2)}, u32[]{:S(2)}) %collective-permute-start.4) | collective-permute-done | bytes 245792 | tf_op jit(solution)/shard_map/ppermute | solution.py:120
  49.8 8.5 %collective-permute-done.7.refs_8_ = f32[2,48,640]{2,1,0:T(8,128)S(1)} collective-permute-done((f32[2,48,640]{2,1,0:T(8,128)S(1)}, f32[2,48,640]{2,1,0:T(8,128)S(1)}, u32[]{:S(2)}, u32[]{:S(2)}) %collective-permute-start.7) | collective-permute-done | bytes 245792 | tf_op jit(solution)/shard_map/ppermute | solution.py:120
  62.4 5.2 %all-to-all-start = ((f32[8,2,40,640]{3,2,1,0:T(8,128)}), f32[8,2,40,640]{3,2,1,0:T(8,128)}, u32[]{:S(2)}, u32[]{:S(2)}) async-start(f32[8,2,40,640]{3,2,1,0:T(8,128)} %shard_map.61), calls=%async_computation | async-start | bytes 3276800 | tf_op jit(solution)/shard_map/all_to_all | solution.py:47
  67.6 3.4 %collective-permute-start.9 = (f32[9,48,640]{2,1,0:T(8,128)S(1)}, f32[9,48,640]{2,1,0:T(8,128)S(1)}, u32[]{:S(2)}, u32[]{:S(2)}) collective-permute-start(f32[9,48,640]{2,1,0:T(8,128)S(1)} %get-tuple-element.54), channel_id=1, source_target_pairs={{0,16},{2,18},{4,20},{6,22},{8,24},{10,26},{12,28},{14,30},{16,32}... | collective-permute-start | bytes 3317768 | tf_op jit(solution)/shard_map/ppermute | solution.py:28
  71.0 4.6 %collective-permute-start.10 = (f32[9,48,640]{2,1,0:T(8,128)S(1)}, f32[9,48,640]{2,1,0:T(8,128)S(1)}, u32[]{:S(2)}, u32[]{:S(2)}) collective-permute-start(f32[9,48,640]{2,1,0:T(8,128)S(1)} %get-tuple-element.55), channel_id=1, source_target_pairs={{16,0},{18,2},{20,4},{22,6},{24,8},{26,10},{28,12},{30,14},{32,16}... | collective-permute-start | bytes 3317768 | tf_op jit(solution)/shard_map/ppermute | solution.py:28
  75.5 22.1 %collective-permute-done.9.refs_1_ = f32[9,48,640]{2,1,0:T(8,128)S(1)} collective-permute-done((f32[9,48,640]{2,1,0:T(8,128)S(1)}, f32[9,48,640]{2,1,0:T(8,128)S(1)}, u32[]{:S(2)}, u32[]{:S(2)}) %collective-permute-start.9) | collective-permute-done | bytes 1105952 | tf_op jit(solution)/shard_map/ppermute | solution.py:28
  100.3 7.9 %shard_map.62 = (f32[75,48,640]{2,1,0:T(8,128)S(1)}, f32[41,48,640]{2,1,0:T(8,128)S(1)}, f32[25,48,640]{2,1,0:T(8,128)S(1)}, f32[17,48,640]{2,1,0:T(8,128)S(1)}, f32[5,48,640]{2,1,0:T(8,128)S(1)}) custom-call(f32[16,48,640]{2,1,0:T(8,128)S(1)} %copy-done.12, f32[9,48,640]{2,1,0:T(8,128)S(1)} %collective-permute-done.9.refs_1_, ...), custom_call_target="tpu_custom_call" | custom-call | flops 12000000000 | bytes 36000000 | tf_op jit(solution)/shard_map/pallas_call | solution.py:107
  112.0 3.5 %copy-done.17 = f32[75,48,640]{2,1,0:T(8,128)} copy-done((f32[75,48,640]{2,1,0:T(8,128)}, f32[75,48,640]{2,1,0:T(8,128)S(1)}, u32[]{:S(2)}) %copy-start.17) | copy-done | bytes 9216024
  116.6 6.5 %collective-permute-start.12 = (f32[2,40,640]{2,1,0:T(8,128)S(1)}, f32[2,40,640]{2,1,0:T(8,128)S(1)}, u32[]{:S(2)}, u32[]{:S(2)}) collective-permute-start(f32[2,40,640]{2,1,0:T(8,128)S(1)} %get-tuple-element.87), channel_id=1, source_target_pairs={{16,0},{18,2},{20,4},{22,6},{24,8},{26,10},{28,12},{30,14},{32,16}... | collective-permute-start | bytes 614408 | tf_op jit(solution)/shard_map/ppermute | solution.py:28
  126.3 6.5 %collective-permute-done.11.refs_1_ = f32[2,40,640]{2,1,0:T(8,128)S(1)} collective-permute-done((f32[2,40,640]{2,1,0:T(8,128)S(1)}, f32[2,40,640]{2,1,0:T(8,128)S(1)}, u32[]{:S(2)}, u32[]{:S(2)}) %collective-permute-start.11) | collective-permute-done | bytes 204832 | tf_op jit(solution)/shard_map/ppermute | solution.py:28
  135.3 3.6 %copy-done.18 = f32[75,48,640]{2,1,0:T(8,128)S(1)} copy-done((f32[75,48,640]{2,1,0:T(8,128)S(1)}, f32[75,48,640]{2,1,0:T(8,128)}, u32[]{:S(2)}) %copy-start.18) | copy-done | bytes 9216024
  138.9 6.8 %shard_map.64 = (f32[8,2,32,640]{3,2,1,0:T(8,128)S(1)}, f32[8,48,640]{2,1,0:T(8,128)S(1)}, f32[2,48,640]{2,1,0:T(8,128)S(1)}, f32[2,48,640]{2,1,0:T(8,128)S(1)}) custom-call(f32[16,40,640]{2,1,0:T(8,128)} %bitcast.1.refs_0_, f32[2,40,640]{2,1,0:T(8,128)S(1)} %collective-permute-done.11.refs_1_, f32[2,40,640]{2,1,0:T(8,128)S(1)} %collective-permute-done.12.refs_2_, ...), custom_call_target="tpu_custom_call" | custom-call | flops 8000000000 | bytes 24000000 | tf_op jit(solution)/shard_map/pallas_call | solution.py:107
  147.6 6.2 %collective-permute-start.14 = (f32[2,48,640]{2,1,0:T(8,128)S(1)}, f32[2,48,640]{2,1,0:T(8,128)S(1)}, u32[]{:S(2)}, u32[]{:S(2)}) collective-permute-start(f32[2,48,640]{2,1,0:T(8,128)S(1)} %get-tuple-element.61), channel_id=1, source_target_pairs={{16,0},{18,2},{20,4},{22,6},{24,8},{26,10},{28,12},{30,14},{32,16}... | collective-permute-start | bytes 737288 | tf_op jit(solution)/shard_map/ppermute | solution.py:28
  160.1 4.3 %collective-permute-start.15 = (f32[4,8,640]{2,1,0:T(8,128)S(1)}, f32[4,8,640]{2,1,0:T(8,128)S(1)}, u32[]{:S(2)}, u32[]{:S(2)}) collective-permute-start(f32[4,8,640]{2,1,0:T(8,128)S(1)} %get-tuple-element.63), channel_id=1, source_target_pairs={{0,2},{2,4},{4,6},{6,8},{8,10},{10,12},{12,14},{14,1},{1,3},{3,5},... | collective-permute-start | bytes 245768 | tf_op jit(solution)/shard_map/ppermute | solution.py:38
  166.5 4.3 %collective-permute-done.16.refs_2_ = f32[4,8,640]{2,1,0:T(8,128)S(1)} collective-permute-done((f32[4,8,640]{2,1,0:T(8,128)S(1)}, f32[4,8,640]{2,1,0:T(8,128)S(1)}, u32[]{:S(2)}, u32[]{:S(2)}) %collective-permute-start.16) | collective-permute-done | bytes 81952 | tf_op jit(solution)/shard_map/ppermute | solution.py:38
  173.6 6.3 %all-to-all-start.1 = ((f32[8,3,32,640]{3,2,1,0:T(8,128)}), f32[8,3,32,640]{3,2,1,0:T(8,128)}, u32[]{:S(2)}, u32[]{:S(2)}) async-start(f32[8,3,32,640]{3,2,1,0:T(8,128)} %copy-done.3), calls=%async_computation.1 | async-start | bytes 3932160 | tf_op jit(solution)/shard_map/all_to_all | solution.py:47
  181.8 6.5 %collective-permute-start.18 = (f32[2,48,640]{2,1,0:T(8,128)}, f32[2,48,640]{2,1,0:T(8,128)}, u32[]{:S(2)}, u32[]{:S(2)}) collective-permute-start(f32[2,48,640]{2,1,0:T(8,128)} %copy-done.13), channel_id=1, source_target_pairs={{16,0},{18,2},{20,4},{22,6},{24,8},{26,10},{28,12},{30,14},{32,16}... | collective-permute-start | bytes 737288 | tf_op jit(solution)/shard_map/ppermute | solution.py:28
  197.8 3.9 %collective-permute-start.19 = (f32[2,48,640]{2,1,0:T(8,128)S(1)}, f32[2,48,640]{2,1,0:T(8,128)S(1)}, u32[]{:S(2)}, u32[]{:S(2)}) collective-permute-start(f32[2,48,640]{2,1,0:T(8,128)S(1)} %get-tuple-element.74), channel_id=1, source_target_pairs={{0,16},{2,18},{4,20},{6,22},{8,24},{10,26},{12,28},{14,30},{16,32}... | collective-permute-start | bytes 737288 | tf_op jit(solution)/shard_map/ppermute | solution.py:28
  201.7 4.5 %collective-permute-start.20 = (f32[2,48,640]{2,1,0:T(8,128)S(1)}, f32[2,48,640]{2,1,0:T(8,128)S(1)}, u32[]{:S(2)}, u32[]{:S(2)}) collective-permute-start(f32[2,48,640]{2,1,0:T(8,128)S(1)} %get-tuple-element.75), channel_id=1, source_target_pairs={{16,0},{18,2},{20,4},{22,6},{24,8},{26,10},{28,12},{30,14},{32,16}... | collective-permute-start | bytes 737288 | tf_op jit(solution)/shard_map/ppermute | solution.py:28
  211.7 6.4 %collective-permute-start.22 = (f32[1,48,640]{2,1,0:T(8,128)S(1)}, f32[1,48,640]{2,1,0:T(8,128)S(1)}, u32[]{:S(2)}, u32[]{:S(2)}) collective-permute-start(f32[1,48,640]{2,1,0:T(8,128)S(1)} %get-tuple-element.77.refs_1_), channel_id=1, source_target_pairs={{16,0},{18,2},{20,4},{22,6},{24,8},{26,10},{28,12},{30,14},{32,16}... | collective-permute-start | bytes 368648 | tf_op jit(solution)/shard_map/ppermute | solution.py:28
  220.5 6.5 %collective-permute-done.21.refs_2_ = f32[1,48,640]{2,1,0:T(8,128)S(1)} collective-permute-done((f32[1,48,640]{2,1,0:T(8,128)S(1)}, f32[1,48,640]{2,1,0:T(8,128)S(1)}, u32[]{:S(2)}, u32[]{:S(2)}) %collective-permute-start.21) | collective-permute-done | bytes 122912 | tf_op jit(solution)/shard_map/ppermute | solution.py:28
  229.1 3.9 %collective-permute-start.23 = (f32[1,48,640]{2,1,0:T(8,128)S(1)}, f32[1,48,640]{2,1,0:T(8,128)S(1)}, u32[]{:S(2)}, u32[]{:S(2)}) collective-permute-start(f32[1,48,640]{2,1,0:T(8,128)S(1)} %get-tuple-element.79.refs_2_.refs_11_), channel_id=1, source_target_pairs={{0,16},{2,18},{4,20},{6,22},{8,24},{10,26},{12,28},{14,30},{16,32}... | collective-permute-start | bytes 368648 | tf_op jit(solution)/shard_map/ppermute | solution.py:28
  235.1 4.1 %collective-permute-done.23.refs_3_ = f32[1,48,640]{2,1,0:T(8,128)S(1)} collective-permute-done((f32[1,48,640]{2,1,0:T(8,128)S(1)}, f32[1,48,640]{2,1,0:T(8,128)S(1)}, u32[]{:S(2)}, u32[]{:S(2)}) %collective-permute-start.23) | collective-permute-done | bytes 122912 | tf_op jit(solution)/shard_map/ppermute | solution.py:28
  239.7 5.2 %collective-permute-done.25 = f32[1,48,640]{2,1,0:T(8,128)S(1)} collective-permute-done((f32[1,48,640]{2,1,0:T(8,128)S(1)}, f32[1,48,640]{2,1,0:T(8,128)S(1)}, u32[]{:S(2)}, u32[]{:S(2)}) %collective-permute-start.25) | collective-permute-done | bytes 122912 | tf_op jit(solution)/shard_map/ppermute | solution.py:43
  246.9 5.4 %collective-permute-start.27 = (f32[1,48,640]{2,1,0:T(8,128)S(1)}, f32[1,48,640]{2,1,0:T(8,128)S(1)}, u32[]{:S(2)}, u32[]{:S(2)}) collective-permute-start(f32[1,48,640]{2,1,0:T(8,128)S(1)} %get-tuple-element.85.refs_1_), channel_id=1, source_target_pairs={{0,32},{2,34},{4,36},{6,38},{8,40},{10,42},{12,44},{14,46},{16,48}... | collective-permute-start | bytes 368648 | tf_op jit(solution)/shard_map/ppermute | solution.py:28
  257.1 6.7 %all-to-all-start.2 = ((f32[8,32,640]{2,1,0:T(8,128)}), f32[8,32,640]{2,1,0:T(8,128)S(1)}, u32[]{:S(2)}, u32[]{:S(2)}) async-start(f32[8,32,640]{2,1,0:T(8,128)} %shard_map.72), calls=%async_computation.2 | async-start | bytes 1310720 | tf_op jit(solution)/shard_map/all_to_all | solution.py:47
  268.4 10.1 %all-to-all-done.2 = f32[8,32,640]{2,1,0:T(8,128)S(1)} async-done(((f32[8,32,640]{2,1,0:T(8,128)}), f32[8,32,640]{2,1,0:T(8,128)S(1)}, u32[]{:S(2)}, u32[]{:S(2)}) %all-to-all-start.2) | async-done | bytes 655392 | tf_op jit(solution)/shard_map/all_to_all | solution.py:47
  (100 shorter events, 78.6 us)
Async XLA Ops:
  1.5 1.3 collective-permute-start.1
  5.9 15.0 %collective-permute-start.2 = (f32[2,48,640]{2,1,0:T(8,128)S(1)}, f32[2,48,640]{2,1,0:T(8,128)S(1)}, u32[]{:S(2)}, u32[]{:S(2)}) collective-permute-start(f32[2,48,640]{2,1,0:T(8,128)S(1)} %get-tuple-element.45), channel_id=1, source_target_pairs={{0,2},{2,4},{4,6},{6,8},{8,10},{10,12},{12,14},{14,0},{16,18},{18,... | collective-permute-start | bytes 737288 | tf_op jit(solution)/shard_map/ppermute | solution.py:120
  7.9 23.9 %collective-permute-start.3 = (f32[2,48,640]{2,1,0:T(8,128)S(1)}, f32[2,48,640]{2,1,0:T(8,128)S(1)}, u32[]{:S(2)}, u32[]{:S(2)}) collective-permute-start(f32[2,48,640]{2,1,0:T(8,128)S(1)} %get-tuple-element.46), channel_id=1, source_target_pairs={{0,4},{2,6},{4,8},{6,10},{8,12},{10,14},{12,0},{14,2},{16,20},{18,... | collective-permute-start | bytes 737288 | tf_op jit(solution)/shard_map/ppermute | solution.py:120
  11.1 4.9 %collective-permute-start = (f32[2,8,640]{2,1,0:T(8,128)S(1)}, f32[2,8,640]{2,1,0:T(8,128)S(1)}, u32[]{:S(2)}, u32[]{:S(2)}) collective-permute-start(f32[2,8,640]{2,1,0:T(8,128)S(1)} %slice_select_fusion.3), channel_id=1, source_target_pairs={{0,1},{1,0},{2,3},{3,2},{4,5},{5,4},{6,7},{7,6},{8,9},{9,8},{10,11... | collective-permute-start | bytes 122888 | tf_op jit(solution)/shard_map/ppermute | solution.py:425
  11.2 38.6 %collective-permute-start.4 = (f32[2,48,640]{2,1,0:T(8,128)S(1)}, f32[2,48,640]{2,1,0:T(8,128)S(1)}, u32[]{:S(2)}, u32[]{:S(2)}) collective-permute-start(f32[2,48,640]{2,1,0:T(8,128)S(1)} %get-tuple-element.47), channel_id=1, source_target_pairs={{0,6},{2,8},{4,10},{6,12},{8,14},{10,0},{12,2},{14,4},{16,22},{18,... | collective-permute-start | bytes 737288 | tf_op jit(solution)/shard_map/ppermute | solution.py:120
  15.4 34.5 %collective-permute-start.5 = (f32[2,48,640]{2,1,0:T(8,128)S(1)}, f32[2,48,640]{2,1,0:T(8,128)S(1)}, u32[]{:S(2)}, u32[]{:S(2)}) collective-permute-start(f32[2,48,640]{2,1,0:T(8,128)S(1)} %get-tuple-element.48), channel_id=1, source_target_pairs={{0,8},{2,10},{4,12},{6,14},{8,0},{10,2},{12,4},{14,6},{16,24},{18,... | collective-permute-start | bytes 737288 | tf_op jit(solution)/shard_map/ppermute | solution.py:120
  16.1 33.8 %collective-permute-start.6 = (f32[2,48,640]{2,1,0:T(8,128)S(1)}, f32[2,48,640]{2,1,0:T(8,128)S(1)}, u32[]{:S(2)}, u32[]{:S(2)}) collective-permute-start(f32[2,48,640]{2,1,0:T(8,128)S(1)} %get-tuple-element.49), channel_id=1, source_target_pairs={{0,10},{2,12},{4,14},{6,0},{8,2},{10,4},{12,6},{14,8},{16,26},{18,... | collective-permute-start | bytes 737288 | tf_op jit(solution)/shard_map/ppermute | solution.py:120
  20.9 37.5 %collective-permute-start.7 = (f32[2,48,640]{2,1,0:T(8,128)S(1)}, f32[2,48,640]{2,1,0:T(8,128)S(1)}, u32[]{:S(2)}, u32[]{:S(2)}) collective-permute-start(f32[2,48,640]{2,1,0:T(8,128)S(1)} %get-tuple-element.50), channel_id=1, source_target_pairs={{0,12},{2,14},{4,0},{6,2},{8,4},{10,6},{12,8},{14,10},{16,28},{18,... | collective-permute-start | bytes 737288 | tf_op jit(solution)/shard_map/ppermute | solution.py:120
  31.7 29.0 %collective-permute-start.8 = (f32[2,48,640]{2,1,0:T(8,128)S(1)}, f32[2,48,640]{2,1,0:T(8,128)S(1)}, u32[]{:S(2)}, u32[]{:S(2)}) collective-permute-start(f32[2,48,640]{2,1,0:T(8,128)S(1)} %get-tuple-element.51), channel_id=1, source_target_pairs={{0,14},{2,0},{4,2},{6,4},{8,6},{10,8},{12,10},{14,12},{16,30},{18,... | collective-permute-start | bytes 737288 | tf_op jit(solution)/shard_map/ppermute | solution.py:120
  62.4 53.1 %all-to-all-start = ((f32[8,2,40,640]{3,2,1,0:T(8,128)}), f32[8,2,40,640]{3,2,1,0:T(8,128)}, u32[]{:S(2)}, u32[]{:S(2)}) async-start(f32[8,2,40,640]{3,2,1,0:T(8,128)} %shard_map.61), calls=%async_computation | async-start | bytes 3276800 | tf_op jit(solution)/shard_map/all_to_all | solution.py:47
  67.6 30.0 %collective-permute-start.9 = (f32[9,48,640]{2,1,0:T(8,128)S(1)}, f32[9,48,640]{2,1,0:T(8,128)S(1)}, u32[]{:S(2)}, u32[]{:S(2)}) collective-permute-start(f32[9,48,640]{2,1,0:T(8,128)S(1)} %get-tuple-element.54), channel_id=1, source_target_pairs={{0,16},{2,18},{4,20},{6,22},{8,24},{10,26},{12,28},{14,30},{16,32}... | collective-permute-start | bytes 3317768 | tf_op jit(solution)/shard_map/ppermute | solution.py:28
  71.0 27.8 %collective-permute-start.10 = (f32[9,48,640]{2,1,0:T(8,128)S(1)}, f32[9,48,640]{2,1,0:T(8,128)S(1)}, u32[]{:S(2)}, u32[]{:S(2)}) collective-permute-start(f32[9,48,640]{2,1,0:T(8,128)S(1)} %get-tuple-element.55), channel_id=1, source_target_pairs={{16,0},{18,2},{20,4},{22,6},{24,8},{26,10},{28,12},{30,14},{32,16}... | collective-permute-start | bytes 3317768 | tf_op jit(solution)/shard_map/ppermute | solution.py:28
  116.6 9.8 %collective-permute-start.12 = (f32[2,40,640]{2,1,0:T(8,128)S(1)}, f32[2,40,640]{2,1,0:T(8,128)S(1)}, u32[]{:S(2)}, u32[]{:S(2)}) collective-permute-start(f32[2,40,640]{2,1,0:T(8,128)S(1)} %get-tuple-element.87), channel_id=1, source_target_pairs={{16,0},{18,2},{20,4},{22,6},{24,8},{26,10},{28,12},{30,14},{32,16}... | collective-permute-start | bytes 614408 | tf_op jit(solution)/shard_map/ppermute | solution.py:28
  123.1 9.8 %collective-permute-start.11 = (f32[2,40,640]{2,1,0:T(8,128)S(1)}, f32[2,40,640]{2,1,0:T(8,128)S(1)}, u32[]{:S(2)}, u32[]{:S(2)}) collective-permute-start(f32[2,40,640]{2,1,0:T(8,128)S(1)} %get-tuple-element.88), channel_id=1, source_target_pairs={{0,16},{2,18},{4,20},{6,22},{8,24},{10,26},{12,28},{14,30},{16,32}... | collective-permute-start | bytes 614408 | tf_op jit(solution)/shard_map/ppermute | solution.py:28
  145.7 10.2 %collective-permute-start.13 = (f32[2,48,640]{2,1,0:T(8,128)S(1)}, f32[2,48,640]{2,1,0:T(8,128)S(1)}, u32[]{:S(2)}, u32[]{:S(2)}) collective-permute-start(f32[2,48,640]{2,1,0:T(8,128)S(1)} %get-tuple-element.60), channel_id=1, source_target_pairs={{0,16},{2,18},{4,20},{6,22},{8,24},{10,26},{12,28},{14,30},{16,32}... | collective-permute-start | bytes 737288 | tf_op jit(solution)/shard_map/ppermute | solution.py:28
  147.6 9.7 %collective-permute-start.14 = (f32[2,48,640]{2,1,0:T(8,128)S(1)}, f32[2,48,640]{2,1,0:T(8,128)S(1)}, u32[]{:S(2)}, u32[]{:S(2)}) collective-permute-start(f32[2,48,640]{2,1,0:T(8,128)S(1)} %get-tuple-element.61), channel_id=1, source_target_pairs={{16,0},{18,2},{20,4},{22,6},{24,8},{26,10},{28,12},{30,14},{32,16}... | collective-permute-start | bytes 737288 | tf_op jit(solution)/shard_map/ppermute | solution.py:28
  160.1 6.4 %collective-permute-start.15 = (f32[4,8,640]{2,1,0:T(8,128)S(1)}, f32[4,8,640]{2,1,0:T(8,128)S(1)}, u32[]{:S(2)}, u32[]{:S(2)}) collective-permute-start(f32[4,8,640]{2,1,0:T(8,128)S(1)} %get-tuple-element.63), channel_id=1, source_target_pairs={{0,2},{2,4},{4,6},{6,8},{8,10},{10,12},{12,14},{14,1},{1,3},{3,5},... | collective-permute-start | bytes 245768 | tf_op jit(solution)/shard_map/ppermute | solution.py:38
  164.4 6.3 %collective-permute-start.16 = (f32[4,8,640]{2,1,0:T(8,128)S(1)}, f32[4,8,640]{2,1,0:T(8,128)S(1)}, u32[]{:S(2)}, u32[]{:S(2)}) collective-permute-start(f32[4,8,640]{2,1,0:T(8,128)S(1)} %get-tuple-element.64), channel_id=1, source_target_pairs={{2,0},{4,2},{6,4},{8,6},{10,8},{12,10},{14,12},{1,14},{3,1},{5,3},... | collective-permute-start | bytes 245768 | tf_op jit(solution)/shard_map/ppermute | solution.py:38
  173.6 78.8 %all-to-all-start.1 = ((f32[8,3,32,640]{3,2,1,0:T(8,128)}), f32[8,3,32,640]{3,2,1,0:T(8,128)}, u32[]{:S(2)}, u32[]{:S(2)}) async-start(f32[8,3,32,640]{3,2,1,0:T(8,128)} %copy-done.3), calls=%async_computation.1 | async-start | bytes 3932160 | tf_op jit(solution)/shard_map/all_to_all | solution.py:47
  179.9 10.9 %collective-permute-start.17 = (f32[2,48,640]{2,1,0:T(8,128)}, f32[2,48,640]{2,1,0:T(8,128)S(1)}, u32[]{:S(2)}, u32[]{:S(2)}) collective-permute-start(f32[2,48,640]{2,1,0:T(8,128)} %copy-done.14), channel_id=1, source_target_pairs={{0,16},{2,18},{4,20},{6,22},{8,24},{10,26},{12,28},{14,30},{16,32}... | collective-permute-start | bytes 737288 | tf_op jit(solution)/shard_map/ppermute | solution.py:28
  181.8 10.5 %collective-permute-start.18 = (f32[2,48,640]{2,1,0:T(8,128)}, f32[2,48,640]{2,1,0:T(8,128)}, u32[]{:S(2)}, u32[]{:S(2)}) collective-permute-start(f32[2,48,640]{2,1,0:T(8,128)} %copy-done.13), channel_id=1, source_target_pairs={{16,0},{18,2},{20,4},{22,6},{24,8},{26,10},{28,12},{30,14},{32,16}... | collective-permute-start | bytes 737288 | tf_op jit(solution)/shard_map/ppermute | solution.py:28
  197.8 10.7 %collective-permute-start.19 = (f32[2,48,640]{2,1,0:T(8,128)S(1)}, f32[2,48,640]{2,1,0:T(8,128)S(1)}, u32[]{:S(2)}, u32[]{:S(2)}) collective-permute-start(f32[2,48,640]{2,1,0:T(8,128)S(1)} %get-tuple-element.74), channel_id=1, source_target_pairs={{0,16},{2,18},{4,20},{6,22},{8,24},{10,26},{12,28},{14,30},{16,32}... | collective-permute-start | bytes 737288 | tf_op jit(solution)/shard_map/ppermute | solution.py:28
  201.7 8.3 %collective-permute-start.20 = (f32[2,48,640]{2,1,0:T(8,128)S(1)}, f32[2,48,640]{2,1,0:T(8,128)S(1)}, u32[]{:S(2)}, u32[]{:S(2)}) collective-permute-start(f32[2,48,640]{2,1,0:T(8,128)S(1)} %get-tuple-element.75), channel_id=1, source_target_pairs={{16,0},{18,2},{20,4},{22,6},{24,8},{26,10},{28,12},{30,14},{32,16}... | collective-permute-start | bytes 737288 | tf_op jit(solution)/shard_map/ppermute | solution.py:28
  206.3 33.2 %collective-permute-start.26 = (f32[3,48,640]{2,1,0:T(8,128)S(1)}, f32[3,48,640]{2,1,0:T(8,128)S(1)}, u32[]{:S(2)}, u32[]{:S(2)}) collective-permute-start(f32[3,48,640]{2,1,0:T(8,128)S(1)} %pad_maximum_fusion), channel_id=1, source_target_pairs={{0,16},{2,18},{4,20},{6,22},{8,24},{10,26},{12,28},{14,30},{16,0},... | collective-permute-start | bytes 1105928 | tf_op jit(solution)/shard_map/ppermute | solution.py:43
  211.7 8.8 %collective-permute-start.22 = (f32[1,48,640]{2,1,0:T(8,128)S(1)}, f32[1,48,640]{2,1,0:T(8,128)S(1)}, u32[]{:S(2)}, u32[]{:S(2)}) collective-permute-start(f32[1,48,640]{2,1,0:T(8,128)S(1)} %get-tuple-element.77.refs_1_), channel_id=1, source_target_pairs={{16,0},{18,2},{20,4},{22,6},{24,8},{26,10},{28,12},{30,14},{32,16}... | collective-permute-start | bytes 368648 | tf_op jit(solution)/shard_map/ppermute | solution.py:28
  218.1 8.9 %collective-permute-start.21 = (f32[1,48,640]{2,1,0:T(8,128)S(1)}, f32[1,48,640]{2,1,0:T(8,128)S(1)}, u32[]{:S(2)}, u32[]{:S(2)}) collective-permute-start(f32[1,48,640]{2,1,0:T(8,128)S(1)} %get-tuple-element.77.refs_1_), channel_id=1, source_target_pairs={{0,16},{2,18},{4,20},{6,22},{8,24},{10,26},{12,28},{14,30},{16,32}... | collective-permute-start | bytes 368648 | tf_op jit(solution)/shard_map/ppermute | solution.py:28
  227.2 8.0 %collective-permute-start.24 = (f32[1,48,640]{2,1,0:T(8,128)S(1)}, f32[1,48,640]{2,1,0:T(8,128)S(1)}, u32[]{:S(2)}, u32[]{:S(2)}) collective-permute-start(f32[1,48,640]{2,1,0:T(8,128)S(1)} %get-tuple-element.79.refs_2_.refs_11_), channel_id=1, source_target_pairs={{16,0},{18,2},{20,4},{22,6},{24,8},{26,10},{28,12},{30,14},{32,16}... | collective-permute-start | bytes 368648 | tf_op jit(solution)/shard_map/ppermute | solution.py:28
  229.1 10.2 %collective-permute-start.23 = (f32[1,48,640]{2,1,0:T(8,128)S(1)}, f32[1,48,640]{2,1,0:T(8,128)S(1)}, u32[]{:S(2)}, u32[]{:S(2)}) collective-permute-start(f32[1,48,640]{2,1,0:T(8,128)S(1)} %get-tuple-element.79.refs_2_.refs_11_), channel_id=1, source_target_pairs={{0,16},{2,18},{4,20},{6,22},{8,24},{10,26},{12,28},{14,30},{16,32}... | collective-permute-start | bytes 368648 | tf_op jit(solution)/shard_map/ppermute | solution.py:28
  239.5 5.5 %collective-permute-start.25 = (f32[1,48,640]{2,1,0:T(8,128)S(1)}, f32[1,48,640]{2,1,0:T(8,128)S(1)}, u32[]{:S(2)}, u32[]{:S(2)}) collective-permute-start(f32[1,48,640]{2,1,0:T(8,128)S(1)} %shard_map.70), channel_id=1, source_target_pairs={{0,16},{2,18},{4,20},{6,22},{8,24},{10,26},{12,28},{14,30},{16,0},... | collective-permute-start | bytes 368648 | tf_op jit(solution)/shard_map/ppermute | solution.py:43
  245.0 8.3 %collective-permute-start.28 = (f32[1,48,640]{2,1,0:T(8,128)S(1)}, f32[1,48,640]{2,1,0:T(8,128)S(1)}, u32[]{:S(2)}, u32[]{:S(2)}) collective-permute-start(f32[1,48,640]{2,1,0:T(8,128)S(1)} %get-tuple-element.85.refs_1_), channel_id=1, source_target_pairs={{32,0},{34,2},{36,4},{38,6},{40,8},{42,10},{44,12},{46,14},{48,16}... | collective-permute-start | bytes 368648 | tf_op jit(solution)/shard_map/ppermute | solution.py:28
  246.9 9.2 %collective-permute-start.27 = (f32[1,48,640]{2,1,0:T(8,128)S(1)}, f32[1,48,640]{2,1,0:T(8,128)S(1)}, u32[]{:S(2)}, u32[]{:S(2)}) collective-permute-start(f32[1,48,640]{2,1,0:T(8,128)S(1)} %get-tuple-element.85.refs_1_), channel_id=1, source_target_pairs={{0,32},{2,34},{4,36},{6,38},{8,40},{10,42},{12,44},{14,46},{16,48}... | collective-permute-start | bytes 368648 | tf_op jit(solution)/shard_map/ppermute | solution.py:28
  257.1 21.3 %all-to-all-start.2 = ((f32[8,32,640]{2,1,0:T(8,128)}), f32[8,32,640]{2,1,0:T(8,128)S(1)}, u32[]{:S(2)}, u32[]{:S(2)}) async-start(f32[8,32,640]{2,1,0:T(8,128)} %shard_map.72), calls=%async_computation.2 | async-start | bytes 1310720 | tf_op jit(solution)/shard_map/all_to_all | solution.py:47
  (19 other events, 61.6 us)

commit v6 on v5

--- a/solution.py
+++ b/solution.py
@@ -113,6 +113,9 @@
         compiler_params=pltpu.CompilerParams(vmem_limit_bytes=limit * 1024 * 1024),
         cost_estimate=cost,
     )(*settled, *args)
+
+
+ORDER = (3, 5, 4, 2, 6, 1, 7)
 
 
 def ring_permuted(value, by):
@@ -188,7 +191,7 @@
     return 4 * count + 1 + (0 if count == 1 else 10 if count == 16 else 8)
 
 
-def make_faces(c, low, high, faces0, faces1, faces2, faces3, faces4):
+def make_faces(place, c, low, high, faces0, faces1, faces2, faces3, faces4, pack):
     east0, north0, z0, w0, halo0 = parts(faces0, 16)
 
     def z_face(p):
@@ -247,15 +250,25 @@
             halo[2 + side] = north_sum
             halo[4 + side] = outer
             halo[6 + side] = weight(near, east_sum, north_sum, shared, outer)
-
-
-def make_last_faces(faces4, other, down, up, east5, north5, w5):
-    east4, north4, _, w4, _ = parts(faces4, 1)
-    east5[0] = east4[0] + other[0]
-    north5[0] = north4[0] + other[1]
-    w5[0] = weight(w4[0], east5[0], north5[0], down[0], up[0])
-
-
+    pack[0] = faces4[0]
+    pack[1] = faces4[1]
+    pack[2] = jnp.where(place[1] == 0, faces4[2], faces4[3])
+
+
+def make_last_faces(place, faces4, other, faces5):
+    east4, north4, z4, w4, _ = parts(faces4, 1)
+    lower = place[1] == 0
+    east = east4[0] + other[0]
+    north = north4[0] + other[1]
+    down = jnp.where(lower, z4[0], other[2])
+    up = jnp.where(lower, other[2], z4[1])
+    for k, value in enumerate((east, north, down, up, weight(w4[0], east, north, down, up))):
+        faces5[k] = value
+
+
+def begin_last(rest4, other, faces5, s, first):
+    s[0] = rest4[0] + other[0]
+    first[0] = faces5[4] * s[0]
 def sweep_and_rest(s, first, total, second, faces, count):
     east, north, z, w, halo = parts(faces, count)
 
@@ -402,9 +415,10 @@
     out[0] = s[0] - damping * total[0] + neighbours(second[0], low[0], high[0], east[0], north[0], z[0], z[1])
 
 
-def finish(s, first, low, high, east, north, down, up, w, second2, second3, second4, settled, out):
+def finish(s, first, low, high, faces5, second2, second3, second4, out):
     strip = out.shape[1]
-    second5 = w[0] * (1.2 * s[0] + neighbours(first[0], low[0], high[0], east[0], north[0], down[0], up[0]))
+    east, north, down, up, w = (faces5[k] for k in range(5))
+    second5 = w * (1.2 * s[0] + neighbours(first[0], low[0], high[0], east, north, down, up))
     own = slice(HALO, HALO + strip)
     for k in range(RING):
         out[k] = ((second2[k // 2] + second3[k // 4]) + second4[0, own]) + second5[own]
@@ -419,7 +433,6 @@
     strip = rows // RING
     frame = strip + 2 * HALO
     at_core = lax.axis_index("xy")
-    even_ring = (lax.axis_index("gz") // RING) % 2 == 0
 
     def edges_of(first_rows, last_rows):
         got = lax.ppermute(jnp.where(at_core == 0, last_rows, first_rows), "xy", [(0, 1), (1, 0)])
@@ -428,7 +441,8 @@
     def shape(n):
         return (n, frame, columns)
 
-    place = jnp.reshape(lax.axis_index("gz") % RING, (1,)).astype(jnp.int32)
+    at_ring = lax.axis_index("gz")
+    place = jnp.stack([at_ring % RING, at_ring // RING % 2]).astype(jnp.int32)
     c_top, c_bottom = edges_of(conductivity(labels[:, :HALO], fraction[:, :HALO]),
                                conductivity(labels[:, rows - HALO:], fraction[:, rows - HALO:]))
     cuts = call(cut_conduct, [(planes, frame, columns)] * RING, [(planes, rows + 2 * HALO, columns)],
@@ -436,19 +450,16 @@
     s_top, s_bottom = edges_of(right_side[:, :HALO], right_side[:, rows - HALO:])
     thin = strip + 2 * THIN
     (s_cut,) = call(cut_source, [(RING, planes, thin, columns)], [], right_side, s_top, s_bottom, limit=10)
-    c_parts = [cuts[0]] + [ring_permuted(cuts[k], k) for k in range(1, RING)]
+    came = {k: ring_permuted(cuts[k], k) for k in ORDER}
+    c_parts = [cuts[0]] + [came[k] for k in range(1, RING)]
     c, bundle_down, bundle_up, ready = call(join, [shape(16), shape(REACH), shape(REACH), (HALO, columns)], [], place, *c_parts, limit=10, settled=(s_cut,))
     s_own = transposed(after(s_cut, ready))
     c_low, c_high = exchange(bundle_down, bundle_up)
-    faces0, faces1, faces2, faces3, faces4 = call(
-        make_faces, [shape(planes_of(n)) for n in (16, 8, 4, 2, 1)], [], c, c_low, c_high, limit=28, work=12.0)
-    east4, north4, z_low, z_high = faces4[0:1], faces4[1:2], faces4[2:3], faces4[3:4]
-    other = partner(jnp.concatenate([east4, north4, jnp.where(even_ring, z_low, z_high)], axis=0))
-    down5 = jnp.where(even_ring, z_low, other[2:])
-    up5 = jnp.where(even_ring, other[2:], z_high)
-    east5, north5, w5 = call(make_last_faces, [shape(1)] * 3, [], faces4, other, down5, up5)
-
-    s_own = after(s_own, faces4).reshape(RING * planes, thin, columns)
+    faces0, faces1, faces2, faces3, faces4, pack = call(
+        make_faces, [shape(planes_of(n)) for n in (16, 8, 4, 2, 1)] + [shape(3)], [], place, c, c_low, c_high, limit=28, work=12.0)
+    (faces5,) = call(make_last_faces, [shape(5)], [], place, faces4, partner(pack))
+
+    s_own = s_own.reshape(RING * planes, thin, columns)
     s_low, s_high = exchange(s_own[:2], s_own[-2:])
     fine, s1, edge_down, edge_up = call(
         fine_level, [(RING, planes, strip, columns), shape(8), shape(2), shape(2)],
@@ -477,12 +488,11 @@
     total4, second4 = call(sweep_last, [shape(1), shape(1)], [], s4, first4, low, high, faces4)
     low, high = exchange(second4, second4)
     (rest4,) = call(rest_last, [shape(1)], [], s4, total4, second4, low, high, faces4)
-    s5 = rest4 + partner(rest4)
-    first5 = w5 * s5
+    s5, first5 = call(begin_last, [shape(1), shape(1)], [], rest4, partner(rest4), faces5)
     low, high = exchange(first5, first5, 2 * RING)
     back = transposed(back)
     (summed,) = call(finish, [(RING, strip, columns)], [],
-                     s5, first5, low, high, east5, north5, down5, up5, w5, second2, second3, second4, back[0, 0, :HALO])
+                     s5, first5, low, high, faces5, second2, second3, second4, settled=(back,))
 
     fine_iterate = jnp.transpose(back[:, :planes], (1, 0, 2, 3)).reshape(planes, rows, columns)
     plane_iterate = back[:, planes].reshape(1, rows, columns)

time: 281 us -> 266 us (0.947)
  local copies, waits for them, and re-layouts: 32.8 us -> 18.7 us
  waiting for transfers between devices: 110 us -> 107 us
    all_to_all x3, waiting for transfers between devices: 10.1 us -> 46.2 us  [transposed(): lax.all_to_all(value, 'gz', 0, 0, axis_index_groups=ring_groups(lax.axis_...]
    ppermute x16, waiting for transfers between devices: 57.7 us -> 22.3 us  [shifted(): return lax.ppermute(value, 'gz', pairs)]
    unnamed x39 -> x33, local copies, waits for them, and re-layouts: 26.4 us -> 16.6 us
    ppermute x2, waiting for transfers between devices: 5.25 us -> 2.26 us  [partner(): lax.ppermute(value, 'gz', [(i, i + RING if i // RING % 2 == 0 else i - RI...]
    pallas_call x13 -> x14, Pallas kernels: 24.8 us -> 25.7 us  [call(): pl.pallas_call(body, out_shape=shapes, in_specs=[pl.BlockSpec(memory_spac...]
  transfers between devices with their start and end apart: 32 -> 32, of which waited for: 25 -> 22; matrix products, arithmetic and copies ran while one was open for 2% -> 1% of each run, Pallas kernels for 5% -> 6%
where the time goes in v6:
time: 266 us; the launch traced here: 263 us
  starting transfers between devices  109 us (41%)
  waiting for transfers between devices  107 us (40%)
  Pallas kernels  25.8 us (10%)
  local copies, waits for them, and re-layouts  18.7 us (7%)
    ppermute x16, starting transfers between devices, shifted(): return lax.ppermute(value, 'gz', pairs)  64.1 us
    all_to_all x3, waiting for transfers between devices, transposed(): lax.all_to_all(value, 'gz', 0, 0, axis_index_groups=ring_groups(lax.axis_...  46.2 us
    ppermute x7, waiting for transfers between devices, ring_permuted(): lax.ppermute(value, 'gz', [(i, i // RING * RING + (i + by) % RING) for i...  30.4 us
    pallas_call x14, Pallas kernels, call(): pl.pallas_call(body, out_shape=shapes, in_specs=[pl.BlockSpec(memory_spac...  25.7 us
    ppermute x7, starting transfers between devices, ring_permuted(): lax.ppermute(value, 'gz', [(i, i // RING * RING + (i + by) % RING) for i...  23 us
    ppermute x16, waiting for transfers between devices, shifted(): return lax.ppermute(value, 'gz', pairs)  22.3 us
    unnamed x33, local copies, waits for them, and re-layouts  16.6 us
    all_to_all x3, starting transfers between devices, transposed(): lax.all_to_all(value, 'gz', 0, 0, axis_index_groups=ring_groups(lax.axis_...  16 us
  transfers between devices with their start and end apart: 32, of which 22 were waited for; matrix products, arithmetic and copies ran while one was open for 1% of the time, Pallas kernels for 6%

profile of v6, /device:TPU:8, one launch (start us, length us, event | category | flops | bytes accessed | tf_op | source)
XLA Modules:
  0.0 263.0 jit_solution(7086962862177669694)
XLA Ops:
  8.4 3.3 %collective-permute-start.3 = (f32[2,48,640]{2,1,0:T(8,128)S(1)}, f32[2,48,640]{2,1,0:T(8,128)S(1)}, u32[]{:S(2)}, u32[]{:S(2)}) collective-permute-start(f32[2,48,640]{2,1,0:T(8,128)S(1)} %get-tuple-element.46), channel_id=1, source_target_pairs={{0,4},{2,6},{4,8},{6,10},{8,12},{10,14},{12,0},{14,2},{16,20},{18,... | collective-permute-start | bytes 737288 | tf_op jit(solution)/shard_map/ppermute | solution.py:123
  11.8 4.1 %collective-permute-start.4 = (f32[2,48,640]{2,1,0:T(8,128)S(1)}, f32[2,48,640]{2,1,0:T(8,128)S(1)}, u32[]{:S(2)}, u32[]{:S(2)}) collective-permute-start(f32[2,48,640]{2,1,0:T(8,128)S(1)} %get-tuple-element.47), channel_id=1, source_target_pairs={{0,6},{2,8},{4,10},{6,12},{8,14},{10,0},{12,2},{14,4},{16,22},{18,... | collective-permute-start | bytes 737288 | tf_op jit(solution)/shard_map/ppermute | solution.py:123
  16.4 4.9 %collective-permute-start.6 = (f32[2,48,640]{2,1,0:T(8,128)S(1)}, f32[2,48,640]{2,1,0:T(8,128)S(1)}, u32[]{:S(2)}, u32[]{:S(2)}) collective-permute-start(f32[2,48,640]{2,1,0:T(8,128)S(1)} %get-tuple-element.49), channel_id=1, source_target_pairs={{0,10},{2,12},{4,14},{6,0},{8,2},{10,4},{12,6},{14,8},{16,26},{18,... | collective-permute-start | bytes 737288 | tf_op jit(solution)/shard_map/ppermute | solution.py:123
  21.4 5.3 %collective-permute-start.7 = (f32[2,48,640]{2,1,0:T(8,128)S(1)}, f32[2,48,640]{2,1,0:T(8,128)S(1)}, u32[]{:S(2)}, u32[]{:S(2)}) collective-permute-start(f32[2,48,640]{2,1,0:T(8,128)S(1)} %get-tuple-element.50), channel_id=1, source_target_pairs={{0,12},{2,14},{4,0},{6,2},{8,4},{10,6},{12,8},{14,10},{16,28},{18,... | collective-permute-start | bytes 737288 | tf_op jit(solution)/shard_map/ppermute | solution.py:123
  26.7 5.5 %collective-permute-done.3.refs_4_ = f32[2,48,640]{2,1,0:T(8,128)S(1)} collective-permute-done((f32[2,48,640]{2,1,0:T(8,128)S(1)}, f32[2,48,640]{2,1,0:T(8,128)S(1)}, u32[]{:S(2)}, u32[]{:S(2)}) %collective-permute-start.3) | collective-permute-done | bytes 245792 | tf_op jit(solution)/shard_map/ppermute | solution.py:123
  32.2 2.9 %collective-permute-start.8 = (f32[2,48,640]{2,1,0:T(8,128)S(1)}, f32[2,48,640]{2,1,0:T(8,128)S(1)}, u32[]{:S(2)}, u32[]{:S(2)}) collective-permute-start(f32[2,48,640]{2,1,0:T(8,128)S(1)} %get-tuple-element.51), channel_id=1, source_target_pairs={{0,14},{2,0},{4,2},{6,4},{8,6},{10,8},{12,10},{14,12},{16,30},{18,... | collective-permute-start | bytes 737288 | tf_op jit(solution)/shard_map/ppermute | solution.py:123
  36.4 13.9 %collective-permute-done.4.refs_5_ = f32[2,48,640]{2,1,0:T(8,128)S(1)} collective-permute-done((f32[2,48,640]{2,1,0:T(8,128)S(1)}, f32[2,48,640]{2,1,0:T(8,128)S(1)}, u32[]{:S(2)}, u32[]{:S(2)}) %collective-permute-start.4) | collective-permute-done | bytes 245792 | tf_op jit(solution)/shard_map/ppermute | solution.py:123
  50.4 8.5 %collective-permute-done.7.refs_8_ = f32[2,48,640]{2,1,0:T(8,128)S(1)} collective-permute-done((f32[2,48,640]{2,1,0:T(8,128)S(1)}, f32[2,48,640]{2,1,0:T(8,128)S(1)}, u32[]{:S(2)}, u32[]{:S(2)}) %collective-permute-start.7) | collective-permute-done | bytes 245792 | tf_op jit(solution)/shard_map/ppermute | solution.py:123
  64.4 5.2 %all-to-all-start = ((f32[8,2,40,640]{3,2,1,0:T(8,128)}), f32[8,2,40,640]{3,2,1,0:T(8,128)S(1)}, u32[]{:S(2)}, u32[]{:S(2)}) async-start(f32[8,2,40,640]{3,2,1,0:T(8,128)} %shard_map.61), calls=%async_computation | async-start | bytes 3276800 | tf_op jit(solution)/shard_map/all_to_all | solution.py:47
  69.6 3.4 %collective-permute-start.11 = (f32[9,48,640]{2,1,0:T(8,128)}, f32[9,48,640]{2,1,0:T(8,128)}, u32[]{:S(2)}, u32[]{:S(2)}) collective-permute-start(f32[9,48,640]{2,1,0:T(8,128)} %copy-done.13), channel_id=1, source_target_pairs={{0,16},{2,18},{4,20},{6,22},{8,24},{10,26},{12,28},{14,30},{16,32}... | collective-permute-start | bytes 3317768 | tf_op jit(solution)/shard_map/ppermute | solution.py:28
  73.0 4.6 %collective-permute-start.12 = (f32[9,48,640]{2,1,0:T(8,128)S(1)}, f32[9,48,640]{2,1,0:T(8,128)}, u32[]{:S(2)}, u32[]{:S(2)}) collective-permute-start(f32[9,48,640]{2,1,0:T(8,128)S(1)} %get-tuple-element.55), channel_id=1, source_target_pairs={{16,0},{18,2},{20,4},{22,6},{24,8},{26,10},{28,12},{30,14},{32,16}... | collective-permute-start | bytes 3317768 | tf_op jit(solution)/shard_map/ppermute | solution.py:28
  77.6 33.6 %all-to-all-done = f32[8,2,40,640]{3,2,1,0:T(8,128)S(1)} async-done(((f32[8,2,40,640]{3,2,1,0:T(8,128)}), f32[8,2,40,640]{3,2,1,0:T(8,128)S(1)}, u32[]{:S(2)}, u32[]{:S(2)}) %all-to-all-start) | async-done | bytes 1638432 | tf_op jit(solution)/shard_map/all_to_all | solution.py:47
  111.2 4.6 %collective-permute-start.10 = (f32[2,40,640]{2,1,0:T(8,128)S(1)}, f32[2,40,640]{2,1,0:T(8,128)S(1)}, u32[]{:S(2)}, u32[]{:S(2)}) collective-permute-start(f32[2,40,640]{2,1,0:T(8,128)S(1)} %get-tuple-element.85), channel_id=1, source_target_pairs={{16,0},{18,2},{20,4},{22,6},{24,8},{26,10},{28,12},{30,14},{32,16}... | collective-permute-start | bytes 614408 | tf_op jit(solution)/shard_map/ppermute | solution.py:28
  119.3 9.5 %shard_map.62 = (f32[75,48,640]{2,1,0:T(8,128)S(1)}, f32[41,48,640]{2,1,0:T(8,128)S(1)}, f32[25,48,640]{2,1,0:T(8,128)S(1)}, f32[17,48,640]{2,1,0:T(8,128)S(1)},...) custom-call(s32[2]{0:T(128)S(1)} %pad_add_fusion.refs_0_.refs_1_, f32[16,48,640]{2,1,0:T(8,128)S(1)} %copy-done.12, ...), custom_call_target="tpu_custom_call" | custom-call | flops 12000000000 | bytes 36000000 | tf_op jit(solution)/shard_map/pallas_call | solution.py:107
  130.1 6.2 %shard_map.63 = (f32[8,2,32,640]{3,2,1,0:T(8,128)S(1)}, f32[8,48,640]{2,1,0:T(8,128)S(1)}, f32[2,48,640]{2,1,0:T(8,128)S(1)}, f32[2,48,640]{2,1,0:T(8,128)S(1)}) custom-call(f32[16,40,640]{2,1,0:T(8,128)S(1)} %bitcast.12, f32[2,40,640]{2,1,0:T(8,128)S(1)} %collective-permute-done.9.refs_1_, f32[2,40,640]{2,1,0:T(8,128)S(1)} %collective-permute-done.10.refs_2_, ...), custom_call_target="tpu_custom_call" | custom-call | flops 8000000000 | bytes 24000000 | tf_op jit(solution)/shard_map/pallas_call | solution.py:107
  136.3 2.8 %collective-permute-start.13 = (f32[2,48,640]{2,1,0:T(8,128)S(1)}, f32[2,48,640]{2,1,0:T(8,128)S(1)}, u32[]{:S(2)}, u32[]{:S(2)}) collective-permute-start(f32[2,48,640]{2,1,0:T(8,128)S(1)} %get-tuple-element.59), channel_id=1, source_target_pairs={{0,16},{2,18},{4,20},{6,22},{8,24},{10,26},{12,28},{14,30},{16,32}... | collective-permute-start | bytes 737288 | tf_op jit(solution)/shard_map/ppermute | solution.py:28
  139.1 5.4 %collective-permute-start.14 = (f32[2,48,640]{2,1,0:T(8,128)S(1)}, f32[2,48,640]{2,1,0:T(8,128)S(1)}, u32[]{:S(2)}, u32[]{:S(2)}) collective-permute-start(f32[2,48,640]{2,1,0:T(8,128)S(1)} %get-tuple-element.60), channel_id=1, source_target_pairs={{16,0},{18,2},{20,4},{22,6},{24,8},{26,10},{28,12},{30,14},{32,16}... | collective-permute-start | bytes 737288 | tf_op jit(solution)/shard_map/ppermute | solution.py:28
  148.0 2.8 %shard_map.64 = (f32[8,32,640]{2,1,0:T(8,128)S(1)}, f32[4,32,640]{2,1,0:T(8,128)S(1)}, f32[4,8,640]{2,1,0:T(8,128)S(1)}, f32[4,8,640]{2,1,0:T(8,128)S(1)}) custom-call(f32[8,48,640]{2,1,0:T(8,128)S(1)} %get-tuple-element.58.refs_0_, f32[2,48,640]{2,1,0:T(8,128)S(1)} %collective-permute-done.13.refs_1_, f32[2,48,640]{2,1,0:T(8,128)S(1)} %collective-permute-done.14.refs_2_, ...), custom_call_target="tpu_custom_call" | custom-call | flops 4000000000 | bytes 12000000 | tf_op jit(solution)/shard_map/pallas_call | solution.py:107
  155.3 4.3 %collective-permute-done.16.refs_2_ = f32[4,8,640]{2,1,0:T(8,128)S(1)} collective-permute-done((f32[4,8,640]{2,1,0:T(8,128)S(1)}, f32[4,8,640]{2,1,0:T(8,128)S(1)}, u32[]{:S(2)}, u32[]{:S(2)}) %collective-permute-start.16) | collective-permute-done | bytes 81952 | tf_op jit(solution)/shard_map/ppermute | solution.py:38
  162.5 3.6 %all-to-all-start.1 = ((f32[8,3,32,640]{3,2,1,0:T(8,128)}), f32[8,3,32,640]{3,2,1,0:T(8,128)S(1)}, u32[]{:S(2)}, u32[]{:S(2)}) async-start(f32[8,3,32,640]{3,2,1,0:T(8,128)} %copy-done.5), calls=%async_computation.1 | async-start | bytes 3932160 | tf_op jit(solution)/shard_map/all_to_all | solution.py:47
  166.2 3.9 %collective-permute-start.17 = (f32[2,48,640]{2,1,0:T(8,128)}, f32[2,48,640]{2,1,0:T(8,128)S(1)}, u32[]{:S(2)}, u32[]{:S(2)}) collective-permute-start(f32[2,48,640]{2,1,0:T(8,128)} %copy-done.15), channel_id=1, source_target_pairs={{0,16},{2,18},{4,20},{6,22},{8,24},{10,26},{12,28},{14,30},{16,32}... | collective-permute-start | bytes 737288 | tf_op jit(solution)/shard_map/ppermute | solution.py:28
  170.1 4.5 %collective-permute-start.18 = (f32[2,48,640]{2,1,0:T(8,128)}, f32[2,48,640]{2,1,0:T(8,128)S(1)}, u32[]{:S(2)}, u32[]{:S(2)}) collective-permute-start(f32[2,48,640]{2,1,0:T(8,128)} %copy-done.14), channel_id=1, source_target_pairs={{16,0},{18,2},{20,4},{22,6},{24,8},{26,10},{28,12},{30,14},{32,16}... | collective-permute-start | bytes 737288 | tf_op jit(solution)/shard_map/ppermute | solution.py:28
  183.8 3.8 %collective-permute-start.19 = (f32[2,48,640]{2,1,0:T(8,128)S(1)}, f32[2,48,640]{2,1,0:T(8,128)S(1)}, u32[]{:S(2)}, u32[]{:S(2)}) collective-permute-start(f32[2,48,640]{2,1,0:T(8,128)S(1)} %get-tuple-element.73), channel_id=1, source_target_pairs={{0,16},{2,18},{4,20},{6,22},{8,24},{10,26},{12,28},{14,30},{16,32}... | collective-permute-start | bytes 737288 | tf_op jit(solution)/shard_map/ppermute | solution.py:28
  187.6 4.5 %collective-permute-start.20 = (f32[2,48,640]{2,1,0:T(8,128)S(1)}, f32[2,48,640]{2,1,0:T(8,128)S(1)}, u32[]{:S(2)}, u32[]{:S(2)}) collective-permute-start(f32[2,48,640]{2,1,0:T(8,128)S(1)} %get-tuple-element.74), channel_id=1, source_target_pairs={{16,0},{18,2},{20,4},{22,6},{24,8},{26,10},{28,12},{30,14},{32,16}... | collective-permute-start | bytes 737288 | tf_op jit(solution)/shard_map/ppermute | solution.py:28
  196.8 3.9 %collective-permute-start.21 = (f32[1,48,640]{2,1,0:T(8,128)S(1)}, f32[1,48,640]{2,1,0:T(8,128)S(1)}, u32[]{:S(2)}, u32[]{:S(2)}) collective-permute-start(f32[1,48,640]{2,1,0:T(8,128)S(1)} %get-tuple-element.77.refs_1_), channel_id=1, source_target_pairs={{0,16},{2,18},{4,20},{6,22},{8,24},{10,26},{12,28},{14,30},{16,32}... | collective-permute-start | bytes 368648 | tf_op jit(solution)/shard_map/ppermute | solution.py:28
  200.7 4.5 %collective-permute-start.22 = (f32[1,48,640]{2,1,0:T(8,128)S(1)}, f32[1,48,640]{2,1,0:T(8,128)S(1)}, u32[]{:S(2)}, u32[]{:S(2)}) collective-permute-start(f32[1,48,640]{2,1,0:T(8,128)S(1)} %get-tuple-element.77.refs_1_), channel_id=1, source_target_pairs={{16,0},{18,2},{20,4},{22,6},{24,8},{26,10},{28,12},{30,14},{32,16}... | collective-permute-start | bytes 368648 | tf_op jit(solution)/shard_map/ppermute | solution.py:28
  208.1 3.6 %collective-permute-start.23 = (f32[1,48,640]{2,1,0:T(8,128)S(1)}, f32[1,48,640]{2,1,0:T(8,128)S(1)}, u32[]{:S(2)}, u32[]{:S(2)}) collective-permute-start(f32[1,48,640]{2,1,0:T(8,128)S(1)} %get-tuple-element.79.refs_2_.refs_8_), channel_id=1, source_target_pairs={{0,16},{2,18},{4,20},{6,22},{8,24},{10,26},{12,28},{14,30},{16,32}... | collective-permute-start | bytes 368648 | tf_op jit(solution)/shard_map/ppermute | solution.py:28
  211.7 4.5 %collective-permute-start.24 = (f32[1,48,640]{2,1,0:T(8,128)S(1)}, f32[1,48,640]{2,1,0:T(8,128)S(1)}, u32[]{:S(2)}, u32[]{:S(2)}) collective-permute-start(f32[1,48,640]{2,1,0:T(8,128)S(1)} %get-tuple-element.79.refs_2_.refs_8_), channel_id=1, source_target_pairs={{16,0},{18,2},{20,4},{22,6},{24,8},{26,10},{28,12},{30,14},{32,16}... | collective-permute-start | bytes 368648 | tf_op jit(solution)/shard_map/ppermute | solution.py:28
  223.8 6.1 %collective-permute-start.27 = (f32[1,48,640]{2,1,0:T(8,128)S(1)}, f32[1,48,640]{2,1,0:T(8,128)S(1)}, u32[]{:S(2)}, u32[]{:S(2)}) collective-permute-start(f32[1,48,640]{2,1,0:T(8,128)S(1)} %get-tuple-element.82.refs_2_), channel_id=1, source_target_pairs={{0,32},{2,34},{4,36},{6,38},{8,40},{10,42},{12,44},{14,46},{16,48}... | collective-permute-start | bytes 368648 | tf_op jit(solution)/shard_map/ppermute | solution.py:28
  233.0 5.2 %collective-permute-done.28.refs_4_ = f32[1,48,640]{2,1,0:T(8,128)S(1)} collective-permute-done((f32[1,48,640]{2,1,0:T(8,128)S(1)}, f32[1,48,640]{2,1,0:T(8,128)S(1)}, u32[]{:S(2)}, u32[]{:S(2)}) %collective-permute-start.28) | collective-permute-done | bytes 122912 | tf_op jit(solution)/shard_map/ppermute | solution.py:28
  240.2 7.2 %all-to-all-start.2 = ((f32[8,32,640]{2,1,0:T(8,128)}), f32[8,32,640]{2,1,0:T(8,128)S(1)}, u32[]{:S(2)}, u32[]{:S(2)}) async-start(f32[8,32,640]{2,1,0:T(8,128)} %copy-done.4), calls=%async_computation.2 | async-start | bytes 1310720 | tf_op jit(solution)/shard_map/all_to_all | solution.py:47
  249.5 12.6 %all-to-all-done.2 = f32[8,32,640]{2,1,0:T(8,128)S(1)} async-done(((f32[8,32,640]{2,1,0:T(8,128)}), f32[8,32,640]{2,1,0:T(8,128)S(1)}, u32[]{:S(2)}, u32[]{:S(2)}) %all-to-all-start.2) | async-done | bytes 655392 | tf_op jit(solution)/shard_map/all_to_all | solution.py:47
  (89 shorter events, 63.3 us)
Async XLA Ops:
  1.5 1.3 collective-permute-start.1
  6.4 15.0 %collective-permute-start.2 = (f32[2,48,640]{2,1,0:T(8,128)S(1)}, f32[2,48,640]{2,1,0:T(8,128)S(1)}, u32[]{:S(2)}, u32[]{:S(2)}) collective-permute-start(f32[2,48,640]{2,1,0:T(8,128)S(1)} %get-tuple-element.45), channel_id=1, source_target_pairs={{0,2},{2,4},{4,6},{6,8},{8,10},{10,12},{12,14},{14,0},{16,18},{18,... | collective-permute-start | bytes 737288 | tf_op jit(solution)/shard_map/ppermute | solution.py:123
  8.4 23.9 %collective-permute-start.3 = (f32[2,48,640]{2,1,0:T(8,128)S(1)}, f32[2,48,640]{2,1,0:T(8,128)S(1)}, u32[]{:S(2)}, u32[]{:S(2)}) collective-permute-start(f32[2,48,640]{2,1,0:T(8,128)S(1)} %get-tuple-element.46), channel_id=1, source_target_pairs={{0,4},{2,6},{4,8},{6,10},{8,12},{10,14},{12,0},{14,2},{16,20},{18,... | collective-permute-start | bytes 737288 | tf_op jit(solution)/shard_map/ppermute | solution.py:123
  11.7 4.8 %collective-permute-start = (f32[2,8,640]{2,1,0:T(8,128)S(1)}, f32[2,8,640]{2,1,0:T(8,128)S(1)}, u32[]{:S(2)}, u32[]{:S(2)}) collective-permute-start(f32[2,8,640]{2,1,0:T(8,128)S(1)} %slice_select_fusion), channel_id=1, source_target_pairs={{0,1},{1,0},{2,3},{3,2},{4,5},{5,4},{6,7},{7,6},{8,9},{9,8},{10,11... | collective-permute-start | bytes 122888 | tf_op jit(solution)/shard_map/ppermute | solution.py:438
  11.8 38.6 %collective-permute-start.4 = (f32[2,48,640]{2,1,0:T(8,128)S(1)}, f32[2,48,640]{2,1,0:T(8,128)S(1)}, u32[]{:S(2)}, u32[]{:S(2)}) collective-permute-start(f32[2,48,640]{2,1,0:T(8,128)S(1)} %get-tuple-element.47), channel_id=1, source_target_pairs={{0,6},{2,8},{4,10},{6,12},{8,14},{10,0},{12,2},{14,4},{16,22},{18,... | collective-permute-start | bytes 737288 | tf_op jit(solution)/shard_map/ppermute | solution.py:123
  15.9 34.5 %collective-permute-start.5 = (f32[2,48,640]{2,1,0:T(8,128)S(1)}, f32[2,48,640]{2,1,0:T(8,128)S(1)}, u32[]{:S(2)}, u32[]{:S(2)}) collective-permute-start(f32[2,48,640]{2,1,0:T(8,128)S(1)} %get-tuple-element.48), channel_id=1, source_target_pairs={{0,8},{2,10},{4,12},{6,14},{8,0},{10,2},{12,4},{14,6},{16,24},{18,... | collective-permute-start | bytes 737288 | tf_op jit(solution)/shard_map/ppermute | solution.py:123
  16.4 33.9 %collective-permute-start.6 = (f32[2,48,640]{2,1,0:T(8,128)S(1)}, f32[2,48,640]{2,1,0:T(8,128)S(1)}, u32[]{:S(2)}, u32[]{:S(2)}) collective-permute-start(f32[2,48,640]{2,1,0:T(8,128)S(1)} %get-tuple-element.49), channel_id=1, source_target_pairs={{0,10},{2,12},{4,14},{6,0},{8,2},{10,4},{12,6},{14,8},{16,26},{18,... | collective-permute-start | bytes 737288 | tf_op jit(solution)/shard_map/ppermute | solution.py:123
  21.4 37.5 %collective-permute-start.7 = (f32[2,48,640]{2,1,0:T(8,128)S(1)}, f32[2,48,640]{2,1,0:T(8,128)S(1)}, u32[]{:S(2)}, u32[]{:S(2)}) collective-permute-start(f32[2,48,640]{2,1,0:T(8,128)S(1)} %get-tuple-element.50), channel_id=1, source_target_pairs={{0,12},{2,14},{4,0},{6,2},{8,4},{10,6},{12,8},{14,10},{16,28},{18,... | collective-permute-start | bytes 737288 | tf_op jit(solution)/shard_map/ppermute | solution.py:123
  32.2 29.0 %collective-permute-start.8 = (f32[2,48,640]{2,1,0:T(8,128)S(1)}, f32[2,48,640]{2,1,0:T(8,128)S(1)}, u32[]{:S(2)}, u32[]{:S(2)}) collective-permute-start(f32[2,48,640]{2,1,0:T(8,128)S(1)} %get-tuple-element.51), channel_id=1, source_target_pairs={{0,14},{2,0},{4,2},{6,4},{8,6},{10,8},{12,10},{14,12},{16,30},{18,... | collective-permute-start | bytes 737288 | tf_op jit(solution)/shard_map/ppermute | solution.py:123
  64.4 46.7 %all-to-all-start = ((f32[8,2,40,640]{3,2,1,0:T(8,128)}), f32[8,2,40,640]{3,2,1,0:T(8,128)S(1)}, u32[]{:S(2)}, u32[]{:S(2)}) async-start(f32[8,2,40,640]{3,2,1,0:T(8,128)} %shard_map.61), calls=%async_computation | async-start | bytes 3276800 | tf_op jit(solution)/shard_map/all_to_all | solution.py:47
  69.6 48.1 %collective-permute-start.11 = (f32[9,48,640]{2,1,0:T(8,128)}, f32[9,48,640]{2,1,0:T(8,128)}, u32[]{:S(2)}, u32[]{:S(2)}) collective-permute-start(f32[9,48,640]{2,1,0:T(8,128)} %copy-done.13), channel_id=1, source_target_pairs={{0,16},{2,18},{4,20},{6,22},{8,24},{10,26},{12,28},{14,30},{16,32}... | collective-permute-start | bytes 3317768 | tf_op jit(solution)/shard_map/ppermute | solution.py:28
  73.0 44.7 %collective-permute-start.12 = (f32[9,48,640]{2,1,0:T(8,128)S(1)}, f32[9,48,640]{2,1,0:T(8,128)}, u32[]{:S(2)}, u32[]{:S(2)}) collective-permute-start(f32[9,48,640]{2,1,0:T(8,128)S(1)} %get-tuple-element.55), channel_id=1, source_target_pairs={{16,0},{18,2},{20,4},{22,6},{24,8},{26,10},{28,12},{30,14},{32,16}... | collective-permute-start | bytes 3317768 | tf_op jit(solution)/shard_map/ppermute | solution.py:28
  111.2 18.9 %collective-permute-start.10 = (f32[2,40,640]{2,1,0:T(8,128)S(1)}, f32[2,40,640]{2,1,0:T(8,128)S(1)}, u32[]{:S(2)}, u32[]{:S(2)}) collective-permute-start(f32[2,40,640]{2,1,0:T(8,128)S(1)} %get-tuple-element.85), channel_id=1, source_target_pairs={{16,0},{18,2},{20,4},{22,6},{24,8},{26,10},{28,12},{30,14},{32,16}... | collective-permute-start | bytes 614408 | tf_op jit(solution)/shard_map/ppermute | solution.py:28
  115.8 14.4 %collective-permute-start.9 = (f32[2,40,640]{2,1,0:T(8,128)S(1)}, f32[2,40,640]{2,1,0:T(8,128)S(1)}, u32[]{:S(2)}, u32[]{:S(2)}) collective-permute-start(f32[2,40,640]{2,1,0:T(8,128)S(1)} %get-tuple-element.86), channel_id=1, source_target_pairs={{0,16},{2,18},{4,20},{6,22},{8,24},{10,26},{12,28},{14,30},{16,32}... | collective-permute-start | bytes 614408 | tf_op jit(solution)/shard_map/ppermute | solution.py:28
  136.3 10.2 %collective-permute-start.13 = (f32[2,48,640]{2,1,0:T(8,128)S(1)}, f32[2,48,640]{2,1,0:T(8,128)S(1)}, u32[]{:S(2)}, u32[]{:S(2)}) collective-permute-start(f32[2,48,640]{2,1,0:T(8,128)S(1)} %get-tuple-element.59), channel_id=1, source_target_pairs={{0,16},{2,18},{4,20},{6,22},{8,24},{10,26},{12,28},{14,30},{16,32}... | collective-permute-start | bytes 737288 | tf_op jit(solution)/shard_map/ppermute | solution.py:28
  139.1 8.9 %collective-permute-start.14 = (f32[2,48,640]{2,1,0:T(8,128)S(1)}, f32[2,48,640]{2,1,0:T(8,128)S(1)}, u32[]{:S(2)}, u32[]{:S(2)}) collective-permute-start(f32[2,48,640]{2,1,0:T(8,128)S(1)} %get-tuple-element.60), channel_id=1, source_target_pairs={{16,0},{18,2},{20,4},{22,6},{24,8},{26,10},{28,12},{30,14},{32,16}... | collective-permute-start | bytes 737288 | tf_op jit(solution)/shard_map/ppermute | solution.py:28
  150.8 4.5 %collective-permute-start.15 = (f32[4,8,640]{2,1,0:T(8,128)S(1)}, f32[4,8,640]{2,1,0:T(8,128)S(1)}, u32[]{:S(2)}, u32[]{:S(2)}) collective-permute-start(f32[4,8,640]{2,1,0:T(8,128)S(1)} %get-tuple-element.62), channel_id=1, source_target_pairs={{0,2},{2,4},{4,6},{6,8},{8,10},{10,12},{12,14},{14,1},{1,3},{3,5},... | collective-permute-start | bytes 245768 | tf_op jit(solution)/shard_map/ppermute | solution.py:38
  153.3 6.3 %collective-permute-start.16 = (f32[4,8,640]{2,1,0:T(8,128)S(1)}, f32[4,8,640]{2,1,0:T(8,128)S(1)}, u32[]{:S(2)}, u32[]{:S(2)}) collective-permute-start(f32[4,8,640]{2,1,0:T(8,128)S(1)} %get-tuple-element.63), channel_id=1, source_target_pairs={{2,0},{4,2},{6,4},{8,6},{10,8},{12,10},{14,12},{1,14},{3,1},{5,3},... | collective-permute-start | bytes 245768 | tf_op jit(solution)/shard_map/ppermute | solution.py:38
  162.5 75.7 %all-to-all-start.1 = ((f32[8,3,32,640]{3,2,1,0:T(8,128)}), f32[8,3,32,640]{3,2,1,0:T(8,128)S(1)}, u32[]{:S(2)}, u32[]{:S(2)}) async-start(f32[8,3,32,640]{3,2,1,0:T(8,128)} %copy-done.5), calls=%async_computation.1 | async-start | bytes 3932160 | tf_op jit(solution)/shard_map/all_to_all | solution.py:47
  166.2 10.9 %collective-permute-start.17 = (f32[2,48,640]{2,1,0:T(8,128)}, f32[2,48,640]{2,1,0:T(8,128)S(1)}, u32[]{:S(2)}, u32[]{:S(2)}) collective-permute-start(f32[2,48,640]{2,1,0:T(8,128)} %copy-done.15), channel_id=1, source_target_pairs={{0,16},{2,18},{4,20},{6,22},{8,24},{10,26},{12,28},{14,30},{16,32}... | collective-permute-start | bytes 737288 | tf_op jit(solution)/shard_map/ppermute | solution.py:28
  170.1 8.5 %collective-permute-start.18 = (f32[2,48,640]{2,1,0:T(8,128)}, f32[2,48,640]{2,1,0:T(8,128)S(1)}, u32[]{:S(2)}, u32[]{:S(2)}) collective-permute-start(f32[2,48,640]{2,1,0:T(8,128)} %copy-done.14), channel_id=1, source_target_pairs={{16,0},{18,2},{20,4},{22,6},{24,8},{26,10},{28,12},{30,14},{32,16}... | collective-permute-start | bytes 737288 | tf_op jit(solution)/shard_map/ppermute | solution.py:28
  183.8 10.6 %collective-permute-start.19 = (f32[2,48,640]{2,1,0:T(8,128)S(1)}, f32[2,48,640]{2,1,0:T(8,128)S(1)}, u32[]{:S(2)}, u32[]{:S(2)}) collective-permute-start(f32[2,48,640]{2,1,0:T(8,128)S(1)} %get-tuple-element.73), channel_id=1, source_target_pairs={{0,16},{2,18},{4,20},{6,22},{8,24},{10,26},{12,28},{14,30},{16,32}... | collective-permute-start | bytes 737288 | tf_op jit(solution)/shard_map/ppermute | solution.py:28
  187.6 8.2 %collective-permute-start.20 = (f32[2,48,640]{2,1,0:T(8,128)S(1)}, f32[2,48,640]{2,1,0:T(8,128)S(1)}, u32[]{:S(2)}, u32[]{:S(2)}) collective-permute-start(f32[2,48,640]{2,1,0:T(8,128)S(1)} %get-tuple-element.74), channel_id=1, source_target_pairs={{16,0},{18,2},{20,4},{22,6},{24,8},{26,10},{28,12},{30,14},{32,16}... | collective-permute-start | bytes 737288 | tf_op jit(solution)/shard_map/ppermute | solution.py:28
  196.8 9.4 %collective-permute-start.21 = (f32[1,48,640]{2,1,0:T(8,128)S(1)}, f32[1,48,640]{2,1,0:T(8,128)S(1)}, u32[]{:S(2)}, u32[]{:S(2)}) collective-permute-start(f32[1,48,640]{2,1,0:T(8,128)S(1)} %get-tuple-element.77.refs_1_), channel_id=1, source_target_pairs={{0,16},{2,18},{4,20},{6,22},{8,24},{10,26},{12,28},{14,30},{16,32}... | collective-permute-start | bytes 368648 | tf_op jit(solution)/shard_map/ppermute | solution.py:28
  200.7 7.2 %collective-permute-start.22 = (f32[1,48,640]{2,1,0:T(8,128)S(1)}, f32[1,48,640]{2,1,0:T(8,128)S(1)}, u32[]{:S(2)}, u32[]{:S(2)}) collective-permute-start(f32[1,48,640]{2,1,0:T(8,128)S(1)} %get-tuple-element.77.refs_1_), channel_id=1, source_target_pairs={{16,0},{18,2},{20,4},{22,6},{24,8},{26,10},{28,12},{30,14},{32,16}... | collective-permute-start | bytes 368648 | tf_op jit(solution)/shard_map/ppermute | solution.py:28
  205.3 15.6 %collective-permute-start.26 = (f32[3,48,640]{2,1,0:T(8,128)S(1)}, f32[3,48,640]{2,1,0:T(8,128)S(1)}, u32[]{:S(2)}, u32[]{:S(2)}) collective-permute-start(f32[3,48,640]{2,1,0:T(8,128)S(1)} %get-tuple-element.80), channel_id=1, source_target_pairs={{0,16},{2,18},{4,20},{6,22},{8,24},{10,26},{12,28},{14,30},{16,0},... | collective-permute-start | bytes 1105928 | tf_op jit(solution)/shard_map/ppermute | solution.py:43
  208.1 9.1 %collective-permute-start.23 = (f32[1,48,640]{2,1,0:T(8,128)S(1)}, f32[1,48,640]{2,1,0:T(8,128)S(1)}, u32[]{:S(2)}, u32[]{:S(2)}) collective-permute-start(f32[1,48,640]{2,1,0:T(8,128)S(1)} %get-tuple-element.79.refs_2_.refs_8_), channel_id=1, source_target_pairs={{0,16},{2,18},{4,20},{6,22},{8,24},{10,26},{12,28},{14,30},{16,32}... | collective-permute-start | bytes 368648 | tf_op jit(solution)/shard_map/ppermute | solution.py:28
  211.7 7.0 %collective-permute-start.24 = (f32[1,48,640]{2,1,0:T(8,128)S(1)}, f32[1,48,640]{2,1,0:T(8,128)S(1)}, u32[]{:S(2)}, u32[]{:S(2)}) collective-permute-start(f32[1,48,640]{2,1,0:T(8,128)S(1)} %get-tuple-element.79.refs_2_.refs_8_), channel_id=1, source_target_pairs={{16,0},{18,2},{20,4},{22,6},{24,8},{26,10},{28,12},{30,14},{32,16}... | collective-permute-start | bytes 368648 | tf_op jit(solution)/shard_map/ppermute | solution.py:28
  218.9 5.0 %collective-permute-start.25 = (f32[1,48,640]{2,1,0:T(8,128)S(1)}, f32[1,48,640]{2,1,0:T(8,128)S(1)}, u32[]{:S(2)}, u32[]{:S(2)}) collective-permute-start(f32[1,48,640]{2,1,0:T(8,128)S(1)} %shard_map.69.refs_0_), channel_id=1, source_target_pairs={{0,16},{2,18},{4,20},{6,22},{8,24},{10,26},{12,28},{14,30},{16,0},... | collective-permute-start | bytes 368648 | tf_op jit(solution)/shard_map/ppermute | solution.py:43
  223.8 9.2 %collective-permute-start.27 = (f32[1,48,640]{2,1,0:T(8,128)S(1)}, f32[1,48,640]{2,1,0:T(8,128)S(1)}, u32[]{:S(2)}, u32[]{:S(2)}) collective-permute-start(f32[1,48,640]{2,1,0:T(8,128)S(1)} %get-tuple-element.82.refs_2_), channel_id=1, source_target_pairs={{0,32},{2,34},{4,36},{6,38},{8,40},{10,42},{12,44},{14,46},{16,48}... | collective-permute-start | bytes 368648 | tf_op jit(solution)/shard_map/ppermute | solution.py:28
  230.0 8.3 %collective-permute-start.28 = (f32[1,48,640]{2,1,0:T(8,128)S(1)}, f32[1,48,640]{2,1,0:T(8,128)S(1)}, u32[]{:S(2)}, u32[]{:S(2)}) collective-permute-start(f32[1,48,640]{2,1,0:T(8,128)S(1)} %get-tuple-element.82.refs_2_), channel_id=1, source_target_pairs={{32,0},{34,2},{36,4},{38,6},{40,8},{42,10},{44,12},{46,14},{48,16}... | collective-permute-start | bytes 368648 | tf_op jit(solution)/shard_map/ppermute | solution.py:28
  240.2 21.9 %all-to-all-start.2 = ((f32[8,32,640]{2,1,0:T(8,128)}), f32[8,32,640]{2,1,0:T(8,128)S(1)}, u32[]{:S(2)}, u32[]{:S(2)}) async-start(f32[8,32,640]{2,1,0:T(8,128)} %copy-done.4), calls=%async_computation.2 | async-start | bytes 1310720 | tf_op jit(solution)/shard_map/all_to_all | solution.py:47
  (16 other events, 64.5 us)

commit v7 on v6

--- a/solution.py
+++ b/solution.py
@@ -15,7 +15,7 @@
 pore_value = 1.0
 grain_value = 0.1
 clay_value = 0.3
-TINY = 1e-30
+TINY = 1e-6
 
 
 def ring_groups(count):
@@ -51,8 +51,13 @@
     return jnp.where(labels == 0, pore_value, jnp.where(labels == 1, grain_value, clay_value)) * fraction
 
 
+def inverse(x):
+    guess = pl.reciprocal(x, approx=True)
+    return guess * (2.0 - x * guess)
+
+
 def harmonic(one_side, other_side):
-    return (2.0 * one_side * other_side) / jnp.maximum(one_side + other_side, TINY)
+    return (2.0 * one_side * other_side) * inverse(jnp.maximum(one_side + other_side, TINY))
 
 
 def next_row(v):
@@ -84,7 +89,7 @@
 
 def weight(c, east, north, down, up):
     diagonal = east + previous_row(east) + north + previous_column(north) + down + up
-    return jnp.where(c > 0, damping / jnp.where(c > 0, diagonal, 1.0), 0.0)
+    return jnp.where(c > 0, damping * inverse(jnp.where(c > 0, diagonal, 1.0)), 0.0)
 
 
 def loop(count, body):
@@ -167,10 +172,10 @@
 def join(place, *refs):
     out, low, high, ready = refs[RING:]
     ready[...] = refs[0][0, :HALO]
-    for k in range(RING):
+    for k, ref in zip((0,) + ORDER, refs):
         start = ((place[0] + RING - k) % RING) * 2
-        out[start] = refs[k][0]
-        out[start + 1] = refs[k][1]
+        out[start] = ref[0]
+        out[start + 1] = ref[1]
     reach = low.shape[0]
     loop(reach, lambda p: low.__setitem__(p, out[p]))
     loop(reach, lambda p: high.__setitem__(p, out[p + 16 - reach]))
@@ -450,8 +455,7 @@
     s_top, s_bottom = edges_of(right_side[:, :HALO], right_side[:, rows - HALO:])
     thin = strip + 2 * THIN
     (s_cut,) = call(cut_source, [(RING, planes, thin, columns)], [], right_side, s_top, s_bottom, limit=10)
-    came = {k: ring_permuted(cuts[k], k) for k in ORDER}
-    c_parts = [cuts[0]] + [came[k] for k in range(1, RING)]
+    c_parts = [cuts[0]] + [ring_permuted(cuts[k], k) for k in ORDER]
     c, bundle_down, bundle_up, ready = call(join, [shape(16), shape(REACH), shape(REACH), (HALO, columns)], [], place, *c_parts, limit=10, settled=(s_cut,))
     s_own = transposed(after(s_cut, ready))
     c_low, c_high = exchange(bundle_down, bundle_up)

time: 266 us -> 264 us (level)
  waiting for transfers between devices: 107 us -> 103 us
    ppermute x7, waiting for transfers between devices: 30.4 us -> 26.4 us  [ring_permuted(): lax.ppermute(value, 'gz', [(i, i // RING * RING + (i + by) % RING) for i...]
  transfers between devices with their start and end apart: 32 -> 32, of which waited for: 22 -> 24; matrix products, arithmetic and copies ran while one was open for 1% -> 1% of each run, Pallas kernels for 6% -> 6%
where the time goes in v7:
time: 264 us; the launch traced here: 261 us
  starting transfers between devices  110 us (42%)
  waiting for transfers between devices  103 us (39%)
  Pallas kernels  27.2 us (10%)
  local copies, waits for them, and re-layouts  18.7 us (7%)
    ppermute x16, starting transfers between devices, shifted(): return lax.ppermute(value, 'gz', pairs)  64.3 us
    all_to_all x3, waiting for transfers between devices, transposed(): lax.all_to_all(value, 'gz', 0, 0, axis_index_groups=ring_groups(lax.axis_...  45.8 us
    pallas_call x14, Pallas kernels, call(): pl.pallas_call(body, out_shape=shapes, in_specs=[pl.BlockSpec(memory_spac...  27.2 us
    ppermute x7, waiting for transfers between devices, ring_permuted(): lax.ppermute(value, 'gz', [(i, i // RING * RING + (i + by) % RING) for i...  26.4 us
    ppermute x7, starting transfers between devices, ring_permuted(): lax.ppermute(value, 'gz', [(i, i // RING * RING + (i + by) % RING) for i...  23 us
    ppermute x16, waiting for transfers between devices, shifted(): return lax.ppermute(value, 'gz', pairs)  21.9 us
    all_to_all x3, starting transfers between devices, transposed(): lax.all_to_all(value, 'gz', 0, 0, axis_index_groups=ring_groups(lax.axis_...  16.9 us
    unnamed x33, local copies, waits for them, and re-layouts  16.6 us
  transfers between devices with their start and end apart: 32, of which 24 were waited for; matrix products, arithmetic and copies ran while one was open for 1% of the time, Pallas kernels for 6%

profile of v7, /device:TPU:8, one launch (start us, length us, event | category | flops | bytes accessed | tf_op | source)
XLA Modules:
  0.0 261.0 jit_solution(15944898815231102162)
XLA Ops:
  6.4 4.7 %collective-permute-start.2 = (f32[2,48,640]{2,1,0:T(8,128)S(1)}, f32[2,48,640]{2,1,0:T(8,128)S(1)}, u32[]{:S(2)}, u32[]{:S(2)}) collective-permute-start(f32[2,48,640]{2,1,0:T(8,128)S(1)} %get-tuple-element.45), channel_id=1, source_target_pairs={{0,6},{2,8},{4,10},{6,12},{8,14},{10,0},{12,2},{14,4},{16,22},{18,... | collective-permute-start | bytes 737288 | tf_op jit(solution)/shard_map/ppermute | solution.py:128
  13.4 5.5 %collective-permute-start.4 = (f32[2,48,640]{2,1,0:T(8,128)S(1)}, f32[2,48,640]{2,1,0:T(8,128)S(1)}, u32[]{:S(2)}, u32[]{:S(2)}) collective-permute-start(f32[2,48,640]{2,1,0:T(8,128)S(1)} %get-tuple-element.47), channel_id=1, source_target_pairs={{0,8},{2,10},{4,12},{6,14},{8,0},{10,2},{12,4},{14,6},{16,24},{18,... | collective-permute-start | bytes 737288 | tf_op jit(solution)/shard_map/ppermute | solution.py:128
  20.4 2.7 %collective-permute-start.6 = (f32[2,48,640]{2,1,0:T(8,128)S(1)}, f32[2,48,640]{2,1,0:T(8,128)S(1)}, u32[]{:S(2)}, u32[]{:S(2)}) collective-permute-start(f32[2,48,640]{2,1,0:T(8,128)S(1)} %get-tuple-element.49), channel_id=1, source_target_pairs={{0,12},{2,14},{4,0},{6,2},{8,4},{10,6},{12,8},{14,10},{16,28},{18,... | collective-permute-start | bytes 737288 | tf_op jit(solution)/shard_map/ppermute | solution.py:128
  23.0 7.7 %collective-permute-done.2.refs_3_ = f32[2,48,640]{2,1,0:T(8,128)S(1)} collective-permute-done((f32[2,48,640]{2,1,0:T(8,128)S(1)}, f32[2,48,640]{2,1,0:T(8,128)S(1)}, u32[]{:S(2)}, u32[]{:S(2)}) %collective-permute-start.2) | collective-permute-done | bytes 245792 | tf_op jit(solution)/shard_map/ppermute | solution.py:128
  30.8 5.0 %collective-permute-start.7 = (f32[2,48,640]{2,1,0:T(8,128)S(1)}, f32[2,48,640]{2,1,0:T(8,128)S(1)}, u32[]{:S(2)}, u32[]{:S(2)}) collective-permute-start(f32[2,48,640]{2,1,0:T(8,128)S(1)} %get-tuple-element.50), channel_id=1, source_target_pairs={{0,2},{2,4},{4,6},{6,8},{8,10},{10,12},{12,14},{14,0},{16,18},{18,... | collective-permute-start | bytes 737288 | tf_op jit(solution)/shard_map/ppermute | solution.py:128
  38.6 3.6 %collective-permute-done.4.refs_5_ = f32[2,48,640]{2,1,0:T(8,128)S(1)} collective-permute-done((f32[2,48,640]{2,1,0:T(8,128)S(1)}, f32[2,48,640]{2,1,0:T(8,128)S(1)}, u32[]{:S(2)}, u32[]{:S(2)}) %collective-permute-start.4) | collective-permute-done | bytes 245792 | tf_op jit(solution)/shard_map/ppermute | solution.py:128
  42.1 9.1 %collective-permute-done.5.refs_6_ = f32[2,48,640]{2,1,0:T(8,128)S(1)} collective-permute-done((f32[2,48,640]{2,1,0:T(8,128)S(1)}, f32[2,48,640]{2,1,0:T(8,128)S(1)}, u32[]{:S(2)}, u32[]{:S(2)}) %collective-permute-start.5) | collective-permute-done | bytes 245792 | tf_op jit(solution)/shard_map/ppermute | solution.py:128
  52.9 2.7 %collective-permute-done.7.refs_8_ = f32[2,48,640]{2,1,0:T(8,128)S(1)} collective-permute-done((f32[2,48,640]{2,1,0:T(8,128)S(1)}, f32[2,48,640]{2,1,0:T(8,128)S(1)}, u32[]{:S(2)}, u32[]{:S(2)}) %collective-permute-start.7) | collective-permute-done | bytes 245792 | tf_op jit(solution)/shard_map/ppermute | solution.py:128
  60.4 6.1 %all-to-all-start = ((f32[8,2,40,640]{3,2,1,0:T(8,128)}), f32[8,2,40,640]{3,2,1,0:T(8,128)S(1)}, u32[]{:S(2)}, u32[]{:S(2)}) async-start(f32[8,2,40,640]{3,2,1,0:T(8,128)} %shard_map.61), calls=%async_computation | async-start | bytes 3276800 | tf_op jit(solution)/shard_map/all_to_all | solution.py:47
  66.5 3.4 %collective-permute-start.11 = (f32[9,48,640]{2,1,0:T(8,128)}, f32[9,48,640]{2,1,0:T(8,128)}, u32[]{:S(2)}, u32[]{:S(2)}) collective-permute-start(f32[9,48,640]{2,1,0:T(8,128)} %copy-done.13), channel_id=1, source_target_pairs={{0,16},{2,18},{4,20},{6,22},{8,24},{10,26},{12,28},{14,30},{16,32}... | collective-permute-start | bytes 3317768 | tf_op jit(solution)/shard_map/ppermute | solution.py:28
  69.9 4.6 %collective-permute-start.12 = (f32[9,48,640]{2,1,0:T(8,128)S(1)}, f32[9,48,640]{2,1,0:T(8,128)}, u32[]{:S(2)}, u32[]{:S(2)}) collective-permute-start(f32[9,48,640]{2,1,0:T(8,128)S(1)} %get-tuple-element.55), channel_id=1, source_target_pairs={{16,0},{18,2},{20,4},{22,6},{24,8},{26,10},{28,12},{30,14},{32,16}... | collective-permute-start | bytes 3317768 | tf_op jit(solution)/shard_map/ppermute | solution.py:28
  74.5 33.2 %all-to-all-done = f32[8,2,40,640]{3,2,1,0:T(8,128)S(1)} async-done(((f32[8,2,40,640]{3,2,1,0:T(8,128)}), f32[8,2,40,640]{3,2,1,0:T(8,128)S(1)}, u32[]{:S(2)}, u32[]{:S(2)}) %all-to-all-start) | async-done | bytes 1638432 | tf_op jit(solution)/shard_map/all_to_all | solution.py:47
  107.7 4.6 %collective-permute-start.10 = (f32[2,40,640]{2,1,0:T(8,128)S(1)}, f32[2,40,640]{2,1,0:T(8,128)S(1)}, u32[]{:S(2)}, u32[]{:S(2)}) collective-permute-start(f32[2,40,640]{2,1,0:T(8,128)S(1)} %get-tuple-element.85), channel_id=1, source_target_pairs={{16,0},{18,2},{20,4},{22,6},{24,8},{26,10},{28,12},{30,14},{32,16}... | collective-permute-start | bytes 614408 | tf_op jit(solution)/shard_map/ppermute | solution.py:28
  115.9 11.0 %shard_map.62 = (f32[75,48,640]{2,1,0:T(8,128)S(1)}, f32[41,48,640]{2,1,0:T(8,128)S(1)}, f32[25,48,640]{2,1,0:T(8,128)S(1)}, f32[17,48,640]{2,1,0:T(8,128)S(1)},...) custom-call(s32[2]{0:T(128)S(1)} %pad_add_fusion.refs_0_.refs_1_, f32[16,48,640]{2,1,0:T(8,128)S(1)} %copy-done.12, ...), custom_call_target="tpu_custom_call" | custom-call | flops 12000000000 | bytes 36000000 | tf_op jit(solution)/shard_map/pallas_call | solution.py:112
  128.3 6.2 %shard_map.63 = (f32[8,2,32,640]{3,2,1,0:T(8,128)S(1)}, f32[8,48,640]{2,1,0:T(8,128)S(1)}, f32[2,48,640]{2,1,0:T(8,128)S(1)}, f32[2,48,640]{2,1,0:T(8,128)S(1)}) custom-call(f32[16,40,640]{2,1,0:T(8,128)S(1)} %bitcast.12, f32[2,40,640]{2,1,0:T(8,128)S(1)} %collective-permute-done.9.refs_1_, f32[2,40,640]{2,1,0:T(8,128)S(1)} %collective-permute-done.10.refs_2_, ...), custom_call_target="tpu_custom_call" | custom-call | flops 8000000000 | bytes 24000000 | tf_op jit(solution)/shard_map/pallas_call | solution.py:112
  134.4 2.8 %collective-permute-start.13 = (f32[2,48,640]{2,1,0:T(8,128)S(1)}, f32[2,48,640]{2,1,0:T(8,128)S(1)}, u32[]{:S(2)}, u32[]{:S(2)}) collective-permute-start(f32[2,48,640]{2,1,0:T(8,128)S(1)} %get-tuple-element.59), channel_id=1, source_target_pairs={{0,16},{2,18},{4,20},{6,22},{8,24},{10,26},{12,28},{14,30},{16,32}... | collective-permute-start | bytes 737288 | tf_op jit(solution)/shard_map/ppermute | solution.py:28
  137.2 5.2 %collective-permute-start.14 = (f32[2,48,640]{2,1,0:T(8,128)S(1)}, f32[2,48,640]{2,1,0:T(8,128)S(1)}, u32[]{:S(2)}, u32[]{:S(2)}) collective-permute-start(f32[2,48,640]{2,1,0:T(8,128)S(1)} %get-tuple-element.60), channel_id=1, source_target_pairs={{16,0},{18,2},{20,4},{22,6},{24,8},{26,10},{28,12},{30,14},{32,16}... | collective-permute-start | bytes 737288 | tf_op jit(solution)/shard_map/ppermute | solution.py:28
  146.1 2.8 %shard_map.64 = (f32[8,32,640]{2,1,0:T(8,128)S(1)}, f32[4,32,640]{2,1,0:T(8,128)S(1)}, f32[4,8,640]{2,1,0:T(8,128)S(1)}, f32[4,8,640]{2,1,0:T(8,128)S(1)}) custom-call(f32[8,48,640]{2,1,0:T(8,128)S(1)} %get-tuple-element.58.refs_0_, f32[2,48,640]{2,1,0:T(8,128)S(1)} %collective-permute-done.13.refs_1_, f32[2,48,640]{2,1,0:T(8,128)S(1)} %collective-permute-done.14.refs_2_, ...), custom_call_target="tpu_custom_call" | custom-call | flops 4000000000 | bytes 12000000 | tf_op jit(solution)/shard_map/pallas_call | solution.py:112
  153.4 4.3 %collective-permute-done.16.refs_2_ = f32[4,8,640]{2,1,0:T(8,128)S(1)} collective-permute-done((f32[4,8,640]{2,1,0:T(8,128)S(1)}, f32[4,8,640]{2,1,0:T(8,128)S(1)}, u32[]{:S(2)}, u32[]{:S(2)}) %collective-permute-start.16) | collective-permute-done | bytes 81952 | tf_op jit(solution)/shard_map/ppermute | solution.py:38
  160.6 3.6 %all-to-all-start.1 = ((f32[8,3,32,640]{3,2,1,0:T(8,128)}), f32[8,3,32,640]{3,2,1,0:T(8,128)S(1)}, u32[]{:S(2)}, u32[]{:S(2)}) async-start(f32[8,3,32,640]{3,2,1,0:T(8,128)} %copy-done.5), calls=%async_computation.1 | async-start | bytes 3932160 | tf_op jit(solution)/shard_map/all_to_all | solution.py:47
  164.2 3.9 %collective-permute-start.17 = (f32[2,48,640]{2,1,0:T(8,128)}, f32[2,48,640]{2,1,0:T(8,128)S(1)}, u32[]{:S(2)}, u32[]{:S(2)}) collective-permute-start(f32[2,48,640]{2,1,0:T(8,128)} %copy-done.15), channel_id=1, source_target_pairs={{0,16},{2,18},{4,20},{6,22},{8,24},{10,26},{12,28},{14,30},{16,32}... | collective-permute-start | bytes 737288 | tf_op jit(solution)/shard_map/ppermute | solution.py:28
  168.1 4.5 %collective-permute-start.18 = (f32[2,48,640]{2,1,0:T(8,128)}, f32[2,48,640]{2,1,0:T(8,128)S(1)}, u32[]{:S(2)}, u32[]{:S(2)}) collective-permute-start(f32[2,48,640]{2,1,0:T(8,128)} %copy-done.14), channel_id=1, source_target_pairs={{16,0},{18,2},{20,4},{22,6},{24,8},{26,10},{28,12},{30,14},{32,16}... | collective-permute-start | bytes 737288 | tf_op jit(solution)/shard_map/ppermute | solution.py:28
  181.8 3.8 %collective-permute-start.19 = (f32[2,48,640]{2,1,0:T(8,128)S(1)}, f32[2,48,640]{2,1,0:T(8,128)S(1)}, u32[]{:S(2)}, u32[]{:S(2)}) collective-permute-start(f32[2,48,640]{2,1,0:T(8,128)S(1)} %get-tuple-element.73), channel_id=1, source_target_pairs={{0,16},{2,18},{4,20},{6,22},{8,24},{10,26},{12,28},{14,30},{16,32}... | collective-permute-start | bytes 737288 | tf_op jit(solution)/shard_map/ppermute | solution.py:28
  185.6 4.5 %collective-permute-start.20 = (f32[2,48,640]{2,1,0:T(8,128)S(1)}, f32[2,48,640]{2,1,0:T(8,128)S(1)}, u32[]{:S(2)}, u32[]{:S(2)}) collective-permute-start(f32[2,48,640]{2,1,0:T(8,128)S(1)} %get-tuple-element.74), channel_id=1, source_target_pairs={{16,0},{18,2},{20,4},{22,6},{24,8},{26,10},{28,12},{30,14},{32,16}... | collective-permute-start | bytes 737288 | tf_op jit(solution)/shard_map/ppermute | solution.py:28
  194.9 3.9 %collective-permute-start.21 = (f32[1,48,640]{2,1,0:T(8,128)S(1)}, f32[1,48,640]{2,1,0:T(8,128)S(1)}, u32[]{:S(2)}, u32[]{:S(2)}) collective-permute-start(f32[1,48,640]{2,1,0:T(8,128)S(1)} %get-tuple-element.77.refs_1_), channel_id=1, source_target_pairs={{0,16},{2,18},{4,20},{6,22},{8,24},{10,26},{12,28},{14,30},{16,32}... | collective-permute-start | bytes 368648 | tf_op jit(solution)/shard_map/ppermute | solution.py:28
  198.8 4.5 %collective-permute-start.22 = (f32[1,48,640]{2,1,0:T(8,128)S(1)}, f32[1,48,640]{2,1,0:T(8,128)S(1)}, u32[]{:S(2)}, u32[]{:S(2)}) collective-permute-start(f32[1,48,640]{2,1,0:T(8,128)S(1)} %get-tuple-element.77.refs_1_), channel_id=1, source_target_pairs={{16,0},{18,2},{20,4},{22,6},{24,8},{26,10},{28,12},{30,14},{32,16}... | collective-permute-start | bytes 368648 | tf_op jit(solution)/shard_map/ppermute | solution.py:28
  205.9 3.9 %collective-permute-start.23 = (f32[1,48,640]{2,1,0:T(8,128)S(1)}, f32[1,48,640]{2,1,0:T(8,128)S(1)}, u32[]{:S(2)}, u32[]{:S(2)}) collective-permute-start(f32[1,48,640]{2,1,0:T(8,128)S(1)} %get-tuple-element.79.refs_2_.refs_8_), channel_id=1, source_target_pairs={{0,16},{2,18},{4,20},{6,22},{8,24},{10,26},{12,28},{14,30},{16,32}... | collective-permute-start | bytes 368648 | tf_op jit(solution)/shard_map/ppermute | solution.py:28
  209.8 4.5 %collective-permute-start.24 = (f32[1,48,640]{2,1,0:T(8,128)S(1)}, f32[1,48,640]{2,1,0:T(8,128)S(1)}, u32[]{:S(2)}, u32[]{:S(2)}) collective-permute-start(f32[1,48,640]{2,1,0:T(8,128)S(1)} %get-tuple-element.79.refs_2_.refs_8_), channel_id=1, source_target_pairs={{16,0},{18,2},{20,4},{22,6},{24,8},{26,10},{28,12},{30,14},{32,16}... | collective-permute-start | bytes 368648 | tf_op jit(solution)/shard_map/ppermute | solution.py:28
  222.2 5.8 %collective-permute-start.27 = (f32[1,48,640]{2,1,0:T(8,128)S(1)}, f32[1,48,640]{2,1,0:T(8,128)S(1)}, u32[]{:S(2)}, u32[]{:S(2)}) collective-permute-start(f32[1,48,640]{2,1,0:T(8,128)S(1)} %get-tuple-element.82.refs_2_), channel_id=1, source_target_pairs={{0,32},{2,34},{4,36},{6,38},{8,40},{10,42},{12,44},{14,46},{16,48}... | collective-permute-start | bytes 368648 | tf_op jit(solution)/shard_map/ppermute | solution.py:28
  231.4 4.9 %collective-permute-done.28.refs_4_ = f32[1,48,640]{2,1,0:T(8,128)S(1)} collective-permute-done((f32[1,48,640]{2,1,0:T(8,128)S(1)}, f32[1,48,640]{2,1,0:T(8,128)S(1)}, u32[]{:S(2)}, u32[]{:S(2)}) %collective-permute-start.28) | collective-permute-done | bytes 122912 | tf_op jit(solution)/shard_map/ppermute | solution.py:28
  238.2 7.2 %all-to-all-start.2 = ((f32[8,32,640]{2,1,0:T(8,128)}), f32[8,32,640]{2,1,0:T(8,128)S(1)}, u32[]{:S(2)}, u32[]{:S(2)}) async-start(f32[8,32,640]{2,1,0:T(8,128)} %copy-done.4), calls=%async_computation.2 | async-start | bytes 1310720 | tf_op jit(solution)/shard_map/all_to_all | solution.py:47
  247.6 12.6 %all-to-all-done.2 = f32[8,32,640]{2,1,0:T(8,128)S(1)} async-done(((f32[8,32,640]{2,1,0:T(8,128)}), f32[8,32,640]{2,1,0:T(8,128)S(1)}, u32[]{:S(2)}, u32[]{:S(2)}) %all-to-all-start.2) | async-done | bytes 655392 | tf_op jit(solution)/shard_map/all_to_all | solution.py:47
  (89 shorter events, 67.5 us)
Async XLA Ops:
  1.5 1.3 collective-permute-start.1
  6.4 24.4 %collective-permute-start.2 = (f32[2,48,640]{2,1,0:T(8,128)S(1)}, f32[2,48,640]{2,1,0:T(8,128)S(1)}, u32[]{:S(2)}, u32[]{:S(2)}) collective-permute-start(f32[2,48,640]{2,1,0:T(8,128)S(1)} %get-tuple-element.45), channel_id=1, source_target_pairs={{0,6},{2,8},{4,10},{6,12},{8,14},{10,0},{12,2},{14,4},{16,22},{18,... | collective-permute-start | bytes 737288 | tf_op jit(solution)/shard_map/ppermute | solution.py:128
  11.1 24.7 %collective-permute-start.3 = (f32[2,48,640]{2,1,0:T(8,128)S(1)}, f32[2,48,640]{2,1,0:T(8,128)S(1)}, u32[]{:S(2)}, u32[]{:S(2)}) collective-permute-start(f32[2,48,640]{2,1,0:T(8,128)S(1)} %get-tuple-element.46), channel_id=1, source_target_pairs={{0,10},{2,12},{4,14},{6,0},{8,2},{10,4},{12,6},{14,8},{16,26},{18,... | collective-permute-start | bytes 737288 | tf_op jit(solution)/shard_map/ppermute | solution.py:128
  13.3 7.1 %collective-permute-start = (f32[2,8,640]{2,1,0:T(8,128)S(1)}, f32[2,8,640]{2,1,0:T(8,128)S(1)}, u32[]{:S(2)}, u32[]{:S(2)}) collective-permute-start(f32[2,8,640]{2,1,0:T(8,128)S(1)} %slice_select_fusion), channel_id=1, source_target_pairs={{0,1},{1,0},{2,3},{3,2},{4,5},{5,4},{6,7},{7,6},{8,9},{9,8},{10,11... | collective-permute-start | bytes 122888 | tf_op jit(solution)/shard_map/ppermute | solution.py:443
  13.4 28.7 %collective-permute-start.4 = (f32[2,48,640]{2,1,0:T(8,128)S(1)}, f32[2,48,640]{2,1,0:T(8,128)S(1)}, u32[]{:S(2)}, u32[]{:S(2)}) collective-permute-start(f32[2,48,640]{2,1,0:T(8,128)S(1)} %get-tuple-element.47), channel_id=1, source_target_pairs={{0,8},{2,10},{4,12},{6,14},{8,0},{10,2},{12,4},{14,6},{16,24},{18,... | collective-permute-start | bytes 737288 | tf_op jit(solution)/shard_map/ppermute | solution.py:128
  18.9 32.3 %collective-permute-start.5 = (f32[2,48,640]{2,1,0:T(8,128)S(1)}, f32[2,48,640]{2,1,0:T(8,128)S(1)}, u32[]{:S(2)}, u32[]{:S(2)}) collective-permute-start(f32[2,48,640]{2,1,0:T(8,128)S(1)} %get-tuple-element.48), channel_id=1, source_target_pairs={{0,4},{2,6},{4,8},{6,10},{8,12},{10,14},{12,0},{14,2},{16,20},{18,... | collective-permute-start | bytes 737288 | tf_op jit(solution)/shard_map/ppermute | solution.py:128
  20.4 32.6 %collective-permute-start.6 = (f32[2,48,640]{2,1,0:T(8,128)S(1)}, f32[2,48,640]{2,1,0:T(8,128)S(1)}, u32[]{:S(2)}, u32[]{:S(2)}) collective-permute-start(f32[2,48,640]{2,1,0:T(8,128)S(1)} %get-tuple-element.49), channel_id=1, source_target_pairs={{0,12},{2,14},{4,0},{6,2},{8,4},{10,6},{12,8},{14,10},{16,28},{18,... | collective-permute-start | bytes 737288 | tf_op jit(solution)/shard_map/ppermute | solution.py:128
  30.8 24.8 %collective-permute-start.7 = (f32[2,48,640]{2,1,0:T(8,128)S(1)}, f32[2,48,640]{2,1,0:T(8,128)S(1)}, u32[]{:S(2)}, u32[]{:S(2)}) collective-permute-start(f32[2,48,640]{2,1,0:T(8,128)S(1)} %get-tuple-element.50), channel_id=1, source_target_pairs={{0,2},{2,4},{4,6},{6,8},{8,10},{10,12},{12,14},{14,0},{16,18},{18,... | collective-permute-start | bytes 737288 | tf_op jit(solution)/shard_map/ppermute | solution.py:128
  35.8 21.5 %collective-permute-start.8 = (f32[2,48,640]{2,1,0:T(8,128)S(1)}, f32[2,48,640]{2,1,0:T(8,128)S(1)}, u32[]{:S(2)}, u32[]{:S(2)}) collective-permute-start(f32[2,48,640]{2,1,0:T(8,128)S(1)} %get-tuple-element.51), channel_id=1, source_target_pairs={{0,14},{2,0},{4,2},{6,4},{8,6},{10,8},{12,10},{14,12},{16,30},{18,... | collective-permute-start | bytes 737288 | tf_op jit(solution)/shard_map/ppermute | solution.py:128
  60.4 47.2 %all-to-all-start = ((f32[8,2,40,640]{3,2,1,0:T(8,128)}), f32[8,2,40,640]{3,2,1,0:T(8,128)S(1)}, u32[]{:S(2)}, u32[]{:S(2)}) async-start(f32[8,2,40,640]{3,2,1,0:T(8,128)} %shard_map.61), calls=%async_computation | async-start | bytes 3276800 | tf_op jit(solution)/shard_map/all_to_all | solution.py:47
  66.5 47.8 %collective-permute-start.11 = (f32[9,48,640]{2,1,0:T(8,128)}, f32[9,48,640]{2,1,0:T(8,128)}, u32[]{:S(2)}, u32[]{:S(2)}) collective-permute-start(f32[9,48,640]{2,1,0:T(8,128)} %copy-done.13), channel_id=1, source_target_pairs={{0,16},{2,18},{4,20},{6,22},{8,24},{10,26},{12,28},{14,30},{16,32}... | collective-permute-start | bytes 3317768 | tf_op jit(solution)/shard_map/ppermute | solution.py:28
  69.9 44.5 %collective-permute-start.12 = (f32[9,48,640]{2,1,0:T(8,128)S(1)}, f32[9,48,640]{2,1,0:T(8,128)}, u32[]{:S(2)}, u32[]{:S(2)}) collective-permute-start(f32[9,48,640]{2,1,0:T(8,128)S(1)} %get-tuple-element.55), channel_id=1, source_target_pairs={{16,0},{18,2},{20,4},{22,6},{24,8},{26,10},{28,12},{30,14},{32,16}... | collective-permute-start | bytes 3317768 | tf_op jit(solution)/shard_map/ppermute | solution.py:28
  107.7 20.6 %collective-permute-start.10 = (f32[2,40,640]{2,1,0:T(8,128)S(1)}, f32[2,40,640]{2,1,0:T(8,128)S(1)}, u32[]{:S(2)}, u32[]{:S(2)}) collective-permute-start(f32[2,40,640]{2,1,0:T(8,128)S(1)} %get-tuple-element.85), channel_id=1, source_target_pairs={{16,0},{18,2},{20,4},{22,6},{24,8},{26,10},{28,12},{30,14},{32,16}... | collective-permute-start | bytes 614408 | tf_op jit(solution)/shard_map/ppermute | solution.py:28
  112.2 16.0 %collective-permute-start.9 = (f32[2,40,640]{2,1,0:T(8,128)S(1)}, f32[2,40,640]{2,1,0:T(8,128)S(1)}, u32[]{:S(2)}, u32[]{:S(2)}) collective-permute-start(f32[2,40,640]{2,1,0:T(8,128)S(1)} %get-tuple-element.86), channel_id=1, source_target_pairs={{0,16},{2,18},{4,20},{6,22},{8,24},{10,26},{12,28},{14,30},{16,32}... | collective-permute-start | bytes 614408 | tf_op jit(solution)/shard_map/ppermute | solution.py:28
  134.4 10.2 %collective-permute-start.13 = (f32[2,48,640]{2,1,0:T(8,128)S(1)}, f32[2,48,640]{2,1,0:T(8,128)S(1)}, u32[]{:S(2)}, u32[]{:S(2)}) collective-permute-start(f32[2,48,640]{2,1,0:T(8,128)S(1)} %get-tuple-element.59), channel_id=1, source_target_pairs={{0,16},{2,18},{4,20},{6,22},{8,24},{10,26},{12,28},{14,30},{16,32}... | collective-permute-start | bytes 737288 | tf_op jit(solution)/shard_map/ppermute | solution.py:28
  137.2 8.9 %collective-permute-start.14 = (f32[2,48,640]{2,1,0:T(8,128)S(1)}, f32[2,48,640]{2,1,0:T(8,128)S(1)}, u32[]{:S(2)}, u32[]{:S(2)}) collective-permute-start(f32[2,48,640]{2,1,0:T(8,128)S(1)} %get-tuple-element.60), channel_id=1, source_target_pairs={{16,0},{18,2},{20,4},{22,6},{24,8},{26,10},{28,12},{30,14},{32,16}... | collective-permute-start | bytes 737288 | tf_op jit(solution)/shard_map/ppermute | solution.py:28
  148.9 4.4 %collective-permute-start.15 = (f32[4,8,640]{2,1,0:T(8,128)S(1)}, f32[4,8,640]{2,1,0:T(8,128)S(1)}, u32[]{:S(2)}, u32[]{:S(2)}) collective-permute-start(f32[4,8,640]{2,1,0:T(8,128)S(1)} %get-tuple-element.62), channel_id=1, source_target_pairs={{0,2},{2,4},{4,6},{6,8},{8,10},{10,12},{12,14},{14,1},{1,3},{3,5},... | collective-permute-start | bytes 245768 | tf_op jit(solution)/shard_map/ppermute | solution.py:38
  151.3 6.3 %collective-permute-start.16 = (f32[4,8,640]{2,1,0:T(8,128)S(1)}, f32[4,8,640]{2,1,0:T(8,128)S(1)}, u32[]{:S(2)}, u32[]{:S(2)}) collective-permute-start(f32[4,8,640]{2,1,0:T(8,128)S(1)} %get-tuple-element.63), channel_id=1, source_target_pairs={{2,0},{4,2},{6,4},{8,6},{10,8},{12,10},{14,12},{1,14},{3,1},{5,3},... | collective-permute-start | bytes 245768 | tf_op jit(solution)/shard_map/ppermute | solution.py:38
  160.6 75.7 %all-to-all-start.1 = ((f32[8,3,32,640]{3,2,1,0:T(8,128)}), f32[8,3,32,640]{3,2,1,0:T(8,128)S(1)}, u32[]{:S(2)}, u32[]{:S(2)}) async-start(f32[8,3,32,640]{3,2,1,0:T(8,128)} %copy-done.5), calls=%async_computation.1 | async-start | bytes 3932160 | tf_op jit(solution)/shard_map/all_to_all | solution.py:47
  164.2 10.9 %collective-permute-start.17 = (f32[2,48,640]{2,1,0:T(8,128)}, f32[2,48,640]{2,1,0:T(8,128)S(1)}, u32[]{:S(2)}, u32[]{:S(2)}) collective-permute-start(f32[2,48,640]{2,1,0:T(8,128)} %copy-done.15), channel_id=1, source_target_pairs={{0,16},{2,18},{4,20},{6,22},{8,24},{10,26},{12,28},{14,30},{16,32}... | collective-permute-start | bytes 737288 | tf_op jit(solution)/shard_map/ppermute | solution.py:28
  168.1 8.5 %collective-permute-start.18 = (f32[2,48,640]{2,1,0:T(8,128)}, f32[2,48,640]{2,1,0:T(8,128)S(1)}, u32[]{:S(2)}, u32[]{:S(2)}) collective-permute-start(f32[2,48,640]{2,1,0:T(8,128)} %copy-done.14), channel_id=1, source_target_pairs={{16,0},{18,2},{20,4},{22,6},{24,8},{26,10},{28,12},{30,14},{32,16}... | collective-permute-start | bytes 737288 | tf_op jit(solution)/shard_map/ppermute | solution.py:28
  181.8 10.6 %collective-permute-start.19 = (f32[2,48,640]{2,1,0:T(8,128)S(1)}, f32[2,48,640]{2,1,0:T(8,128)S(1)}, u32[]{:S(2)}, u32[]{:S(2)}) collective-permute-start(f32[2,48,640]{2,1,0:T(8,128)S(1)} %get-tuple-element.73), channel_id=1, source_target_pairs={{0,16},{2,18},{4,20},{6,22},{8,24},{10,26},{12,28},{14,30},{16,32}... | collective-permute-start | bytes 737288 | tf_op jit(solution)/shard_map/ppermute | solution.py:28
  185.6 8.2 %collective-permute-start.20 = (f32[2,48,640]{2,1,0:T(8,128)S(1)}, f32[2,48,640]{2,1,0:T(8,128)S(1)}, u32[]{:S(2)}, u32[]{:S(2)}) collective-permute-start(f32[2,48,640]{2,1,0:T(8,128)S(1)} %get-tuple-element.74), channel_id=1, source_target_pairs={{16,0},{18,2},{20,4},{22,6},{24,8},{26,10},{28,12},{30,14},{32,16}... | collective-permute-start | bytes 737288 | tf_op jit(solution)/shard_map/ppermute | solution.py:28
  194.9 9.4 %collective-permute-start.21 = (f32[1,48,640]{2,1,0:T(8,128)S(1)}, f32[1,48,640]{2,1,0:T(8,128)S(1)}, u32[]{:S(2)}, u32[]{:S(2)}) collective-permute-start(f32[1,48,640]{2,1,0:T(8,128)S(1)} %get-tuple-element.77.refs_1_), channel_id=1, source_target_pairs={{0,16},{2,18},{4,20},{6,22},{8,24},{10,26},{12,28},{14,30},{16,32}... | collective-permute-start | bytes 368648 | tf_op jit(solution)/shard_map/ppermute | solution.py:28
  198.8 7.0 %collective-permute-start.22 = (f32[1,48,640]{2,1,0:T(8,128)S(1)}, f32[1,48,640]{2,1,0:T(8,128)S(1)}, u32[]{:S(2)}, u32[]{:S(2)}) collective-permute-start(f32[1,48,640]{2,1,0:T(8,128)S(1)} %get-tuple-element.77.refs_1_), channel_id=1, source_target_pairs={{16,0},{18,2},{20,4},{22,6},{24,8},{26,10},{28,12},{30,14},{32,16}... | collective-permute-start | bytes 368648 | tf_op jit(solution)/shard_map/ppermute | solution.py:28
  203.3 15.6 %collective-permute-start.26 = (f32[3,48,640]{2,1,0:T(8,128)S(1)}, f32[3,48,640]{2,1,0:T(8,128)S(1)}, u32[]{:S(2)}, u32[]{:S(2)}) collective-permute-start(f32[3,48,640]{2,1,0:T(8,128)S(1)} %get-tuple-element.80), channel_id=1, source_target_pairs={{0,16},{2,18},{4,20},{6,22},{8,24},{10,26},{12,28},{14,30},{16,0},... | collective-permute-start | bytes 1105928 | tf_op jit(solution)/shard_map/ppermute | solution.py:43
  205.9 9.3 %collective-permute-start.23 = (f32[1,48,640]{2,1,0:T(8,128)S(1)}, f32[1,48,640]{2,1,0:T(8,128)S(1)}, u32[]{:S(2)}, u32[]{:S(2)}) collective-permute-start(f32[1,48,640]{2,1,0:T(8,128)S(1)} %get-tuple-element.79.refs_2_.refs_8_), channel_id=1, source_target_pairs={{0,16},{2,18},{4,20},{6,22},{8,24},{10,26},{12,28},{14,30},{16,32}... | collective-permute-start | bytes 368648 | tf_op jit(solution)/shard_map/ppermute | solution.py:28
  209.8 7.0 %collective-permute-start.24 = (f32[1,48,640]{2,1,0:T(8,128)S(1)}, f32[1,48,640]{2,1,0:T(8,128)S(1)}, u32[]{:S(2)}, u32[]{:S(2)}) collective-permute-start(f32[1,48,640]{2,1,0:T(8,128)S(1)} %get-tuple-element.79.refs_2_.refs_8_), channel_id=1, source_target_pairs={{16,0},{18,2},{20,4},{22,6},{24,8},{26,10},{28,12},{30,14},{32,16}... | collective-permute-start | bytes 368648 | tf_op jit(solution)/shard_map/ppermute | solution.py:28
  216.9 5.3 %collective-permute-start.25 = (f32[1,48,640]{2,1,0:T(8,128)S(1)}, f32[1,48,640]{2,1,0:T(8,128)S(1)}, u32[]{:S(2)}, u32[]{:S(2)}) collective-permute-start(f32[1,48,640]{2,1,0:T(8,128)S(1)} %shard_map.69.refs_0_), channel_id=1, source_target_pairs={{0,16},{2,18},{4,20},{6,22},{8,24},{10,26},{12,28},{14,30},{16,0},... | collective-permute-start | bytes 368648 | tf_op jit(solution)/shard_map/ppermute | solution.py:43
  222.2 9.2 %collective-permute-start.27 = (f32[1,48,640]{2,1,0:T(8,128)S(1)}, f32[1,48,640]{2,1,0:T(8,128)S(1)}, u32[]{:S(2)}, u32[]{:S(2)}) collective-permute-start(f32[1,48,640]{2,1,0:T(8,128)S(1)} %get-tuple-element.82.refs_2_), channel_id=1, source_target_pairs={{0,32},{2,34},{4,36},{6,38},{8,40},{10,42},{12,44},{14,46},{16,48}... | collective-permute-start | bytes 368648 | tf_op jit(solution)/shard_map/ppermute | solution.py:28
  228.0 8.3 %collective-permute-start.28 = (f32[1,48,640]{2,1,0:T(8,128)S(1)}, f32[1,48,640]{2,1,0:T(8,128)S(1)}, u32[]{:S(2)}, u32[]{:S(2)}) collective-permute-start(f32[1,48,640]{2,1,0:T(8,128)S(1)} %get-tuple-element.82.refs_2_), channel_id=1, source_target_pairs={{32,0},{34,2},{36,4},{38,6},{40,8},{42,10},{44,12},{46,14},{48,16}... | collective-permute-start | bytes 368648 | tf_op jit(solution)/shard_map/ppermute | solution.py:28
  238.2 21.9 %all-to-all-start.2 = ((f32[8,32,640]{2,1,0:T(8,128)}), f32[8,32,640]{2,1,0:T(8,128)S(1)}, u32[]{:S(2)}, u32[]{:S(2)}) async-start(f32[8,32,640]{2,1,0:T(8,128)} %copy-done.4), calls=%async_computation.2 | async-start | bytes 1310720 | tf_op jit(solution)/shard_map/all_to_all | solution.py:47
  (16 other events, 66.1 us)

commit v8 on v7

--- a/solution.py
+++ b/solution.py
@@ -51,13 +51,8 @@
     return jnp.where(labels == 0, pore_value, jnp.where(labels == 1, grain_value, clay_value)) * fraction
 
 
-def inverse(x):
-    guess = pl.reciprocal(x, approx=True)
-    return guess * (2.0 - x * guess)
-
-
 def harmonic(one_side, other_side):
-    return (2.0 * one_side * other_side) * inverse(jnp.maximum(one_side + other_side, TINY))
+    return (2.0 * one_side * other_side) / jnp.maximum(one_side + other_side, TINY)
 
 
 def next_row(v):
@@ -89,7 +84,7 @@
 
 def weight(c, east, north, down, up):
     diagonal = east + previous_row(east) + north + previous_column(north) + down + up
-    return jnp.where(c > 0, damping * inverse(jnp.where(c > 0, diagonal, 1.0)), 0.0)
+    return jnp.where(c > 0, damping / jnp.where(c > 0, diagonal, 1.0), 0.0)
 
 
 def loop(count, body):
@@ -100,21 +95,25 @@
     lax.fori_loop(0, count, step, 0)
 
 
-def call(kernel, outs, scratch, *args, limit=8, work=0.0, settled=()):
-    shapes = [jax.ShapeDtypeStruct(s, jnp.float32) for s in outs]
+def call(kernel, outs, scratch, *args, limit=8, work=0.0, settled=(), hbm_in=(), hbm_out=(), copies=0):
+    shapes = [(pltpu.HBM if i in hbm_out else jax.ShapeDtypeStruct)(s, jnp.float32) for i, s in enumerate(outs)]
     vmem = pl.BlockSpec(memory_space=pltpu.VMEM)
     smem = pl.BlockSpec(memory_space=pltpu.SMEM)
+    hbm = pl.BlockSpec(memory_space=pltpu.HBM)
+    kinds = [hbm if i in hbm_in else smem if a.dtype == jnp.int32 and a.ndim == 1 else vmem for i, a in enumerate(args)]
     cost = pl.CostEstimate(flops=int(work * 1.0e9), bytes_accessed=int(work * 3.0e6), transcendentals=0) if work else None
 
     def body(*refs):
         kernel(*refs[len(settled):])
+
+    args = [pltpu.with_memory_space_constraint(a, pltpu.HBM) if i in hbm_in else a for i, a in enumerate(args)]
 
     return pl.pallas_call(
         body,
         out_shape=shapes,
-        in_specs=[pl.BlockSpec(memory_space=pl.ANY)] * len(settled) + [smem if a.dtype == jnp.int32 and a.ndim == 1 else vmem for a in args],
-        out_specs=[vmem] * len(shapes),
-        scratch_shapes=[pltpu.VMEM(s, jnp.float32) for s in scratch],
+        in_specs=[pl.BlockSpec(memory_space=pl.ANY)] * len(settled) + kinds,
+        out_specs=[hbm if i in hbm_out else vmem for i in range(len(shapes))],
+        scratch_shapes=[pltpu.VMEM(s, jnp.float32) for s in scratch] + ([pltpu.SemaphoreType.DMA((copies,))] if copies else []),
         compiler_params=pltpu.CompilerParams(vmem_limit_bytes=limit * 1024 * 1024),
         cost_estimate=cost,
     )(*settled, *args)
@@ -141,6 +140,17 @@
         compiler_params=pltpu.CompilerParams(vmem_limit_bytes=1024 * 1024),
         input_output_aliases={0: 0},
     )(value, *settled)
+
+
+class Copies:
+    def __init__(self, semaphores):
+        self.semaphores, self.started = semaphores, []
+
+    def start(self, source, target):
+        copy = pltpu.make_async_copy(source, target, self.semaphores.at[len(self.started)])
+        copy.start()
+        self.started.append(copy)
+        return copy
 
 
 def cut_conduct(place, labels, fraction, top, bottom, *rest):
@@ -196,7 +206,7 @@
     return 4 * count + 1 + (0 if count == 1 else 10 if count == 16 else 8)
 
 
-def make_faces(place, c, low, high, faces0, faces1, faces2, faces3, faces4, pack):
+def make_faces(place, c, low, high, out0, out1, out2, out3, out4, pack, ready, faces0, faces1, faces2, faces3, faces4, semaphores):
     east0, north0, z0, w0, halo0 = parts(faces0, 16)
 
     def z_face(p):
@@ -212,7 +222,9 @@
         north0[p] = north
         w0[p] = weight(c[p], east, north, z0[p], z0[p + 1])
 
+    copies = Copies(semaphores)
     loop(16, weigh)
+    copies.start(faces0.at[0:65], out0.at[0:65])
     finer, count = faces0, 16
     for coarser in (faces1, faces2, faces3, faces4):
         east_f, north_f, z_f, _, _ = parts(finer, count)
@@ -230,6 +242,10 @@
         loop(count, faces_and_weight)
         z[count] = z_f[2 * count]
         finer = coarser
+    copies.start(faces1.at[0:33], out1.at[0:33])
+    copies.start(faces2.at[0:17], out2.at[0:17])
+    copies.start(faces3.at[0:9], out3.at[0:9])
+    copies.start(faces4, out4)
 
     for side, ref, at, face in ((0, low, [REACH - 1 - k for k in range(REACH)], 0), (1, high, list(range(REACH)), 16)):
         shared = z0[face]
@@ -255,9 +271,16 @@
             halo[2 + side] = north_sum
             halo[4 + side] = outer
             halo[6 + side] = weight(near, east_sum, north_sum, shared, outer)
+    copies.start(faces0.at[65:75], out0.at[65:75])
+    copies.start(faces1.at[33:41], out1.at[33:41])
+    copies.start(faces2.at[17:25], out2.at[17:25])
+    copies.start(faces3.at[9:17], out3.at[9:17])
+    ready[...] = faces4[0, :HALO]
     pack[0] = faces4[0]
     pack[1] = faces4[1]
     pack[2] = jnp.where(place[1] == 0, faces4[2], faces4[3])
+    for copy in copies.started:
+        copy.wait()
 
 
 def make_last_faces(place, faces4, other, faces5):
@@ -274,7 +297,7 @@
 def begin_last(rest4, other, faces5, s, first):
     s[0] = rest4[0] + other[0]
     first[0] = faces5[4] * s[0]
-def sweep_and_rest(s, first, total, second, faces, count):
+def sweep_and_rest(s, first, total, second, faces, count, groups=()):
     east, north, z, w, halo = parts(faces, count)
 
     def sweep(q):
@@ -282,7 +305,14 @@
         total[q] = t
         second[q + 1] = w[q] * t
 
-    loop(count, sweep)
+    if groups:
+        each = count // len(groups)
+        for k, group in enumerate(groups):
+            for copy in group:
+                copy.wait()
+            loop(each, lambda q: sweep(q + k * each))
+    else:
+        loop(count, sweep)
     for side, q, down, up in ((0, -1, halo[4], z[0]), (1, count, z[count], halo[5])):
         second[q + 1] = halo[6 + side] * (1.2 * s[q + 1] + neighbours(
             first[q + 2], first[q + 1], first[q + 3], halo[side], halo[2 + side], down, up))
@@ -294,11 +324,17 @@
     return rest
 
 
-def fine_level(s_own, s_low, s_high, faces, faces_next, fine, s_next, edge_down, edge_up, s, first, total, second):
+def fine_level(s_own, s_low, s_high, there, there_next, fine, s_next, edge_down, edge_up, s, first, total, second, faces, w_next, semaphores):
     strip = fine.shape[2]
     columns = s.shape[2]
     _, _, _, w, halo = parts(faces, 16)
-    w_next = parts(faces_next, 8)[3]
+    copies = Copies(semaphores)
+    weights = copies.start(there.at[49:75], faces.at[49:75])
+    groups = []
+    for k in range(4):
+        spans = ((4 * k, 4), (16 + 4 * k, 4), (32, 5) if k == 0 else (33 + 4 * k, 4))
+        groups.append([copies.start(there.at[a:a + n], faces.at[a:a + n]) for a, n in spans])
+    later = copies.start(there_next.at[25:33], w_next)
     blank = jnp.zeros((HALO - THIN, columns), jnp.float32)
 
     def place(k, value):
@@ -306,6 +342,8 @@
         s[k, HALO - THIN:HALO + strip + THIN] = value
         s[k, HALO + strip + THIN:] = blank
 
+    loop(16, lambda q: place(q + 1, s_own[q]))
+    weights.wait()
     place(0, s_low[0])
     first[0] = halo[8] * s[0]
     place(0, s_high[1])
@@ -316,11 +354,10 @@
     first[18] = halo[7] * s[17]
 
     def start(q):
-        place(q + 1, s_own[q])
         first[q + 2] = w[q] * s[q + 1]
 
     loop(16, start)
-    rest = sweep_and_rest(s, first, total, second, faces, 16)
+    rest = sweep_and_rest(s, first, total, second, faces, 16, groups)
 
     def pair(q):
         s_next[q] = rest(2 * q) + rest(2 * q + 1)
@@ -328,6 +365,7 @@
         fine[q, 1] = second[2 * q + 2, HALO:HALO + strip]
 
     loop(8, pair)
+    later.wait()
     edge_down[0] = s_next[0]
     edge_down[1] = w_next[1] * s_next[1]
     edge_up[0] = w_next[6] * s_next[6]
@@ -367,15 +405,23 @@
     loop(4, pair)
 
 
-def middle_level(s_own, low, high, faces, faces_next, out, s_next, *rest_refs):
-    edges, (s, first, total, second) = rest_refs[:-4], rest_refs[-4:]
+def middle_level(s_own, low, high, there, there_next, out, s_next, *rest_refs):
+    edges, (s, first, total, second, faces, w_next, semaphores) = rest_refs[:-7], rest_refs[-7:]
     count = s_own.shape[0]
-    w_next = parts(faces_next, count // 2)[3]
     strip = out.shape[1]
+    copies = Copies(semaphores)
+    at, size = 3 * count + 1, planes_of(count)
+    weights = copies.start(there.at[at:size], faces.at[at:size])
+    others = copies.start(there.at[0:at], faces.at[0:at])
+    at, size = 3 * (count // 2) + 1, 4 * (count // 2) + 1
+    later = copies.start(there_next.at[at:size], w_next)
+    weights.wait()
     open_level(s_own, faces, low, high, s, first)
+    others.wait()
     rest = sweep_and_rest(s, first, total, second, faces, s_own.shape[0])
     for q in range(count // 2):
         s_next[q] = rest(2 * q) + rest(2 * q + 1)
+    later.wait()
     for q in range(count):
         out[q] = second[q + 1, HALO:HALO + strip]
     if len(edges) == 2:
@@ -388,7 +434,10 @@
         edges[0][0] = w_next[0] * s_next[0]
 
 
-def widen(source2, above, below, faces2, fine, plane_out, s, edge_down, edge_up, back):
+def widen(source2, above, below, faces2, fine, plane_out, s, edge_down, edge_up, back, semaphores):
+    copies = Copies(semaphores)
+    copies.start(fine, back.at[:, 0:2])
+    copies.start(plane_out, back.at[:, 2])
     count, strip, _ = source2.shape
     w2 = parts(faces2, count)[3]
     for q in range(count):
@@ -400,12 +449,8 @@
     edge_up[0] = w2[count - 2] * s[count - 2]
     edge_up[1] = s[count - 1]
 
-    def gather(k):
-        back[k, 0] = fine[k, 0]
-        back[k, 1] = fine[k, 1]
-        back[k, 2] = plane_out[k]
-
-    loop(RING, gather)
+    for copy in copies.started:
+        copy.wait()
 
 
 def sweep_last(s, first, low, high, faces, total, second):
@@ -420,13 +465,19 @@
     out[0] = s[0] - damping * total[0] + neighbours(second[0], low[0], high[0], east[0], north[0], z[0], z[1])
 
 
-def finish(s, first, low, high, faces5, second2, second3, second4, out):
-    strip = out.shape[1]
+def finish(place, s, first, low, high, faces5, second2, second3, second4, *outs):
+    own = slice(HALO, HALO + outs[0].shape[0])
     east, north, down, up, w = (faces5[k] for k in range(5))
-    second5 = w * (1.2 * s[0] + neighbours(first[0], low[0], high[0], east, north, down, up))
-    own = slice(HALO, HALO + strip)
+    second5 = (w * (1.2 * s[0] + neighbours(first[0], low[0], high[0], east, north, down, up)))[own]
     for k in range(RING):
-        out[k] = ((second2[k // 2] + second3[k // 4]) + second4[0, own]) + second5[own]
+        at = (place[0] + k) % RING
+        outs[k][...] = ((second2[at // 2] + second3[at // 4]) + second4[0, own]) + second5
+
+
+def collect(place, *refs):
+    out = refs[RING]
+    for k, ref in zip((0,) + ORDER, refs):
+        out[(place[0] + RING - k) % RING] = ref[...]
 
 
 def exchange(edge_low, edge_high, distance=RING):
@@ -459,16 +510,18 @@
     c, bundle_down, bundle_up, ready = call(join, [shape(16), shape(REACH), shape(REACH), (HALO, columns)], [], place, *c_parts, limit=10, settled=(s_cut,))
     s_own = transposed(after(s_cut, ready))
     c_low, c_high = exchange(bundle_down, bundle_up)
-    faces0, faces1, faces2, faces3, faces4, pack = call(
-        make_faces, [shape(planes_of(n)) for n in (16, 8, 4, 2, 1)] + [shape(3)], [], place, c, c_low, c_high, limit=28, work=12.0)
+    sizes = [shape(planes_of(n)) for n in (16, 8, 4, 2, 1)]
+    faces0, faces1, faces2, faces3, faces4, pack, ready = call(
+        make_faces, sizes + [shape(3), (HALO, columns)], sizes, place, c, c_low, c_high,
+        limit=30, work=12.0, hbm_out=range(5), copies=9)
     (faces5,) = call(make_last_faces, [shape(5)], [], place, faces4, partner(pack))
 
-    s_own = s_own.reshape(RING * planes, thin, columns)
+    s_own = after(s_own, ready).reshape(RING * planes, thin, columns)
     s_low, s_high = exchange(s_own[:2], s_own[-2:])
     fine, s1, edge_down, edge_up = call(
         fine_level, [(RING, planes, strip, columns), shape(8), shape(2), shape(2)],
-        [shape(18), shape(20), shape(16), shape(18)],
-        s_own, s_low, s_high, faces0, faces1, limit=30, work=8.0)
+        [shape(18), shape(20), shape(16), shape(18), shape(75), shape(8)],
+        s_own, s_low, s_high, faces0, faces1, limit=28, work=8.0, hbm_in=(3, 4), copies=14)
 
     low, high = exchange(edge_down, edge_up)
     plane_out, s2, top, bottom = call(
@@ -479,15 +532,18 @@
     above = row_shifted(bottom, 1)
     below = row_shifted(top, -1)
     s2, edge_down, edge_up, back = call(
-        widen, [shape(4), shape(2), shape(2), (RING, planes + 1, strip, columns)], [], s2, above, below, faces2, fine, plane_out, limit=10)
+        widen, [shape(4), shape(2), shape(2), (RING, planes + 1, strip, columns)], [], s2, above, below, faces2, fine, plane_out, limit=10,
+        hbm_out=(3,), copies=2)
     low, high = exchange(edge_down, edge_up)
     second2, s3, edge_down, edge_up = call(
-        middle_level, [(4, strip, columns), shape(2), shape(2), shape(2)], [shape(6), shape(8), shape(4), shape(6)],
-        s2, low, high, faces2, faces3, limit=10)
+        middle_level, [(4, strip, columns), shape(2), shape(2), shape(2)],
+        [shape(6), shape(8), shape(4), shape(6), shape(planes_of(4)), shape(2)],
+        s2, low, high, faces2, faces3, limit=14, hbm_in=(3, 4), copies=3)
     low, high = exchange(edge_down, edge_up)
     second3, s4, first4 = call(
-        middle_level, [(2, strip, columns), shape(1), shape(1)], [shape(4), shape(6), shape(2), shape(4)],
-        s3, low, high, faces3, faces4)
+        middle_level, [(2, strip, columns), shape(1), shape(1)],
+        [shape(4), shape(6), shape(2), shape(4), shape(planes_of(2)), shape(1)],
+        s3, low, high, faces3, faces4, limit=12, hbm_in=(3, 4), copies=3)
     low, high = exchange(first4, first4)
     total4, second4 = call(sweep_last, [shape(1), shape(1)], [], s4, first4, low, high, faces4)
     low, high = exchange(second4, second4)
@@ -495,13 +551,13 @@
     s5, first5 = call(begin_last, [shape(1), shape(1)], [], rest4, partner(rest4), faces5)
     low, high = exchange(first5, first5, 2 * RING)
     back = transposed(back)
-    (summed,) = call(finish, [(RING, strip, columns)], [],
-                     s5, first5, low, high, faces5, second2, second3, second4, settled=(back,))
+    sums = call(finish, [(strip, columns)] * RING, [],
+                place, s5, first5, low, high, faces5, second2, second3, second4, settled=(back,))
+    (coarse_return,) = call(collect, [(RING, strip, columns)], [], place, sums[0], *[ring_permuted(sums[k], k) for k in ORDER])
 
     fine_iterate = jnp.transpose(back[:, :planes], (1, 0, 2, 3)).reshape(planes, rows, columns)
     plane_iterate = back[:, planes].reshape(1, rows, columns)
-    coarse_return = transposed(summed).reshape(1, rows, columns)
-    return fine_iterate, plane_iterate, coarse_return
+    return fine_iterate, plane_iterate, coarse_return.reshape(1, rows, columns)
 
 
 def solution(mesh):

time: 264 us -> 268 us (1.015)
  starting transfers between devices: 110 us -> 123 us
  waiting for transfers between devices: 103 us -> 94.5 us
  Pallas kernels: 27.2 us -> 35.4 us
  local copies, waits for them, and re-layouts: 18.7 us -> 11.7 us
    all_to_all x3 -> x2, waiting for transfers between devices: 45.8 us -> 0.01 us  [transposed(): lax.all_to_all(value, 'gz', 0, 0, axis_index_groups=ring_groups(lax.axis_...]
    ppermute x16, waiting for transfers between devices: 21.9 us -> 57.5 us  [shifted(): return lax.ppermute(value, 'gz', pairs)]
    ppermute x7 -> x14, starting transfers between devices: 23 us -> 41.4 us  [ring_permuted(): lax.ppermute(value, 'gz', [(i, i // RING * RING + (i + by) % RING) for i...]
    pallas_call x14 -> x15, Pallas kernels: 27.2 us -> 35.4 us  [call(): pl.pallas_call(body, out_shape=shapes, in_specs=[pl.BlockSpec(memory_spac...]
    unnamed x33 -> x28, local copies, waits for them, and re-layouts: 16.6 us -> 9.55 us
    all_to_all x3 -> x2, starting transfers between devices: 16.9 us -> 13.1 us  [transposed(): lax.all_to_all(value, 'gz', 0, 0, axis_index_groups=ring_groups(lax.axis_...]
    ppermute x7 -> x14, waiting for transfers between devices: 26.4 us -> 26.7 us  [ring_permuted(): lax.ppermute(value, 'gz', [(i, i // RING * RING + (i + by) % RING) for i...]
  transfers between devices with their start and end apart: 32 -> 38, of which waited for: 24 -> 27; matrix products, arithmetic and copies ran while one was open for 1% -> 1% of each run, Pallas kernels for 6% -> 7%
where the time goes in v8:
time: 268 us; the launch traced here: 267 us
  starting transfers between devices  123 us (46%)
  waiting for transfers between devices  94.5 us (35%)
  Pallas kernels  35.4 us (13%)
  local copies, waits for them, and re-layouts  11.7 us (4%)
    ppermute x16, starting transfers between devices, shifted(): return lax.ppermute(value, 'gz', pairs)  63.2 us
    ppermute x16, waiting for transfers between devices, shifted(): return lax.ppermute(value, 'gz', pairs)  57.5 us
    ppermute x14, starting transfers between devices, ring_permuted(): lax.ppermute(value, 'gz', [(i, i // RING * RING + (i + by) % RING) for i...  41.4 us
    pallas_call x15, Pallas kernels, call(): pl.pallas_call(body, out_shape=shapes, in_specs=[pl.BlockSpec(memory_spac...  35.4 us
    ppermute x14, waiting for transfers between devices, ring_permuted(): lax.ppermute(value, 'gz', [(i, i // RING * RING + (i + by) % RING) for i...  26.7 us
    all_to_all x2, starting transfers between devices, transposed(): lax.all_to_all(value, 'gz', 0, 0, axis_index_groups=ring_groups(lax.axis_...  13.1 us
    unnamed x28, local copies, waits for them, and re-layouts  9.55 us
  transfers between devices with their start and end apart: 38, of which 27 were waited for; matrix products, arithmetic and copies ran while one was open for 1% of the time, Pallas kernels for 7%

profile of v8, /device:TPU:8, one launch (start us, length us, event | category | flops | bytes accessed | tf_op | source)
XLA Modules:
  0.0 266.6 jit_solution(16680441253451430323)
XLA Ops:
  6.4 4.7 %collective-permute-start.2 = (f32[2,48,640]{2,1,0:T(8,128)S(1)}, f32[2,48,640]{2,1,0:T(8,128)S(1)}, u32[]{:S(2)}, u32[]{:S(2)}) collective-permute-start(f32[2,48,640]{2,1,0:T(8,128)S(1)} %get-tuple-element.54), channel_id=1, source_target_pairs={{0,6},{2,8},{4,10},{6,12},{8,14},{10,0},{12,2},{14,4},{16,22},{18,... | collective-permute-start | bytes 737288 | tf_op jit(solution)/shard_map/ppermute | solution.py:127
  13.4 5.5 %collective-permute-start.4 = (f32[2,48,640]{2,1,0:T(8,128)S(1)}, f32[2,48,640]{2,1,0:T(8,128)S(1)}, u32[]{:S(2)}, u32[]{:S(2)}) collective-permute-start(f32[2,48,640]{2,1,0:T(8,128)S(1)} %get-tuple-element.56), channel_id=1, source_target_pairs={{0,8},{2,10},{4,12},{6,14},{8,0},{10,2},{12,4},{14,6},{16,24},{18,... | collective-permute-start | bytes 737288 | tf_op jit(solution)/shard_map/ppermute | solution.py:127
  20.4 2.7 collective-permute-start.6
  23.0 7.7 %collective-permute-done.2.refs_3_ = f32[2,48,640]{2,1,0:T(8,128)S(1)} collective-permute-done((f32[2,48,640]{2,1,0:T(8,128)S(1)}, f32[2,48,640]{2,1,0:T(8,128)S(1)}, u32[]{:S(2)}, u32[]{:S(2)}) %collective-permute-start.2) | collective-permute-done | bytes 245792 | tf_op jit(solution)/shard_map/ppermute | solution.py:127
  30.8 5.0 %collective-permute-start.7 = (f32[2,48,640]{2,1,0:T(8,128)S(1)}, f32[2,48,640]{2,1,0:T(8,128)S(1)}, u32[]{:S(2)}, u32[]{:S(2)}) collective-permute-start(f32[2,48,640]{2,1,0:T(8,128)S(1)} %get-tuple-element.59), channel_id=1, source_target_pairs={{0,2},{2,4},{4,6},{6,8},{8,10},{10,12},{12,14},{14,0},{16,18},{18,... | collective-permute-start | bytes 737288 | tf_op jit(solution)/shard_map/ppermute | solution.py:127
  38.6 3.5 %collective-permute-done.4.refs_5_ = f32[2,48,640]{2,1,0:T(8,128)S(1)} collective-permute-done((f32[2,48,640]{2,1,0:T(8,128)S(1)}, f32[2,48,640]{2,1,0:T(8,128)S(1)}, u32[]{:S(2)}, u32[]{:S(2)}) %collective-permute-start.4) | collective-permute-done | bytes 245792 | tf_op jit(solution)/shard_map/ppermute | solution.py:127
  42.1 9.1 %collective-permute-done.5.refs_6_ = f32[2,48,640]{2,1,0:T(8,128)S(1)} collective-permute-done((f32[2,48,640]{2,1,0:T(8,128)S(1)}, f32[2,48,640]{2,1,0:T(8,128)S(1)}, u32[]{:S(2)}, u32[]{:S(2)}) %collective-permute-start.5) | collective-permute-done | bytes 245792 | tf_op jit(solution)/shard_map/ppermute | solution.py:127
  60.4 6.1 %all-to-all-start = ((f32[8,2,40,640]{3,2,1,0:T(8,128)}), f32[8,2,40,640]{3,2,1,0:T(8,128)S(1)}, u32[]{:S(2)}, u32[]{:S(2)}) async-start(f32[8,2,40,640]{3,2,1,0:T(8,128)} %shard_map.61), calls=%async_computation | async-start | bytes 3276800 | tf_op jit(solution)/shard_map/all_to_all | solution.py:47
  66.5 3.4 %collective-permute-start.9 = (f32[9,48,640]{2,1,0:T(8,128)}, f32[9,48,640]{2,1,0:T(8,128)S(1)}, u32[]{:S(2)}, u32[]{:S(2)}) collective-permute-start(f32[9,48,640]{2,1,0:T(8,128)} %copy-done.11), channel_id=1, source_target_pairs={{0,16},{2,18},{4,20},{6,22},{8,24},{10,26},{12,28},{14,30},{16,32}... | collective-permute-start | bytes 3317768 | tf_op jit(solution)/shard_map/ppermute | solution.py:28
  69.9 4.6 %collective-permute-start.10 = (f32[9,48,640]{2,1,0:T(8,128)S(1)}, f32[9,48,640]{2,1,0:T(8,128)S(1)}, u32[]{:S(2)}, u32[]{:S(2)}) collective-permute-start(f32[9,48,640]{2,1,0:T(8,128)S(1)} %get-tuple-element.64), channel_id=1, source_target_pairs={{16,0},{18,2},{20,4},{22,6},{24,8},{26,10},{28,12},{30,14},{32,16}... | collective-permute-start | bytes 3317768 | tf_op jit(solution)/shard_map/ppermute | solution.py:28
  74.4 21.8 %collective-permute-done.9.refs_2_ = f32[9,48,640]{2,1,0:T(8,128)S(1)} collective-permute-done((f32[9,48,640]{2,1,0:T(8,128)}, f32[9,48,640]{2,1,0:T(8,128)S(1)}, u32[]{:S(2)}, u32[]{:S(2)}) %collective-permute-start.9) | collective-permute-done | bytes 1105952 | tf_op jit(solution)/shard_map/ppermute | solution.py:28
  98.7 11.5 %shard_map.62 = (f32[75,48,640]{2,1,0:T(8,128)}, f32[41,48,640]{2,1,0:T(8,128)}, f32[25,48,640]{2,1,0:T(8,128)}, f32[17,48,640]{2,1,0:T(8,128)}, f32[5,48,640]{2...) custom-call(s32[2]{0:T(128)S(1)} %pad_add_fusion.refs_0_.refs_1_, f32[16,48,640]{2,1,0:T(8,128)S(1)} %copy-done.10, ...), custom_call_target="tpu_custom_call" | custom-call | flops 12000000000 | bytes 36000000 | tf_op jit(solution)/shard_map/pallas_call | solution.py:111
  110.3 6.8 %collective-permute-start.12 = (f32[2,40,640]{2,1,0:T(8,128)S(1)}, f32[2,40,640]{2,1,0:T(8,128)S(1)}, u32[]{:S(2)}, u32[]{:S(2)}) collective-permute-start(f32[2,40,640]{2,1,0:T(8,128)S(1)} %get-tuple-element.103), channel_id=1, source_target_pairs={{16,0},{18,2},{20,4},{22,6},{24,8},{26,10},{28,12},{30,14},{32,16}... | collective-permute-start | bytes 614408 | tf_op jit(solution)/shard_map/ppermute | solution.py:28
  120.4 6.5 %collective-permute-done.11.refs_1_ = f32[2,40,640]{2,1,0:T(8,128)S(1)} collective-permute-done((f32[2,40,640]{2,1,0:T(8,128)S(1)}, f32[2,40,640]{2,1,0:T(8,128)S(1)}, u32[]{:S(2)}, u32[]{:S(2)}) %collective-permute-start.11) | collective-permute-done | bytes 204832 | tf_op jit(solution)/shard_map/ppermute | solution.py:28
  126.9 7.8 %shard_map.64 = (f32[8,2,32,640]{3,2,1,0:T(8,128)S(1)}, f32[8,48,640]{2,1,0:T(8,128)S(1)}, f32[2,48,640]{2,1,0:T(8,128)S(1)}, f32[2,48,640]{2,1,0:T(8,128)S(1)}) custom-call(f32[16,40,640]{2,1,0:T(8,128)S(1)} %bitcast.12, f32[2,40,640]{2,1,0:T(8,128)S(1)} %collective-permute-done.11.refs_1_, f32[2,40,640]{2,1,0:T(8,128)S(1)} %collective-permute-done.12.refs_2_, ...), custom_call_target="tpu_custom_call" | custom-call | flops 8000000000 | bytes 24000000 | tf_op jit(solution)/shard_map/pallas_call | solution.py:111
  136.8 6.0 %collective-permute-start.14 = (f32[2,48,640]{2,1,0:T(8,128)S(1)}, f32[2,48,640]{2,1,0:T(8,128)S(1)}, u32[]{:S(2)}, u32[]{:S(2)}) collective-permute-start(f32[2,48,640]{2,1,0:T(8,128)S(1)} %get-tuple-element.70), channel_id=1, source_target_pairs={{16,0},{18,2},{20,4},{22,6},{24,8},{26,10},{28,12},{30,14},{32,16}... | collective-permute-start | bytes 737288 | tf_op jit(solution)/shard_map/ppermute | solution.py:28
  149.2 3.6 %collective-permute-start.15 = (f32[4,8,640]{2,1,0:T(8,128)S(1)}, f32[4,8,640]{2,1,0:T(8,128)S(1)}, u32[]{:S(2)}, u32[]{:S(2)}) collective-permute-start(f32[4,8,640]{2,1,0:T(8,128)S(1)} %get-tuple-element.72), channel_id=1, source_target_pairs={{0,2},{2,4},{4,6},{6,8},{8,10},{10,12},{12,14},{14,1},{1,3},{3,5},... | collective-permute-start | bytes 245768 | tf_op jit(solution)/shard_map/ppermute | solution.py:38
  154.9 4.3 %collective-permute-done.16.refs_2_ = f32[4,8,640]{2,1,0:T(8,128)S(1)} collective-permute-done((f32[4,8,640]{2,1,0:T(8,128)S(1)}, f32[4,8,640]{2,1,0:T(8,128)S(1)}, u32[]{:S(2)}, u32[]{:S(2)}) %collective-permute-start.16) | collective-permute-done | bytes 81952 | tf_op jit(solution)/shard_map/ppermute | solution.py:38
  160.6 7.0 %all-to-all-start.1 = ((f32[8,3,32,640]{3,2,1,0:T(8,128)}), f32[8,3,32,640]{3,2,1,0:T(8,128)S(1)}, u32[]{:S(2)}, u32[]{:S(2)}) async-start(f32[8,3,32,640]{3,2,1,0:T(8,128)} %get-tuple-element.77), calls=%async_computation.1 | async-start | bytes 3932160 | tf_op jit(solution)/shard_map/all_to_all | solution.py:47
  169.5 6.5 %collective-permute-start.18 = (f32[2,48,640]{2,1,0:T(8,128)S(1)}, f32[2,48,640]{2,1,0:T(8,128)S(1)}, u32[]{:S(2)}, u32[]{:S(2)}) collective-permute-start(f32[2,48,640]{2,1,0:T(8,128)S(1)} %get-tuple-element.80), channel_id=1, source_target_pairs={{16,0},{18,2},{20,4},{22,6},{24,8},{26,10},{28,12},{30,14},{32,16}... | collective-permute-start | bytes 737288 | tf_op jit(solution)/shard_map/ppermute | solution.py:28
  179.7 3.2 %shard_map.67 = (f32[4,32,640]{2,1,0:T(8,128)S(1)}, f32[2,48,640]{2,1,0:T(8,128)S(1)}, f32[2,48,640]{2,1,0:T(8,128)S(1)}, f32[2,48,640]{2,1,0:T(8,128)S(1)}) custom-call(f32[4,48,640]{2,1,0:T(8,128)S(1)} %get-tuple-element.78.refs_0_, f32[2,48,640]{2,1,0:T(8,128)S(1)} %collective-permute-done.17.refs_1_, f32[2,48,640]{2,1,0:T(8,128)S(1)} %collective-permute-done.18.refs_2_, ...), custom_call_target="tpu_custom_call" | custom-call | tf_op jit(solution)/shard_map/pallas_call | solution.py:111
  182.9 3.9 %collective-permute-start.19 = (f32[2,48,640]{2,1,0:T(8,128)S(1)}, f32[2,48,640]{2,1,0:T(8,128)S(1)}, u32[]{:S(2)}, u32[]{:S(2)}) collective-permute-start(f32[2,48,640]{2,1,0:T(8,128)S(1)} %get-tuple-element.83), channel_id=1, source_target_pairs={{0,16},{2,18},{4,20},{6,22},{8,24},{10,26},{12,28},{14,30},{16,32}... | collective-permute-start | bytes 737288 | tf_op jit(solution)/shard_map/ppermute | solution.py:28
  186.9 4.5 %collective-permute-start.20 = (f32[2,48,640]{2,1,0:T(8,128)S(1)}, f32[2,48,640]{2,1,0:T(8,128)S(1)}, u32[]{:S(2)}, u32[]{:S(2)}) collective-permute-start(f32[2,48,640]{2,1,0:T(8,128)S(1)} %get-tuple-element.84), channel_id=1, source_target_pairs={{16,0},{18,2},{20,4},{22,6},{24,8},{26,10},{28,12},{30,14},{32,16}... | collective-permute-start | bytes 737288 | tf_op jit(solution)/shard_map/ppermute | solution.py:28
  197.5 6.5 %collective-permute-start.22 = (f32[1,48,640]{2,1,0:T(8,128)S(1)}, f32[1,48,640]{2,1,0:T(8,128)S(1)}, u32[]{:S(2)}, u32[]{:S(2)}) collective-permute-start(f32[1,48,640]{2,1,0:T(8,128)S(1)} %get-tuple-element.87.refs_1_), channel_id=1, source_target_pairs={{16,0},{18,2},{20,4},{22,6},{24,8},{26,10},{28,12},{30,14},{32,16}... | collective-permute-start | bytes 368648 | tf_op jit(solution)/shard_map/ppermute | solution.py:28
  206.4 6.5 %collective-permute-done.21.refs_2_ = f32[1,48,640]{2,1,0:T(8,128)S(1)} collective-permute-done((f32[1,48,640]{2,1,0:T(8,128)S(1)}, f32[1,48,640]{2,1,0:T(8,128)S(1)}, u32[]{:S(2)}, u32[]{:S(2)}) %collective-permute-start.21) | collective-permute-done | bytes 122912 | tf_op jit(solution)/shard_map/ppermute | solution.py:28
  215.0 3.9 %collective-permute-start.23 = (f32[1,48,640]{2,1,0:T(8,128)S(1)}, f32[1,48,640]{2,1,0:T(8,128)S(1)}, u32[]{:S(2)}, u32[]{:S(2)}) collective-permute-start(f32[1,48,640]{2,1,0:T(8,128)S(1)} %get-tuple-element.89.refs_2_.refs_9_), channel_id=1, source_target_pairs={{0,16},{2,18},{4,20},{6,22},{8,24},{10,26},{12,28},{14,30},{16,32}... | collective-permute-start | bytes 368648 | tf_op jit(solution)/shard_map/ppermute | solution.py:28
  219.9 5.0 %collective-permute-done.23.refs_3_ = f32[1,48,640]{2,1,0:T(8,128)S(1)} collective-permute-done((f32[1,48,640]{2,1,0:T(8,128)S(1)}, f32[1,48,640]{2,1,0:T(8,128)S(1)}, u32[]{:S(2)}, u32[]{:S(2)}) %collective-permute-start.23) | collective-permute-done | bytes 122912 | tf_op jit(solution)/shard_map/ppermute | solution.py:28
  225.8 4.2 %collective-permute-done.25.refs_1_ = f32[1,48,640]{2,1,0:T(8,128)S(1)} collective-permute-done((f32[1,48,640]{2,1,0:T(8,128)S(1)}, f32[1,48,640]{2,1,0:T(8,128)S(1)}, u32[]{:S(2)}, u32[]{:S(2)}) %collective-permute-start.25) | collective-permute-done | bytes 122912 | tf_op jit(solution)/shard_map/ppermute | solution.py:43
  231.9 5.4 %collective-permute-start.27 = (f32[1,48,640]{2,1,0:T(8,128)S(1)}, f32[1,48,640]{2,1,0:T(8,128)S(1)}, u32[]{:S(2)}, u32[]{:S(2)}) collective-permute-start(f32[1,48,640]{2,1,0:T(8,128)S(1)} %get-tuple-element.92.refs_3_), channel_id=1, source_target_pairs={{0,32},{2,34},{4,36},{6,38},{8,40},{10,42},{12,44},{14,46},{16,48}... | collective-permute-start | bytes 368648 | tf_op jit(solution)/shard_map/ppermute | solution.py:28
  244.3 3.9 %collective-permute-start.29 = (f32[32,640]{1,0:T(8,128)S(1)}, f32[32,640]{1,0:T(8,128)S(1)}, u32[]{:S(2)}, u32[]{:S(2)}) collective-permute-start(f32[32,640]{1,0:T(8,128)S(1)} %get-tuple-element.96), channel_id=1, source_target_pairs={{0,6},{2,8},{4,10},{6,12},{8,14},{10,0},{12,2},{14,4},{16,22},{18,... | collective-permute-start | bytes 245768 | tf_op jit(solution)/shard_map/ppermute | solution.py:127
  249.7 5.7 %collective-permute-start.31 = (f32[32,640]{1,0:T(8,128)S(1)}, f32[32,640]{1,0:T(8,128)S(1)}, u32[]{:S(2)}, u32[]{:S(2)}) collective-permute-start(f32[32,640]{1,0:T(8,128)S(1)} %get-tuple-element.98), channel_id=1, source_target_pairs={{0,8},{2,10},{4,12},{6,14},{8,0},{10,2},{12,4},{14,6},{16,24},{18,... | collective-permute-start | bytes 245768 | tf_op jit(solution)/shard_map/ppermute | solution.py:127
  256.1 3.4 %collective-permute-start.33 = (f32[32,640]{1,0:T(8,128)S(1)}, f32[32,640]{1,0:T(8,128)S(1)}, u32[]{:S(2)}, u32[]{:S(2)}) collective-permute-start(f32[32,640]{1,0:T(8,128)S(1)} %get-tuple-element.100), channel_id=1, source_target_pairs={{0,12},{2,14},{4,0},{6,2},{8,4},{10,6},{12,8},{14,10},{16,28},{18,... | collective-permute-start | bytes 245768 | tf_op jit(solution)/shard_map/ppermute | solution.py:127
  (99 shorter events, 75.4 us)
Async XLA Ops:
  6.4 24.4 %collective-permute-start.2 = (f32[2,48,640]{2,1,0:T(8,128)S(1)}, f32[2,48,640]{2,1,0:T(8,128)S(1)}, u32[]{:S(2)}, u32[]{:S(2)}) collective-permute-start(f32[2,48,640]{2,1,0:T(8,128)S(1)} %get-tuple-element.54), channel_id=1, source_target_pairs={{0,6},{2,8},{4,10},{6,12},{8,14},{10,0},{12,2},{14,4},{16,22},{18,... | collective-permute-start | bytes 737288 | tf_op jit(solution)/shard_map/ppermute | solution.py:127
  11.1 24.7 %collective-permute-start.3 = (f32[2,48,640]{2,1,0:T(8,128)S(1)}, f32[2,48,640]{2,1,0:T(8,128)S(1)}, u32[]{:S(2)}, u32[]{:S(2)}) collective-permute-start(f32[2,48,640]{2,1,0:T(8,128)S(1)} %get-tuple-element.55), channel_id=1, source_target_pairs={{0,10},{2,12},{4,14},{6,0},{8,2},{10,4},{12,6},{14,8},{16,26},{18,... | collective-permute-start | bytes 737288 | tf_op jit(solution)/shard_map/ppermute | solution.py:127
  13.3 7.1 %collective-permute-start = (f32[2,8,640]{2,1,0:T(8,128)S(1)}, f32[2,8,640]{2,1,0:T(8,128)S(1)}, u32[]{:S(2)}, u32[]{:S(2)}) collective-permute-start(f32[2,8,640]{2,1,0:T(8,128)S(1)} %slice_select_fusion), channel_id=1, source_target_pairs={{0,1},{1,0},{2,3},{3,2},{4,5},{5,4},{6,7},{7,6},{8,9},{9,8},{10,11... | collective-permute-start | bytes 122888 | tf_op jit(solution)/shard_map/ppermute | solution.py:494
  13.4 28.7 %collective-permute-start.4 = (f32[2,48,640]{2,1,0:T(8,128)S(1)}, f32[2,48,640]{2,1,0:T(8,128)S(1)}, u32[]{:S(2)}, u32[]{:S(2)}) collective-permute-start(f32[2,48,640]{2,1,0:T(8,128)S(1)} %get-tuple-element.56), channel_id=1, source_target_pairs={{0,8},{2,10},{4,12},{6,14},{8,0},{10,2},{12,4},{14,6},{16,24},{18,... | collective-permute-start | bytes 737288 | tf_op jit(solution)/shard_map/ppermute | solution.py:127
  18.9 32.3 %collective-permute-start.5 = (f32[2,48,640]{2,1,0:T(8,128)S(1)}, f32[2,48,640]{2,1,0:T(8,128)S(1)}, u32[]{:S(2)}, u32[]{:S(2)}) collective-permute-start(f32[2,48,640]{2,1,0:T(8,128)S(1)} %get-tuple-element.57), channel_id=1, source_target_pairs={{0,4},{2,6},{4,8},{6,10},{8,12},{10,14},{12,0},{14,2},{16,20},{18,... | collective-permute-start | bytes 737288 | tf_op jit(solution)/shard_map/ppermute | solution.py:127
  20.4 32.6 %collective-permute-start.6 = (f32[2,48,640]{2,1,0:T(8,128)S(1)}, f32[2,48,640]{2,1,0:T(8,128)S(1)}, u32[]{:S(2)}, u32[]{:S(2)}) collective-permute-start(f32[2,48,640]{2,1,0:T(8,128)S(1)} %get-tuple-element.58), channel_id=1, source_target_pairs={{0,12},{2,14},{4,0},{6,2},{8,4},{10,6},{12,8},{14,10},{16,28},{18,... | collective-permute-start | bytes 737288 | tf_op jit(solution)/shard_map/ppermute | solution.py:127
  30.8 24.8 %collective-permute-start.7 = (f32[2,48,640]{2,1,0:T(8,128)S(1)}, f32[2,48,640]{2,1,0:T(8,128)S(1)}, u32[]{:S(2)}, u32[]{:S(2)}) collective-permute-start(f32[2,48,640]{2,1,0:T(8,128)S(1)} %get-tuple-element.59), channel_id=1, source_target_pairs={{0,2},{2,4},{4,6},{6,8},{8,10},{10,12},{12,14},{14,0},{16,18},{18,... | collective-permute-start | bytes 737288 | tf_op jit(solution)/shard_map/ppermute | solution.py:127
  35.8 21.5 %collective-permute-start.8 = (f32[2,48,640]{2,1,0:T(8,128)S(1)}, f32[2,48,640]{2,1,0:T(8,128)S(1)}, u32[]{:S(2)}, u32[]{:S(2)}) collective-permute-start(f32[2,48,640]{2,1,0:T(8,128)S(1)} %get-tuple-element.60), channel_id=1, source_target_pairs={{0,14},{2,0},{4,2},{6,4},{8,6},{10,8},{12,10},{14,12},{16,30},{18,... | collective-permute-start | bytes 737288 | tf_op jit(solution)/shard_map/ppermute | solution.py:127
  60.4 49.9 %all-to-all-start = ((f32[8,2,40,640]{3,2,1,0:T(8,128)}), f32[8,2,40,640]{3,2,1,0:T(8,128)S(1)}, u32[]{:S(2)}, u32[]{:S(2)}) async-start(f32[8,2,40,640]{3,2,1,0:T(8,128)} %shard_map.61), calls=%async_computation | async-start | bytes 3276800 | tf_op jit(solution)/shard_map/all_to_all | solution.py:47
  66.5 29.7 %collective-permute-start.9 = (f32[9,48,640]{2,1,0:T(8,128)}, f32[9,48,640]{2,1,0:T(8,128)S(1)}, u32[]{:S(2)}, u32[]{:S(2)}) collective-permute-start(f32[9,48,640]{2,1,0:T(8,128)} %copy-done.11), channel_id=1, source_target_pairs={{0,16},{2,18},{4,20},{6,22},{8,24},{10,26},{12,28},{14,30},{16,32}... | collective-permute-start | bytes 3317768 | tf_op jit(solution)/shard_map/ppermute | solution.py:28
  69.9 27.3 %collective-permute-start.10 = (f32[9,48,640]{2,1,0:T(8,128)S(1)}, f32[9,48,640]{2,1,0:T(8,128)S(1)}, u32[]{:S(2)}, u32[]{:S(2)}) collective-permute-start(f32[9,48,640]{2,1,0:T(8,128)S(1)} %get-tuple-element.64), channel_id=1, source_target_pairs={{16,0},{18,2},{20,4},{22,6},{24,8},{26,10},{28,12},{30,14},{32,16}... | collective-permute-start | bytes 3317768 | tf_op jit(solution)/shard_map/ppermute | solution.py:28
  110.3 10.0 %collective-permute-start.12 = (f32[2,40,640]{2,1,0:T(8,128)S(1)}, f32[2,40,640]{2,1,0:T(8,128)S(1)}, u32[]{:S(2)}, u32[]{:S(2)}) collective-permute-start(f32[2,40,640]{2,1,0:T(8,128)S(1)} %get-tuple-element.103), channel_id=1, source_target_pairs={{16,0},{18,2},{20,4},{22,6},{24,8},{26,10},{28,12},{30,14},{32,16}... | collective-permute-start | bytes 614408 | tf_op jit(solution)/shard_map/ppermute | solution.py:28
  117.1 9.8 %collective-permute-start.11 = (f32[2,40,640]{2,1,0:T(8,128)S(1)}, f32[2,40,640]{2,1,0:T(8,128)S(1)}, u32[]{:S(2)}, u32[]{:S(2)}) collective-permute-start(f32[2,40,640]{2,1,0:T(8,128)S(1)} %get-tuple-element.104), channel_id=1, source_target_pairs={{0,16},{2,18},{4,20},{6,22},{8,24},{10,26},{12,28},{14,30},{16,32}... | collective-permute-start | bytes 614408 | tf_op jit(solution)/shard_map/ppermute | solution.py:28
  134.7 10.2 %collective-permute-start.13 = (f32[2,48,640]{2,1,0:T(8,128)S(1)}, f32[2,48,640]{2,1,0:T(8,128)S(1)}, u32[]{:S(2)}, u32[]{:S(2)}) collective-permute-start(f32[2,48,640]{2,1,0:T(8,128)S(1)} %get-tuple-element.69), channel_id=1, source_target_pairs={{0,16},{2,18},{4,20},{6,22},{8,24},{10,26},{12,28},{14,30},{16,32}... | collective-permute-start | bytes 737288 | tf_op jit(solution)/shard_map/ppermute | solution.py:28
  136.8 9.7 %collective-permute-start.14 = (f32[2,48,640]{2,1,0:T(8,128)S(1)}, f32[2,48,640]{2,1,0:T(8,128)S(1)}, u32[]{:S(2)}, u32[]{:S(2)}) collective-permute-start(f32[2,48,640]{2,1,0:T(8,128)S(1)} %get-tuple-element.70), channel_id=1, source_target_pairs={{16,0},{18,2},{20,4},{22,6},{24,8},{26,10},{28,12},{30,14},{32,16}... | collective-permute-start | bytes 737288 | tf_op jit(solution)/shard_map/ppermute | solution.py:28
  160.6 81.2 %all-to-all-start.1 = ((f32[8,3,32,640]{3,2,1,0:T(8,128)}), f32[8,3,32,640]{3,2,1,0:T(8,128)S(1)}, u32[]{:S(2)}, u32[]{:S(2)}) async-start(f32[8,3,32,640]{3,2,1,0:T(8,128)} %get-tuple-element.77), calls=%async_computation.1 | async-start | bytes 3932160 | tf_op jit(solution)/shard_map/all_to_all | solution.py:47
  167.6 10.7 %collective-permute-start.17 = (f32[2,48,640]{2,1,0:T(8,128)S(1)}, f32[2,48,640]{2,1,0:T(8,128)S(1)}, u32[]{:S(2)}, u32[]{:S(2)}) collective-permute-start(f32[2,48,640]{2,1,0:T(8,128)S(1)} %get-tuple-element.79), channel_id=1, source_target_pairs={{0,16},{2,18},{4,20},{6,22},{8,24},{10,26},{12,28},{14,30},{16,32}... | collective-permute-start | bytes 737288 | tf_op jit(solution)/shard_map/ppermute | solution.py:28
  169.5 10.2 %collective-permute-start.18 = (f32[2,48,640]{2,1,0:T(8,128)S(1)}, f32[2,48,640]{2,1,0:T(8,128)S(1)}, u32[]{:S(2)}, u32[]{:S(2)}) collective-permute-start(f32[2,48,640]{2,1,0:T(8,128)S(1)} %get-tuple-element.80), channel_id=1, source_target_pairs={{16,0},{18,2},{20,4},{22,6},{24,8},{26,10},{28,12},{30,14},{32,16}... | collective-permute-start | bytes 737288 | tf_op jit(solution)/shard_map/ppermute | solution.py:28
  182.9 10.7 %collective-permute-start.19 = (f32[2,48,640]{2,1,0:T(8,128)S(1)}, f32[2,48,640]{2,1,0:T(8,128)S(1)}, u32[]{:S(2)}, u32[]{:S(2)}) collective-permute-start(f32[2,48,640]{2,1,0:T(8,128)S(1)} %get-tuple-element.83), channel_id=1, source_target_pairs={{0,16},{2,18},{4,20},{6,22},{8,24},{10,26},{12,28},{14,30},{16,32}... | collective-permute-start | bytes 737288 | tf_op jit(solution)/shard_map/ppermute | solution.py:28
  186.9 8.2 %collective-permute-start.20 = (f32[2,48,640]{2,1,0:T(8,128)S(1)}, f32[2,48,640]{2,1,0:T(8,128)S(1)}, u32[]{:S(2)}, u32[]{:S(2)}) collective-permute-start(f32[2,48,640]{2,1,0:T(8,128)S(1)} %get-tuple-element.84), channel_id=1, source_target_pairs={{16,0},{18,2},{20,4},{22,6},{24,8},{26,10},{28,12},{30,14},{32,16}... | collective-permute-start | bytes 737288 | tf_op jit(solution)/shard_map/ppermute | solution.py:28
  197.5 8.9 %collective-permute-start.22 = (f32[1,48,640]{2,1,0:T(8,128)S(1)}, f32[1,48,640]{2,1,0:T(8,128)S(1)}, u32[]{:S(2)}, u32[]{:S(2)}) collective-permute-start(f32[1,48,640]{2,1,0:T(8,128)S(1)} %get-tuple-element.87.refs_1_), channel_id=1, source_target_pairs={{16,0},{18,2},{20,4},{22,6},{24,8},{26,10},{28,12},{30,14},{32,16}... | collective-permute-start | bytes 368648 | tf_op jit(solution)/shard_map/ppermute | solution.py:28
  204.0 8.9 %collective-permute-start.21 = (f32[1,48,640]{2,1,0:T(8,128)S(1)}, f32[1,48,640]{2,1,0:T(8,128)S(1)}, u32[]{:S(2)}, u32[]{:S(2)}) collective-permute-start(f32[1,48,640]{2,1,0:T(8,128)S(1)} %get-tuple-element.87.refs_1_), channel_id=1, source_target_pairs={{0,16},{2,18},{4,20},{6,22},{8,24},{10,26},{12,28},{14,30},{16,32}... | collective-permute-start | bytes 368648 | tf_op jit(solution)/shard_map/ppermute | solution.py:28
  205.9 19.2 %collective-permute-start.26 = (f32[3,48,640]{2,1,0:T(8,128)S(1)}, f32[3,48,640]{2,1,0:T(8,128)S(1)}, u32[]{:S(2)}, u32[]{:S(2)}) collective-permute-start(f32[3,48,640]{2,1,0:T(8,128)S(1)} %get-tuple-element.90), channel_id=1, source_target_pairs={{0,16},{2,18},{4,20},{6,22},{8,24},{10,26},{12,28},{14,30},{16,0},... | collective-permute-start | bytes 1105928 | tf_op jit(solution)/shard_map/ppermute | solution.py:43
  213.1 6.8 %collective-permute-start.24 = (f32[1,48,640]{2,1,0:T(8,128)S(1)}, f32[1,48,640]{2,1,0:T(8,128)S(1)}, u32[]{:S(2)}, u32[]{:S(2)}) collective-permute-start(f32[1,48,640]{2,1,0:T(8,128)S(1)} %get-tuple-element.89.refs_2_.refs_9_), channel_id=1, source_target_pairs={{16,0},{18,2},{20,4},{22,6},{24,8},{26,10},{28,12},{30,14},{32,16}... | collective-permute-start | bytes 368648 | tf_op jit(solution)/shard_map/ppermute | solution.py:28
  215.0 9.8 %collective-permute-start.23 = (f32[1,48,640]{2,1,0:T(8,128)S(1)}, f32[1,48,640]{2,1,0:T(8,128)S(1)}, u32[]{:S(2)}, u32[]{:S(2)}) collective-permute-start(f32[1,48,640]{2,1,0:T(8,128)S(1)} %get-tuple-element.89.refs_2_.refs_9_), channel_id=1, source_target_pairs={{0,16},{2,18},{4,20},{6,22},{8,24},{10,26},{12,28},{14,30},{16,32}... | collective-permute-start | bytes 368648 | tf_op jit(solution)/shard_map/ppermute | solution.py:28
  230.0 8.3 %collective-permute-start.28 = (f32[1,48,640]{2,1,0:T(8,128)S(1)}, f32[1,48,640]{2,1,0:T(8,128)S(1)}, u32[]{:S(2)}, u32[]{:S(2)}) collective-permute-start(f32[1,48,640]{2,1,0:T(8,128)S(1)} %get-tuple-element.92.refs_3_), channel_id=1, source_target_pairs={{32,0},{34,2},{36,4},{38,6},{40,8},{42,10},{44,12},{46,14},{48,16}... | collective-permute-start | bytes 368648 | tf_op jit(solution)/shard_map/ppermute | solution.py:28
  231.9 9.2 %collective-permute-start.27 = (f32[1,48,640]{2,1,0:T(8,128)S(1)}, f32[1,48,640]{2,1,0:T(8,128)S(1)}, u32[]{:S(2)}, u32[]{:S(2)}) collective-permute-start(f32[1,48,640]{2,1,0:T(8,128)S(1)} %get-tuple-element.92.refs_3_), channel_id=1, source_target_pairs={{0,32},{2,34},{4,36},{6,38},{8,40},{10,42},{12,44},{14,46},{16,48}... | collective-permute-start | bytes 368648 | tf_op jit(solution)/shard_map/ppermute | solution.py:28
  244.3 15.2 %collective-permute-start.29 = (f32[32,640]{1,0:T(8,128)S(1)}, f32[32,640]{1,0:T(8,128)S(1)}, u32[]{:S(2)}, u32[]{:S(2)}) collective-permute-start(f32[32,640]{1,0:T(8,128)S(1)} %get-tuple-element.96), channel_id=1, source_target_pairs={{0,6},{2,8},{4,10},{6,12},{8,14},{10,0},{12,2},{14,4},{16,22},{18,... | collective-permute-start | bytes 245768 | tf_op jit(solution)/shard_map/ppermute | solution.py:127
  248.2 12.0 %collective-permute-start.30 = (f32[32,640]{1,0:T(8,128)S(1)}, f32[32,640]{1,0:T(8,128)S(1)}, u32[]{:S(2)}, u32[]{:S(2)}) collective-permute-start(f32[32,640]{1,0:T(8,128)S(1)} %get-tuple-element.97), channel_id=1, source_target_pairs={{0,10},{2,12},{4,14},{6,0},{8,2},{10,4},{12,6},{14,8},{16,26},{18,... | collective-permute-start | bytes 245768 | tf_op jit(solution)/shard_map/ppermute | solution.py:127
  249.7 15.2 %collective-permute-start.31 = (f32[32,640]{1,0:T(8,128)S(1)}, f32[32,640]{1,0:T(8,128)S(1)}, u32[]{:S(2)}, u32[]{:S(2)}) collective-permute-start(f32[32,640]{1,0:T(8,128)S(1)} %get-tuple-element.98), channel_id=1, source_target_pairs={{0,8},{2,10},{4,12},{6,14},{8,0},{10,2},{12,4},{14,6},{16,24},{18,... | collective-permute-start | bytes 245768 | tf_op jit(solution)/shard_map/ppermute | solution.py:127
  255.4 9.5 %collective-permute-start.32 = (f32[32,640]{1,0:T(8,128)S(1)}, f32[32,640]{1,0:T(8,128)S(1)}, u32[]{:S(2)}, u32[]{:S(2)}) collective-permute-start(f32[32,640]{1,0:T(8,128)S(1)} %get-tuple-element.99), channel_id=1, source_target_pairs={{0,4},{2,6},{4,8},{6,10},{8,12},{10,14},{12,0},{14,2},{16,20},{18,... | collective-permute-start | bytes 245768 | tf_op jit(solution)/shard_map/ppermute | solution.py:127
  256.1 8.8 %collective-permute-start.33 = (f32[32,640]{1,0:T(8,128)S(1)}, f32[32,640]{1,0:T(8,128)S(1)}, u32[]{:S(2)}, u32[]{:S(2)}) collective-permute-start(f32[32,640]{1,0:T(8,128)S(1)} %get-tuple-element.100), channel_id=1, source_target_pairs={{0,12},{2,14},{4,0},{6,2},{8,4},{10,6},{12,8},{14,10},{16,28},{18,... | collective-permute-start | bytes 245768 | tf_op jit(solution)/shard_map/ppermute | solution.py:127
  (20 other events, 132.6 us)

commit v9 on v8

--- a/solution.py
+++ b/solution.py
@@ -9,7 +9,7 @@
 
 RING = 8
 HALO = 8
-REACH = 9
+NEAR, FAR = 3, 6
 THIN = 4
 damping = 0.8
 pore_value = 1.0
@@ -180,15 +180,17 @@
 
 
 def join(place, *refs):
-    out, low, high, ready = refs[RING:]
+    c, near_low, near_high, far_low, far_high, ready, out, semaphores = refs[RING:]
     ready[...] = refs[0][0, :HALO]
     for k, ref in zip((0,) + ORDER, refs):
         start = ((place[0] + RING - k) % RING) * 2
         out[start] = ref[0]
         out[start + 1] = ref[1]
-    reach = low.shape[0]
-    loop(reach, lambda p: low.__setitem__(p, out[p]))
-    loop(reach, lambda p: high.__setitem__(p, out[p + 16 - reach]))
+    copies = Copies(semaphores)
+    for ref, first in ((near_low, 0), (near_high, 16 - NEAR), (far_low, NEAR), (far_high, 16 - NEAR - FAR), (c, 0)):
+        copies.start(out.at[first:first + ref.shape[0]], ref)
+    for copy in copies.started:
+        copy.wait()
 
 
 def plane_faces(c):
@@ -199,21 +201,25 @@
 def parts(faces, count):
     east, north = faces.at[0:count], faces.at[count:2 * count]
     z, w = faces.at[2 * count:3 * count + 1], faces.at[3 * count + 1:4 * count + 1]
-    return east, north, z, w, faces.at[4 * count + 1:] if count > 1 else None
+    return east, north, z, w, faces.at[4 * count + 1:] if faces.shape[0] > 4 * count + 1 else None
 
 
 def planes_of(count):
     return 4 * count + 1 + (0 if count == 1 else 10 if count == 16 else 8)
 
 
-def make_faces(place, c, low, high, out0, out1, out2, out3, out4, pack, ready, faces0, faces1, faces2, faces3, faces4, semaphores):
+def own_planes_of(count):
+    return planes_of(count) if count > 4 else 4 * count + 1
+
+
+def make_faces(place, c, low, high, out0, out1, out2, out3, out4, pack, edge, faces0, faces1, faces2, faces3, faces4, semaphores):
     east0, north0, z0, w0, halo0 = parts(faces0, 16)
 
     def z_face(p):
         z0[p] = harmonic(c[p - 1], c[p])
 
     loop(15, lambda k: z_face(k + 1))
-    z0[0] = jnp.where(low[REACH - 1] > 0, harmonic(low[REACH - 1], c[0]), 2.0 * c[0])
+    z0[0] = jnp.where(low[NEAR - 1] > 0, harmonic(low[NEAR - 1], c[0]), 2.0 * c[0])
     z0[16] = jnp.where(high[0] > 0, harmonic(c[15], high[0]), 2.0 * c[15])
 
     def weigh(p):
@@ -247,38 +253,58 @@
     copies.start(faces3.at[0:9], out3.at[0:9])
     copies.start(faces4, out4)
 
-    for side, ref, at, face in ((0, low, [REACH - 1 - k for k in range(REACH)], 0), (1, high, list(range(REACH)), 16)):
+    for side, ref, at, face in ((0, low, (2, 1, 0), 0), (1, high, (0, 1, 2), 16)):
         shared = z0[face]
-        near = ref[at[0]]
-        middle = harmonic(near, ref[at[1]])
-        east_sum, north_sum = plane_faces(near)
-        halo0[side] = east_sum
-        halo0[2 + side] = north_sum
+        near, after_near, third = (ref[k] for k in at)
+        middle = harmonic(near, after_near)
+        outer = harmonic(after_near, third)
+        east_near, north_near = plane_faces(near)
+        east_next, north_next = plane_faces(after_near)
+        east_sum, north_sum = east_near + east_next, north_near + north_next
+        halo0[side] = east_near
+        halo0[2 + side] = north_near
         halo0[4 + side] = middle
-        halo0[6 + side] = weight(near, east_sum, north_sum, shared, middle)
-        thick = 1
-        for faces, count in ((faces1, 8), (faces2, 4), (faces3, 2)):
-            for k in range(thick, 2 * thick):
-                east_k, north_k = plane_faces(ref[at[k]])
-                if k == 1:
-                    halo0[8 + side] = weight(ref[at[1]], east_k, north_k, middle, harmonic(ref[at[1]], ref[at[2]]))
-                east_sum = east_sum + east_k
-                north_sum = north_sum + north_k
-            thick *= 2
-            halo = parts(faces, count)[4]
-            outer = harmonic(ref[at[thick - 1]], ref[at[thick]])
+        halo0[6 + side] = weight(near, east_near, north_near, shared, middle)
+        halo0[8 + side] = weight(after_near, east_next, north_next, middle, outer)
+        halo1 = parts(faces1, 8)[4]
+        halo1[side] = east_sum
+        halo1[2 + side] = north_sum
+        halo1[4 + side] = outer
+        halo1[6 + side] = weight(near, east_sum, north_sum, shared, outer)
+        edge[side] = east_sum
+        edge[2 + side] = north_sum
+        edge[4 + side] = shared
+    copies.start(faces0.at[65:75], out0.at[65:75])
+    copies.start(faces1.at[33:41], out1.at[33:41])
+    pack[0] = faces4[0]
+    pack[1] = faces4[1]
+    pack[2] = jnp.where(place[1] == 0, faces4[2], faces4[3])
+    for copy in copies.started:
+        copy.wait()
+
+
+def make_far_halos(edge, low, high, far_low, far_high, out2, out3, ready, halo2, halo3, semaphores):
+    for side in range(2):
+        def at(k):
+            if side == 0:
+                return low[NEAR - 1 - k] if k < NEAR else far_low[NEAR + FAR - 1 - k]
+            return high[k] if k < NEAR else far_high[k - NEAR]
+
+        near, east_sum, north_sum, shared = at(0), edge[side], edge[2 + side], edge[4 + side]
+        for halo, thick in ((halo2, 4), (halo3, 8)):
+            for k in range(thick // 2, thick):
+                east, north = plane_faces(at(k))
+                east_sum = east_sum + east
+                north_sum = north_sum + north
+            outer = harmonic(at(thick - 1), at(thick))
             halo[side] = east_sum
             halo[2 + side] = north_sum
             halo[4 + side] = outer
             halo[6 + side] = weight(near, east_sum, north_sum, shared, outer)
-    copies.start(faces0.at[65:75], out0.at[65:75])
-    copies.start(faces1.at[33:41], out1.at[33:41])
-    copies.start(faces2.at[17:25], out2.at[17:25])
-    copies.start(faces3.at[9:17], out3.at[9:17])
-    ready[...] = faces4[0, :HALO]
-    pack[0] = faces4[0]
-    pack[1] = faces4[1]
-    pack[2] = jnp.where(place[1] == 0, faces4[2], faces4[3])
+    copies = Copies(semaphores)
+    copies.start(halo2, out2)
+    copies.start(halo3, out3)
+    ready[...] = edge[0, :HALO]
     for copy in copies.started:
         copy.wait()
 
@@ -405,23 +431,31 @@
     loop(4, pair)
 
 
-def middle_level(s_own, low, high, there, there_next, out, s_next, *rest_refs):
-    edges, (s, first, total, second, faces, w_next, semaphores) = rest_refs[:-7], rest_refs[-7:]
+def middle_level(s_own, low, high, there, there_halo, there_next, out, s_next, faces_next, *rest_refs):
+    edges, (s, first, total, second, faces, halo_next, semaphores) = rest_refs[:-7], rest_refs[-7:]
     count = s_own.shape[0]
     strip = out.shape[1]
     copies = Copies(semaphores)
-    at, size = 3 * count + 1, planes_of(count)
-    weights = copies.start(there.at[at:size], faces.at[at:size])
-    others = copies.start(there.at[0:at], faces.at[0:at])
-    at, size = 3 * (count // 2) + 1, 4 * (count // 2) + 1
-    later = copies.start(there_next.at[at:size], w_next)
-    weights.wait()
+    at = 3 * count + 1
+    if count == 4:
+        weights = [copies.start(there.at[at:at + count], faces.at[at:at + count]),
+                   copies.start(there_halo, faces.at[at + count:at + count + 8])]
+        others = copies.start(there.at[0:at], faces.at[0:at])
+        later = [copies.start(there_next.at[0:9], faces_next.at[0:9]), copies.start(halo_next, faces_next.at[9:17])]
+        for copy in weights:
+            copy.wait()
+    else:
+        faces = there
+        later = [copies.start(there_next, faces_next)]
     open_level(s_own, faces, low, high, s, first)
-    others.wait()
-    rest = sweep_and_rest(s, first, total, second, faces, s_own.shape[0])
+    if count == 4:
+        others.wait()
+    rest = sweep_and_rest(s, first, total, second, faces, count)
     for q in range(count // 2):
         s_next[q] = rest(2 * q) + rest(2 * q + 1)
-    later.wait()
+    for copy in later:
+        copy.wait()
+    w_next = parts(faces_next, count // 2)[3]
     for q in range(count):
         out[q] = second[q + 1, HALO:HALO + strip]
     if len(edges) == 2:
@@ -434,12 +468,23 @@
         edges[0][0] = w_next[0] * s_next[0]
 
 
+def second_level(s_own, low, high, there, there_halo, there_next, halo_next, out, s_next, faces_next, edge_down, edge_up,
+                 s, first, total, second, faces, semaphores):
+    middle_level(s_own, low, high, there, there_halo, there_next, out, s_next, faces_next, edge_down, edge_up,
+                 s, first, total, second, faces, halo_next, semaphores)
+
+
+def third_level(s_own, low, high, faces, there_next, out, s_next, faces_next, first_next, s, first, total, second, semaphores):
+    middle_level(s_own, low, high, faces, None, there_next, out, s_next, faces_next, first_next,
+                 s, first, total, second, None, None, semaphores)
+
+
 def widen(source2, above, below, faces2, fine, plane_out, s, edge_down, edge_up, back, semaphores):
     copies = Copies(semaphores)
     copies.start(fine, back.at[:, 0:2])
     copies.start(plane_out, back.at[:, 2])
     count, strip, _ = source2.shape
-    w2 = parts(faces2, count)[3]
+    w2 = faces2.at[3 * count + 1:4 * count + 1]
     for q in range(count):
         s[q, :HALO] = above[q]
         s[q, HALO:HALO + strip] = source2[q]
@@ -507,13 +552,19 @@
     thin = strip + 2 * THIN
     (s_cut,) = call(cut_source, [(RING, planes, thin, columns)], [], right_side, s_top, s_bottom, limit=10)
     c_parts = [cuts[0]] + [ring_permuted(cuts[k], k) for k in ORDER]
-    c, bundle_down, bundle_up, ready = call(join, [shape(16), shape(REACH), shape(REACH), (HALO, columns)], [], place, *c_parts, limit=10, settled=(s_cut,))
+    c, near_down, near_up, far_down, far_up, ready = call(
+        join, [shape(n) for n in (16, NEAR, NEAR, FAR, FAR)] + [(HALO, columns)], [shape(16)], place, *c_parts, limit=10,
+        settled=(s_cut,), hbm_out=range(5), copies=5)
     s_own = transposed(after(s_cut, ready))
-    c_low, c_high = exchange(bundle_down, bundle_up)
-    sizes = [shape(planes_of(n)) for n in (16, 8, 4, 2, 1)]
-    faces0, faces1, faces2, faces3, faces4, pack, ready = call(
-        make_faces, sizes + [shape(3), (HALO, columns)], sizes, place, c, c_low, c_high,
-        limit=30, work=12.0, hbm_out=range(5), copies=9)
+    c_low, c_high = exchange(near_down, near_up)
+    far_low, far_high = exchange(far_down, far_up)
+    sizes = [shape(own_planes_of(n)) for n in (16, 8, 4, 2, 1)]
+    faces0, faces1, faces2, faces3, faces4, pack, edge = call(
+        make_faces, sizes + [shape(3), shape(6)], sizes, place, c, c_low, c_high,
+        limit=30, work=10.0, hbm_out=range(5), copies=7)
+    halo2, halo3, ready = call(
+        make_far_halos, [shape(8), shape(8), (HALO, columns)], [shape(8), shape(8)], edge, c_low, c_high, far_low, far_high,
+        limit=10, work=3.0, hbm_out=range(2), copies=2)
     (faces5,) = call(make_last_faces, [shape(5)], [], place, faces4, partner(pack))
 
     s_own = after(s_own, ready).reshape(RING * planes, thin, columns)
@@ -535,15 +586,15 @@
         widen, [shape(4), shape(2), shape(2), (RING, planes + 1, strip, columns)], [], s2, above, below, faces2, fine, plane_out, limit=10,
         hbm_out=(3,), copies=2)
     low, high = exchange(edge_down, edge_up)
-    second2, s3, edge_down, edge_up = call(
-        middle_level, [(4, strip, columns), shape(2), shape(2), shape(2)],
-        [shape(6), shape(8), shape(4), shape(6), shape(planes_of(4)), shape(2)],
-        s2, low, high, faces2, faces3, limit=14, hbm_in=(3, 4), copies=3)
+    second2, s3, faces3, edge_down, edge_up = call(
+        second_level, [(4, strip, columns), shape(2), shape(17), shape(2), shape(2)],
+        [shape(6), shape(8), shape(4), shape(6), shape(25)],
+        s2, low, high, faces2, halo2, faces3, halo3, limit=14, hbm_in=(3, 4, 5, 6), copies=5)
     low, high = exchange(edge_down, edge_up)
-    second3, s4, first4 = call(
-        middle_level, [(2, strip, columns), shape(1), shape(1)],
-        [shape(4), shape(6), shape(2), shape(4), shape(planes_of(2)), shape(1)],
-        s3, low, high, faces3, faces4, limit=12, hbm_in=(3, 4), copies=3)
+    second3, s4, faces4, first4 = call(
+        third_level, [(2, strip, columns), shape(1), shape(5), shape(1)],
+        [shape(4), shape(6), shape(2), shape(4)],
+        s3, low, high, faces3, faces4, limit=12, hbm_in=(4,), copies=1)
     low, high = exchange(first4, first4)
     total4, second4 = call(sweep_last, [shape(1), shape(1)], [], s4, first4, low, high, faces4)
     low, high = exchange(second4, second4)
@@ -552,8 +603,8 @@
     low, high = exchange(first5, first5, 2 * RING)
     back = transposed(back)
     sums = call(finish, [(strip, columns)] * RING, [],
-                place, s5, first5, low, high, faces5, second2, second3, second4, settled=(back,))
-    (coarse_return,) = call(collect, [(RING, strip, columns)], [], place, sums[0], *[ring_permuted(sums[k], k) for k in ORDER])
+                place, s5, first5, low, high, faces5, second2, second3, second4)
+    (coarse_return,) = call(collect, [(RING, strip, columns)], [], place, sums[0], *[ring_permuted(sums[k], k) for k in ORDER], settled=(back,))
 
     fine_iterate = jnp.transpose(back[:, :planes], (1, 0, 2, 3)).reshape(planes, rows, columns)
     plane_iterate = back[:, planes].reshape(1, rows, columns)

time: 268 us -> 251 us (0.937)
  waiting for transfers between devices: 94.5 us -> 70.3 us
  starting transfers between devices: 123 us -> 132 us
  local copies, waits for them, and re-layouts: 11.7 us -> 6.36 us
    ppermute x16 -> x18, waiting for transfers between devices: 57.5 us -> 26.7 us  [shifted(): return lax.ppermute(value, 'gz', pairs)]
    ppermute x16 -> x18, starting transfers between devices: 63.2 us -> 74.7 us  [shifted(): return lax.ppermute(value, 'gz', pairs)]
    all_to_all x2, waiting for transfers between devices: 0.01 us -> 7.8 us  [transposed(): lax.all_to_all(value, 'gz', 0, 0, axis_index_groups=ring_groups(lax.axis_...]
    unnamed x28 -> x22, local copies, waits for them, and re-layouts: 9.55 us -> 4.21 us
    all_to_all x2, starting transfers between devices: 13.1 us -> 9.9 us  [transposed(): lax.all_to_all(value, 'gz', 0, 0, axis_index_groups=ring_groups(lax.axis_...]
    pallas_call x15 -> x16, Pallas kernels: 35.4 us -> 37.9 us  [call(): pl.pallas_call(body, out_shape=shapes, in_specs=[pl.BlockSpec(memory_spac...]
  transfers between devices with their start and end apart: 38 -> 40, of which waited for: 27 -> 29; matrix products, arithmetic and copies ran while one was open for 1% -> 1% of each run, Pallas kernels for 7% -> 8%
where the time goes in v9:
time: 251 us; the launch traced here: 248 us
  starting transfers between devices  132 us (53%)
  waiting for transfers between devices  70.3 us (28%)
  Pallas kernels  37.9 us (15%)
  local copies, waits for them, and re-layouts  6.36 us (3%)
    ppermute x18, starting transfers between devices, shifted(): return lax.ppermute(value, 'gz', pairs)  74.7 us
    ppermute x14, starting transfers between devices, ring_permuted(): lax.ppermute(value, 'gz', [(i, i // RING * RING + (i + by) % RING) for i...  41.2 us
    pallas_call x16, Pallas kernels, call(): pl.pallas_call(body, out_shape=shapes, in_specs=[pl.BlockSpec(memory_spac...  37.9 us
    ppermute x14, waiting for transfers between devices, ring_permuted(): lax.ppermute(value, 'gz', [(i, i // RING * RING + (i + by) % RING) for i...  26.7 us
    ppermute x18, waiting for transfers between devices, shifted(): return lax.ppermute(value, 'gz', pairs)  26.7 us
    all_to_all x2, starting transfers between devices, transposed(): lax.all_to_all(value, 'gz', 0, 0, axis_index_groups=ring_groups(lax.axis_...  9.9 us
    all_to_all x2, waiting for transfers between devices, transposed(): lax.all_to_all(value, 'gz', 0, 0, axis_index_groups=ring_groups(lax.axis_...  7.8 us
    ppermute x2, waiting for transfers between devices, row_shifted(): return lax.ppermute(value, ('gz', 'xy'), pairs)  5.03 us
  transfers between devices with their start and end apart: 40, of which 29 were waited for; matrix products, arithmetic and copies ran while one was open for 1% of the time, Pallas kernels for 8%

profile of v9, /device:TPU:8, one launch (start us, length us, event | category | flops | bytes accessed | tf_op | source)
XLA Modules:
  0.0 248.5 jit_solution(2692044804306742150)
XLA Ops:
  6.4 4.7 %collective-permute-start.2 = (f32[2,48,640]{2,1,0:T(8,128)S(1)}, f32[2,48,640]{2,1,0:T(8,128)S(1)}, u32[]{:S(2)}, u32[]{:S(2)}) collective-permute-start(f32[2,48,640]{2,1,0:T(8,128)S(1)} %get-tuple-element.61), channel_id=1, source_target_pairs={{0,6},{2,8},{4,10},{6,12},{8,14},{10,0},{12,2},{14,4},{16,22},{18,... | collective-permute-start | bytes 737288 | tf_op jit(solution)/shard_map/ppermute | solution.py:127
  13.4 5.5 %collective-permute-start.4 = (f32[2,48,640]{2,1,0:T(8,128)S(1)}, f32[2,48,640]{2,1,0:T(8,128)S(1)}, u32[]{:S(2)}, u32[]{:S(2)}) collective-permute-start(f32[2,48,640]{2,1,0:T(8,128)S(1)} %get-tuple-element.63), channel_id=1, source_target_pairs={{0,8},{2,10},{4,12},{6,14},{8,0},{10,2},{12,4},{14,6},{16,24},{18,... | collective-permute-start | bytes 737288 | tf_op jit(solution)/shard_map/ppermute | solution.py:127
  23.0 7.7 %collective-permute-done.2.refs_3_ = f32[2,48,640]{2,1,0:T(8,128)S(1)} collective-permute-done((f32[2,48,640]{2,1,0:T(8,128)S(1)}, f32[2,48,640]{2,1,0:T(8,128)S(1)}, u32[]{:S(2)}, u32[]{:S(2)}) %collective-permute-start.2) | collective-permute-done | bytes 245792 | tf_op jit(solution)/shard_map/ppermute | solution.py:127
  30.8 5.0 %collective-permute-start.7 = (f32[2,48,640]{2,1,0:T(8,128)S(1)}, f32[2,48,640]{2,1,0:T(8,128)S(1)}, u32[]{:S(2)}, u32[]{:S(2)}) collective-permute-start(f32[2,48,640]{2,1,0:T(8,128)S(1)} %get-tuple-element.66), channel_id=1, source_target_pairs={{0,2},{2,4},{4,6},{6,8},{8,10},{10,12},{12,14},{14,0},{16,18},{18,... | collective-permute-start | bytes 737288 | tf_op jit(solution)/shard_map/ppermute | solution.py:127
  38.6 3.5 %collective-permute-done.4.refs_5_ = f32[2,48,640]{2,1,0:T(8,128)S(1)} collective-permute-done((f32[2,48,640]{2,1,0:T(8,128)S(1)}, f32[2,48,640]{2,1,0:T(8,128)S(1)}, u32[]{:S(2)}, u32[]{:S(2)}) %collective-permute-start.4) | collective-permute-done | bytes 245792 | tf_op jit(solution)/shard_map/ppermute | solution.py:127
  42.2 9.1 %collective-permute-done.5.refs_6_ = f32[2,48,640]{2,1,0:T(8,128)S(1)} collective-permute-done((f32[2,48,640]{2,1,0:T(8,128)S(1)}, f32[2,48,640]{2,1,0:T(8,128)S(1)}, u32[]{:S(2)}, u32[]{:S(2)}) %collective-permute-start.5) | collective-permute-done | bytes 245792 | tf_op jit(solution)/shard_map/ppermute | solution.py:127
  60.1 6.2 %all-to-all-start = ((f32[8,2,40,640]{3,2,1,0:T(8,128)}), f32[8,2,40,640]{3,2,1,0:T(8,128)S(1)}, u32[]{:S(2)}, u32[]{:S(2)}) async-start(f32[8,2,40,640]{3,2,1,0:T(8,128)} %shard_map.61), calls=%async_computation | async-start | bytes 3276800 | tf_op jit(solution)/shard_map/all_to_all | solution.py:47
  66.3 3.4 %collective-permute-start.9 = (f32[3,48,640]{2,1,0:T(8,128)S(1)}, f32[3,48,640]{2,1,0:T(8,128)S(1)}, u32[]{:S(2)}, u32[]{:S(2)}) collective-permute-start(f32[3,48,640]{2,1,0:T(8,128)S(1)} %copy-done.8), channel_id=1, source_target_pairs={{0,16},{2,18},{4,20},{6,22},{8,24},{10,26},{12,28},{14,30},{16,32}... | collective-permute-start | bytes 1105928 | tf_op jit(solution)/shard_map/ppermute | solution.py:28
  69.8 4.6 %collective-permute-start.10 = (f32[3,48,640]{2,1,0:T(8,128)S(1)}, f32[3,48,640]{2,1,0:T(8,128)S(1)}, u32[]{:S(2)}, u32[]{:S(2)}) collective-permute-start(f32[3,48,640]{2,1,0:T(8,128)S(1)} %copy-done.7), channel_id=1, source_target_pairs={{16,0},{18,2},{20,4},{22,6},{24,8},{26,10},{28,12},{30,14},{32,16}... | collective-permute-start | bytes 1105928 | tf_op jit(solution)/shard_map/ppermute | solution.py:28
  76.3 6.0 %collective-permute-start.12 = (f32[6,48,640]{2,1,0:T(8,128)S(1)}, f32[6,48,640]{2,1,0:T(8,128)S(1)}, u32[]{:S(2)}, u32[]{:S(2)}) collective-permute-start(f32[6,48,640]{2,1,0:T(8,128)S(1)} %copy-done.6), channel_id=1, source_target_pairs={{16,0},{18,2},{20,4},{22,6},{24,8},{26,10},{28,12},{30,14},{32,16}... | collective-permute-start | bytes 2211848 | tf_op jit(solution)/shard_map/ppermute | solution.py:28
  84.3 10.9 %shard_map.62 = (f32[75,48,640]{2,1,0:T(8,128)}, f32[41,48,640]{2,1,0:T(8,128)}, f32[17,48,640]{2,1,0:T(8,128)}, f32[9,48,640]{2,1,0:T(8,128)}, f32[5,48,640]{2,...) custom-call(s32[2]{0:T(128)S(1)} %pad_add_fusion.refs_0_.refs_1_, f32[16,48,640]{2,1,0:T(8,128)S(1)} %copy-done.5, ...), custom_call_target="tpu_custom_call" | custom-call | flops 10000000000 | bytes 30000000 | tf_op jit(solution)/shard_map/pallas_call | solution.py:111
  99.7 7.8 %all-to-all-done.refs_0_ = f32[8,2,40,640]{3,2,1,0:T(8,128)S(1)} async-done(((f32[8,2,40,640]{3,2,1,0:T(8,128)}), f32[8,2,40,640]{3,2,1,0:T(8,128)S(1)}, u32[]{:S(2)}, u32[]{:S(2)}) %all-to-all-start) | async-done | bytes 1638432 | tf_op jit(solution)/shard_map/all_to_all | solution.py:47
  107.5 3.7 %collective-permute-start.13 = (f32[2,40,640]{2,1,0:T(8,128)S(1)}, f32[2,40,640]{2,1,0:T(8,128)S(1)}, u32[]{:S(2)}, u32[]{:S(2)}) collective-permute-start(f32[2,40,640]{2,1,0:T(8,128)S(1)} %get-tuple-element.118), channel_id=1, source_target_pairs={{0,16},{2,18},{4,20},{6,22},{8,24},{10,26},{12,28},{14,30},{16,32}... | collective-permute-start | bytes 614408 | tf_op jit(solution)/shard_map/ppermute | solution.py:28
  111.2 4.7 %collective-permute-start.14 = (f32[2,40,640]{2,1,0:T(8,128)S(1)}, f32[2,40,640]{2,1,0:T(8,128)S(1)}, u32[]{:S(2)}, u32[]{:S(2)}) collective-permute-start(f32[2,40,640]{2,1,0:T(8,128)S(1)} %get-tuple-element.117), channel_id=1, source_target_pairs={{16,0},{18,2},{20,4},{22,6},{24,8},{26,10},{28,12},{30,14},{32,16}... | collective-permute-start | bytes 614408 | tf_op jit(solution)/shard_map/ppermute | solution.py:28
  119.0 7.8 %shard_map.65 = (f32[8,2,32,640]{3,2,1,0:T(8,128)S(1)}, f32[8,48,640]{2,1,0:T(8,128)S(1)}, f32[2,48,640]{2,1,0:T(8,128)S(1)}, f32[2,48,640]{2,1,0:T(8,128)S(1)}) custom-call(f32[16,40,640]{2,1,0:T(8,128)S(1)} %bitcast.12, f32[2,40,640]{2,1,0:T(8,128)S(1)} %collective-permute-done.13.refs_1_, f32[2,40,640]{2,1,0:T(8,128)S(1)} %collective-permute-done.14.refs_2_, ...), custom_call_target="tpu_custom_call" | custom-call | flops 8000000000 | bytes 24000000 | tf_op jit(solution)/shard_map/pallas_call | solution.py:111
  130.1 5.2 %collective-permute-start.16 = (f32[2,48,640]{2,1,0:T(8,128)S(1)}, f32[2,48,640]{2,1,0:T(8,128)S(1)}, u32[]{:S(2)}, u32[]{:S(2)}) collective-permute-start(f32[2,48,640]{2,1,0:T(8,128)S(1)} %get-tuple-element.80), channel_id=1, source_target_pairs={{16,0},{18,2},{20,4},{22,6},{24,8},{26,10},{28,12},{30,14},{32,16}... | collective-permute-start | bytes 737288 | tf_op jit(solution)/shard_map/ppermute | solution.py:28
  146.0 4.3 %collective-permute-done.18.refs_2_ = f32[4,8,640]{2,1,0:T(8,128)S(1)} collective-permute-done((f32[4,8,640]{2,1,0:T(8,128)S(1)}, f32[4,8,640]{2,1,0:T(8,128)S(1)}, u32[]{:S(2)}, u32[]{:S(2)}) %collective-permute-start.18) | collective-permute-done | bytes 81952 | tf_op jit(solution)/shard_map/ppermute | solution.py:38
  151.6 3.7 %all-to-all-start.1 = ((f32[8,3,32,640]{3,2,1,0:T(8,128)}), f32[8,3,32,640]{3,2,1,0:T(8,128)S(1)}, u32[]{:S(2)}, u32[]{:S(2)}) async-start(f32[8,3,32,640]{3,2,1,0:T(8,128)} %get-tuple-element.87), calls=%async_computation.1 | async-start | bytes 3932160 | tf_op jit(solution)/shard_map/all_to_all | solution.py:47
  155.3 3.9 %collective-permute-start.19 = (f32[2,48,640]{2,1,0:T(8,128)S(1)}, f32[2,48,640]{2,1,0:T(8,128)S(1)}, u32[]{:S(2)}, u32[]{:S(2)}) collective-permute-start(f32[2,48,640]{2,1,0:T(8,128)S(1)} %get-tuple-element.89), channel_id=1, source_target_pairs={{0,16},{2,18},{4,20},{6,22},{8,24},{10,26},{12,28},{14,30},{16,32}... | collective-permute-start | bytes 737288 | tf_op jit(solution)/shard_map/ppermute | solution.py:28
  159.2 4.5 %collective-permute-start.20 = (f32[2,48,640]{2,1,0:T(8,128)S(1)}, f32[2,48,640]{2,1,0:T(8,128)S(1)}, u32[]{:S(2)}, u32[]{:S(2)}) collective-permute-start(f32[2,48,640]{2,1,0:T(8,128)S(1)} %get-tuple-element.90), channel_id=1, source_target_pairs={{16,0},{18,2},{20,4},{22,6},{24,8},{26,10},{28,12},{30,14},{32,16}... | collective-permute-start | bytes 737288 | tf_op jit(solution)/shard_map/ppermute | solution.py:28
  167.4 3.3 %shard_map.68 = (f32[4,32,640]{2,1,0:T(8,128)S(1)}, f32[2,48,640]{2,1,0:T(8,128)S(1)}, f32[17,48,640]{2,1,0:T(8,128)S(1)}, f32[2,48,640]{2,1,0:T(8,128)S(1)}, f32[2,48,640]{2,1,0:T(8,128)S(1)}) custom-call(f32[4,48,640]{2,1,0:T(8,128)S(1)} %get-tuple-element.88.refs_0_, f32[2,48,640]{2,1,0:T(8,128)S(1)} %collective-permute-done.19.refs_1_, ...), custom_call_target="tpu_custom_call" | custom-call | tf_op jit(solution)/shard_map/pallas_call | solution.py:111
  170.7 3.9 %collective-permute-start.21 = (f32[2,48,640]{2,1,0:T(8,128)S(1)}, f32[2,48,640]{2,1,0:T(8,128)S(1)}, u32[]{:S(2)}, u32[]{:S(2)}) collective-permute-start(f32[2,48,640]{2,1,0:T(8,128)S(1)} %get-tuple-element.95), channel_id=1, source_target_pairs={{0,16},{2,18},{4,20},{6,22},{8,24},{10,26},{12,28},{14,30},{16,32}... | collective-permute-start | bytes 737288 | tf_op jit(solution)/shard_map/ppermute | solution.py:28
  174.6 4.5 %collective-permute-start.22 = (f32[2,48,640]{2,1,0:T(8,128)S(1)}, f32[2,48,640]{2,1,0:T(8,128)S(1)}, u32[]{:S(2)}, u32[]{:S(2)}) collective-permute-start(f32[2,48,640]{2,1,0:T(8,128)S(1)} %get-tuple-element.96), channel_id=1, source_target_pairs={{16,0},{18,2},{20,4},{22,6},{24,8},{26,10},{28,12},{30,14},{32,16}... | collective-permute-start | bytes 737288 | tf_op jit(solution)/shard_map/ppermute | solution.py:28
  184.0 4.0 %collective-permute-start.23 = (f32[1,48,640]{2,1,0:T(8,128)S(1)}, f32[1,48,640]{2,1,0:T(8,128)S(1)}, u32[]{:S(2)}, u32[]{:S(2)}) collective-permute-start(f32[1,48,640]{2,1,0:T(8,128)S(1)} %get-tuple-element.100.refs_1_), channel_id=1, source_target_pairs={{0,16},{2,18},{4,20},{6,22},{8,24},{10,26},{12,28},{14,30},{16,32}... | collective-permute-start | bytes 368648 | tf_op jit(solution)/shard_map/ppermute | solution.py:28
  188.0 4.5 %collective-permute-start.24 = (f32[1,48,640]{2,1,0:T(8,128)S(1)}, f32[1,48,640]{2,1,0:T(8,128)S(1)}, u32[]{:S(2)}, u32[]{:S(2)}) collective-permute-start(f32[1,48,640]{2,1,0:T(8,128)S(1)} %get-tuple-element.100.refs_1_), channel_id=1, source_target_pairs={{16,0},{18,2},{20,4},{22,6},{24,8},{26,10},{28,12},{30,14},{32,16}... | collective-permute-start | bytes 368648 | tf_op jit(solution)/shard_map/ppermute | solution.py:28
  195.2 3.9 %collective-permute-start.25 = (f32[1,48,640]{2,1,0:T(8,128)S(1)}, f32[1,48,640]{2,1,0:T(8,128)S(1)}, u32[]{:S(2)}, u32[]{:S(2)}) collective-permute-start(f32[1,48,640]{2,1,0:T(8,128)S(1)} %get-tuple-element.103.refs_2_.refs_8_), channel_id=1, source_target_pairs={{0,16},{2,18},{4,20},{6,22},{8,24},{10,26},{12,28},{14,30},{16,32}... | collective-permute-start | bytes 368648 | tf_op jit(solution)/shard_map/ppermute | solution.py:28
  199.0 4.5 %collective-permute-start.26 = (f32[1,48,640]{2,1,0:T(8,128)S(1)}, f32[1,48,640]{2,1,0:T(8,128)S(1)}, u32[]{:S(2)}, u32[]{:S(2)}) collective-permute-start(f32[1,48,640]{2,1,0:T(8,128)S(1)} %get-tuple-element.103.refs_2_.refs_8_), channel_id=1, source_target_pairs={{16,0},{18,2},{20,4},{22,6},{24,8},{26,10},{28,12},{30,14},{32,16}... | collective-permute-start | bytes 368648 | tf_op jit(solution)/shard_map/ppermute | solution.py:28
  211.9 5.5 %collective-permute-start.29 = (f32[1,48,640]{2,1,0:T(8,128)S(1)}, f32[1,48,640]{2,1,0:T(8,128)S(1)}, u32[]{:S(2)}, u32[]{:S(2)}) collective-permute-start(f32[1,48,640]{2,1,0:T(8,128)S(1)} %get-tuple-element.106.refs_2_), channel_id=1, source_target_pairs={{0,32},{2,34},{4,36},{6,38},{8,40},{10,42},{12,44},{14,46},{16,48}... | collective-permute-start | bytes 368648 | tf_op jit(solution)/shard_map/ppermute | solution.py:28
  221.1 4.6 %collective-permute-done.30.refs_4_ = f32[1,48,640]{2,1,0:T(8,128)S(1)} collective-permute-done((f32[1,48,640]{2,1,0:T(8,128)S(1)}, f32[1,48,640]{2,1,0:T(8,128)S(1)}, u32[]{:S(2)}, u32[]{:S(2)}) %collective-permute-start.30) | collective-permute-done | bytes 122912 | tf_op jit(solution)/shard_map/ppermute | solution.py:28
  226.4 3.7 %collective-permute-start.31 = (f32[32,640]{1,0:T(8,128)S(1)}, f32[32,640]{1,0:T(8,128)S(1)}, u32[]{:S(2)}, u32[]{:S(2)}) collective-permute-start(f32[32,640]{1,0:T(8,128)S(1)} %get-tuple-element.110), channel_id=1, source_target_pairs={{0,6},{2,8},{4,10},{6,12},{8,14},{10,0},{12,2},{14,4},{16,22},{18,... | collective-permute-start | bytes 245768 | tf_op jit(solution)/shard_map/ppermute | solution.py:127
  231.6 5.7 %collective-permute-start.33 = (f32[32,640]{1,0:T(8,128)S(1)}, f32[32,640]{1,0:T(8,128)S(1)}, u32[]{:S(2)}, u32[]{:S(2)}) collective-permute-start(f32[32,640]{1,0:T(8,128)S(1)} %get-tuple-element.112), channel_id=1, source_target_pairs={{0,8},{2,10},{4,12},{6,14},{8,0},{10,2},{12,4},{14,6},{16,24},{18,... | collective-permute-start | bytes 245768 | tf_op jit(solution)/shard_map/ppermute | solution.py:127
  237.8 3.6 %collective-permute-start.35 = (f32[32,640]{1,0:T(8,128)S(1)}, f32[32,640]{1,0:T(8,128)S(1)}, u32[]{:S(2)}, u32[]{:S(2)}) collective-permute-start(f32[32,640]{1,0:T(8,128)S(1)} %get-tuple-element.114), channel_id=1, source_target_pairs={{0,12},{2,14},{4,0},{6,2},{8,4},{10,6},{12,8},{14,10},{16,28},{18,... | collective-permute-start | bytes 245768 | tf_op jit(solution)/shard_map/ppermute | solution.py:127
  (98 shorter events, 83.5 us)
Async XLA Ops:
  6.4 24.4 %collective-permute-start.2 = (f32[2,48,640]{2,1,0:T(8,128)S(1)}, f32[2,48,640]{2,1,0:T(8,128)S(1)}, u32[]{:S(2)}, u32[]{:S(2)}) collective-permute-start(f32[2,48,640]{2,1,0:T(8,128)S(1)} %get-tuple-element.61), channel_id=1, source_target_pairs={{0,6},{2,8},{4,10},{6,12},{8,14},{10,0},{12,2},{14,4},{16,22},{18,... | collective-permute-start | bytes 737288 | tf_op jit(solution)/shard_map/ppermute | solution.py:127
  11.1 24.7 %collective-permute-start.3 = (f32[2,48,640]{2,1,0:T(8,128)S(1)}, f32[2,48,640]{2,1,0:T(8,128)S(1)}, u32[]{:S(2)}, u32[]{:S(2)}) collective-permute-start(f32[2,48,640]{2,1,0:T(8,128)S(1)} %get-tuple-element.62), channel_id=1, source_target_pairs={{0,10},{2,12},{4,14},{6,0},{8,2},{10,4},{12,6},{14,8},{16,26},{18,... | collective-permute-start | bytes 737288 | tf_op jit(solution)/shard_map/ppermute | solution.py:127
  13.3 7.1 %collective-permute-start = (f32[2,8,640]{2,1,0:T(8,128)S(1)}, f32[2,8,640]{2,1,0:T(8,128)S(1)}, u32[]{:S(2)}, u32[]{:S(2)}) collective-permute-start(f32[2,8,640]{2,1,0:T(8,128)S(1)} %slice_select_fusion), channel_id=1, source_target_pairs={{0,1},{1,0},{2,3},{3,2},{4,5},{5,4},{6,7},{7,6},{8,9},{9,8},{10,11... | collective-permute-start | bytes 122888 | tf_op jit(solution)/shard_map/ppermute | solution.py:539
  13.4 28.7 %collective-permute-start.4 = (f32[2,48,640]{2,1,0:T(8,128)S(1)}, f32[2,48,640]{2,1,0:T(8,128)S(1)}, u32[]{:S(2)}, u32[]{:S(2)}) collective-permute-start(f32[2,48,640]{2,1,0:T(8,128)S(1)} %get-tuple-element.63), channel_id=1, source_target_pairs={{0,8},{2,10},{4,12},{6,14},{8,0},{10,2},{12,4},{14,6},{16,24},{18,... | collective-permute-start | bytes 737288 | tf_op jit(solution)/shard_map/ppermute | solution.py:127
  18.9 32.3 %collective-permute-start.5 = (f32[2,48,640]{2,1,0:T(8,128)S(1)}, f32[2,48,640]{2,1,0:T(8,128)S(1)}, u32[]{:S(2)}, u32[]{:S(2)}) collective-permute-start(f32[2,48,640]{2,1,0:T(8,128)S(1)} %get-tuple-element.64), channel_id=1, source_target_pairs={{0,4},{2,6},{4,8},{6,10},{8,12},{10,14},{12,0},{14,2},{16,20},{18,... | collective-permute-start | bytes 737288 | tf_op jit(solution)/shard_map/ppermute | solution.py:127
  20.4 32.6 %collective-permute-start.6 = (f32[2,48,640]{2,1,0:T(8,128)S(1)}, f32[2,48,640]{2,1,0:T(8,128)S(1)}, u32[]{:S(2)}, u32[]{:S(2)}) collective-permute-start(f32[2,48,640]{2,1,0:T(8,128)S(1)} %get-tuple-element.65), channel_id=1, source_target_pairs={{0,12},{2,14},{4,0},{6,2},{8,4},{10,6},{12,8},{14,10},{16,28},{18,... | collective-permute-start | bytes 737288 | tf_op jit(solution)/shard_map/ppermute | solution.py:127
  30.8 24.8 %collective-permute-start.7 = (f32[2,48,640]{2,1,0:T(8,128)S(1)}, f32[2,48,640]{2,1,0:T(8,128)S(1)}, u32[]{:S(2)}, u32[]{:S(2)}) collective-permute-start(f32[2,48,640]{2,1,0:T(8,128)S(1)} %get-tuple-element.66), channel_id=1, source_target_pairs={{0,2},{2,4},{4,6},{6,8},{8,10},{10,12},{12,14},{14,0},{16,18},{18,... | collective-permute-start | bytes 737288 | tf_op jit(solution)/shard_map/ppermute | solution.py:127
  35.8 21.5 %collective-permute-start.8 = (f32[2,48,640]{2,1,0:T(8,128)S(1)}, f32[2,48,640]{2,1,0:T(8,128)S(1)}, u32[]{:S(2)}, u32[]{:S(2)}) collective-permute-start(f32[2,48,640]{2,1,0:T(8,128)S(1)} %get-tuple-element.67), channel_id=1, source_target_pairs={{0,14},{2,0},{4,2},{6,4},{8,6},{10,8},{12,10},{14,12},{16,30},{18,... | collective-permute-start | bytes 737288 | tf_op jit(solution)/shard_map/ppermute | solution.py:127
  60.1 47.4 %all-to-all-start = ((f32[8,2,40,640]{3,2,1,0:T(8,128)}), f32[8,2,40,640]{3,2,1,0:T(8,128)S(1)}, u32[]{:S(2)}, u32[]{:S(2)}) async-start(f32[8,2,40,640]{3,2,1,0:T(8,128)} %shard_map.61), calls=%async_computation | async-start | bytes 3276800 | tf_op jit(solution)/shard_map/all_to_all | solution.py:47
  66.3 16.0 %collective-permute-start.9 = (f32[3,48,640]{2,1,0:T(8,128)S(1)}, f32[3,48,640]{2,1,0:T(8,128)S(1)}, u32[]{:S(2)}, u32[]{:S(2)}) collective-permute-start(f32[3,48,640]{2,1,0:T(8,128)S(1)} %copy-done.8), channel_id=1, source_target_pairs={{0,16},{2,18},{4,20},{6,22},{8,24},{10,26},{12,28},{14,30},{16,32}... | collective-permute-start | bytes 1105928 | tf_op jit(solution)/shard_map/ppermute | solution.py:28
  69.8 13.0 %collective-permute-start.10 = (f32[3,48,640]{2,1,0:T(8,128)S(1)}, f32[3,48,640]{2,1,0:T(8,128)S(1)}, u32[]{:S(2)}, u32[]{:S(2)}) collective-permute-start(f32[3,48,640]{2,1,0:T(8,128)S(1)} %copy-done.7), channel_id=1, source_target_pairs={{16,0},{18,2},{20,4},{22,6},{24,8},{26,10},{28,12},{30,14},{32,16}... | collective-permute-start | bytes 1105928 | tf_op jit(solution)/shard_map/ppermute | solution.py:28
  74.3 21.6 %collective-permute-start.11 = (f32[6,48,640]{2,1,0:T(8,128)}, f32[6,48,640]{2,1,0:T(8,128)S(1)}, u32[]{:S(2)}, u32[]{:S(2)}) collective-permute-start(f32[6,48,640]{2,1,0:T(8,128)} %get-tuple-element.73), channel_id=1, source_target_pairs={{0,16},{2,18},{4,20},{6,22},{8,24},{10,26},{12,28},{14,30},{16,32}... | collective-permute-start | bytes 2211848 | tf_op jit(solution)/shard_map/ppermute | solution.py:28
  76.3 20.8 %collective-permute-start.12 = (f32[6,48,640]{2,1,0:T(8,128)S(1)}, f32[6,48,640]{2,1,0:T(8,128)S(1)}, u32[]{:S(2)}, u32[]{:S(2)}) collective-permute-start(f32[6,48,640]{2,1,0:T(8,128)S(1)} %copy-done.6), channel_id=1, source_target_pairs={{16,0},{18,2},{20,4},{22,6},{24,8},{26,10},{28,12},{30,14},{32,16}... | collective-permute-start | bytes 2211848 | tf_op jit(solution)/shard_map/ppermute | solution.py:28
  107.5 10.0 %collective-permute-start.13 = (f32[2,40,640]{2,1,0:T(8,128)S(1)}, f32[2,40,640]{2,1,0:T(8,128)S(1)}, u32[]{:S(2)}, u32[]{:S(2)}) collective-permute-start(f32[2,40,640]{2,1,0:T(8,128)S(1)} %get-tuple-element.118), channel_id=1, source_target_pairs={{0,16},{2,18},{4,20},{6,22},{8,24},{10,26},{12,28},{14,30},{16,32}... | collective-permute-start | bytes 614408 | tf_op jit(solution)/shard_map/ppermute | solution.py:28
  111.2 7.8 %collective-permute-start.14 = (f32[2,40,640]{2,1,0:T(8,128)S(1)}, f32[2,40,640]{2,1,0:T(8,128)S(1)}, u32[]{:S(2)}, u32[]{:S(2)}) collective-permute-start(f32[2,40,640]{2,1,0:T(8,128)S(1)} %get-tuple-element.117), channel_id=1, source_target_pairs={{16,0},{18,2},{20,4},{22,6},{24,8},{26,10},{28,12},{30,14},{32,16}... | collective-permute-start | bytes 614408 | tf_op jit(solution)/shard_map/ppermute | solution.py:28
  126.8 10.7 %collective-permute-start.15 = (f32[2,48,640]{2,1,0:T(8,128)S(1)}, f32[2,48,640]{2,1,0:T(8,128)S(1)}, u32[]{:S(2)}, u32[]{:S(2)}) collective-permute-start(f32[2,48,640]{2,1,0:T(8,128)S(1)} %get-tuple-element.79), channel_id=1, source_target_pairs={{0,16},{2,18},{4,20},{6,22},{8,24},{10,26},{12,28},{14,30},{16,32}... | collective-permute-start | bytes 737288 | tf_op jit(solution)/shard_map/ppermute | solution.py:28
  130.1 8.9 %collective-permute-start.16 = (f32[2,48,640]{2,1,0:T(8,128)S(1)}, f32[2,48,640]{2,1,0:T(8,128)S(1)}, u32[]{:S(2)}, u32[]{:S(2)}) collective-permute-start(f32[2,48,640]{2,1,0:T(8,128)S(1)} %get-tuple-element.80), channel_id=1, source_target_pairs={{16,0},{18,2},{20,4},{22,6},{24,8},{26,10},{28,12},{30,14},{32,16}... | collective-permute-start | bytes 737288 | tf_op jit(solution)/shard_map/ppermute | solution.py:28
  151.6 93.0 %all-to-all-start.1 = ((f32[8,3,32,640]{3,2,1,0:T(8,128)}), f32[8,3,32,640]{3,2,1,0:T(8,128)S(1)}, u32[]{:S(2)}, u32[]{:S(2)}) async-start(f32[8,3,32,640]{3,2,1,0:T(8,128)} %get-tuple-element.87), calls=%async_computation.1 | async-start | bytes 3932160 | tf_op jit(solution)/shard_map/all_to_all | solution.py:47
  155.3 10.7 %collective-permute-start.19 = (f32[2,48,640]{2,1,0:T(8,128)S(1)}, f32[2,48,640]{2,1,0:T(8,128)S(1)}, u32[]{:S(2)}, u32[]{:S(2)}) collective-permute-start(f32[2,48,640]{2,1,0:T(8,128)S(1)} %get-tuple-element.89), channel_id=1, source_target_pairs={{0,16},{2,18},{4,20},{6,22},{8,24},{10,26},{12,28},{14,30},{16,32}... | collective-permute-start | bytes 737288 | tf_op jit(solution)/shard_map/ppermute | solution.py:28
  159.2 8.2 %collective-permute-start.20 = (f32[2,48,640]{2,1,0:T(8,128)S(1)}, f32[2,48,640]{2,1,0:T(8,128)S(1)}, u32[]{:S(2)}, u32[]{:S(2)}) collective-permute-start(f32[2,48,640]{2,1,0:T(8,128)S(1)} %get-tuple-element.90), channel_id=1, source_target_pairs={{16,0},{18,2},{20,4},{22,6},{24,8},{26,10},{28,12},{30,14},{32,16}... | collective-permute-start | bytes 737288 | tf_op jit(solution)/shard_map/ppermute | solution.py:28
  170.7 10.7 %collective-permute-start.21 = (f32[2,48,640]{2,1,0:T(8,128)S(1)}, f32[2,48,640]{2,1,0:T(8,128)S(1)}, u32[]{:S(2)}, u32[]{:S(2)}) collective-permute-start(f32[2,48,640]{2,1,0:T(8,128)S(1)} %get-tuple-element.95), channel_id=1, source_target_pairs={{0,16},{2,18},{4,20},{6,22},{8,24},{10,26},{12,28},{14,30},{16,32}... | collective-permute-start | bytes 737288 | tf_op jit(solution)/shard_map/ppermute | solution.py:28
  174.6 8.2 %collective-permute-start.22 = (f32[2,48,640]{2,1,0:T(8,128)S(1)}, f32[2,48,640]{2,1,0:T(8,128)S(1)}, u32[]{:S(2)}, u32[]{:S(2)}) collective-permute-start(f32[2,48,640]{2,1,0:T(8,128)S(1)} %get-tuple-element.96), channel_id=1, source_target_pairs={{16,0},{18,2},{20,4},{22,6},{24,8},{26,10},{28,12},{30,14},{32,16}... | collective-permute-start | bytes 737288 | tf_op jit(solution)/shard_map/ppermute | solution.py:28
  184.0 9.5 %collective-permute-start.23 = (f32[1,48,640]{2,1,0:T(8,128)S(1)}, f32[1,48,640]{2,1,0:T(8,128)S(1)}, u32[]{:S(2)}, u32[]{:S(2)}) collective-permute-start(f32[1,48,640]{2,1,0:T(8,128)S(1)} %get-tuple-element.100.refs_1_), channel_id=1, source_target_pairs={{0,16},{2,18},{4,20},{6,22},{8,24},{10,26},{12,28},{14,30},{16,32}... | collective-permute-start | bytes 368648 | tf_op jit(solution)/shard_map/ppermute | solution.py:28
  192.6 15.6 %collective-permute-start.28 = (f32[3,48,640]{2,1,0:T(8,128)S(1)}, f32[3,48,640]{2,1,0:T(8,128)S(1)}, u32[]{:S(2)}, u32[]{:S(2)}) collective-permute-start(f32[3,48,640]{2,1,0:T(8,128)S(1)} %get-tuple-element.104), channel_id=1, source_target_pairs={{0,16},{2,18},{4,20},{6,22},{8,24},{10,26},{12,28},{14,30},{16,0},... | collective-permute-start | bytes 1105928 | tf_op jit(solution)/shard_map/ppermute | solution.py:43
  195.2 9.3 %collective-permute-start.25 = (f32[1,48,640]{2,1,0:T(8,128)S(1)}, f32[1,48,640]{2,1,0:T(8,128)S(1)}, u32[]{:S(2)}, u32[]{:S(2)}) collective-permute-start(f32[1,48,640]{2,1,0:T(8,128)S(1)} %get-tuple-element.103.refs_2_.refs_8_), channel_id=1, source_target_pairs={{0,16},{2,18},{4,20},{6,22},{8,24},{10,26},{12,28},{14,30},{16,32}... | collective-permute-start | bytes 368648 | tf_op jit(solution)/shard_map/ppermute | solution.py:28
  211.9 9.2 %collective-permute-start.29 = (f32[1,48,640]{2,1,0:T(8,128)S(1)}, f32[1,48,640]{2,1,0:T(8,128)S(1)}, u32[]{:S(2)}, u32[]{:S(2)}) collective-permute-start(f32[1,48,640]{2,1,0:T(8,128)S(1)} %get-tuple-element.106.refs_2_), channel_id=1, source_target_pairs={{0,32},{2,34},{4,36},{6,38},{8,40},{10,42},{12,44},{14,46},{16,48}... | collective-permute-start | bytes 368648 | tf_op jit(solution)/shard_map/ppermute | solution.py:28
  217.4 8.3 %collective-permute-start.30 = (f32[1,48,640]{2,1,0:T(8,128)S(1)}, f32[1,48,640]{2,1,0:T(8,128)S(1)}, u32[]{:S(2)}, u32[]{:S(2)}) collective-permute-start(f32[1,48,640]{2,1,0:T(8,128)S(1)} %get-tuple-element.106.refs_2_), channel_id=1, source_target_pairs={{32,0},{34,2},{36,4},{38,6},{40,8},{42,10},{44,12},{46,14},{48,16}... | collective-permute-start | bytes 368648 | tf_op jit(solution)/shard_map/ppermute | solution.py:28
  226.4 15.0 %collective-permute-start.31 = (f32[32,640]{1,0:T(8,128)S(1)}, f32[32,640]{1,0:T(8,128)S(1)}, u32[]{:S(2)}, u32[]{:S(2)}) collective-permute-start(f32[32,640]{1,0:T(8,128)S(1)} %get-tuple-element.110), channel_id=1, source_target_pairs={{0,6},{2,8},{4,10},{6,12},{8,14},{10,0},{12,2},{14,4},{16,22},{18,... | collective-permute-start | bytes 245768 | tf_op jit(solution)/shard_map/ppermute | solution.py:127
  230.1 12.0 %collective-permute-start.32 = (f32[32,640]{1,0:T(8,128)S(1)}, f32[32,640]{1,0:T(8,128)S(1)}, u32[]{:S(2)}, u32[]{:S(2)}) collective-permute-start(f32[32,640]{1,0:T(8,128)S(1)} %get-tuple-element.111), channel_id=1, source_target_pairs={{0,10},{2,12},{4,14},{6,0},{8,2},{10,4},{12,6},{14,8},{16,26},{18,... | collective-permute-start | bytes 245768 | tf_op jit(solution)/shard_map/ppermute | solution.py:127
  231.6 15.2 %collective-permute-start.33 = (f32[32,640]{1,0:T(8,128)S(1)}, f32[32,640]{1,0:T(8,128)S(1)}, u32[]{:S(2)}, u32[]{:S(2)}) collective-permute-start(f32[32,640]{1,0:T(8,128)S(1)} %get-tuple-element.112), channel_id=1, source_target_pairs={{0,8},{2,10},{4,12},{6,14},{8,0},{10,2},{12,4},{14,6},{16,24},{18,... | collective-permute-start | bytes 245768 | tf_op jit(solution)/shard_map/ppermute | solution.py:127
  237.3 9.5 %collective-permute-start.34 = (f32[32,640]{1,0:T(8,128)S(1)}, f32[32,640]{1,0:T(8,128)S(1)}, u32[]{:S(2)}, u32[]{:S(2)}) collective-permute-start(f32[32,640]{1,0:T(8,128)S(1)} %get-tuple-element.113), channel_id=1, source_target_pairs={{0,4},{2,6},{4,8},{6,10},{8,12},{10,14},{12,0},{14,2},{16,20},{18,... | collective-permute-start | bytes 245768 | tf_op jit(solution)/shard_map/ppermute | solution.py:127
  237.8 9.0 %collective-permute-start.35 = (f32[32,640]{1,0:T(8,128)S(1)}, f32[32,640]{1,0:T(8,128)S(1)}, u32[]{:S(2)}, u32[]{:S(2)}) collective-permute-start(f32[32,640]{1,0:T(8,128)S(1)} %get-tuple-element.114), channel_id=1, source_target_pairs={{0,12},{2,14},{4,0},{6,2},{8,4},{10,6},{12,8},{14,10},{16,28},{18,... | collective-permute-start | bytes 245768 | tf_op jit(solution)/shard_map/ppermute | solution.py:127
  (19 other events, 173.4 us)

commit v10 on v9

--- a/solution.py
+++ b/solution.py
@@ -323,7 +323,7 @@
 def begin_last(rest4, other, faces5, s, first):
     s[0] = rest4[0] + other[0]
     first[0] = faces5[4] * s[0]
-def sweep_and_rest(s, first, total, second, faces, count, groups=()):
+def sweep_and_rest(s, first, total, second, faces, count):
     east, north, z, w, halo = parts(faces, count)
 
     def sweep(q):
@@ -331,14 +331,7 @@
         total[q] = t
         second[q + 1] = w[q] * t
 
-    if groups:
-        each = count // len(groups)
-        for k, group in enumerate(groups):
-            for copy in group:
-                copy.wait()
-            loop(each, lambda q: sweep(q + k * each))
-    else:
-        loop(count, sweep)
+    loop(count, sweep)
     for side, q, down, up in ((0, -1, halo[4], z[0]), (1, count, z[count], halo[5])):
         second[q + 1] = halo[6 + side] * (1.2 * s[q + 1] + neighbours(
             first[q + 2], first[q + 1], first[q + 3], halo[side], halo[2 + side], down, up))
@@ -350,10 +343,18 @@
     return rest
 
 
-def fine_level(s_own, s_low, s_high, there, there_next, fine, s_next, edge_down, edge_up, s, first, total, second, faces, w_next, semaphores):
-    strip = fine.shape[2]
-    columns = s.shape[2]
-    _, _, _, w, halo = parts(faces, 16)
+def put(ref, k, value):
+    rows = value.shape[0]
+    cut = (ref.shape[1] - rows) // 2
+    if cut:
+        blank = jnp.zeros((cut, value.shape[1]), jnp.float32)
+        ref[k, :cut] = blank
+        ref[k, cut + rows:] = blank
+    ref[k, cut:cut + rows] = value
+
+
+def fine_inside(s_own, there, there_next, s, first, total, second, s_next, faces, w_next, semaphores):
+    east, north, z, w, _ = parts(faces, 16)
     copies = Copies(semaphores)
     weights = copies.start(there.at[49:75], faces.at[49:75])
     groups = []
@@ -361,52 +362,87 @@
         spans = ((4 * k, 4), (16 + 4 * k, 4), (32, 5) if k == 0 else (33 + 4 * k, 4))
         groups.append([copies.start(there.at[a:a + n], faces.at[a:a + n]) for a, n in spans])
     later = copies.start(there_next.at[25:33], w_next)
-    blank = jnp.zeros((HALO - THIN, columns), jnp.float32)
-
-    def place(k, value):
-        s[k, :HALO - THIN] = blank
-        s[k, HALO - THIN:HALO + strip + THIN] = value
-        s[k, HALO + strip + THIN:] = blank
-
-    loop(16, lambda q: place(q + 1, s_own[q]))
+    loop(16, lambda q: put(s, q, s_own[q]))
     weights.wait()
-    place(0, s_low[0])
-    first[0] = halo[8] * s[0]
-    place(0, s_high[1])
-    first[19] = halo[9] * s[0]
-    place(0, s_low[1])
-    first[1] = halo[6] * s[0]
-    place(17, s_high[0])
-    first[18] = halo[7] * s[17]
 
     def start(q):
-        first[q + 2] = w[q] * s[q + 1]
+        first[q] = w[q] * s[q]
 
     loop(16, start)
-    rest = sweep_and_rest(s, first, total, second, faces, 16, groups)
+
+    def sweep(q):
+        t = 1.2 * s[q] + neighbours(first[q], first[q - 1], first[q + 1], east[q], north[q], z[q], z[q + 1])
+        total[q] = t
+        second[q] = w[q] * t
+
+    for k, group in enumerate(groups):
+        for copy in group:
+            copy.wait()
+        low, high = max(4 * k, 1), min(4 * k + 4, 15)
+        loop(high - low, lambda q: sweep(q + low))
+
+    def rest(q):
+        return s[q] - damping * total[q] + neighbours(second[q], second[q - 1], second[q + 1], east[q], north[q], z[q], z[q + 1])
 
     def pair(q):
-        s_next[q] = rest(2 * q) + rest(2 * q + 1)
-        fine[q, 0] = second[2 * q + 1, HALO:HALO + strip]
-        fine[q, 1] = second[2 * q + 2, HALO:HALO + strip]
-
-    loop(8, pair)
+        s_next[q + 1] = rest(2 * q + 2) + rest(2 * q + 3)
+
+    loop(6, pair)
     later.wait()
-    edge_down[0] = s_next[0]
-    edge_down[1] = w_next[1] * s_next[1]
-    edge_up[0] = w_next[6] * s_next[6]
-    edge_up[1] = s_next[7]
+
+
+def fine_ends(s_low, s_high, s, first, total, second, s_inside, faces, w_next, fine, s_next, edge_down, edge_up, frames):
+    east, north, z, w, halo = parts(faces, 16)
+    strip = fine.shape[2]
+    own = slice(HALO, HALO + strip)
+    inner = slice(HALO - THIN, HALO + strip + THIN)
+    for k, value in enumerate((s_low[0], s_low[1], s_high[0], s_high[1])):
+        put(frames, k, value)
+
+    def copy(q):
+        s_next[q + 1] = s_inside[q + 1]
+
+    loop(6, copy)
+
+    def keep(q):
+        fine[q, 1] = second[2 * q + 1, own]
+        fine[q + 1, 0] = second[2 * q + 2, own]
+
+    loop(7, keep)
+
+    def residual(q, t, v, below, above):
+        return s[q] - damping * t + neighbours(v, below, above, east[q], north[q], z[q], z[q + 1])
+
+    near = halo[6] * frames[1]
+    t = 1.2 * frames[1] + neighbours(near, halo[8] * frames[0], first[0], halo[0], halo[2], halo[4], z[0])
+    outside = halo[6] * t
+    t = 1.2 * s[0] + neighbours(first[0], near, first[1], east[0], north[0], z[0], z[1])
+    inside = w[0] * t
+    fine[0, 0] = inside[own]
+    s_next[0] = residual(0, t, inside, outside, second[1]) + residual(1, total[1], second[1], inside, second[2])
+    near = halo[7] * frames[2]
+    t = 1.2 * frames[2] + neighbours(near, first[15], halo[9] * frames[3], halo[1], halo[3], z[16], halo[5])
+    outside = halo[7] * t
+    t = 1.2 * s[15] + neighbours(first[15], first[14], near, east[15], north[15], z[15], z[16])
+    inside = w[15] * t
+    fine[7, 1] = inside[own]
+    s_next[7] = residual(14, total[14], second[14], second[13], inside) + residual(15, t, inside, second[14], outside)
+
+    edge_down[0] = s_next[0, inner]
+    edge_down[1] = w_next[1, inner] * s_next[1, inner]
+    edge_up[0] = w_next[6, inner] * s_next[6, inner]
+    edge_up[1] = s_next[7, inner]
 
 
 def open_level(s_own, faces, low, high, s, first):
     count = s_own.shape[0]
     _, _, _, w, halo = parts(faces, count)
-    s[0] = low[1]
-    s[count + 1] = high[0]
-    first[0] = low[0]
-    first[1] = halo[6] * low[1]
-    first[count + 2] = halo[7] * high[0]
-    first[count + 3] = high[1]
+    put(s, 0, low[1])
+    put(s, count + 1, high[0])
+    put(first, 0, low[0])
+    first[1] = halo[6] * s[0]
+    first[count + 2] = halo[7] * s[count + 1]
+    put(first, count + 3, high[1])
 
     def start(q):
         s[q + 1] = s_own[q]
@@ -460,10 +496,11 @@
         out[q] = second[q + 1, HALO:HALO + strip]
     if len(edges) == 2:
         edge_down, edge_up = edges
-        edge_down[0] = s_next[0]
-        edge_down[1] = w_next[1] * s_next[1]
-        edge_up[0] = w_next[count // 2 - 2] * s_next[count // 2 - 2]
-        edge_up[1] = s_next[count // 2 - 1]
+        inner = slice(HALO - THIN, HALO + strip + THIN)
+        edge_down[0] = s_next[0, inner]
+        edge_down[1] = w_next[1, inner] * s_next[1, inner]
+        edge_up[0] = w_next[count // 2 - 2, inner] * s_next[count // 2 - 2, inner]
+        edge_up[1] = s_next[count // 2 - 1, inner]
     else:
         edges[0][0] = w_next[0] * s_next[0]
 
@@ -569,10 +606,12 @@
 
     s_own = after(s_own, ready).reshape(RING * planes, thin, columns)
     s_low, s_high = exchange(s_own[:2], s_own[-2:])
+    inside = call(
+        fine_inside, [shape(n) for n in (16, 16, 16, 16, 8, 75, 8)], [],
+        s_own, faces0, faces1, limit=28, work=8.0, hbm_in=(1, 2), copies=14)
     fine, s1, edge_down, edge_up = call(
-        fine_level, [(RING, planes, strip, columns), shape(8), shape(2), shape(2)],
-        [shape(18), shape(20), shape(16), shape(18), shape(75), shape(8)],
-        s_own, s_low, s_high, faces0, faces1, limit=28, work=8.0, hbm_in=(3, 4), copies=14)
+        fine_ends, [(RING, planes, strip, columns), shape(8), (2, thin, columns), (2, thin, columns)], [shape(4)],
+        s_low, s_high, *inside, limit=28)
 
     low, high = exchange(edge_down, edge_up)
     plane_out, s2, top, bottom = call(
@@ -587,7 +626,7 @@
         hbm_out=(3,), copies=2)
     low, high = exchange(edge_down, edge_up)
     second2, s3, faces3, edge_down, edge_up = call(
-        second_level, [(4, strip, columns), shape(2), shape(17), shape(2), shape(2)],
+        second_level, [(4, strip, columns), shape(2), shape(17), (2, thin, columns), (2, thin, columns)],
         [shape(6), shape(8), shape(4), shape(6), shape(25)],
         s2, low, high, faces2, halo2, faces3, halo3, limit=14, hbm_in=(3, 4, 5, 6), copies=5)
     low, high = exchange(edge_down, edge_up)

time: 251 us -> 248 us (0.988)
    all_to_all x2, waiting for transfers between devices: 7.8 us -> 4.63 us  [transposed(): lax.all_to_all(value, 'gz', 0, 0, axis_index_groups=ring_groups(lax.axis_...]
    pallas_call x16 -> x17, Pallas kernels: 37.9 us -> 38.7 us  [call(): pl.pallas_call(body, out_shape=shapes, in_specs=[pl.BlockSpec(memory_spac...]
  transfers between devices with their start and end apart: 40 -> 40, of which waited for: 29 -> 26; matrix products, arithmetic and copies ran while one was open for 1% -> 1% of each run, Pallas kernels for 8% -> 11%
where the time goes in v10:
time: 248 us; the launch traced here: 245 us
  starting transfers between devices  130 us (52%)
  waiting for transfers between devices  68.1 us (27%)
  Pallas kernels  38.7 us (16%)
  local copies, waits for them, and re-layouts  6.35 us (3%)
    ppermute x18, starting transfers between devices, shifted(): return lax.ppermute(value, 'gz', pairs)  72.8 us
    ppermute x14, starting transfers between devices, ring_permuted(): lax.ppermute(value, 'gz', [(i, i // RING * RING + (i + by) % RING) for i...  41.1 us
    pallas_call x17, Pallas kernels, call(): pl.pallas_call(body, out_shape=shapes, in_specs=[pl.BlockSpec(memory_spac...  38.7 us
    ppermute x18, waiting for transfers between devices, shifted(): return lax.ppermute(value, 'gz', pairs)  27.7 us
    ppermute x14, waiting for transfers between devices, ring_permuted(): lax.ppermute(value, 'gz', [(i, i // RING * RING + (i + by) % RING) for i...  26.7 us
    all_to_all x2, starting transfers between devices, transposed(): lax.all_to_all(value, 'gz', 0, 0, axis_index_groups=ring_groups(lax.axis_...  9.88 us
    ppermute x2, waiting for transfers between devices, row_shifted(): return lax.ppermute(value, ('gz', 'xy'), pairs)  5.03 us
  transfers between devices with their start and end apart: 40, of which 26 were waited for; matrix products, arithmetic and copies ran while one was open for 1% of the time, Pallas kernels for 11%

profile of v10, /device:TPU:8, one launch (start us, length us, event | category | flops | bytes accessed | tf_op | source)
XLA Modules:
  0.0 245.0 jit_solution(16509255996839253436)
XLA Ops:
  6.4 4.7 %collective-permute-start.2 = (f32[2,48,640]{2,1,0:T(8,128)S(1)}, f32[2,48,640]{2,1,0:T(8,128)S(1)}, u32[]{:S(2)}, u32[]{:S(2)}) collective-permute-start(f32[2,48,640]{2,1,0:T(8,128)S(1)} %get-tuple-element.68), channel_id=1, source_target_pairs={{0,6},{2,8},{4,10},{6,12},{8,14},{10,0},{12,2},{14,4},{16,22},{18,... | collective-permute-start | bytes 737288 | tf_op jit(solution)/shard_map/ppermute | solution.py:127
  13.4 5.5 %collective-permute-start.4 = (f32[2,48,640]{2,1,0:T(8,128)S(1)}, f32[2,48,640]{2,1,0:T(8,128)S(1)}, u32[]{:S(2)}, u32[]{:S(2)}) collective-permute-start(f32[2,48,640]{2,1,0:T(8,128)S(1)} %get-tuple-element.70), channel_id=1, source_target_pairs={{0,8},{2,10},{4,12},{6,14},{8,0},{10,2},{12,4},{14,6},{16,24},{18,... | collective-permute-start | bytes 737288 | tf_op jit(solution)/shard_map/ppermute | solution.py:127
  23.0 7.7 %collective-permute-done.2.refs_3_ = f32[2,48,640]{2,1,0:T(8,128)S(1)} collective-permute-done((f32[2,48,640]{2,1,0:T(8,128)S(1)}, f32[2,48,640]{2,1,0:T(8,128)S(1)}, u32[]{:S(2)}, u32[]{:S(2)}) %collective-permute-start.2) | collective-permute-done | bytes 245792 | tf_op jit(solution)/shard_map/ppermute | solution.py:127
  30.8 5.0 %collective-permute-start.7 = (f32[2,48,640]{2,1,0:T(8,128)S(1)}, f32[2,48,640]{2,1,0:T(8,128)S(1)}, u32[]{:S(2)}, u32[]{:S(2)}) collective-permute-start(f32[2,48,640]{2,1,0:T(8,128)S(1)} %get-tuple-element.73), channel_id=1, source_target_pairs={{0,2},{2,4},{4,6},{6,8},{8,10},{10,12},{12,14},{14,0},{16,18},{18,... | collective-permute-start | bytes 737288 | tf_op jit(solution)/shard_map/ppermute | solution.py:127
  38.6 3.5 %collective-permute-done.4.refs_5_ = f32[2,48,640]{2,1,0:T(8,128)S(1)} collective-permute-done((f32[2,48,640]{2,1,0:T(8,128)S(1)}, f32[2,48,640]{2,1,0:T(8,128)S(1)}, u32[]{:S(2)}, u32[]{:S(2)}) %collective-permute-start.4) | collective-permute-done | bytes 245792 | tf_op jit(solution)/shard_map/ppermute | solution.py:127
  42.2 9.1 %collective-permute-done.5.refs_6_ = f32[2,48,640]{2,1,0:T(8,128)S(1)} collective-permute-done((f32[2,48,640]{2,1,0:T(8,128)S(1)}, f32[2,48,640]{2,1,0:T(8,128)S(1)}, u32[]{:S(2)}, u32[]{:S(2)}) %collective-permute-start.5) | collective-permute-done | bytes 245792 | tf_op jit(solution)/shard_map/ppermute | solution.py:127
  60.1 6.2 %all-to-all-start = ((f32[8,2,40,640]{3,2,1,0:T(8,128)}), f32[8,2,40,640]{3,2,1,0:T(8,128)S(1)}, u32[]{:S(2)}, u32[]{:S(2)}) async-start(f32[8,2,40,640]{3,2,1,0:T(8,128)} %shard_map.61), calls=%async_computation | async-start | bytes 3276800 | tf_op jit(solution)/shard_map/all_to_all | solution.py:47
  66.3 4.5 %collective-permute-start.10 = (f32[3,48,640]{2,1,0:T(8,128)}, f32[3,48,640]{2,1,0:T(8,128)S(1)}, u32[]{:S(2)}, u32[]{:S(2)}) collective-permute-start(f32[3,48,640]{2,1,0:T(8,128)} %get-tuple-element.78), channel_id=1, source_target_pairs={{16,0},{18,2},{20,4},{22,6},{24,8},{26,10},{28,12},{30,14},{32,16}... | collective-permute-start | bytes 1105928 | tf_op jit(solution)/shard_map/ppermute | solution.py:28
  75.6 5.2 %collective-permute-start.12 = (f32[6,48,640]{2,1,0:T(8,128)S(1)}, f32[6,48,640]{2,1,0:T(8,128)S(1)}, u32[]{:S(2)}, u32[]{:S(2)}) collective-permute-start(f32[6,48,640]{2,1,0:T(8,128)S(1)} %copy-done.6), channel_id=1, source_target_pairs={{16,0},{18,2},{20,4},{22,6},{24,8},{26,10},{28,12},{30,14},{32,16}... | collective-permute-start | bytes 2211848 | tf_op jit(solution)/shard_map/ppermute | solution.py:28
  80.8 5.6 %collective-permute-done.9.refs_2_.refs_1_ = f32[3,48,640]{2,1,0:T(8,128)S(1)} collective-permute-done((f32[3,48,640]{2,1,0:T(8,128)S(1)}, f32[3,48,640]{2,1,0:T(8,128)S(1)}, u32[]{:S(2)}, u32[]{:S(2)}) %collective-permute-start.9) | collective-permute-done | bytes 368672 | tf_op jit(solution)/shard_map/ppermute | solution.py:28
  87.9 10.9 %shard_map.62 = (f32[75,48,640]{2,1,0:T(8,128)}, f32[41,48,640]{2,1,0:T(8,128)}, f32[17,48,640]{2,1,0:T(8,128)}, f32[9,48,640]{2,1,0:T(8,128)}, f32[5,48,640]{2,...) custom-call(s32[2]{0:T(128)S(1)} %pad_add_fusion.refs_0_.refs_1_, f32[16,48,640]{2,1,0:T(8,128)S(1)} %copy-done.5, ...), custom_call_target="tpu_custom_call" | custom-call | flops 10000000000 | bytes 30000000 | tf_op jit(solution)/shard_map/pallas_call | solution.py:111
  102.8 4.6 %all-to-all-done.refs_0_ = f32[8,2,40,640]{3,2,1,0:T(8,128)S(1)} async-done(((f32[8,2,40,640]{3,2,1,0:T(8,128)}), f32[8,2,40,640]{3,2,1,0:T(8,128)S(1)}, u32[]{:S(2)}, u32[]{:S(2)}) %all-to-all-start) | async-done | bytes 1638432 | tf_op jit(solution)/shard_map/all_to_all | solution.py:47
  107.5 3.7 %collective-permute-start.13 = (f32[2,40,640]{2,1,0:T(8,128)S(1)}, f32[2,40,640]{2,1,0:T(8,128)S(1)}, u32[]{:S(2)}, u32[]{:S(2)}) collective-permute-start(f32[2,40,640]{2,1,0:T(8,128)S(1)} %get-tuple-element.132), channel_id=1, source_target_pairs={{0,16},{2,18},{4,20},{6,22},{8,24},{10,26},{12,28},{14,30},{16,32}... | collective-permute-start | bytes 614408 | tf_op jit(solution)/shard_map/ppermute | solution.py:28
  111.2 4.7 %collective-permute-start.14 = (f32[2,40,640]{2,1,0:T(8,128)S(1)}, f32[2,40,640]{2,1,0:T(8,128)S(1)}, u32[]{:S(2)}, u32[]{:S(2)}) collective-permute-start(f32[2,40,640]{2,1,0:T(8,128)S(1)} %get-tuple-element.131), channel_id=1, source_target_pairs={{16,0},{18,2},{20,4},{22,6},{24,8},{26,10},{28,12},{30,14},{32,16}... | collective-permute-start | bytes 614408 | tf_op jit(solution)/shard_map/ppermute | solution.py:28
  115.9 7.0 %shard_map.65 = (f32[16,48,640]{2,1,0:T(8,128)S(1)}, f32[16,48,640]{2,1,0:T(8,128)S(1)}, f32[16,48,640]{2,1,0:T(8,128)S(1)}, f32[16,48,640]{2,1,0:T(8,128)S(1)},...) custom-call(f32[16,40,640]{2,1,0:T(8,128)S(1)} %bitcast.12, ...), custom_call_target="tpu_custom_call" | custom-call | flops 8000000000 | bytes 24000000 | tf_op jit(solution)/shard_map/pallas_call | solution.py:111
  126.2 6.0 %collective-permute-start.16 = (f32[2,40,640]{2,1,0:T(8,128)S(1)}, f32[2,40,640]{2,1,0:T(8,128)S(1)}, u32[]{:S(2)}, u32[]{:S(2)}) collective-permute-start(f32[2,40,640]{2,1,0:T(8,128)S(1)} %get-tuple-element.94), channel_id=1, source_target_pairs={{16,0},{18,2},{20,4},{22,6},{24,8},{26,10},{28,12},{30,14},{32,16}... | collective-permute-start | bytes 614408 | tf_op jit(solution)/shard_map/ppermute | solution.py:28
  142.6 4.3 %collective-permute-done.18.refs_2_ = f32[4,8,640]{2,1,0:T(8,128)S(1)} collective-permute-done((f32[4,8,640]{2,1,0:T(8,128)S(1)}, f32[4,8,640]{2,1,0:T(8,128)S(1)}, u32[]{:S(2)}, u32[]{:S(2)}) %collective-permute-start.18) | collective-permute-done | bytes 81952 | tf_op jit(solution)/shard_map/ppermute | solution.py:38
  148.3 3.6 %all-to-all-start.1 = ((f32[8,3,32,640]{3,2,1,0:T(8,128)}), f32[8,3,32,640]{3,2,1,0:T(8,128)S(1)}, u32[]{:S(2)}, u32[]{:S(2)}) async-start(f32[8,3,32,640]{3,2,1,0:T(8,128)} %get-tuple-element.101), calls=%async_computation.1 | async-start | bytes 3932160 | tf_op jit(solution)/shard_map/all_to_all | solution.py:47
  153.9 6.5 %collective-permute-start.20 = (f32[2,48,640]{2,1,0:T(8,128)S(1)}, f32[2,48,640]{2,1,0:T(8,128)S(1)}, u32[]{:S(2)}, u32[]{:S(2)}) collective-permute-start(f32[2,48,640]{2,1,0:T(8,128)S(1)} %get-tuple-element.104), channel_id=1, source_target_pairs={{16,0},{18,2},{20,4},{22,6},{24,8},{26,10},{28,12},{30,14},{32,16}... | collective-permute-start | bytes 737288 | tf_op jit(solution)/shard_map/ppermute | solution.py:28
  164.1 3.3 %shard_map.69 = (f32[4,32,640]{2,1,0:T(8,128)S(1)}, f32[2,48,640]{2,1,0:T(8,128)S(1)}, f32[17,48,640]{2,1,0:T(8,128)S(1)}, f32[2,40,640]{2,1,0:T(8,128)S(1)}, f32[2,40,640]{2,1,0:T(8,128)S(1)}) custom-call(f32[4,48,640]{2,1,0:T(8,128)S(1)} %get-tuple-element.102.refs_0_, f32[2,48,640]{2,1,0:T(8,128)S(1)} %collective-permute-done.19.refs_1_, ...), custom_call_target="tpu_custom_call" | custom-call | tf_op jit(solution)/shard_map/pallas_call | solution.py:111
  167.4 3.9 %collective-permute-start.21 = (f32[2,40,640]{2,1,0:T(8,128)S(1)}, f32[2,40,640]{2,1,0:T(8,128)S(1)}, u32[]{:S(2)}, u32[]{:S(2)}) collective-permute-start(f32[2,40,640]{2,1,0:T(8,128)S(1)} %get-tuple-element.109), channel_id=1, source_target_pairs={{0,16},{2,18},{4,20},{6,22},{8,24},{10,26},{12,28},{14,30},{16,32}... | collective-permute-start | bytes 614408 | tf_op jit(solution)/shard_map/ppermute | solution.py:28
  171.3 4.5 %collective-permute-start.22 = (f32[2,40,640]{2,1,0:T(8,128)S(1)}, f32[2,40,640]{2,1,0:T(8,128)S(1)}, u32[]{:S(2)}, u32[]{:S(2)}) collective-permute-start(f32[2,40,640]{2,1,0:T(8,128)S(1)} %get-tuple-element.110), channel_id=1, source_target_pairs={{16,0},{18,2},{20,4},{22,6},{24,8},{26,10},{28,12},{30,14},{32,16}... | collective-permute-start | bytes 614408 | tf_op jit(solution)/shard_map/ppermute | solution.py:28
  180.2 4.0 %collective-permute-start.23 = (f32[1,48,640]{2,1,0:T(8,128)S(1)}, f32[1,48,640]{2,1,0:T(8,128)S(1)}, u32[]{:S(2)}, u32[]{:S(2)}) collective-permute-start(f32[1,48,640]{2,1,0:T(8,128)S(1)} %get-tuple-element.114.refs_1_), channel_id=1, source_target_pairs={{0,16},{2,18},{4,20},{6,22},{8,24},{10,26},{12,28},{14,30},{16,32}... | collective-permute-start | bytes 368648 | tf_op jit(solution)/shard_map/ppermute | solution.py:28
  184.2 4.5 %collective-permute-start.24 = (f32[1,48,640]{2,1,0:T(8,128)S(1)}, f32[1,48,640]{2,1,0:T(8,128)S(1)}, u32[]{:S(2)}, u32[]{:S(2)}) collective-permute-start(f32[1,48,640]{2,1,0:T(8,128)S(1)} %get-tuple-element.114.refs_1_), channel_id=1, source_target_pairs={{16,0},{18,2},{20,4},{22,6},{24,8},{26,10},{28,12},{30,14},{32,16}... | collective-permute-start | bytes 368648 | tf_op jit(solution)/shard_map/ppermute | solution.py:28
  191.4 3.9 %collective-permute-start.25 = (f32[1,48,640]{2,1,0:T(8,128)S(1)}, f32[1,48,640]{2,1,0:T(8,128)S(1)}, u32[]{:S(2)}, u32[]{:S(2)}) collective-permute-start(f32[1,48,640]{2,1,0:T(8,128)S(1)} %get-tuple-element.117.refs_2_.refs_8_), channel_id=1, source_target_pairs={{0,16},{2,18},{4,20},{6,22},{8,24},{10,26},{12,28},{14,30},{16,32}... | collective-permute-start | bytes 368648 | tf_op jit(solution)/shard_map/ppermute | solution.py:28
  195.2 4.5 %collective-permute-start.26 = (f32[1,48,640]{2,1,0:T(8,128)S(1)}, f32[1,48,640]{2,1,0:T(8,128)S(1)}, u32[]{:S(2)}, u32[]{:S(2)}) collective-permute-start(f32[1,48,640]{2,1,0:T(8,128)S(1)} %get-tuple-element.117.refs_2_.refs_8_), channel_id=1, source_target_pairs={{16,0},{18,2},{20,4},{22,6},{24,8},{26,10},{28,12},{30,14},{32,16}... | collective-permute-start | bytes 368648 | tf_op jit(solution)/shard_map/ppermute | solution.py:28
  205.1 3.0 %collective-permute-done.27.refs_1_ = f32[1,48,640]{2,1,0:T(8,128)S(1)} collective-permute-done((f32[1,48,640]{2,1,0:T(8,128)S(1)}, f32[1,48,640]{2,1,0:T(8,128)S(1)}, u32[]{:S(2)}, u32[]{:S(2)}) %collective-permute-start.27) | collective-permute-done | bytes 122912 | tf_op jit(solution)/shard_map/ppermute | solution.py:43
  208.1 5.9 %collective-permute-start.29 = (f32[1,48,640]{2,1,0:T(8,128)S(1)}, f32[1,48,640]{2,1,0:T(8,128)S(1)}, u32[]{:S(2)}, u32[]{:S(2)}) collective-permute-start(f32[1,48,640]{2,1,0:T(8,128)S(1)} %get-tuple-element.120.refs_2_), channel_id=1, source_target_pairs={{0,32},{2,34},{4,36},{6,38},{8,40},{10,42},{12,44},{14,46},{16,48}... | collective-permute-start | bytes 368648 | tf_op jit(solution)/shard_map/ppermute | solution.py:28
  217.2 5.0 %collective-permute-done.30.refs_4_ = f32[1,48,640]{2,1,0:T(8,128)S(1)} collective-permute-done((f32[1,48,640]{2,1,0:T(8,128)S(1)}, f32[1,48,640]{2,1,0:T(8,128)S(1)}, u32[]{:S(2)}, u32[]{:S(2)}) %collective-permute-start.30) | collective-permute-done | bytes 122912 | tf_op jit(solution)/shard_map/ppermute | solution.py:28
  223.0 3.6 %collective-permute-start.31 = (f32[32,640]{1,0:T(8,128)S(1)}, f32[32,640]{1,0:T(8,128)S(1)}, u32[]{:S(2)}, u32[]{:S(2)}) collective-permute-start(f32[32,640]{1,0:T(8,128)S(1)} %get-tuple-element.124), channel_id=1, source_target_pairs={{0,6},{2,8},{4,10},{6,12},{8,14},{10,0},{12,2},{14,4},{16,22},{18,... | collective-permute-start | bytes 245768 | tf_op jit(solution)/shard_map/ppermute | solution.py:127
  228.1 5.7 %collective-permute-start.33 = (f32[32,640]{1,0:T(8,128)S(1)}, f32[32,640]{1,0:T(8,128)S(1)}, u32[]{:S(2)}, u32[]{:S(2)}) collective-permute-start(f32[32,640]{1,0:T(8,128)S(1)} %get-tuple-element.126), channel_id=1, source_target_pairs={{0,8},{2,10},{4,12},{6,14},{8,0},{10,2},{12,4},{14,6},{16,24},{18,... | collective-permute-start | bytes 245768 | tf_op jit(solution)/shard_map/ppermute | solution.py:127
  234.2 3.7 %collective-permute-start.35 = (f32[32,640]{1,0:T(8,128)S(1)}, f32[32,640]{1,0:T(8,128)S(1)}, u32[]{:S(2)}, u32[]{:S(2)}) collective-permute-start(f32[32,640]{1,0:T(8,128)S(1)} %get-tuple-element.128), channel_id=1, source_target_pairs={{0,12},{2,14},{4,0},{6,2},{8,4},{10,6},{12,8},{14,10},{16,28},{18,... | collective-permute-start | bytes 245768 | tf_op jit(solution)/shard_map/ppermute | solution.py:127
  (99 shorter events, 79.8 us)
Async XLA Ops:
  6.4 24.4 %collective-permute-start.2 = (f32[2,48,640]{2,1,0:T(8,128)S(1)}, f32[2,48,640]{2,1,0:T(8,128)S(1)}, u32[]{:S(2)}, u32[]{:S(2)}) collective-permute-start(f32[2,48,640]{2,1,0:T(8,128)S(1)} %get-tuple-element.68), channel_id=1, source_target_pairs={{0,6},{2,8},{4,10},{6,12},{8,14},{10,0},{12,2},{14,4},{16,22},{18,... | collective-permute-start | bytes 737288 | tf_op jit(solution)/shard_map/ppermute | solution.py:127
  11.1 24.7 %collective-permute-start.3 = (f32[2,48,640]{2,1,0:T(8,128)S(1)}, f32[2,48,640]{2,1,0:T(8,128)S(1)}, u32[]{:S(2)}, u32[]{:S(2)}) collective-permute-start(f32[2,48,640]{2,1,0:T(8,128)S(1)} %get-tuple-element.69), channel_id=1, source_target_pairs={{0,10},{2,12},{4,14},{6,0},{8,2},{10,4},{12,6},{14,8},{16,26},{18,... | collective-permute-start | bytes 737288 | tf_op jit(solution)/shard_map/ppermute | solution.py:127
  13.3 7.1 %collective-permute-start = (f32[2,8,640]{2,1,0:T(8,128)S(1)}, f32[2,8,640]{2,1,0:T(8,128)S(1)}, u32[]{:S(2)}, u32[]{:S(2)}) collective-permute-start(f32[2,8,640]{2,1,0:T(8,128)S(1)} %slice_select_fusion), channel_id=1, source_target_pairs={{0,1},{1,0},{2,3},{3,2},{4,5},{5,4},{6,7},{7,6},{8,9},{9,8},{10,11... | collective-permute-start | bytes 122888 | tf_op jit(solution)/shard_map/ppermute | solution.py:576
  13.4 28.7 %collective-permute-start.4 = (f32[2,48,640]{2,1,0:T(8,128)S(1)}, f32[2,48,640]{2,1,0:T(8,128)S(1)}, u32[]{:S(2)}, u32[]{:S(2)}) collective-permute-start(f32[2,48,640]{2,1,0:T(8,128)S(1)} %get-tuple-element.70), channel_id=1, source_target_pairs={{0,8},{2,10},{4,12},{6,14},{8,0},{10,2},{12,4},{14,6},{16,24},{18,... | collective-permute-start | bytes 737288 | tf_op jit(solution)/shard_map/ppermute | solution.py:127
  18.9 32.3 %collective-permute-start.5 = (f32[2,48,640]{2,1,0:T(8,128)S(1)}, f32[2,48,640]{2,1,0:T(8,128)S(1)}, u32[]{:S(2)}, u32[]{:S(2)}) collective-permute-start(f32[2,48,640]{2,1,0:T(8,128)S(1)} %get-tuple-element.71), channel_id=1, source_target_pairs={{0,4},{2,6},{4,8},{6,10},{8,12},{10,14},{12,0},{14,2},{16,20},{18,... | collective-permute-start | bytes 737288 | tf_op jit(solution)/shard_map/ppermute | solution.py:127
  20.4 32.6 %collective-permute-start.6 = (f32[2,48,640]{2,1,0:T(8,128)S(1)}, f32[2,48,640]{2,1,0:T(8,128)S(1)}, u32[]{:S(2)}, u32[]{:S(2)}) collective-permute-start(f32[2,48,640]{2,1,0:T(8,128)S(1)} %get-tuple-element.72), channel_id=1, source_target_pairs={{0,12},{2,14},{4,0},{6,2},{8,4},{10,6},{12,8},{14,10},{16,28},{18,... | collective-permute-start | bytes 737288 | tf_op jit(solution)/shard_map/ppermute | solution.py:127
  30.8 24.8 %collective-permute-start.7 = (f32[2,48,640]{2,1,0:T(8,128)S(1)}, f32[2,48,640]{2,1,0:T(8,128)S(1)}, u32[]{:S(2)}, u32[]{:S(2)}) collective-permute-start(f32[2,48,640]{2,1,0:T(8,128)S(1)} %get-tuple-element.73), channel_id=1, source_target_pairs={{0,2},{2,4},{4,6},{6,8},{8,10},{10,12},{12,14},{14,0},{16,18},{18,... | collective-permute-start | bytes 737288 | tf_op jit(solution)/shard_map/ppermute | solution.py:127
  35.8 21.5 %collective-permute-start.8 = (f32[2,48,640]{2,1,0:T(8,128)S(1)}, f32[2,48,640]{2,1,0:T(8,128)S(1)}, u32[]{:S(2)}, u32[]{:S(2)}) collective-permute-start(f32[2,48,640]{2,1,0:T(8,128)S(1)} %get-tuple-element.74), channel_id=1, source_target_pairs={{0,14},{2,0},{4,2},{6,4},{8,6},{10,8},{12,10},{14,12},{16,30},{18,... | collective-permute-start | bytes 737288 | tf_op jit(solution)/shard_map/ppermute | solution.py:127
  60.1 47.4 %all-to-all-start = ((f32[8,2,40,640]{3,2,1,0:T(8,128)}), f32[8,2,40,640]{3,2,1,0:T(8,128)S(1)}, u32[]{:S(2)}, u32[]{:S(2)}) async-start(f32[8,2,40,640]{3,2,1,0:T(8,128)} %shard_map.61), calls=%async_computation | async-start | bytes 3276800 | tf_op jit(solution)/shard_map/all_to_all | solution.py:47
  66.3 14.5 %collective-permute-start.10 = (f32[3,48,640]{2,1,0:T(8,128)}, f32[3,48,640]{2,1,0:T(8,128)S(1)}, u32[]{:S(2)}, u32[]{:S(2)}) collective-permute-start(f32[3,48,640]{2,1,0:T(8,128)} %get-tuple-element.78), channel_id=1, source_target_pairs={{16,0},{18,2},{20,4},{22,6},{24,8},{26,10},{28,12},{30,14},{32,16}... | collective-permute-start | bytes 1105928 | tf_op jit(solution)/shard_map/ppermute | solution.py:28
  70.9 15.5 %collective-permute-start.9 = (f32[3,48,640]{2,1,0:T(8,128)S(1)}, f32[3,48,640]{2,1,0:T(8,128)S(1)}, u32[]{:S(2)}, u32[]{:S(2)}) collective-permute-start(f32[3,48,640]{2,1,0:T(8,128)S(1)} %copy-done.8), channel_id=1, source_target_pairs={{0,16},{2,18},{4,20},{6,22},{8,24},{10,26},{12,28},{14,30},{16,32}... | collective-permute-start | bytes 1105928 | tf_op jit(solution)/shard_map/ppermute | solution.py:28
  72.8 27.3 %collective-permute-start.11 = (f32[6,48,640]{2,1,0:T(8,128)S(1)}, f32[6,48,640]{2,1,0:T(8,128)S(1)}, u32[]{:S(2)}, u32[]{:S(2)}) collective-permute-start(f32[6,48,640]{2,1,0:T(8,128)S(1)} %copy-done.7), channel_id=1, source_target_pairs={{0,16},{2,18},{4,20},{6,22},{8,24},{10,26},{12,28},{14,30},{16,32}... | collective-permute-start | bytes 2211848 | tf_op jit(solution)/shard_map/ppermute | solution.py:28
  75.6 24.5 %collective-permute-start.12 = (f32[6,48,640]{2,1,0:T(8,128)S(1)}, f32[6,48,640]{2,1,0:T(8,128)S(1)}, u32[]{:S(2)}, u32[]{:S(2)}) collective-permute-start(f32[6,48,640]{2,1,0:T(8,128)S(1)} %copy-done.6), channel_id=1, source_target_pairs={{16,0},{18,2},{20,4},{22,6},{24,8},{26,10},{28,12},{30,14},{32,16}... | collective-permute-start | bytes 2211848 | tf_op jit(solution)/shard_map/ppermute | solution.py:28
  107.5 15.4 %collective-permute-start.13 = (f32[2,40,640]{2,1,0:T(8,128)S(1)}, f32[2,40,640]{2,1,0:T(8,128)S(1)}, u32[]{:S(2)}, u32[]{:S(2)}) collective-permute-start(f32[2,40,640]{2,1,0:T(8,128)S(1)} %get-tuple-element.132), channel_id=1, source_target_pairs={{0,16},{2,18},{4,20},{6,22},{8,24},{10,26},{12,28},{14,30},{16,32}... | collective-permute-start | bytes 614408 | tf_op jit(solution)/shard_map/ppermute | solution.py:28
  111.2 11.7 %collective-permute-start.14 = (f32[2,40,640]{2,1,0:T(8,128)S(1)}, f32[2,40,640]{2,1,0:T(8,128)S(1)}, u32[]{:S(2)}, u32[]{:S(2)}) collective-permute-start(f32[2,40,640]{2,1,0:T(8,128)S(1)} %get-tuple-element.131), channel_id=1, source_target_pairs={{16,0},{18,2},{20,4},{22,6},{24,8},{26,10},{28,12},{30,14},{32,16}... | collective-permute-start | bytes 614408 | tf_op jit(solution)/shard_map/ppermute | solution.py:28
  124.3 9.8 %collective-permute-start.15 = (f32[2,40,640]{2,1,0:T(8,128)S(1)}, f32[2,40,640]{2,1,0:T(8,128)S(1)}, u32[]{:S(2)}, u32[]{:S(2)}) collective-permute-start(f32[2,40,640]{2,1,0:T(8,128)S(1)} %get-tuple-element.93), channel_id=1, source_target_pairs={{0,16},{2,18},{4,20},{6,22},{8,24},{10,26},{12,28},{14,30},{16,32}... | collective-permute-start | bytes 614408 | tf_op jit(solution)/shard_map/ppermute | solution.py:28
  126.2 9.3 %collective-permute-start.16 = (f32[2,40,640]{2,1,0:T(8,128)S(1)}, f32[2,40,640]{2,1,0:T(8,128)S(1)}, u32[]{:S(2)}, u32[]{:S(2)}) collective-permute-start(f32[2,40,640]{2,1,0:T(8,128)S(1)} %get-tuple-element.94), channel_id=1, source_target_pairs={{16,0},{18,2},{20,4},{22,6},{24,8},{26,10},{28,12},{30,14},{32,16}... | collective-permute-start | bytes 614408 | tf_op jit(solution)/shard_map/ppermute | solution.py:28
  148.3 92.9 %all-to-all-start.1 = ((f32[8,3,32,640]{3,2,1,0:T(8,128)}), f32[8,3,32,640]{3,2,1,0:T(8,128)S(1)}, u32[]{:S(2)}, u32[]{:S(2)}) async-start(f32[8,3,32,640]{3,2,1,0:T(8,128)} %get-tuple-element.101), calls=%async_computation.1 | async-start | bytes 3932160 | tf_op jit(solution)/shard_map/all_to_all | solution.py:47
  151.9 10.7 %collective-permute-start.19 = (f32[2,48,640]{2,1,0:T(8,128)S(1)}, f32[2,48,640]{2,1,0:T(8,128)S(1)}, u32[]{:S(2)}, u32[]{:S(2)}) collective-permute-start(f32[2,48,640]{2,1,0:T(8,128)S(1)} %get-tuple-element.103), channel_id=1, source_target_pairs={{0,16},{2,18},{4,20},{6,22},{8,24},{10,26},{12,28},{14,30},{16,32}... | collective-permute-start | bytes 737288 | tf_op jit(solution)/shard_map/ppermute | solution.py:28
  153.9 10.2 %collective-permute-start.20 = (f32[2,48,640]{2,1,0:T(8,128)S(1)}, f32[2,48,640]{2,1,0:T(8,128)S(1)}, u32[]{:S(2)}, u32[]{:S(2)}) collective-permute-start(f32[2,48,640]{2,1,0:T(8,128)S(1)} %get-tuple-element.104), channel_id=1, source_target_pairs={{16,0},{18,2},{20,4},{22,6},{24,8},{26,10},{28,12},{30,14},{32,16}... | collective-permute-start | bytes 737288 | tf_op jit(solution)/shard_map/ppermute | solution.py:28
  167.4 10.2 %collective-permute-start.21 = (f32[2,40,640]{2,1,0:T(8,128)S(1)}, f32[2,40,640]{2,1,0:T(8,128)S(1)}, u32[]{:S(2)}, u32[]{:S(2)}) collective-permute-start(f32[2,40,640]{2,1,0:T(8,128)S(1)} %get-tuple-element.109), channel_id=1, source_target_pairs={{0,16},{2,18},{4,20},{6,22},{8,24},{10,26},{12,28},{14,30},{16,32}... | collective-permute-start | bytes 614408 | tf_op jit(solution)/shard_map/ppermute | solution.py:28
  171.3 7.8 %collective-permute-start.22 = (f32[2,40,640]{2,1,0:T(8,128)S(1)}, f32[2,40,640]{2,1,0:T(8,128)S(1)}, u32[]{:S(2)}, u32[]{:S(2)}) collective-permute-start(f32[2,40,640]{2,1,0:T(8,128)S(1)} %get-tuple-element.110), channel_id=1, source_target_pairs={{16,0},{18,2},{20,4},{22,6},{24,8},{26,10},{28,12},{30,14},{32,16}... | collective-permute-start | bytes 614408 | tf_op jit(solution)/shard_map/ppermute | solution.py:28
  180.2 9.5 %collective-permute-start.23 = (f32[1,48,640]{2,1,0:T(8,128)S(1)}, f32[1,48,640]{2,1,0:T(8,128)S(1)}, u32[]{:S(2)}, u32[]{:S(2)}) collective-permute-start(f32[1,48,640]{2,1,0:T(8,128)S(1)} %get-tuple-element.114.refs_1_), channel_id=1, source_target_pairs={{0,16},{2,18},{4,20},{6,22},{8,24},{10,26},{12,28},{14,30},{16,32}... | collective-permute-start | bytes 368648 | tf_op jit(solution)/shard_map/ppermute | solution.py:28
  188.8 15.6 %collective-permute-start.28 = (f32[3,48,640]{2,1,0:T(8,128)S(1)}, f32[3,48,640]{2,1,0:T(8,128)S(1)}, u32[]{:S(2)}, u32[]{:S(2)}) collective-permute-start(f32[3,48,640]{2,1,0:T(8,128)S(1)} %get-tuple-element.118), channel_id=1, source_target_pairs={{0,16},{2,18},{4,20},{6,22},{8,24},{10,26},{12,28},{14,30},{16,0},... | collective-permute-start | bytes 1105928 | tf_op jit(solution)/shard_map/ppermute | solution.py:43
  191.4 9.3 %collective-permute-start.25 = (f32[1,48,640]{2,1,0:T(8,128)S(1)}, f32[1,48,640]{2,1,0:T(8,128)S(1)}, u32[]{:S(2)}, u32[]{:S(2)}) collective-permute-start(f32[1,48,640]{2,1,0:T(8,128)S(1)} %get-tuple-element.117.refs_2_.refs_8_), channel_id=1, source_target_pairs={{0,16},{2,18},{4,20},{6,22},{8,24},{10,26},{12,28},{14,30},{16,32}... | collective-permute-start | bytes 368648 | tf_op jit(solution)/shard_map/ppermute | solution.py:28
  208.1 9.2 %collective-permute-start.29 = (f32[1,48,640]{2,1,0:T(8,128)S(1)}, f32[1,48,640]{2,1,0:T(8,128)S(1)}, u32[]{:S(2)}, u32[]{:S(2)}) collective-permute-start(f32[1,48,640]{2,1,0:T(8,128)S(1)} %get-tuple-element.120.refs_2_), channel_id=1, source_target_pairs={{0,32},{2,34},{4,36},{6,38},{8,40},{10,42},{12,44},{14,46},{16,48}... | collective-permute-start | bytes 368648 | tf_op jit(solution)/shard_map/ppermute | solution.py:28
  214.0 8.3 %collective-permute-start.30 = (f32[1,48,640]{2,1,0:T(8,128)S(1)}, f32[1,48,640]{2,1,0:T(8,128)S(1)}, u32[]{:S(2)}, u32[]{:S(2)}) collective-permute-start(f32[1,48,640]{2,1,0:T(8,128)S(1)} %get-tuple-element.120.refs_2_), channel_id=1, source_target_pairs={{32,0},{34,2},{36,4},{38,6},{40,8},{42,10},{44,12},{46,14},{48,16}... | collective-permute-start | bytes 368648 | tf_op jit(solution)/shard_map/ppermute | solution.py:28
  223.0 14.9 %collective-permute-start.31 = (f32[32,640]{1,0:T(8,128)S(1)}, f32[32,640]{1,0:T(8,128)S(1)}, u32[]{:S(2)}, u32[]{:S(2)}) collective-permute-start(f32[32,640]{1,0:T(8,128)S(1)} %get-tuple-element.124), channel_id=1, source_target_pairs={{0,6},{2,8},{4,10},{6,12},{8,14},{10,0},{12,2},{14,4},{16,22},{18,... | collective-permute-start | bytes 245768 | tf_op jit(solution)/shard_map/ppermute | solution.py:127
  226.7 11.9 %collective-permute-start.32 = (f32[32,640]{1,0:T(8,128)S(1)}, f32[32,640]{1,0:T(8,128)S(1)}, u32[]{:S(2)}, u32[]{:S(2)}) collective-permute-start(f32[32,640]{1,0:T(8,128)S(1)} %get-tuple-element.125), channel_id=1, source_target_pairs={{0,10},{2,12},{4,14},{6,0},{8,2},{10,4},{12,6},{14,8},{16,26},{18,... | collective-permute-start | bytes 245768 | tf_op jit(solution)/shard_map/ppermute | solution.py:127
  228.1 15.2 %collective-permute-start.33 = (f32[32,640]{1,0:T(8,128)S(1)}, f32[32,640]{1,0:T(8,128)S(1)}, u32[]{:S(2)}, u32[]{:S(2)}) collective-permute-start(f32[32,640]{1,0:T(8,128)S(1)} %get-tuple-element.126), channel_id=1, source_target_pairs={{0,8},{2,10},{4,12},{6,14},{8,0},{10,2},{12,4},{14,6},{16,24},{18,... | collective-permute-start | bytes 245768 | tf_op jit(solution)/shard_map/ppermute | solution.py:127
  233.8 9.5 %collective-permute-start.34 = (f32[32,640]{1,0:T(8,128)S(1)}, f32[32,640]{1,0:T(8,128)S(1)}, u32[]{:S(2)}, u32[]{:S(2)}) collective-permute-start(f32[32,640]{1,0:T(8,128)S(1)} %get-tuple-element.127), channel_id=1, source_target_pairs={{0,4},{2,6},{4,8},{6,10},{8,12},{10,14},{12,0},{14,2},{16,20},{18,... | collective-permute-start | bytes 245768 | tf_op jit(solution)/shard_map/ppermute | solution.py:127
  234.2 9.1 %collective-permute-start.35 = (f32[32,640]{1,0:T(8,128)S(1)}, f32[32,640]{1,0:T(8,128)S(1)}, u32[]{:S(2)}, u32[]{:S(2)}) collective-permute-start(f32[32,640]{1,0:T(8,128)S(1)} %get-tuple-element.128), channel_id=1, source_target_pairs={{0,12},{2,14},{4,0},{6,2},{8,4},{10,6},{12,8},{14,10},{16,28},{18,... | collective-permute-start | bytes 245768 | tf_op jit(solution)/shard_map/ppermute | solution.py:127
  (19 other events, 176.7 us)

commit v11 on v10

--- a/solution.py
+++ b/solution.py
@@ -320,9 +320,10 @@
         faces5[k] = value
 
 
-def begin_last(rest4, other, faces5, s, first):
-    s[0] = rest4[0] + other[0]
+def begin_last(rest4, other, faces5, s, first, edge):
+    put(s, 0, rest4[0] + other[0])
     first[0] = faces5[4] * s[0]
+    edge[0] = first[0, HALO:HALO + edge.shape[1]]
 def sweep_and_rest(s, first, total, second, faces, count):
     east, north, z, w, halo = parts(faces, count)
 
@@ -467,53 +468,40 @@
     loop(4, pair)
 
 
-def middle_level(s_own, low, high, there, there_halo, there_next, out, s_next, faces_next, *rest_refs):
-    edges, (s, first, total, second, faces, halo_next, semaphores) = rest_refs[:-7], rest_refs[-7:]
+def fetch(*refs):
+    faces2, halo2, faces3, halo3, faces4, out2, out3, out4, semaphores = refs
+    copies = Copies(semaphores)
+    copies.start(faces2, out2.at[0:17])
+    copies.start(halo2, out2.at[17:25])
+    copies.start(faces3, out3.at[0:9])
+    copies.start(halo3, out3.at[9:17])
+    copies.start(faces4, out4)
+    for copy in copies.started:
+        copy.wait()
+
+
+def middle_level(s_own, low, high, faces, faces_next, out, s_next, *rest_refs):
+    edges, (s, first, total, second) = rest_refs[:-4], rest_refs[-4:]
     count = s_own.shape[0]
     strip = out.shape[1]
-    copies = Copies(semaphores)
-    at = 3 * count + 1
-    if count == 4:
-        weights = [copies.start(there.at[at:at + count], faces.at[at:at + count]),
-                   copies.start(there_halo, faces.at[at + count:at + count + 8])]
-        others = copies.start(there.at[0:at], faces.at[0:at])
-        later = [copies.start(there_next.at[0:9], faces_next.at[0:9]), copies.start(halo_next, faces_next.at[9:17])]
-        for copy in weights:
-            copy.wait()
-    else:
-        faces = there
-        later = [copies.start(there_next, faces_next)]
+    inner = slice(HALO - THIN, HALO + strip + THIN)
+    w_next = parts(faces_next, count // 2)[3]
     open_level(s_own, faces, low, high, s, first)
-    if count == 4:
-        others.wait()
     rest = sweep_and_rest(s, first, total, second, faces, count)
     for q in range(count // 2):
         s_next[q] = rest(2 * q) + rest(2 * q + 1)
-    for copy in later:
-        copy.wait()
-    w_next = parts(faces_next, count // 2)[3]
     for q in range(count):
         out[q] = second[q + 1, HALO:HALO + strip]
-    if len(edges) == 2:
+    if count == 4:
         edge_down, edge_up = edges
-        inner = slice(HALO - THIN, HALO + strip + THIN)
         edge_down[0] = s_next[0, inner]
         edge_down[1] = w_next[1, inner] * s_next[1, inner]
-        edge_up[0] = w_next[count // 2 - 2, inner] * s_next[count // 2 - 2, inner]
-        edge_up[1] = s_next[count // 2 - 1, inner]
+        edge_up[0] = w_next[0, inner] * s_next[0, inner]
+        edge_up[1] = s_next[1, inner]
     else:
-        edges[0][0] = w_next[0] * s_next[0]
-
-
-def second_level(s_own, low, high, there, there_halo, there_next, halo_next, out, s_next, faces_next, edge_down, edge_up,
-                 s, first, total, second, faces, semaphores):
-    middle_level(s_own, low, high, there, there_halo, there_next, out, s_next, faces_next, edge_down, edge_up,
-                 s, first, total, second, faces, halo_next, semaphores)
-
-
-def third_level(s_own, low, high, faces, there_next, out, s_next, faces_next, first_next, s, first, total, second, semaphores):
-    middle_level(s_own, low, high, faces, None, there_next, out, s_next, faces_next, first_next,
-                 s, first, total, second, None, None, semaphores)
+        first_next, edge = edges
+        first_next[0] = w_next[0] * s_next[0]
+        edge[0] = first_next[0, inner]
 
 
 def widen(source2, above, below, faces2, fine, plane_out, s, edge_down, edge_up, back, semaphores):
@@ -535,22 +523,33 @@
         copy.wait()
 
 
-def sweep_last(s, first, low, high, faces, total, second):
+def sweep_last(s, first, low, high, faces, total, second, edge, frames):
     east, north, z, w, _ = parts(faces, 1)
-    t = 1.2 * s[0] + neighbours(first[0], low[0], high[0], east[0], north[0], z[0], z[1])
+    put(frames, 0, low[0])
+    put(frames, 1, high[0])
+    t = 1.2 * s[0] + neighbours(first[0], frames[0], frames[1], east[0], north[0], z[0], z[1])
     total[0] = t
     second[0] = w[0] * t
-
-
-def rest_last(s, total, second, low, high, faces, out):
+    cut = HALO - THIN
+    edge[0] = second[0, cut:cut + edge.shape[1]]
+
+
+def rest_last(s, total, second, low, high, faces, out, frames):
     east, north, z, _, _ = parts(faces, 1)
-    out[0] = s[0] - damping * total[0] + neighbours(second[0], low[0], high[0], east[0], north[0], z[0], z[1])
-
-
-def finish(place, s, first, low, high, faces5, second2, second3, second4, *outs):
+    put(frames, 0, low[0])
+    put(frames, 1, high[0])
+    frames[0] = s[0] - damping * total[0] + neighbours(second[0], frames[0], frames[1], east[0], north[0], z[0], z[1])
+    cut = HALO - THIN
+    out[0] = frames[0, cut:cut + out.shape[1]]
+
+
+def finish(place, s, first, low, high, faces5, second2, second3, second4, *rest_refs):
+    outs, frames = rest_refs[:-1], rest_refs[-1]
     own = slice(HALO, HALO + outs[0].shape[0])
+    put(frames, 0, low[0])
+    put(frames, 1, high[0])
     east, north, down, up, w = (faces5[k] for k in range(5))
-    second5 = (w * (1.2 * s[0] + neighbours(first[0], low[0], high[0], east, north, down, up)))[own]
+    second5 = (w * (1.2 * s[0] + neighbours(first[0], frames[0], frames[1], east, north, down, up)))[own]
     for k in range(RING):
         at = (place[0] + k) % RING
         outs[k][...] = ((second2[at // 2] + second3[at // 4]) + second4[0, own]) + second5
@@ -625,23 +624,24 @@
         widen, [shape(4), shape(2), shape(2), (RING, planes + 1, strip, columns)], [], s2, above, below, faces2, fine, plane_out, limit=10,
         hbm_out=(3,), copies=2)
     low, high = exchange(edge_down, edge_up)
-    second2, s3, faces3, edge_down, edge_up = call(
-        second_level, [(4, strip, columns), shape(2), shape(17), (2, thin, columns), (2, thin, columns)],
-        [shape(6), shape(8), shape(4), shape(6), shape(25)],
-        s2, low, high, faces2, halo2, faces3, halo3, limit=14, hbm_in=(3, 4, 5, 6), copies=5)
+    faces2, faces3, faces4 = call(
+        fetch, [shape(25), shape(17), shape(5)], [], faces2, halo2, faces3, halo3, faces4,
+        limit=10, work=4.0, settled=(s2,), hbm_in=range(5), copies=5)
+    second2, s3, edge_down, edge_up = call(
+        middle_level, [(4, strip, columns), shape(2), (2, thin, columns), (2, thin, columns)],
+        [shape(6), shape(8), shape(4), shape(6)], s2, low, high, faces2, faces3, limit=12)
     low, high = exchange(edge_down, edge_up)
-    second3, s4, faces4, first4 = call(
-        third_level, [(2, strip, columns), shape(1), shape(5), shape(1)],
-        [shape(4), shape(6), shape(2), shape(4)],
-        s3, low, high, faces3, faces4, limit=12, hbm_in=(4,), copies=1)
-    low, high = exchange(first4, first4)
-    total4, second4 = call(sweep_last, [shape(1), shape(1)], [], s4, first4, low, high, faces4)
-    low, high = exchange(second4, second4)
-    (rest4,) = call(rest_last, [shape(1)], [], s4, total4, second4, low, high, faces4)
-    s5, first5 = call(begin_last, [shape(1), shape(1)], [], rest4, partner(rest4), faces5)
-    low, high = exchange(first5, first5, 2 * RING)
+    second3, s4, first4, edge = call(
+        middle_level, [(2, strip, columns), shape(1), shape(1), (1, thin, columns)],
+        [shape(4), shape(6), shape(2), shape(4)], s3, low, high, faces3, faces4, limit=10)
+    low, high = exchange(edge, edge)
+    total4, second4, edge = call(sweep_last, [shape(1), shape(1), (1, thin, columns)], [shape(2)], s4, first4, low, high, faces4)
+    low, high = exchange(edge, edge)
+    (rest4,) = call(rest_last, [(1, thin, columns)], [shape(2)], s4, total4, second4, low, high, faces4)
+    s5, first5, edge = call(begin_last, [shape(1), shape(1), (1, strip, columns)], [], rest4, partner(rest4), faces5)
+    low, high = exchange(edge, edge, 2 * RING)
     back = transposed(back)
-    sums = call(finish, [(strip, columns)] * RING, [],
+    sums = call(finish, [(strip, columns)] * RING, [shape(2)],
                 place, s5, first5, low, high, faces5, second2, second3, second4)
     (coarse_return,) = call(collect, [(RING, strip, columns)], [], place, sums[0], *[ring_permuted(sums[k], k) for k in ORDER], settled=(back,))
 

time: 248 us -> 243 us (0.980)
  waiting for transfers between devices: 68.1 us -> 64.1 us
    ppermute x18, waiting for transfers between devices: 27.7 us -> 24.6 us  [shifted(): return lax.ppermute(value, 'gz', pairs)]
    pallas_call x17 -> x18, Pallas kernels: 38.7 us -> 39.7 us  [call(): pl.pallas_call(body, out_shape=shapes, in_specs=[pl.BlockSpec(memory_spac...]
  transfers between devices with their start and end apart: 40 -> 40, of which waited for: 26 -> 25; matrix products, arithmetic and copies ran while one was open for 1% -> 1% of each run, Pallas kernels for 11% -> 12%
where the time goes in v11:
time: 243 us; the launch traced here: 242 us
  starting transfers between devices  130 us (53%)
  waiting for transfers between devices  64.1 us (26%)
  Pallas kernels  39.7 us (16%)
  local copies, waits for them, and re-layouts  6.35 us (3%)
    ppermute x18, starting transfers between devices, shifted(): return lax.ppermute(value, 'gz', pairs)  72.7 us
    ppermute x14, starting transfers between devices, ring_permuted(): lax.ppermute(value, 'gz', [(i, i // RING * RING + (i + by) % RING) for i...  41.1 us
    pallas_call x18, Pallas kernels, call(): pl.pallas_call(body, out_shape=shapes, in_specs=[pl.BlockSpec(memory_spac...  39.7 us
    ppermute x14, waiting for transfers between devices, ring_permuted(): lax.ppermute(value, 'gz', [(i, i // RING * RING + (i + by) % RING) for i...  26.7 us
    ppermute x18, waiting for transfers between devices, shifted(): return lax.ppermute(value, 'gz', pairs)  24.6 us
    all_to_all x2, starting transfers between devices, transposed(): lax.all_to_all(value, 'gz', 0, 0, axis_index_groups=ring_groups(lax.axis_...  9.87 us
    ppermute x2, waiting for transfers between devices, row_shifted(): return lax.ppermute(value, ('gz', 'xy'), pairs)  5.03 us
  transfers between devices with their start and end apart: 40, of which 25 were waited for; matrix products, arithmetic and copies ran while one was open for 1% of the time, Pallas kernels for 12%

profile of v11, /device:TPU:8, one launch (start us, length us, event | category | flops | bytes accessed | tf_op | source)
XLA Modules:
  0.0 242.0 jit_solution(5984816223054949382)
XLA Ops:
  6.4 4.7 %collective-permute-start.2 = (f32[2,48,640]{2,1,0:T(8,128)S(1)}, f32[2,48,640]{2,1,0:T(8,128)S(1)}, u32[]{:S(2)}, u32[]{:S(2)}) collective-permute-start(f32[2,48,640]{2,1,0:T(8,128)S(1)} %get-tuple-element.72), channel_id=1, source_target_pairs={{0,6},{2,8},{4,10},{6,12},{8,14},{10,0},{12,2},{14,4},{16,22},{18,... | collective-permute-start | bytes 737288 | tf_op jit(solution)/shard_map/ppermute | solution.py:127
  13.4 5.5 %collective-permute-start.4 = (f32[2,48,640]{2,1,0:T(8,128)S(1)}, f32[2,48,640]{2,1,0:T(8,128)S(1)}, u32[]{:S(2)}, u32[]{:S(2)}) collective-permute-start(f32[2,48,640]{2,1,0:T(8,128)S(1)} %get-tuple-element.74), channel_id=1, source_target_pairs={{0,8},{2,10},{4,12},{6,14},{8,0},{10,2},{12,4},{14,6},{16,24},{18,... | collective-permute-start | bytes 737288 | tf_op jit(solution)/shard_map/ppermute | solution.py:127
  23.0 7.7 %collective-permute-done.2.refs_3_ = f32[2,48,640]{2,1,0:T(8,128)S(1)} collective-permute-done((f32[2,48,640]{2,1,0:T(8,128)S(1)}, f32[2,48,640]{2,1,0:T(8,128)S(1)}, u32[]{:S(2)}, u32[]{:S(2)}) %collective-permute-start.2) | collective-permute-done | bytes 245792 | tf_op jit(solution)/shard_map/ppermute | solution.py:127
  30.8 5.0 %collective-permute-start.7 = (f32[2,48,640]{2,1,0:T(8,128)S(1)}, f32[2,48,640]{2,1,0:T(8,128)S(1)}, u32[]{:S(2)}, u32[]{:S(2)}) collective-permute-start(f32[2,48,640]{2,1,0:T(8,128)S(1)} %get-tuple-element.77), channel_id=1, source_target_pairs={{0,2},{2,4},{4,6},{6,8},{8,10},{10,12},{12,14},{14,0},{16,18},{18,... | collective-permute-start | bytes 737288 | tf_op jit(solution)/shard_map/ppermute | solution.py:127
  38.6 3.5 %collective-permute-done.4.refs_5_ = f32[2,48,640]{2,1,0:T(8,128)S(1)} collective-permute-done((f32[2,48,640]{2,1,0:T(8,128)S(1)}, f32[2,48,640]{2,1,0:T(8,128)S(1)}, u32[]{:S(2)}, u32[]{:S(2)}) %collective-permute-start.4) | collective-permute-done | bytes 245792 | tf_op jit(solution)/shard_map/ppermute | solution.py:127
  42.2 9.1 %collective-permute-done.5.refs_6_ = f32[2,48,640]{2,1,0:T(8,128)S(1)} collective-permute-done((f32[2,48,640]{2,1,0:T(8,128)S(1)}, f32[2,48,640]{2,1,0:T(8,128)S(1)}, u32[]{:S(2)}, u32[]{:S(2)}) %collective-permute-start.5) | collective-permute-done | bytes 245792 | tf_op jit(solution)/shard_map/ppermute | solution.py:127
  57.3 2.7 %shard_map.60 = (f32[16,48,640]{2,1,0:T(8,128)}, f32[3,48,640]{2,1,0:T(8,128)}, f32[3,48,640]{2,1,0:T(8,128)}, f32[6,48,640]{2,1,0:T(8,128)}, f32[6,48,640]{2,1,0:T(8,128)}, /*index=5*/f32[8,640]{1,0:T(8,128)S(1)}) custom-call(f32[8,2,40,640]{3,2,1,0:T(8,128)} %shard_map.58.refs_0_, s32[2]{0:T(128)S(1)} %pad_add_fusion.refs_0_.refs_1_, ...), custom_call_target="tpu_custom_call" | custom-call | tf_op jit(solution)/shard_map/pallas_call | solution.py:111
  60.1 6.2 %all-to-all-start = ((f32[8,2,40,640]{3,2,1,0:T(8,128)}), f32[8,2,40,640]{3,2,1,0:T(8,128)S(1)}, u32[]{:S(2)}, u32[]{:S(2)}) async-start(f32[8,2,40,640]{3,2,1,0:T(8,128)} %shard_map.61), calls=%async_computation | async-start | bytes 3276800 | tf_op jit(solution)/shard_map/all_to_all | solution.py:47
  66.3 4.5 %collective-permute-start.10 = (f32[3,48,640]{2,1,0:T(8,128)}, f32[3,48,640]{2,1,0:T(8,128)S(1)}, u32[]{:S(2)}, u32[]{:S(2)}) collective-permute-start(f32[3,48,640]{2,1,0:T(8,128)} %get-tuple-element.82), channel_id=1, source_target_pairs={{16,0},{18,2},{20,4},{22,6},{24,8},{26,10},{28,12},{30,14},{32,16}... | collective-permute-start | bytes 1105928 | tf_op jit(solution)/shard_map/ppermute | solution.py:28
  72.8 2.8 %collective-permute-start.11 = (f32[6,48,640]{2,1,0:T(8,128)S(1)}, f32[6,48,640]{2,1,0:T(8,128)S(1)}, u32[]{:S(2)}, u32[]{:S(2)}) collective-permute-start(f32[6,48,640]{2,1,0:T(8,128)S(1)} %copy-done.7), channel_id=1, source_target_pairs={{0,16},{2,18},{4,20},{6,22},{8,24},{10,26},{12,28},{14,30},{16,32}... | collective-permute-start | bytes 2211848 | tf_op jit(solution)/shard_map/ppermute | solution.py:28
  75.6 5.2 %collective-permute-start.12 = (f32[6,48,640]{2,1,0:T(8,128)S(1)}, f32[6,48,640]{2,1,0:T(8,128)S(1)}, u32[]{:S(2)}, u32[]{:S(2)}) collective-permute-start(f32[6,48,640]{2,1,0:T(8,128)S(1)} %copy-done.6), channel_id=1, source_target_pairs={{16,0},{18,2},{20,4},{22,6},{24,8},{26,10},{28,12},{30,14},{32,16}... | collective-permute-start | bytes 2211848 | tf_op jit(solution)/shard_map/ppermute | solution.py:28
  80.8 5.6 %collective-permute-done.9.refs_2_.refs_1_ = f32[3,48,640]{2,1,0:T(8,128)S(1)} collective-permute-done((f32[3,48,640]{2,1,0:T(8,128)S(1)}, f32[3,48,640]{2,1,0:T(8,128)S(1)}, u32[]{:S(2)}, u32[]{:S(2)}) %collective-permute-start.9) | collective-permute-done | bytes 368672 | tf_op jit(solution)/shard_map/ppermute | solution.py:28
  87.9 10.9 %shard_map.62 = (f32[75,48,640]{2,1,0:T(8,128)}, f32[41,48,640]{2,1,0:T(8,128)}, f32[17,48,640]{2,1,0:T(8,128)}, f32[9,48,640]{2,1,0:T(8,128)}, f32[5,48,640]{2,...) custom-call(s32[2]{0:T(128)S(1)} %pad_add_fusion.refs_0_.refs_1_, f32[16,48,640]{2,1,0:T(8,128)S(1)} %copy-done.5, ...), custom_call_target="tpu_custom_call" | custom-call | flops 10000000000 | bytes 30000000 | tf_op jit(solution)/shard_map/pallas_call | solution.py:111
  102.8 4.6 %all-to-all-done.refs_0_ = f32[8,2,40,640]{3,2,1,0:T(8,128)S(1)} async-done(((f32[8,2,40,640]{3,2,1,0:T(8,128)}), f32[8,2,40,640]{3,2,1,0:T(8,128)S(1)}, u32[]{:S(2)}, u32[]{:S(2)}) %all-to-all-start) | async-done | bytes 1638432 | tf_op jit(solution)/shard_map/all_to_all | solution.py:47
  107.5 3.7 %collective-permute-start.13 = (f32[2,40,640]{2,1,0:T(8,128)S(1)}, f32[2,40,640]{2,1,0:T(8,128)S(1)}, u32[]{:S(2)}, u32[]{:S(2)}) collective-permute-start(f32[2,40,640]{2,1,0:T(8,128)S(1)} %get-tuple-element.140), channel_id=1, source_target_pairs={{0,16},{2,18},{4,20},{6,22},{8,24},{10,26},{12,28},{14,30},{16,32}... | collective-permute-start | bytes 614408 | tf_op jit(solution)/shard_map/ppermute | solution.py:28
  111.1 4.7 %collective-permute-start.14 = (f32[2,40,640]{2,1,0:T(8,128)S(1)}, f32[2,40,640]{2,1,0:T(8,128)S(1)}, u32[]{:S(2)}, u32[]{:S(2)}) collective-permute-start(f32[2,40,640]{2,1,0:T(8,128)S(1)} %get-tuple-element.139), channel_id=1, source_target_pairs={{16,0},{18,2},{20,4},{22,6},{24,8},{26,10},{28,12},{30,14},{32,16}... | collective-permute-start | bytes 614408 | tf_op jit(solution)/shard_map/ppermute | solution.py:28
  115.9 7.0 %shard_map.65 = (f32[16,48,640]{2,1,0:T(8,128)S(1)}, f32[16,48,640]{2,1,0:T(8,128)S(1)}, f32[16,48,640]{2,1,0:T(8,128)S(1)}, f32[16,48,640]{2,1,0:T(8,128)S(1)},...) custom-call(f32[16,40,640]{2,1,0:T(8,128)S(1)} %bitcast.12, ...), custom_call_target="tpu_custom_call" | custom-call | flops 8000000000 | bytes 24000000 | tf_op jit(solution)/shard_map/pallas_call | solution.py:111
  126.2 6.0 %collective-permute-start.16 = (f32[2,40,640]{2,1,0:T(8,128)S(1)}, f32[2,40,640]{2,1,0:T(8,128)S(1)}, u32[]{:S(2)}, u32[]{:S(2)}) collective-permute-start(f32[2,40,640]{2,1,0:T(8,128)S(1)} %get-tuple-element.98), channel_id=1, source_target_pairs={{16,0},{18,2},{20,4},{22,6},{24,8},{26,10},{28,12},{30,14},{32,16}... | collective-permute-start | bytes 614408 | tf_op jit(solution)/shard_map/ppermute | solution.py:28
  142.6 4.3 %collective-permute-done.18.refs_2_ = f32[4,8,640]{2,1,0:T(8,128)S(1)} collective-permute-done((f32[4,8,640]{2,1,0:T(8,128)S(1)}, f32[4,8,640]{2,1,0:T(8,128)S(1)}, u32[]{:S(2)}, u32[]{:S(2)}) %collective-permute-start.18) | collective-permute-done | bytes 81952 | tf_op jit(solution)/shard_map/ppermute | solution.py:38
  148.3 3.6 %all-to-all-start.1 = ((f32[8,3,32,640]{3,2,1,0:T(8,128)}), f32[8,3,32,640]{3,2,1,0:T(8,128)S(1)}, u32[]{:S(2)}, u32[]{:S(2)}) async-start(f32[8,3,32,640]{3,2,1,0:T(8,128)} %get-tuple-element.105), calls=%async_computation.1 | async-start | bytes 3932160 | tf_op jit(solution)/shard_map/all_to_all | solution.py:47
  153.8 6.5 %collective-permute-start.20 = (f32[2,48,640]{2,1,0:T(8,128)S(1)}, f32[2,48,640]{2,1,0:T(8,128)S(1)}, u32[]{:S(2)}, u32[]{:S(2)}) collective-permute-start(f32[2,48,640]{2,1,0:T(8,128)S(1)} %get-tuple-element.108), channel_id=1, source_target_pairs={{16,0},{18,2},{20,4},{22,6},{24,8},{26,10},{28,12},{30,14},{32,16}... | collective-permute-start | bytes 737288 | tf_op jit(solution)/shard_map/ppermute | solution.py:28
  165.7 3.9 %collective-permute-start.21 = (f32[2,40,640]{2,1,0:T(8,128)S(1)}, f32[2,40,640]{2,1,0:T(8,128)S(1)}, u32[]{:S(2)}, u32[]{:S(2)}) collective-permute-start(f32[2,40,640]{2,1,0:T(8,128)S(1)} %get-tuple-element.116), channel_id=1, source_target_pairs={{0,16},{2,18},{4,20},{6,22},{8,24},{10,26},{12,28},{14,30},{16,32}... | collective-permute-start | bytes 614408 | tf_op jit(solution)/shard_map/ppermute | solution.py:28
  169.6 4.5 %collective-permute-start.22 = (f32[2,40,640]{2,1,0:T(8,128)S(1)}, f32[2,40,640]{2,1,0:T(8,128)S(1)}, u32[]{:S(2)}, u32[]{:S(2)}) collective-permute-start(f32[2,40,640]{2,1,0:T(8,128)S(1)} %get-tuple-element.117), channel_id=1, source_target_pairs={{16,0},{18,2},{20,4},{22,6},{24,8},{26,10},{28,12},{30,14},{32,16}... | collective-permute-start | bytes 614408 | tf_op jit(solution)/shard_map/ppermute | solution.py:28
  178.5 4.0 %collective-permute-start.23 = (f32[1,40,640]{2,1,0:T(8,128)S(1)}, f32[1,40,640]{2,1,0:T(8,128)S(1)}, u32[]{:S(2)}, u32[]{:S(2)}) collective-permute-start(f32[1,40,640]{2,1,0:T(8,128)S(1)} %get-tuple-element.121), channel_id=1, source_target_pairs={{0,16},{2,18},{4,20},{6,22},{8,24},{10,26},{12,28},{14,30},{16,32}... | collective-permute-start | bytes 307208 | tf_op jit(solution)/shard_map/ppermute | solution.py:28
  182.5 4.5 %collective-permute-start.24 = (f32[1,40,640]{2,1,0:T(8,128)S(1)}, f32[1,40,640]{2,1,0:T(8,128)S(1)}, u32[]{:S(2)}, u32[]{:S(2)}) collective-permute-start(f32[1,40,640]{2,1,0:T(8,128)S(1)} %get-tuple-element.121), channel_id=1, source_target_pairs={{16,0},{18,2},{20,4},{22,6},{24,8},{26,10},{28,12},{30,14},{32,16}... | collective-permute-start | bytes 307208 | tf_op jit(solution)/shard_map/ppermute | solution.py:28
  189.5 3.8 %collective-permute-start.25 = (f32[1,40,640]{2,1,0:T(8,128)S(1)}, f32[1,40,640]{2,1,0:T(8,128)S(1)}, u32[]{:S(2)}, u32[]{:S(2)}) collective-permute-start(f32[1,40,640]{2,1,0:T(8,128)S(1)} %get-tuple-element.124), channel_id=1, source_target_pairs={{0,16},{2,18},{4,20},{6,22},{8,24},{10,26},{12,28},{14,30},{16,32}... | collective-permute-start | bytes 307208 | tf_op jit(solution)/shard_map/ppermute | solution.py:28
  193.3 4.5 %collective-permute-start.26 = (f32[1,40,640]{2,1,0:T(8,128)S(1)}, f32[1,40,640]{2,1,0:T(8,128)S(1)}, u32[]{:S(2)}, u32[]{:S(2)}) collective-permute-start(f32[1,40,640]{2,1,0:T(8,128)S(1)} %get-tuple-element.124), channel_id=1, source_target_pairs={{16,0},{18,2},{20,4},{22,6},{24,8},{26,10},{28,12},{30,14},{32,16}... | collective-permute-start | bytes 307208 | tf_op jit(solution)/shard_map/ppermute | solution.py:28
  205.1 6.3 %collective-permute-start.29 = (f32[1,32,640]{2,1,0:T(8,128)S(1)}, f32[1,32,640]{2,1,0:T(8,128)S(1)}, u32[]{:S(2)}, u32[]{:S(2)}) collective-permute-start(f32[1,32,640]{2,1,0:T(8,128)S(1)} %get-tuple-element.128), channel_id=1, source_target_pairs={{0,32},{2,34},{4,36},{6,38},{8,40},{10,42},{12,44},{14,46},{16,48}... | collective-permute-start | bytes 245768 | tf_op jit(solution)/shard_map/ppermute | solution.py:28
  213.8 5.4 %collective-permute-done.30.refs_4_ = f32[1,32,640]{2,1,0:T(8,128)S(1)} collective-permute-done((f32[1,32,640]{2,1,0:T(8,128)S(1)}, f32[1,32,640]{2,1,0:T(8,128)S(1)}, u32[]{:S(2)}, u32[]{:S(2)}) %collective-permute-start.30) | collective-permute-done | bytes 81952 | tf_op jit(solution)/shard_map/ppermute | solution.py:28
  220.0 4.0 %collective-permute-start.31 = (f32[32,640]{1,0:T(8,128)S(1)}, f32[32,640]{1,0:T(8,128)S(1)}, u32[]{:S(2)}, u32[]{:S(2)}) collective-permute-start(f32[32,640]{1,0:T(8,128)S(1)} %get-tuple-element.132), channel_id=1, source_target_pairs={{0,6},{2,8},{4,10},{6,12},{8,14},{10,0},{12,2},{14,4},{16,22},{18,... | collective-permute-start | bytes 245768 | tf_op jit(solution)/shard_map/ppermute | solution.py:127
  225.1 5.6 %collective-permute-start.33 = (f32[32,640]{1,0:T(8,128)S(1)}, f32[32,640]{1,0:T(8,128)S(1)}, u32[]{:S(2)}, u32[]{:S(2)}) collective-permute-start(f32[32,640]{1,0:T(8,128)S(1)} %get-tuple-element.134), channel_id=1, source_target_pairs={{0,8},{2,10},{4,12},{6,14},{8,0},{10,2},{12,4},{14,6},{16,24},{18,... | collective-permute-start | bytes 245768 | tf_op jit(solution)/shard_map/ppermute | solution.py:127
  231.6 3.3 %collective-permute-start.35 = (f32[32,640]{1,0:T(8,128)S(1)}, f32[32,640]{1,0:T(8,128)S(1)}, u32[]{:S(2)}, u32[]{:S(2)}) collective-permute-start(f32[32,640]{1,0:T(8,128)S(1)} %get-tuple-element.136), channel_id=1, source_target_pairs={{0,12},{2,14},{4,0},{6,2},{8,4},{10,6},{12,8},{14,10},{16,28},{18,... | collective-permute-start | bytes 245768 | tf_op jit(solution)/shard_map/ppermute | solution.py:127
  (100 shorter events, 76.9 us)
Async XLA Ops:
  6.4 24.4 %collective-permute-start.2 = (f32[2,48,640]{2,1,0:T(8,128)S(1)}, f32[2,48,640]{2,1,0:T(8,128)S(1)}, u32[]{:S(2)}, u32[]{:S(2)}) collective-permute-start(f32[2,48,640]{2,1,0:T(8,128)S(1)} %get-tuple-element.72), channel_id=1, source_target_pairs={{0,6},{2,8},{4,10},{6,12},{8,14},{10,0},{12,2},{14,4},{16,22},{18,... | collective-permute-start | bytes 737288 | tf_op jit(solution)/shard_map/ppermute | solution.py:127
  11.1 24.7 %collective-permute-start.3 = (f32[2,48,640]{2,1,0:T(8,128)S(1)}, f32[2,48,640]{2,1,0:T(8,128)S(1)}, u32[]{:S(2)}, u32[]{:S(2)}) collective-permute-start(f32[2,48,640]{2,1,0:T(8,128)S(1)} %get-tuple-element.73), channel_id=1, source_target_pairs={{0,10},{2,12},{4,14},{6,0},{8,2},{10,4},{12,6},{14,8},{16,26},{18,... | collective-permute-start | bytes 737288 | tf_op jit(solution)/shard_map/ppermute | solution.py:127
  13.3 7.1 %collective-permute-start = (f32[2,8,640]{2,1,0:T(8,128)S(1)}, f32[2,8,640]{2,1,0:T(8,128)S(1)}, u32[]{:S(2)}, u32[]{:S(2)}) collective-permute-start(f32[2,8,640]{2,1,0:T(8,128)S(1)} %slice_select_fusion), channel_id=1, source_target_pairs={{0,1},{1,0},{2,3},{3,2},{4,5},{5,4},{6,7},{7,6},{8,9},{9,8},{10,11... | collective-permute-start | bytes 122888 | tf_op jit(solution)/shard_map/ppermute | solution.py:575
  13.4 28.7 %collective-permute-start.4 = (f32[2,48,640]{2,1,0:T(8,128)S(1)}, f32[2,48,640]{2,1,0:T(8,128)S(1)}, u32[]{:S(2)}, u32[]{:S(2)}) collective-permute-start(f32[2,48,640]{2,1,0:T(8,128)S(1)} %get-tuple-element.74), channel_id=1, source_target_pairs={{0,8},{2,10},{4,12},{6,14},{8,0},{10,2},{12,4},{14,6},{16,24},{18,... | collective-permute-start | bytes 737288 | tf_op jit(solution)/shard_map/ppermute | solution.py:127
  18.9 32.3 %collective-permute-start.5 = (f32[2,48,640]{2,1,0:T(8,128)S(1)}, f32[2,48,640]{2,1,0:T(8,128)S(1)}, u32[]{:S(2)}, u32[]{:S(2)}) collective-permute-start(f32[2,48,640]{2,1,0:T(8,128)S(1)} %get-tuple-element.75), channel_id=1, source_target_pairs={{0,4},{2,6},{4,8},{6,10},{8,12},{10,14},{12,0},{14,2},{16,20},{18,... | collective-permute-start | bytes 737288 | tf_op jit(solution)/shard_map/ppermute | solution.py:127
  20.4 32.6 %collective-permute-start.6 = (f32[2,48,640]{2,1,0:T(8,128)S(1)}, f32[2,48,640]{2,1,0:T(8,128)S(1)}, u32[]{:S(2)}, u32[]{:S(2)}) collective-permute-start(f32[2,48,640]{2,1,0:T(8,128)S(1)} %get-tuple-element.76), channel_id=1, source_target_pairs={{0,12},{2,14},{4,0},{6,2},{8,4},{10,6},{12,8},{14,10},{16,28},{18,... | collective-permute-start | bytes 737288 | tf_op jit(solution)/shard_map/ppermute | solution.py:127
  30.8 24.8 %collective-permute-start.7 = (f32[2,48,640]{2,1,0:T(8,128)S(1)}, f32[2,48,640]{2,1,0:T(8,128)S(1)}, u32[]{:S(2)}, u32[]{:S(2)}) collective-permute-start(f32[2,48,640]{2,1,0:T(8,128)S(1)} %get-tuple-element.77), channel_id=1, source_target_pairs={{0,2},{2,4},{4,6},{6,8},{8,10},{10,12},{12,14},{14,0},{16,18},{18,... | collective-permute-start | bytes 737288 | tf_op jit(solution)/shard_map/ppermute | solution.py:127
  35.8 21.5 %collective-permute-start.8 = (f32[2,48,640]{2,1,0:T(8,128)S(1)}, f32[2,48,640]{2,1,0:T(8,128)S(1)}, u32[]{:S(2)}, u32[]{:S(2)}) collective-permute-start(f32[2,48,640]{2,1,0:T(8,128)S(1)} %get-tuple-element.78), channel_id=1, source_target_pairs={{0,14},{2,0},{4,2},{6,4},{8,6},{10,8},{12,10},{14,12},{16,30},{18,... | collective-permute-start | bytes 737288 | tf_op jit(solution)/shard_map/ppermute | solution.py:127
  60.1 47.4 %all-to-all-start = ((f32[8,2,40,640]{3,2,1,0:T(8,128)}), f32[8,2,40,640]{3,2,1,0:T(8,128)S(1)}, u32[]{:S(2)}, u32[]{:S(2)}) async-start(f32[8,2,40,640]{3,2,1,0:T(8,128)} %shard_map.61), calls=%async_computation | async-start | bytes 3276800 | tf_op jit(solution)/shard_map/all_to_all | solution.py:47
  66.3 14.5 %collective-permute-start.10 = (f32[3,48,640]{2,1,0:T(8,128)}, f32[3,48,640]{2,1,0:T(8,128)S(1)}, u32[]{:S(2)}, u32[]{:S(2)}) collective-permute-start(f32[3,48,640]{2,1,0:T(8,128)} %get-tuple-element.82), channel_id=1, source_target_pairs={{16,0},{18,2},{20,4},{22,6},{24,8},{26,10},{28,12},{30,14},{32,16}... | collective-permute-start | bytes 1105928 | tf_op jit(solution)/shard_map/ppermute | solution.py:28
  70.9 15.5 %collective-permute-start.9 = (f32[3,48,640]{2,1,0:T(8,128)S(1)}, f32[3,48,640]{2,1,0:T(8,128)S(1)}, u32[]{:S(2)}, u32[]{:S(2)}) collective-permute-start(f32[3,48,640]{2,1,0:T(8,128)S(1)} %copy-done.8), channel_id=1, source_target_pairs={{0,16},{2,18},{4,20},{6,22},{8,24},{10,26},{12,28},{14,30},{16,32}... | collective-permute-start | bytes 1105928 | tf_op jit(solution)/shard_map/ppermute | solution.py:28
  72.8 27.3 %collective-permute-start.11 = (f32[6,48,640]{2,1,0:T(8,128)S(1)}, f32[6,48,640]{2,1,0:T(8,128)S(1)}, u32[]{:S(2)}, u32[]{:S(2)}) collective-permute-start(f32[6,48,640]{2,1,0:T(8,128)S(1)} %copy-done.7), channel_id=1, source_target_pairs={{0,16},{2,18},{4,20},{6,22},{8,24},{10,26},{12,28},{14,30},{16,32}... | collective-permute-start | bytes 2211848 | tf_op jit(solution)/shard_map/ppermute | solution.py:28
  75.6 24.5 %collective-permute-start.12 = (f32[6,48,640]{2,1,0:T(8,128)S(1)}, f32[6,48,640]{2,1,0:T(8,128)S(1)}, u32[]{:S(2)}, u32[]{:S(2)}) collective-permute-start(f32[6,48,640]{2,1,0:T(8,128)S(1)} %copy-done.6), channel_id=1, source_target_pairs={{16,0},{18,2},{20,4},{22,6},{24,8},{26,10},{28,12},{30,14},{32,16}... | collective-permute-start | bytes 2211848 | tf_op jit(solution)/shard_map/ppermute | solution.py:28
  107.5 15.4 %collective-permute-start.13 = (f32[2,40,640]{2,1,0:T(8,128)S(1)}, f32[2,40,640]{2,1,0:T(8,128)S(1)}, u32[]{:S(2)}, u32[]{:S(2)}) collective-permute-start(f32[2,40,640]{2,1,0:T(8,128)S(1)} %get-tuple-element.140), channel_id=1, source_target_pairs={{0,16},{2,18},{4,20},{6,22},{8,24},{10,26},{12,28},{14,30},{16,32}... | collective-permute-start | bytes 614408 | tf_op jit(solution)/shard_map/ppermute | solution.py:28
  111.1 11.7 %collective-permute-start.14 = (f32[2,40,640]{2,1,0:T(8,128)S(1)}, f32[2,40,640]{2,1,0:T(8,128)S(1)}, u32[]{:S(2)}, u32[]{:S(2)}) collective-permute-start(f32[2,40,640]{2,1,0:T(8,128)S(1)} %get-tuple-element.139), channel_id=1, source_target_pairs={{16,0},{18,2},{20,4},{22,6},{24,8},{26,10},{28,12},{30,14},{32,16}... | collective-permute-start | bytes 614408 | tf_op jit(solution)/shard_map/ppermute | solution.py:28
  124.3 9.8 %collective-permute-start.15 = (f32[2,40,640]{2,1,0:T(8,128)S(1)}, f32[2,40,640]{2,1,0:T(8,128)S(1)}, u32[]{:S(2)}, u32[]{:S(2)}) collective-permute-start(f32[2,40,640]{2,1,0:T(8,128)S(1)} %get-tuple-element.97), channel_id=1, source_target_pairs={{0,16},{2,18},{4,20},{6,22},{8,24},{10,26},{12,28},{14,30},{16,32}... | collective-permute-start | bytes 614408 | tf_op jit(solution)/shard_map/ppermute | solution.py:28
  126.2 9.3 %collective-permute-start.16 = (f32[2,40,640]{2,1,0:T(8,128)S(1)}, f32[2,40,640]{2,1,0:T(8,128)S(1)}, u32[]{:S(2)}, u32[]{:S(2)}) collective-permute-start(f32[2,40,640]{2,1,0:T(8,128)S(1)} %get-tuple-element.98), channel_id=1, source_target_pairs={{16,0},{18,2},{20,4},{22,6},{24,8},{26,10},{28,12},{30,14},{32,16}... | collective-permute-start | bytes 614408 | tf_op jit(solution)/shard_map/ppermute | solution.py:28
  148.3 89.9 %all-to-all-start.1 = ((f32[8,3,32,640]{3,2,1,0:T(8,128)}), f32[8,3,32,640]{3,2,1,0:T(8,128)S(1)}, u32[]{:S(2)}, u32[]{:S(2)}) async-start(f32[8,3,32,640]{3,2,1,0:T(8,128)} %get-tuple-element.105), calls=%async_computation.1 | async-start | bytes 3932160 | tf_op jit(solution)/shard_map/all_to_all | solution.py:47
  151.9 11.1 %collective-permute-start.19 = (f32[2,48,640]{2,1,0:T(8,128)S(1)}, f32[2,48,640]{2,1,0:T(8,128)S(1)}, u32[]{:S(2)}, u32[]{:S(2)}) collective-permute-start(f32[2,48,640]{2,1,0:T(8,128)S(1)} %get-tuple-element.107), channel_id=1, source_target_pairs={{0,16},{2,18},{4,20},{6,22},{8,24},{10,26},{12,28},{14,30},{16,32}... | collective-permute-start | bytes 737288 | tf_op jit(solution)/shard_map/ppermute | solution.py:28
  153.8 10.2 %collective-permute-start.20 = (f32[2,48,640]{2,1,0:T(8,128)S(1)}, f32[2,48,640]{2,1,0:T(8,128)S(1)}, u32[]{:S(2)}, u32[]{:S(2)}) collective-permute-start(f32[2,48,640]{2,1,0:T(8,128)S(1)} %get-tuple-element.108), channel_id=1, source_target_pairs={{16,0},{18,2},{20,4},{22,6},{24,8},{26,10},{28,12},{30,14},{32,16}... | collective-permute-start | bytes 737288 | tf_op jit(solution)/shard_map/ppermute | solution.py:28
  165.7 10.2 %collective-permute-start.21 = (f32[2,40,640]{2,1,0:T(8,128)S(1)}, f32[2,40,640]{2,1,0:T(8,128)S(1)}, u32[]{:S(2)}, u32[]{:S(2)}) collective-permute-start(f32[2,40,640]{2,1,0:T(8,128)S(1)} %get-tuple-element.116), channel_id=1, source_target_pairs={{0,16},{2,18},{4,20},{6,22},{8,24},{10,26},{12,28},{14,30},{16,32}... | collective-permute-start | bytes 614408 | tf_op jit(solution)/shard_map/ppermute | solution.py:28
  169.6 7.8 %collective-permute-start.22 = (f32[2,40,640]{2,1,0:T(8,128)S(1)}, f32[2,40,640]{2,1,0:T(8,128)S(1)}, u32[]{:S(2)}, u32[]{:S(2)}) collective-permute-start(f32[2,40,640]{2,1,0:T(8,128)S(1)} %get-tuple-element.117), channel_id=1, source_target_pairs={{16,0},{18,2},{20,4},{22,6},{24,8},{26,10},{28,12},{30,14},{32,16}... | collective-permute-start | bytes 614408 | tf_op jit(solution)/shard_map/ppermute | solution.py:28
  174.2 28.1 %collective-permute-start.28 = (f32[3,48,640]{2,1,0:T(8,128)S(1)}, f32[3,48,640]{2,1,0:T(8,128)S(1)}, u32[]{:S(2)}, u32[]{:S(2)}) collective-permute-start(f32[3,48,640]{2,1,0:T(8,128)S(1)} %get-tuple-element.125), channel_id=1, source_target_pairs={{0,16},{2,18},{4,20},{6,22},{8,24},{10,26},{12,28},{14,30},{16,0},... | collective-permute-start | bytes 1105928 | tf_op jit(solution)/shard_map/ppermute | solution.py:43
  178.5 9.3 %collective-permute-start.23 = (f32[1,40,640]{2,1,0:T(8,128)S(1)}, f32[1,40,640]{2,1,0:T(8,128)S(1)}, u32[]{:S(2)}, u32[]{:S(2)}) collective-permute-start(f32[1,40,640]{2,1,0:T(8,128)S(1)} %get-tuple-element.121), channel_id=1, source_target_pairs={{0,16},{2,18},{4,20},{6,22},{8,24},{10,26},{12,28},{14,30},{16,32}... | collective-permute-start | bytes 307208 | tf_op jit(solution)/shard_map/ppermute | solution.py:28
  189.5 9.1 %collective-permute-start.25 = (f32[1,40,640]{2,1,0:T(8,128)S(1)}, f32[1,40,640]{2,1,0:T(8,128)S(1)}, u32[]{:S(2)}, u32[]{:S(2)}) collective-permute-start(f32[1,40,640]{2,1,0:T(8,128)S(1)} %get-tuple-element.124), channel_id=1, source_target_pairs={{0,16},{2,18},{4,20},{6,22},{8,24},{10,26},{12,28},{14,30},{16,32}... | collective-permute-start | bytes 307208 | tf_op jit(solution)/shard_map/ppermute | solution.py:28
  205.1 8.7 %collective-permute-start.29 = (f32[1,32,640]{2,1,0:T(8,128)S(1)}, f32[1,32,640]{2,1,0:T(8,128)S(1)}, u32[]{:S(2)}, u32[]{:S(2)}) collective-permute-start(f32[1,32,640]{2,1,0:T(8,128)S(1)} %get-tuple-element.128), channel_id=1, source_target_pairs={{0,32},{2,34},{4,36},{6,38},{8,40},{10,42},{12,44},{14,46},{16,48}... | collective-permute-start | bytes 245768 | tf_op jit(solution)/shard_map/ppermute | solution.py:28
  211.4 7.8 %collective-permute-start.30 = (f32[1,32,640]{2,1,0:T(8,128)S(1)}, f32[1,32,640]{2,1,0:T(8,128)S(1)}, u32[]{:S(2)}, u32[]{:S(2)}) collective-permute-start(f32[1,32,640]{2,1,0:T(8,128)S(1)} %get-tuple-element.128), channel_id=1, source_target_pairs={{32,0},{34,2},{36,4},{38,6},{40,8},{42,10},{44,12},{46,14},{48,16}... | collective-permute-start | bytes 245768 | tf_op jit(solution)/shard_map/ppermute | solution.py:28
  220.0 14.9 %collective-permute-start.31 = (f32[32,640]{1,0:T(8,128)S(1)}, f32[32,640]{1,0:T(8,128)S(1)}, u32[]{:S(2)}, u32[]{:S(2)}) collective-permute-start(f32[32,640]{1,0:T(8,128)S(1)} %get-tuple-element.132), channel_id=1, source_target_pairs={{0,6},{2,8},{4,10},{6,12},{8,14},{10,0},{12,2},{14,4},{16,22},{18,... | collective-permute-start | bytes 245768 | tf_op jit(solution)/shard_map/ppermute | solution.py:127
  224.0 11.7 %collective-permute-start.32 = (f32[32,640]{1,0:T(8,128)S(1)}, f32[32,640]{1,0:T(8,128)S(1)}, u32[]{:S(2)}, u32[]{:S(2)}) collective-permute-start(f32[32,640]{1,0:T(8,128)S(1)} %get-tuple-element.133), channel_id=1, source_target_pairs={{0,10},{2,12},{4,14},{6,0},{8,2},{10,4},{12,6},{14,8},{16,26},{18,... | collective-permute-start | bytes 245768 | tf_op jit(solution)/shard_map/ppermute | solution.py:127
  225.1 15.1 %collective-permute-start.33 = (f32[32,640]{1,0:T(8,128)S(1)}, f32[32,640]{1,0:T(8,128)S(1)}, u32[]{:S(2)}, u32[]{:S(2)}) collective-permute-start(f32[32,640]{1,0:T(8,128)S(1)} %get-tuple-element.134), channel_id=1, source_target_pairs={{0,8},{2,10},{4,12},{6,14},{8,0},{10,2},{12,4},{14,6},{16,24},{18,... | collective-permute-start | bytes 245768 | tf_op jit(solution)/shard_map/ppermute | solution.py:127
  230.8 9.5 %collective-permute-start.34 = (f32[32,640]{1,0:T(8,128)S(1)}, f32[32,640]{1,0:T(8,128)S(1)}, u32[]{:S(2)}, u32[]{:S(2)}) collective-permute-start(f32[32,640]{1,0:T(8,128)S(1)} %get-tuple-element.135), channel_id=1, source_target_pairs={{0,4},{2,6},{4,8},{6,10},{8,12},{10,14},{12,0},{14,2},{16,20},{18,... | collective-permute-start | bytes 245768 | tf_op jit(solution)/shard_map/ppermute | solution.py:127
  231.6 8.7 %collective-permute-start.35 = (f32[32,640]{1,0:T(8,128)S(1)}, f32[32,640]{1,0:T(8,128)S(1)}, u32[]{:S(2)}, u32[]{:S(2)}) collective-permute-start(f32[32,640]{1,0:T(8,128)S(1)} %get-tuple-element.136), channel_id=1, source_target_pairs={{0,12},{2,14},{4,0},{6,2},{8,4},{10,6},{12,8},{14,10},{16,28},{18,... | collective-permute-start | bytes 245768 | tf_op jit(solution)/shard_map/ppermute | solution.py:127
  (19 other events, 174.9 us)

commit v12 on v11

--- a/solution.py
+++ b/solution.py
@@ -113,7 +113,7 @@
         out_shape=shapes,
         in_specs=[pl.BlockSpec(memory_space=pl.ANY)] * len(settled) + kinds,
         out_specs=[hbm if i in hbm_out else vmem for i in range(len(shapes))],
-        scratch_shapes=[pltpu.VMEM(s, jnp.float32) for s in scratch] + ([pltpu.SemaphoreType.DMA((copies,))] if copies else []),
+        scratch_shapes=[pltpu.VMEM(s, jnp.float32) if isinstance(s, tuple) else s for s in scratch] + ([pltpu.SemaphoreType.DMA((copies,))] if copies else []),
         compiler_params=pltpu.CompilerParams(vmem_limit_bytes=limit * 1024 * 1024),
         cost_estimate=cost,
     )(*settled, *args)
@@ -153,13 +153,19 @@
         return copy
 
 
-def cut_conduct(place, labels, fraction, top, bottom, *rest):
-    outs, full = rest[:-1], rest[-1]
+def cut_conduct(place, labels_there, fraction_there, top, bottom, *rest):
+    outs, (full, labels, fraction, semaphores) = rest[:RING], rest[RING:]
     planes, rows, _ = labels.shape
     strip = rows // RING
+    copies = Copies(semaphores)
+    for p in range(planes):
+        copies.start(labels_there.at[p], labels.at[p])
+        copies.start(fraction_there.at[p], fraction.at[p])
     for p in range(planes):
         full[p, :HALO] = top[p]
         full[p, HALO + rows:] = bottom[p]
+        copies.started[2 * p].wait()
+        copies.started[2 * p + 1].wait()
         for k in range(RING):
             at = k * strip
             full[p, HALO + at:HALO + at + strip] = conductivity(labels[p, at:at + strip], fraction[p, at:at + strip])
@@ -582,8 +588,9 @@
     place = jnp.stack([at_ring % RING, at_ring // RING % 2]).astype(jnp.int32)
     c_top, c_bottom = edges_of(conductivity(labels[:, :HALO], fraction[:, :HALO]),
                                conductivity(labels[:, rows - HALO:], fraction[:, rows - HALO:]))
-    cuts = call(cut_conduct, [(planes, frame, columns)] * RING, [(planes, rows + 2 * HALO, columns)],
-                place, labels, fraction, c_top, c_bottom, limit=10)
+    cuts = call(cut_conduct, [(planes, frame, columns)] * RING,
+                [(planes, rows + 2 * HALO, columns), pltpu.VMEM((planes, rows, columns), jnp.int32), (planes, rows, columns)],
+                place, labels, fraction, c_top, c_bottom, limit=14, hbm_in=(1, 2), copies=4)
     s_top, s_bottom = edges_of(right_side[:, :HALO], right_side[:, rows - HALO:])
     thin = strip + 2 * THIN
     (s_cut,) = call(cut_source, [(RING, planes, thin, columns)], [], right_side, s_top, s_bottom, limit=10)

time: 243 us -> 242 us (level)
  local copies, waits for them, and re-layouts: 6.35 us -> 3.73 us
    unnamed x22 -> x18, local copies, waits for them, and re-layouts: 4.21 us -> 1.58 us
where the time goes in v12:
time: 242 us; the launch traced here: 241 us
  starting transfers between devices  130 us (54%)
  waiting for transfers between devices  64.2 us (27%)
  Pallas kernels  41.3 us (17%)
  local copies, waits for them, and re-layouts  3.73 us (2%)
    ppermute x18, starting transfers between devices, shifted(): return lax.ppermute(value, 'gz', pairs)  72.7 us
    pallas_call x18, Pallas kernels, call(): pl.pallas_call(body, out_shape=shapes, in_specs=[pl.BlockSpec(memory_spac...  41.3 us
    ppermute x14, starting transfers between devices, ring_permuted(): lax.ppermute(value, 'gz', [(i, i // RING * RING + (i + by) % RING) for i...  41.1 us
    ppermute x14, waiting for transfers between devices, ring_permuted(): lax.ppermute(value, 'gz', [(i, i // RING * RING + (i + by) % RING) for i...  26.7 us
    ppermute x18, waiting for transfers between devices, shifted(): return lax.ppermute(value, 'gz', pairs)  24.6 us
    all_to_all x2, starting transfers between devices, transposed(): lax.all_to_all(value, 'gz', 0, 0, axis_index_groups=ring_groups(lax.axis_...  9.88 us
    ppermute x2, waiting for transfers between devices, row_shifted(): return lax.ppermute(value, ('gz', 'xy'), pairs)  5.03 us
  transfers between devices with their start and end apart: 40, of which 25 were waited for; matrix products, arithmetic and copies ran while one was open for 1% of the time, Pallas kernels for 12%

profile of v12, /device:TPU:8, one launch (start us, length us, event | category | flops | bytes accessed | tf_op | source)
XLA Modules:
  0.0 241.0 jit_solution(17001606544981257825)
XLA Ops:
  5.4 4.7 %collective-permute-start.2 = (f32[2,48,640]{2,1,0:T(8,128)S(1)}, f32[2,48,640]{2,1,0:T(8,128)S(1)}, u32[]{:S(2)}, u32[]{:S(2)}) collective-permute-start(f32[2,48,640]{2,1,0:T(8,128)S(1)} %get-tuple-element.72), channel_id=1, source_target_pairs={{0,6},{2,8},{4,10},{6,12},{8,14},{10,0},{12,2},{14,4},{16,22},{18,... | collective-permute-start | bytes 737288 | tf_op jit(solution)/shard_map/ppermute | solution.py:127
  12.5 5.5 %collective-permute-start.4 = (f32[2,48,640]{2,1,0:T(8,128)S(1)}, f32[2,48,640]{2,1,0:T(8,128)S(1)}, u32[]{:S(2)}, u32[]{:S(2)}) collective-permute-start(f32[2,48,640]{2,1,0:T(8,128)S(1)} %get-tuple-element.74), channel_id=1, source_target_pairs={{0,8},{2,10},{4,12},{6,14},{8,0},{10,2},{12,4},{14,6},{16,24},{18,... | collective-permute-start | bytes 737288 | tf_op jit(solution)/shard_map/ppermute | solution.py:127
  22.1 7.7 %collective-permute-done.2.refs_3_ = f32[2,48,640]{2,1,0:T(8,128)S(1)} collective-permute-done((f32[2,48,640]{2,1,0:T(8,128)S(1)}, f32[2,48,640]{2,1,0:T(8,128)S(1)}, u32[]{:S(2)}, u32[]{:S(2)}) %collective-permute-start.2) | collective-permute-done | bytes 245792 | tf_op jit(solution)/shard_map/ppermute | solution.py:127
  29.8 5.0 %collective-permute-start.7 = (f32[2,48,640]{2,1,0:T(8,128)S(1)}, f32[2,48,640]{2,1,0:T(8,128)S(1)}, u32[]{:S(2)}, u32[]{:S(2)}) collective-permute-start(f32[2,48,640]{2,1,0:T(8,128)S(1)} %get-tuple-element.77), channel_id=1, source_target_pairs={{0,2},{2,4},{4,6},{6,8},{8,10},{10,12},{12,14},{14,0},{16,18},{18,... | collective-permute-start | bytes 737288 | tf_op jit(solution)/shard_map/ppermute | solution.py:127
  37.7 3.5 %collective-permute-done.4.refs_5_ = f32[2,48,640]{2,1,0:T(8,128)S(1)} collective-permute-done((f32[2,48,640]{2,1,0:T(8,128)S(1)}, f32[2,48,640]{2,1,0:T(8,128)S(1)}, u32[]{:S(2)}, u32[]{:S(2)}) %collective-permute-start.4) | collective-permute-done | bytes 245792 | tf_op jit(solution)/shard_map/ppermute | solution.py:127
  41.2 9.1 %collective-permute-done.5.refs_6_ = f32[2,48,640]{2,1,0:T(8,128)S(1)} collective-permute-done((f32[2,48,640]{2,1,0:T(8,128)S(1)}, f32[2,48,640]{2,1,0:T(8,128)S(1)}, u32[]{:S(2)}, u32[]{:S(2)}) %collective-permute-start.5) | collective-permute-done | bytes 245792 | tf_op jit(solution)/shard_map/ppermute | solution.py:127
  56.3 2.7 %shard_map.60 = (f32[16,48,640]{2,1,0:T(8,128)}, f32[3,48,640]{2,1,0:T(8,128)}, f32[3,48,640]{2,1,0:T(8,128)}, f32[6,48,640]{2,1,0:T(8,128)}, f32[6,48,640]{2,1,0:T(8,128)}, /*index=5*/f32[8,640]{1,0:T(8,128)S(1)}) custom-call(f32[8,2,40,640]{3,2,1,0:T(8,128)} %shard_map.58.refs_0_, s32[2]{0:T(128)S(1)} %pad_add_fusion.refs_0_.refs_1_, ...), custom_call_target="tpu_custom_call" | custom-call | tf_op jit(solution)/shard_map/pallas_call | solution.py:111
  59.1 6.2 %all-to-all-start = ((f32[8,2,40,640]{3,2,1,0:T(8,128)}), f32[8,2,40,640]{3,2,1,0:T(8,128)S(1)}, u32[]{:S(2)}, u32[]{:S(2)}) async-start(f32[8,2,40,640]{3,2,1,0:T(8,128)} %shard_map.61), calls=%async_computation | async-start | bytes 3276800 | tf_op jit(solution)/shard_map/all_to_all | solution.py:47
  65.3 4.5 %collective-permute-start.10 = (f32[3,48,640]{2,1,0:T(8,128)}, f32[3,48,640]{2,1,0:T(8,128)S(1)}, u32[]{:S(2)}, u32[]{:S(2)}) collective-permute-start(f32[3,48,640]{2,1,0:T(8,128)} %get-tuple-element.82), channel_id=1, source_target_pairs={{16,0},{18,2},{20,4},{22,6},{24,8},{26,10},{28,12},{30,14},{32,16}... | collective-permute-start | bytes 1105928 | tf_op jit(solution)/shard_map/ppermute | solution.py:28
  71.8 2.8 %collective-permute-start.11 = (f32[6,48,640]{2,1,0:T(8,128)S(1)}, f32[6,48,640]{2,1,0:T(8,128)S(1)}, u32[]{:S(2)}, u32[]{:S(2)}) collective-permute-start(f32[6,48,640]{2,1,0:T(8,128)S(1)} %copy-done.5), channel_id=1, source_target_pairs={{0,16},{2,18},{4,20},{6,22},{8,24},{10,26},{12,28},{14,30},{16,32}... | collective-permute-start | bytes 2211848 | tf_op jit(solution)/shard_map/ppermute | solution.py:28
  74.6 5.2 %collective-permute-start.12 = (f32[6,48,640]{2,1,0:T(8,128)S(1)}, f32[6,48,640]{2,1,0:T(8,128)S(1)}, u32[]{:S(2)}, u32[]{:S(2)}) collective-permute-start(f32[6,48,640]{2,1,0:T(8,128)S(1)} %copy-done.4), channel_id=1, source_target_pairs={{16,0},{18,2},{20,4},{22,6},{24,8},{26,10},{28,12},{30,14},{32,16}... | collective-permute-start | bytes 2211848 | tf_op jit(solution)/shard_map/ppermute | solution.py:28
  79.8 5.6 %collective-permute-done.9.refs_2_.refs_1_ = f32[3,48,640]{2,1,0:T(8,128)S(1)} collective-permute-done((f32[3,48,640]{2,1,0:T(8,128)S(1)}, f32[3,48,640]{2,1,0:T(8,128)S(1)}, u32[]{:S(2)}, u32[]{:S(2)}) %collective-permute-start.9) | collective-permute-done | bytes 368672 | tf_op jit(solution)/shard_map/ppermute | solution.py:28
  87.0 10.9 %shard_map.62 = (f32[75,48,640]{2,1,0:T(8,128)}, f32[41,48,640]{2,1,0:T(8,128)}, f32[17,48,640]{2,1,0:T(8,128)}, f32[9,48,640]{2,1,0:T(8,128)}, f32[5,48,640]{2,...) custom-call(s32[2]{0:T(128)S(1)} %pad_add_fusion.refs_0_.refs_1_, f32[16,48,640]{2,1,0:T(8,128)S(1)} %copy-done.3, ...), custom_call_target="tpu_custom_call" | custom-call | flops 10000000000 | bytes 30000000 | tf_op jit(solution)/shard_map/pallas_call | solution.py:111
  101.9 4.6 %all-to-all-done.refs_0_ = f32[8,2,40,640]{3,2,1,0:T(8,128)S(1)} async-done(((f32[8,2,40,640]{3,2,1,0:T(8,128)}), f32[8,2,40,640]{3,2,1,0:T(8,128)S(1)}, u32[]{:S(2)}, u32[]{:S(2)}) %all-to-all-start) | async-done | bytes 1638432 | tf_op jit(solution)/shard_map/all_to_all | solution.py:47
  106.5 3.7 %collective-permute-start.13 = (f32[2,40,640]{2,1,0:T(8,128)S(1)}, f32[2,40,640]{2,1,0:T(8,128)S(1)}, u32[]{:S(2)}, u32[]{:S(2)}) collective-permute-start(f32[2,40,640]{2,1,0:T(8,128)S(1)} %get-tuple-element.140), channel_id=1, source_target_pairs={{0,16},{2,18},{4,20},{6,22},{8,24},{10,26},{12,28},{14,30},{16,32}... | collective-permute-start | bytes 614408 | tf_op jit(solution)/shard_map/ppermute | solution.py:28
  110.2 4.7 %collective-permute-start.14 = (f32[2,40,640]{2,1,0:T(8,128)S(1)}, f32[2,40,640]{2,1,0:T(8,128)S(1)}, u32[]{:S(2)}, u32[]{:S(2)}) collective-permute-start(f32[2,40,640]{2,1,0:T(8,128)S(1)} %get-tuple-element.139), channel_id=1, source_target_pairs={{16,0},{18,2},{20,4},{22,6},{24,8},{26,10},{28,12},{30,14},{32,16}... | collective-permute-start | bytes 614408 | tf_op jit(solution)/shard_map/ppermute | solution.py:28
  114.9 7.0 %shard_map.65 = (f32[16,48,640]{2,1,0:T(8,128)S(1)}, f32[16,48,640]{2,1,0:T(8,128)S(1)}, f32[16,48,640]{2,1,0:T(8,128)S(1)}, f32[16,48,640]{2,1,0:T(8,128)S(1)},...) custom-call(f32[16,40,640]{2,1,0:T(8,128)S(1)} %bitcast.12, ...), custom_call_target="tpu_custom_call" | custom-call | flops 8000000000 | bytes 24000000 | tf_op jit(solution)/shard_map/pallas_call | solution.py:111
  125.3 6.0 %collective-permute-start.16 = (f32[2,40,640]{2,1,0:T(8,128)S(1)}, f32[2,40,640]{2,1,0:T(8,128)S(1)}, u32[]{:S(2)}, u32[]{:S(2)}) collective-permute-start(f32[2,40,640]{2,1,0:T(8,128)S(1)} %get-tuple-element.98), channel_id=1, source_target_pairs={{16,0},{18,2},{20,4},{22,6},{24,8},{26,10},{28,12},{30,14},{32,16}... | collective-permute-start | bytes 614408 | tf_op jit(solution)/shard_map/ppermute | solution.py:28
  141.7 4.3 %collective-permute-done.18.refs_2_ = f32[4,8,640]{2,1,0:T(8,128)S(1)} collective-permute-done((f32[4,8,640]{2,1,0:T(8,128)S(1)}, f32[4,8,640]{2,1,0:T(8,128)S(1)}, u32[]{:S(2)}, u32[]{:S(2)}) %collective-permute-start.18) | collective-permute-done | bytes 81952 | tf_op jit(solution)/shard_map/ppermute | solution.py:38
  147.3 3.6 %all-to-all-start.1 = ((f32[8,3,32,640]{3,2,1,0:T(8,128)}), f32[8,3,32,640]{3,2,1,0:T(8,128)S(1)}, u32[]{:S(2)}, u32[]{:S(2)}) async-start(f32[8,3,32,640]{3,2,1,0:T(8,128)} %get-tuple-element.105), calls=%async_computation.1 | async-start | bytes 3932160 | tf_op jit(solution)/shard_map/all_to_all | solution.py:47
  152.9 6.5 %collective-permute-start.20 = (f32[2,48,640]{2,1,0:T(8,128)S(1)}, f32[2,48,640]{2,1,0:T(8,128)S(1)}, u32[]{:S(2)}, u32[]{:S(2)}) collective-permute-start(f32[2,48,640]{2,1,0:T(8,128)S(1)} %get-tuple-element.108), channel_id=1, source_target_pairs={{16,0},{18,2},{20,4},{22,6},{24,8},{26,10},{28,12},{30,14},{32,16}... | collective-permute-start | bytes 737288 | tf_op jit(solution)/shard_map/ppermute | solution.py:28
  164.8 3.9 %collective-permute-start.21 = (f32[2,40,640]{2,1,0:T(8,128)S(1)}, f32[2,40,640]{2,1,0:T(8,128)S(1)}, u32[]{:S(2)}, u32[]{:S(2)}) collective-permute-start(f32[2,40,640]{2,1,0:T(8,128)S(1)} %get-tuple-element.116), channel_id=1, source_target_pairs={{0,16},{2,18},{4,20},{6,22},{8,24},{10,26},{12,28},{14,30},{16,32}... | collective-permute-start | bytes 614408 | tf_op jit(solution)/shard_map/ppermute | solution.py:28
  168.7 4.5 %collective-permute-start.22 = (f32[2,40,640]{2,1,0:T(8,128)S(1)}, f32[2,40,640]{2,1,0:T(8,128)S(1)}, u32[]{:S(2)}, u32[]{:S(2)}) collective-permute-start(f32[2,40,640]{2,1,0:T(8,128)S(1)} %get-tuple-element.117), channel_id=1, source_target_pairs={{16,0},{18,2},{20,4},{22,6},{24,8},{26,10},{28,12},{30,14},{32,16}... | collective-permute-start | bytes 614408 | tf_op jit(solution)/shard_map/ppermute | solution.py:28
  177.6 4.0 %collective-permute-start.23 = (f32[1,40,640]{2,1,0:T(8,128)S(1)}, f32[1,40,640]{2,1,0:T(8,128)S(1)}, u32[]{:S(2)}, u32[]{:S(2)}) collective-permute-start(f32[1,40,640]{2,1,0:T(8,128)S(1)} %get-tuple-element.121), channel_id=1, source_target_pairs={{0,16},{2,18},{4,20},{6,22},{8,24},{10,26},{12,28},{14,30},{16,32}... | collective-permute-start | bytes 307208 | tf_op jit(solution)/shard_map/ppermute | solution.py:28
  181.6 4.5 %collective-permute-start.24 = (f32[1,40,640]{2,1,0:T(8,128)S(1)}, f32[1,40,640]{2,1,0:T(8,128)S(1)}, u32[]{:S(2)}, u32[]{:S(2)}) collective-permute-start(f32[1,40,640]{2,1,0:T(8,128)S(1)} %get-tuple-element.121), channel_id=1, source_target_pairs={{16,0},{18,2},{20,4},{22,6},{24,8},{26,10},{28,12},{30,14},{32,16}... | collective-permute-start | bytes 307208 | tf_op jit(solution)/shard_map/ppermute | solution.py:28
  188.6 3.8 %collective-permute-start.25 = (f32[1,40,640]{2,1,0:T(8,128)S(1)}, f32[1,40,640]{2,1,0:T(8,128)S(1)}, u32[]{:S(2)}, u32[]{:S(2)}) collective-permute-start(f32[1,40,640]{2,1,0:T(8,128)S(1)} %get-tuple-element.124), channel_id=1, source_target_pairs={{0,16},{2,18},{4,20},{6,22},{8,24},{10,26},{12,28},{14,30},{16,32}... | collective-permute-start | bytes 307208 | tf_op jit(solution)/shard_map/ppermute | solution.py:28
  192.4 4.5 %collective-permute-start.26 = (f32[1,40,640]{2,1,0:T(8,128)S(1)}, f32[1,40,640]{2,1,0:T(8,128)S(1)}, u32[]{:S(2)}, u32[]{:S(2)}) collective-permute-start(f32[1,40,640]{2,1,0:T(8,128)S(1)} %get-tuple-element.124), channel_id=1, source_target_pairs={{16,0},{18,2},{20,4},{22,6},{24,8},{26,10},{28,12},{30,14},{32,16}... | collective-permute-start | bytes 307208 | tf_op jit(solution)/shard_map/ppermute | solution.py:28
  204.2 6.3 %collective-permute-start.29 = (f32[1,32,640]{2,1,0:T(8,128)S(1)}, f32[1,32,640]{2,1,0:T(8,128)S(1)}, u32[]{:S(2)}, u32[]{:S(2)}) collective-permute-start(f32[1,32,640]{2,1,0:T(8,128)S(1)} %get-tuple-element.128), channel_id=1, source_target_pairs={{0,32},{2,34},{4,36},{6,38},{8,40},{10,42},{12,44},{14,46},{16,48}... | collective-permute-start | bytes 245768 | tf_op jit(solution)/shard_map/ppermute | solution.py:28
  212.9 5.4 %collective-permute-done.30.refs_4_ = f32[1,32,640]{2,1,0:T(8,128)S(1)} collective-permute-done((f32[1,32,640]{2,1,0:T(8,128)S(1)}, f32[1,32,640]{2,1,0:T(8,128)S(1)}, u32[]{:S(2)}, u32[]{:S(2)}) %collective-permute-start.30) | collective-permute-done | bytes 81952 | tf_op jit(solution)/shard_map/ppermute | solution.py:28
  219.1 3.9 %collective-permute-start.31 = (f32[32,640]{1,0:T(8,128)S(1)}, f32[32,640]{1,0:T(8,128)S(1)}, u32[]{:S(2)}, u32[]{:S(2)}) collective-permute-start(f32[32,640]{1,0:T(8,128)S(1)} %get-tuple-element.132), channel_id=1, source_target_pairs={{0,6},{2,8},{4,10},{6,12},{8,14},{10,0},{12,2},{14,4},{16,22},{18,... | collective-permute-start | bytes 245768 | tf_op jit(solution)/shard_map/ppermute | solution.py:127
  224.2 5.6 %collective-permute-start.33 = (f32[32,640]{1,0:T(8,128)S(1)}, f32[32,640]{1,0:T(8,128)S(1)}, u32[]{:S(2)}, u32[]{:S(2)}) collective-permute-start(f32[32,640]{1,0:T(8,128)S(1)} %get-tuple-element.134), channel_id=1, source_target_pairs={{0,8},{2,10},{4,12},{6,14},{8,0},{10,2},{12,4},{14,6},{16,24},{18,... | collective-permute-start | bytes 245768 | tf_op jit(solution)/shard_map/ppermute | solution.py:127
  230.7 3.3 %collective-permute-start.35 = (f32[32,640]{1,0:T(8,128)S(1)}, f32[32,640]{1,0:T(8,128)S(1)}, u32[]{:S(2)}, u32[]{:S(2)}) collective-permute-start(f32[32,640]{1,0:T(8,128)S(1)} %get-tuple-element.136), channel_id=1, source_target_pairs={{0,12},{2,14},{4,0},{6,2},{8,4},{10,6},{12,8},{14,10},{16,28},{18,... | collective-permute-start | bytes 245768 | tf_op jit(solution)/shard_map/ppermute | solution.py:127
  (96 shorter events, 76.1 us)
Async XLA Ops:
  5.4 24.4 %collective-permute-start.2 = (f32[2,48,640]{2,1,0:T(8,128)S(1)}, f32[2,48,640]{2,1,0:T(8,128)S(1)}, u32[]{:S(2)}, u32[]{:S(2)}) collective-permute-start(f32[2,48,640]{2,1,0:T(8,128)S(1)} %get-tuple-element.72), channel_id=1, source_target_pairs={{0,6},{2,8},{4,10},{6,12},{8,14},{10,0},{12,2},{14,4},{16,22},{18,... | collective-permute-start | bytes 737288 | tf_op jit(solution)/shard_map/ppermute | solution.py:127
  10.2 24.7 %collective-permute-start.3 = (f32[2,48,640]{2,1,0:T(8,128)S(1)}, f32[2,48,640]{2,1,0:T(8,128)S(1)}, u32[]{:S(2)}, u32[]{:S(2)}) collective-permute-start(f32[2,48,640]{2,1,0:T(8,128)S(1)} %get-tuple-element.73), channel_id=1, source_target_pairs={{0,10},{2,12},{4,14},{6,0},{8,2},{10,4},{12,6},{14,8},{16,26},{18,... | collective-permute-start | bytes 737288 | tf_op jit(solution)/shard_map/ppermute | solution.py:127
  12.4 7.1 %collective-permute-start = (f32[2,8,640]{2,1,0:T(8,128)S(1)}, f32[2,8,640]{2,1,0:T(8,128)S(1)}, u32[]{:S(2)}, u32[]{:S(2)}) collective-permute-start(f32[2,8,640]{2,1,0:T(8,128)S(1)} %slice_select_fusion), channel_id=1, source_target_pairs={{0,1},{1,0},{2,3},{3,2},{4,5},{5,4},{6,7},{7,6},{8,9},{9,8},{10,11... | collective-permute-start | bytes 122888 | tf_op jit(solution)/shard_map/ppermute | solution.py:581
  12.5 28.7 %collective-permute-start.4 = (f32[2,48,640]{2,1,0:T(8,128)S(1)}, f32[2,48,640]{2,1,0:T(8,128)S(1)}, u32[]{:S(2)}, u32[]{:S(2)}) collective-permute-start(f32[2,48,640]{2,1,0:T(8,128)S(1)} %get-tuple-element.74), channel_id=1, source_target_pairs={{0,8},{2,10},{4,12},{6,14},{8,0},{10,2},{12,4},{14,6},{16,24},{18,... | collective-permute-start | bytes 737288 | tf_op jit(solution)/shard_map/ppermute | solution.py:127
  18.0 32.3 %collective-permute-start.5 = (f32[2,48,640]{2,1,0:T(8,128)S(1)}, f32[2,48,640]{2,1,0:T(8,128)S(1)}, u32[]{:S(2)}, u32[]{:S(2)}) collective-permute-start(f32[2,48,640]{2,1,0:T(8,128)S(1)} %get-tuple-element.75), channel_id=1, source_target_pairs={{0,4},{2,6},{4,8},{6,10},{8,12},{10,14},{12,0},{14,2},{16,20},{18,... | collective-permute-start | bytes 737288 | tf_op jit(solution)/shard_map/ppermute | solution.py:127
  19.4 32.6 %collective-permute-start.6 = (f32[2,48,640]{2,1,0:T(8,128)S(1)}, f32[2,48,640]{2,1,0:T(8,128)S(1)}, u32[]{:S(2)}, u32[]{:S(2)}) collective-permute-start(f32[2,48,640]{2,1,0:T(8,128)S(1)} %get-tuple-element.76), channel_id=1, source_target_pairs={{0,12},{2,14},{4,0},{6,2},{8,4},{10,6},{12,8},{14,10},{16,28},{18,... | collective-permute-start | bytes 737288 | tf_op jit(solution)/shard_map/ppermute | solution.py:127
  29.8 24.8 %collective-permute-start.7 = (f32[2,48,640]{2,1,0:T(8,128)S(1)}, f32[2,48,640]{2,1,0:T(8,128)S(1)}, u32[]{:S(2)}, u32[]{:S(2)}) collective-permute-start(f32[2,48,640]{2,1,0:T(8,128)S(1)} %get-tuple-element.77), channel_id=1, source_target_pairs={{0,2},{2,4},{4,6},{6,8},{8,10},{10,12},{12,14},{14,0},{16,18},{18,... | collective-permute-start | bytes 737288 | tf_op jit(solution)/shard_map/ppermute | solution.py:127
  34.9 21.5 %collective-permute-start.8 = (f32[2,48,640]{2,1,0:T(8,128)S(1)}, f32[2,48,640]{2,1,0:T(8,128)S(1)}, u32[]{:S(2)}, u32[]{:S(2)}) collective-permute-start(f32[2,48,640]{2,1,0:T(8,128)S(1)} %get-tuple-element.78), channel_id=1, source_target_pairs={{0,14},{2,0},{4,2},{6,4},{8,6},{10,8},{12,10},{14,12},{16,30},{18,... | collective-permute-start | bytes 737288 | tf_op jit(solution)/shard_map/ppermute | solution.py:127
  59.1 47.4 %all-to-all-start = ((f32[8,2,40,640]{3,2,1,0:T(8,128)}), f32[8,2,40,640]{3,2,1,0:T(8,128)S(1)}, u32[]{:S(2)}, u32[]{:S(2)}) async-start(f32[8,2,40,640]{3,2,1,0:T(8,128)} %shard_map.61), calls=%async_computation | async-start | bytes 3276800 | tf_op jit(solution)/shard_map/all_to_all | solution.py:47
  65.3 14.5 %collective-permute-start.10 = (f32[3,48,640]{2,1,0:T(8,128)}, f32[3,48,640]{2,1,0:T(8,128)S(1)}, u32[]{:S(2)}, u32[]{:S(2)}) collective-permute-start(f32[3,48,640]{2,1,0:T(8,128)} %get-tuple-element.82), channel_id=1, source_target_pairs={{16,0},{18,2},{20,4},{22,6},{24,8},{26,10},{28,12},{30,14},{32,16}... | collective-permute-start | bytes 1105928 | tf_op jit(solution)/shard_map/ppermute | solution.py:28
  69.9 15.5 %collective-permute-start.9 = (f32[3,48,640]{2,1,0:T(8,128)S(1)}, f32[3,48,640]{2,1,0:T(8,128)S(1)}, u32[]{:S(2)}, u32[]{:S(2)}) collective-permute-start(f32[3,48,640]{2,1,0:T(8,128)S(1)} %copy-done.6), channel_id=1, source_target_pairs={{0,16},{2,18},{4,20},{6,22},{8,24},{10,26},{12,28},{14,30},{16,32}... | collective-permute-start | bytes 1105928 | tf_op jit(solution)/shard_map/ppermute | solution.py:28
  71.8 27.3 %collective-permute-start.11 = (f32[6,48,640]{2,1,0:T(8,128)S(1)}, f32[6,48,640]{2,1,0:T(8,128)S(1)}, u32[]{:S(2)}, u32[]{:S(2)}) collective-permute-start(f32[6,48,640]{2,1,0:T(8,128)S(1)} %copy-done.5), channel_id=1, source_target_pairs={{0,16},{2,18},{4,20},{6,22},{8,24},{10,26},{12,28},{14,30},{16,32}... | collective-permute-start | bytes 2211848 | tf_op jit(solution)/shard_map/ppermute | solution.py:28
  74.6 24.5 %collective-permute-start.12 = (f32[6,48,640]{2,1,0:T(8,128)S(1)}, f32[6,48,640]{2,1,0:T(8,128)S(1)}, u32[]{:S(2)}, u32[]{:S(2)}) collective-permute-start(f32[6,48,640]{2,1,0:T(8,128)S(1)} %copy-done.4), channel_id=1, source_target_pairs={{16,0},{18,2},{20,4},{22,6},{24,8},{26,10},{28,12},{30,14},{32,16}... | collective-permute-start | bytes 2211848 | tf_op jit(solution)/shard_map/ppermute | solution.py:28
  106.5 15.4 %collective-permute-start.13 = (f32[2,40,640]{2,1,0:T(8,128)S(1)}, f32[2,40,640]{2,1,0:T(8,128)S(1)}, u32[]{:S(2)}, u32[]{:S(2)}) collective-permute-start(f32[2,40,640]{2,1,0:T(8,128)S(1)} %get-tuple-element.140), channel_id=1, source_target_pairs={{0,16},{2,18},{4,20},{6,22},{8,24},{10,26},{12,28},{14,30},{16,32}... | collective-permute-start | bytes 614408 | tf_op jit(solution)/shard_map/ppermute | solution.py:28
  110.2 11.7 %collective-permute-start.14 = (f32[2,40,640]{2,1,0:T(8,128)S(1)}, f32[2,40,640]{2,1,0:T(8,128)S(1)}, u32[]{:S(2)}, u32[]{:S(2)}) collective-permute-start(f32[2,40,640]{2,1,0:T(8,128)S(1)} %get-tuple-element.139), channel_id=1, source_target_pairs={{16,0},{18,2},{20,4},{22,6},{24,8},{26,10},{28,12},{30,14},{32,16}... | collective-permute-start | bytes 614408 | tf_op jit(solution)/shard_map/ppermute | solution.py:28
  123.3 9.8 %collective-permute-start.15 = (f32[2,40,640]{2,1,0:T(8,128)S(1)}, f32[2,40,640]{2,1,0:T(8,128)S(1)}, u32[]{:S(2)}, u32[]{:S(2)}) collective-permute-start(f32[2,40,640]{2,1,0:T(8,128)S(1)} %get-tuple-element.97), channel_id=1, source_target_pairs={{0,16},{2,18},{4,20},{6,22},{8,24},{10,26},{12,28},{14,30},{16,32}... | collective-permute-start | bytes 614408 | tf_op jit(solution)/shard_map/ppermute | solution.py:28
  125.3 9.3 %collective-permute-start.16 = (f32[2,40,640]{2,1,0:T(8,128)S(1)}, f32[2,40,640]{2,1,0:T(8,128)S(1)}, u32[]{:S(2)}, u32[]{:S(2)}) collective-permute-start(f32[2,40,640]{2,1,0:T(8,128)S(1)} %get-tuple-element.98), channel_id=1, source_target_pairs={{16,0},{18,2},{20,4},{22,6},{24,8},{26,10},{28,12},{30,14},{32,16}... | collective-permute-start | bytes 614408 | tf_op jit(solution)/shard_map/ppermute | solution.py:28
  147.3 89.9 %all-to-all-start.1 = ((f32[8,3,32,640]{3,2,1,0:T(8,128)}), f32[8,3,32,640]{3,2,1,0:T(8,128)S(1)}, u32[]{:S(2)}, u32[]{:S(2)}) async-start(f32[8,3,32,640]{3,2,1,0:T(8,128)} %get-tuple-element.105), calls=%async_computation.1 | async-start | bytes 3932160 | tf_op jit(solution)/shard_map/all_to_all | solution.py:47
  151.0 11.1 %collective-permute-start.19 = (f32[2,48,640]{2,1,0:T(8,128)S(1)}, f32[2,48,640]{2,1,0:T(8,128)S(1)}, u32[]{:S(2)}, u32[]{:S(2)}) collective-permute-start(f32[2,48,640]{2,1,0:T(8,128)S(1)} %get-tuple-element.107), channel_id=1, source_target_pairs={{0,16},{2,18},{4,20},{6,22},{8,24},{10,26},{12,28},{14,30},{16,32}... | collective-permute-start | bytes 737288 | tf_op jit(solution)/shard_map/ppermute | solution.py:28
  152.9 10.2 %collective-permute-start.20 = (f32[2,48,640]{2,1,0:T(8,128)S(1)}, f32[2,48,640]{2,1,0:T(8,128)S(1)}, u32[]{:S(2)}, u32[]{:S(2)}) collective-permute-start(f32[2,48,640]{2,1,0:T(8,128)S(1)} %get-tuple-element.108), channel_id=1, source_target_pairs={{16,0},{18,2},{20,4},{22,6},{24,8},{26,10},{28,12},{30,14},{32,16}... | collective-permute-start | bytes 737288 | tf_op jit(solution)/shard_map/ppermute | solution.py:28
  164.8 10.2 %collective-permute-start.21 = (f32[2,40,640]{2,1,0:T(8,128)S(1)}, f32[2,40,640]{2,1,0:T(8,128)S(1)}, u32[]{:S(2)}, u32[]{:S(2)}) collective-permute-start(f32[2,40,640]{2,1,0:T(8,128)S(1)} %get-tuple-element.116), channel_id=1, source_target_pairs={{0,16},{2,18},{4,20},{6,22},{8,24},{10,26},{12,28},{14,30},{16,32}... | collective-permute-start | bytes 614408 | tf_op jit(solution)/shard_map/ppermute | solution.py:28
  168.7 7.8 %collective-permute-start.22 = (f32[2,40,640]{2,1,0:T(8,128)S(1)}, f32[2,40,640]{2,1,0:T(8,128)S(1)}, u32[]{:S(2)}, u32[]{:S(2)}) collective-permute-start(f32[2,40,640]{2,1,0:T(8,128)S(1)} %get-tuple-element.117), channel_id=1, source_target_pairs={{16,0},{18,2},{20,4},{22,6},{24,8},{26,10},{28,12},{30,14},{32,16}... | collective-permute-start | bytes 614408 | tf_op jit(solution)/shard_map/ppermute | solution.py:28
  173.2 28.1 %collective-permute-start.28 = (f32[3,48,640]{2,1,0:T(8,128)S(1)}, f32[3,48,640]{2,1,0:T(8,128)S(1)}, u32[]{:S(2)}, u32[]{:S(2)}) collective-permute-start(f32[3,48,640]{2,1,0:T(8,128)S(1)} %get-tuple-element.125), channel_id=1, source_target_pairs={{0,16},{2,18},{4,20},{6,22},{8,24},{10,26},{12,28},{14,30},{16,0},... | collective-permute-start | bytes 1105928 | tf_op jit(solution)/shard_map/ppermute | solution.py:43
  177.6 9.3 %collective-permute-start.23 = (f32[1,40,640]{2,1,0:T(8,128)S(1)}, f32[1,40,640]{2,1,0:T(8,128)S(1)}, u32[]{:S(2)}, u32[]{:S(2)}) collective-permute-start(f32[1,40,640]{2,1,0:T(8,128)S(1)} %get-tuple-element.121), channel_id=1, source_target_pairs={{0,16},{2,18},{4,20},{6,22},{8,24},{10,26},{12,28},{14,30},{16,32}... | collective-permute-start | bytes 307208 | tf_op jit(solution)/shard_map/ppermute | solution.py:28
  188.6 9.1 %collective-permute-start.25 = (f32[1,40,640]{2,1,0:T(8,128)S(1)}, f32[1,40,640]{2,1,0:T(8,128)S(1)}, u32[]{:S(2)}, u32[]{:S(2)}) collective-permute-start(f32[1,40,640]{2,1,0:T(8,128)S(1)} %get-tuple-element.124), channel_id=1, source_target_pairs={{0,16},{2,18},{4,20},{6,22},{8,24},{10,26},{12,28},{14,30},{16,32}... | collective-permute-start | bytes 307208 | tf_op jit(solution)/shard_map/ppermute | solution.py:28
  204.2 8.7 %collective-permute-start.29 = (f32[1,32,640]{2,1,0:T(8,128)S(1)}, f32[1,32,640]{2,1,0:T(8,128)S(1)}, u32[]{:S(2)}, u32[]{:S(2)}) collective-permute-start(f32[1,32,640]{2,1,0:T(8,128)S(1)} %get-tuple-element.128), channel_id=1, source_target_pairs={{0,32},{2,34},{4,36},{6,38},{8,40},{10,42},{12,44},{14,46},{16,48}... | collective-permute-start | bytes 245768 | tf_op jit(solution)/shard_map/ppermute | solution.py:28
  210.5 7.8 %collective-permute-start.30 = (f32[1,32,640]{2,1,0:T(8,128)S(1)}, f32[1,32,640]{2,1,0:T(8,128)S(1)}, u32[]{:S(2)}, u32[]{:S(2)}) collective-permute-start(f32[1,32,640]{2,1,0:T(8,128)S(1)} %get-tuple-element.128), channel_id=1, source_target_pairs={{32,0},{34,2},{36,4},{38,6},{40,8},{42,10},{44,12},{46,14},{48,16}... | collective-permute-start | bytes 245768 | tf_op jit(solution)/shard_map/ppermute | solution.py:28
  219.1 14.9 %collective-permute-start.31 = (f32[32,640]{1,0:T(8,128)S(1)}, f32[32,640]{1,0:T(8,128)S(1)}, u32[]{:S(2)}, u32[]{:S(2)}) collective-permute-start(f32[32,640]{1,0:T(8,128)S(1)} %get-tuple-element.132), channel_id=1, source_target_pairs={{0,6},{2,8},{4,10},{6,12},{8,14},{10,0},{12,2},{14,4},{16,22},{18,... | collective-permute-start | bytes 245768 | tf_op jit(solution)/shard_map/ppermute | solution.py:127
  223.0 11.7 %collective-permute-start.32 = (f32[32,640]{1,0:T(8,128)S(1)}, f32[32,640]{1,0:T(8,128)S(1)}, u32[]{:S(2)}, u32[]{:S(2)}) collective-permute-start(f32[32,640]{1,0:T(8,128)S(1)} %get-tuple-element.133), channel_id=1, source_target_pairs={{0,10},{2,12},{4,14},{6,0},{8,2},{10,4},{12,6},{14,8},{16,26},{18,... | collective-permute-start | bytes 245768 | tf_op jit(solution)/shard_map/ppermute | solution.py:127
  224.2 15.1 %collective-permute-start.33 = (f32[32,640]{1,0:T(8,128)S(1)}, f32[32,640]{1,0:T(8,128)S(1)}, u32[]{:S(2)}, u32[]{:S(2)}) collective-permute-start(f32[32,640]{1,0:T(8,128)S(1)} %get-tuple-element.134), channel_id=1, source_target_pairs={{0,8},{2,10},{4,12},{6,14},{8,0},{10,2},{12,4},{14,6},{16,24},{18,... | collective-permute-start | bytes 245768 | tf_op jit(solution)/shard_map/ppermute | solution.py:127
  229.8 9.5 %collective-permute-start.34 = (f32[32,640]{1,0:T(8,128)S(1)}, f32[32,640]{1,0:T(8,128)S(1)}, u32[]{:S(2)}, u32[]{:S(2)}) collective-permute-start(f32[32,640]{1,0:T(8,128)S(1)} %get-tuple-element.135), channel_id=1, source_target_pairs={{0,4},{2,6},{4,8},{6,10},{8,12},{10,14},{12,0},{14,2},{16,20},{18,... | collective-permute-start | bytes 245768 | tf_op jit(solution)/shard_map/ppermute | solution.py:127
  230.7 8.7 %collective-permute-start.35 = (f32[32,640]{1,0:T(8,128)S(1)}, f32[32,640]{1,0:T(8,128)S(1)}, u32[]{:S(2)}, u32[]{:S(2)}) collective-permute-start(f32[32,640]{1,0:T(8,128)S(1)} %get-tuple-element.136), channel_id=1, source_target_pairs={{0,12},{2,14},{4,0},{6,2},{8,4},{10,6},{12,8},{14,10},{16,28},{18,... | collective-permute-start | bytes 245768 | tf_op jit(solution)/shard_map/ppermute | solution.py:127
  (17 other events, 176.2 us)
